TPU v7x, 32 devices: a whole 2x2x4 slice. The times are simulated.
32 devices in a mesh: tok: 8 (over z, x), chan: 4 (over y, core).
Axes of the slice: x: 2, y: 2, z: 4, core: 2. Of those that a mesh axis runs over, the one named last changes fastest.
Arguments:
- query: bfloat16 [2048, 8192], P('tok', 'chan'), may hold values from -12 to 12
- key_in: bfloat16 [2048, 8192], P('tok', 'chan'), may hold values from -6 to 6
- value_in: bfloat16 [2048, 8192], P('tok', 'chan'), may hold values from -6 to 6
- filter_store: bfloat16 [2048, 8192], P('tok', 'chan'), may hold values from -0.125 to 0.125
- lag_of_block: int32 [8], replicated, may hold values from 0 to 7, each once
- skip: float32 [8192], P('chan'), may hold values from 0.3 to 1.5
- out_gain: float32 [8192], P('chan'), may hold values from 0.1 to 1.9
Outputs:
- output: float32 [2048, 8192], P('tok', 'chan')
Inputs may be any that keep to these rules, and one draw needn't show every extreme that they name: `lag_of_block`: each of the 8 lag blocks is held by exactly one stored block.
All inputs are finite; a program needn't handle non-finite values.
Results may differ from a plain program's by a relative error of at most 0.0029.
Values may be sent and summed in bfloat16 or wider, within the bound.
No kernel may reach another device: no remote copies, remote signals or barrier semaphores. Data moves between devices by JAX's collectives and lax.ppermute only.
A program may use at most 192 MiB of HBM per device.

v0:
```python
import math

import jax
import jax.numpy as jnp
from jax import lax
from jax.sharding import PartitionSpec as P

HIGHEST = lax.Precision.HIGHEST
THREE_PASS = lax.Precision.HIGH


def forward_tables(width):
    period = 2 * width
    freq = lax.broadcasted_iota(jnp.int32, (width + 1, width), 0)
    place = lax.broadcasted_iota(jnp.int32, (width + 1, width), 1)
    angle = 2.0 * math.pi / period * (freq * place % period).astype(jnp.float32)
    return (jnp.cos(angle), jnp.sin(angle))


def inverse_tables(width):
    period = 2 * width
    place = lax.broadcasted_iota(jnp.int32, (period, width + 1), 0)
    freq = lax.broadcasted_iota(jnp.int32, (period, width + 1), 1)
    angle = 2.0 * math.pi / period * (freq * place % period).astype(jnp.float32)
    weight = jnp.where((freq == 0) | (freq == width), 1.0, 2.0) / period
    return (weight * jnp.cos(angle), weight * jnp.sin(angle))


def spectra(cos_tab, sin_tab, blocks):
    real_part = jnp.einsum("fp,kpc->kfc", cos_tab, blocks, precision=THREE_PASS)
    imag_part = -jnp.einsum("fp,kpc->kfc", sin_tab, blocks, precision=THREE_PASS)
    return (real_part, imag_part)


def accumulate(filt_re, filt_im, stored, lag_of_block, in_re, in_im, my_block):
    count = lag_of_block.shape[0]
    onehot = (stored[:, None] == jnp.arange(count, dtype=jnp.int32)[None, :]).astype(jnp.int32)
    lags = jnp.sum(onehot * lag_of_block[None, :], axis=1)
    results = []
    for offset in range(2):
        source = my_block - offset - lags
        valid = (source >= 0).astype(jnp.float32)[:, None, None]
        picked = jnp.clip(source, 0, count - 1)
        src_re = jnp.take(in_re, picked, axis=0)
        src_im = jnp.take(in_im, picked, axis=0)
        prod_re = jnp.sum((filt_re * src_re - filt_im * src_im) * valid, axis=0)
        prod_im = jnp.sum((filt_re * src_im + filt_im * src_re) * valid, axis=0)
        results.append(prod_re)
        results.append(prod_im)
    return tuple(results)


def local(query, key_in, value_in, filter_store, lag_of_block, skip, out_gain):
    width = query.shape[0]
    columns = query.shape[1]
    gated = (key_in.astype(jnp.float32) * value_in.astype(jnp.float32)).astype(jnp.bfloat16)
    my_block = lax.axis_index("tok")
    cos_tab, sin_tab = forward_tables(width)
    inv_cos, inv_sin = inverse_tables(width)
    every_input = lax.all_gather(gated, "tok", axis=0, tiled=True)
    in_blocks = every_input.astype(jnp.float32).reshape(-1, width, columns)
    in_re, in_im = spectra(cos_tab, sin_tab, in_blocks)
    blocks = (
        lax.all_gather(filter_store, "tok", axis=0, tiled=True)
        .astype(jnp.float32)
        .reshape(-1, width, columns)
    )
    filt_re, filt_im = spectra(cos_tab, sin_tab, blocks)
    stored = jnp.arange(blocks.shape[0], dtype=jnp.int32)
    sums = accumulate(filt_re, filt_im, stored, lag_of_block, in_re, in_im, my_block)
    low_re, low_im, high_re, high_im = sums
    conv = jnp.dot(inv_cos[:width], low_re, precision=HIGHEST) - jnp.dot(
        inv_sin[:width], low_im, precision=HIGHEST
    )
    conv = (
        conv
        + jnp.dot(inv_cos[width:], high_re, precision=HIGHEST)
        - jnp.dot(inv_sin[width:], high_im, precision=HIGHEST)
    )
    pre = query.astype(jnp.float32) * (conv + skip[None, :] * gated.astype(jnp.float32))
    total = lax.psum(jnp.sum(pre * pre, axis=1), "chan")
    mean_sq = total / (columns * lax.axis_size("chan"))
    return out_gain[None, :] * pre * lax.rsqrt(mean_sq + 1e-06)[:, None]


def solution(mesh):
    in_specs = (
        P("tok", "chan"),
        P("tok", "chan"),
        P("tok", "chan"),
        P("tok", "chan"),
        P(),
        P("chan"),
        P("chan"),
    )
    out_specs = P("tok", "chan")
    return jax.shard_map(local, mesh=mesh, in_specs=in_specs, out_specs=out_specs, check_vma=False)
```

profile of v0, /device:TPU:0, one launch (start us, length us, event | category | flops | bytes accessed | tf_op | source)
XLA Modules:
  0.0 347.0 jit_solution(7580376304731541523)
XLA Ops:
  6.5 2.9 multiply_convert_fusion
  9.4 0.0 all-gather.5.cloned.1.call-update
  9.5 0.0 all-gather.3.cloned.1.call-start
  9.5 0.7 all-gather.3.cloned.1.call-update
  10.2 0.8 select_reduce_fusion
  11.0 3.1 sine_multiply_fusion
  14.2 123.1 %all-gather.5.cloned.1.call-done = bf16[2048,2048]{1,0:T(8,128)(2,1)} async-done(((bf16[256,2048]{1,0:T(8,128)(2,1)}), bf16[2048,2048]{1,0:T(8,128)(2,1)}) %all-gather.5.cloned.1.call-update) | async-done | bytes 8388624 | tf_op jit(solution)/shard_map/all_gather | solution.py:60
  137.2 18.3 %convolution_bitcast_fusion = f32[8,257,2048]{2,1,0:T(8,128)} fusion(bf16[8,256,2048]{2,1,0:T(8,128)(2,1)} %bitcast.68), kind=kOutput, calls=%fused_computation.25 | convolution fusion | flops 6468537856 | bytes 25231360 | tf_op jit(solution)/shard_map/fp,kpc->kfc/dot_general | solution.py:30
  155.5 13.7 %gather_fusion = f32[8,257,2048]{2,1,0:T(8,128)} fusion(f32[8,257,2048]{2,1,0:T(8,128)} %convolution_bitcast_fusion, s32[1024]{0:T(1024)S(1)} %get-tuple-element.25), kind=kCustom, calls=%fused_computation.clone | custom fusion | bytes 33685536 | tf_op jit(solution)/shard_map/jit(_take)/gather | solution.py:44
  169.2 18.1 %negate_bitcast_fusion = f32[8,257,2048]{2,1,0:T(8,128)} fusion(bf16[8,256,2048]{2,1,0:T(8,128)(2,1)} %bitcast.69), kind=kOutput, calls=%fused_computation.24 | convolution fusion | flops 6472748544 | bytes 25231360 | tf_op jit(solution)/shard_map/fp,kpc->kfc/dot_general | solution.py:31
  187.3 14.7 %gather_fusion.1 = f32[8,257,2048]{2,1,0:T(8,128)} fusion(f32[8,257,2048]{2,1,0:T(8,128)} %negate_bitcast_fusion, s32[1024]{0:T(1024)S(1)} %get-tuple-element.25), kind=kCustom, calls=%fused_computation.1.clone | custom fusion | bytes 33685536 | tf_op jit(solution)/shard_map/jit(_take)/gather | solution.py:45
  202.1 14.0 %gather_fusion.2 = f32[8,257,2048]{2,1,0:T(8,128)} fusion(f32[8,257,2048]{2,1,0:T(8,128)} %convolution_bitcast_fusion, s32[1024]{0:T(1024)S(1)} %get-tuple-element.24), kind=kCustom, calls=%fused_computation.2.clone | custom fusion | bytes 33685536 | tf_op jit(solution)/shard_map/jit(_take)/gather | solution.py:44
  216.0 13.7 %gather_fusion.3 = f32[8,257,2048]{2,1,0:T(8,128)} fusion(f32[8,257,2048]{2,1,0:T(8,128)} %negate_bitcast_fusion, s32[1024]{0:T(1024)S(1)} %get-tuple-element.24), kind=kCustom, calls=%fused_computation.3.clone | custom fusion | bytes 33685536 | tf_op jit(solution)/shard_map/jit(_take)/gather | solution.py:45
  229.7 32.8 %all-gather.3.cloned.1.call-done = bf16[2048,2048]{1,0:T(8,128)(2,1)} async-done(((bf16[256,2048]{1,0:T(8,128)(2,1)}), bf16[2048,2048]{1,0:T(8,128)(2,1)}) %all-gather.3.cloned.1.call-update) | async-done | bytes 8388624 | tf_op jit(solution)/shard_map/all_gather | solution.py:64
  262.5 12.9 %fusion.29 = f32[257,8,2048]{2,0,1:T(8,128)} fusion(bf16[8,256,2048]{2,1,0:T(8,128)(2,1)} %bitcast.70), kind=kOutput, calls=%fused_computation.57 | convolution fusion | flops 6468537856 | bytes 25231360 | tf_op jit(solution)/shard_map/fp,kpc->kfc/dot_general | solution.py:31
  275.4 38.6 %fusion.11 = (f32[257,2048]{1,0:T(8,128)}, f32[257,2048]{1,0:T(8,128)}, f32[257,2048]{1,0:T(8,128)}, f32[257,2048]{1,0:T(8,128)}) fusion(f32[8,257,2048]{2,1,0:T(8,128)} %gather_fusion.3, f32[8,257,2048]{2,1,0:T(8,128)} %gather_fusion.2, f32[257,8,2048]{2,0,1:T(8,128)} %fusion.29, f32[8]{0:T(128)S(1)} %get-tuple-element.19, ...), kind=kOutput, calls=%fused_computation.19 | convolution fusion | flops 6571699712 | bytes 101023824 | tf_op jit(solution)/shard_map/fp,kpc->kfc/dot_general | solution.py:30
  313.9 5.3 %fusion.23 = f32[256,2048]{1,0:T(8,128)S(1)} fusion(f32[257,2048]{1,0:T(8,128)} %get-tuple-element.10, f32[512,257]{1,0:T(8,128)S(1)} %get-tuple-element.17), kind=kOutput, calls=%fused_computation.51 | convolution fusion | flops 1616904192 | bytes 4595712 | tf_op jit(solution)/shard_map/dot_general | solution.py:72
  319.2 5.2 %convolution_subtract_fusion.1 = f32[256,2048]{1,0:T(8,128)S(1)} fusion(f32[256,2048]{1,0:T(8,128)S(1)} %fusion.23, f32[257,2048]{1,0:T(8,128)} %get-tuple-element.11, f32[512,257]{1,0:T(8,128)S(1)} %get-tuple-element.16), kind=kOutput, calls=%fused_computation.28 | convolution fusion | flops 1617428480 | bytes 6692864 | tf_op jit(solution)/shard_map/dot_general | solution.py:72
  324.4 0.0 copy-start.4
  324.4 3.6 %convolution_add_fusion = f32[256,2048]{1,0:T(8,128)S(1)} fusion(f32[256,2048]{1,0:T(8,128)S(1)} %convolution_subtract_fusion.1, f32[257,2048]{1,0:T(8,128)S(1)} %copy-done.1, f32[512,257]{1,0:T(8,128)S(1)} %get-tuple-element.17), kind=kOutput, calls=%fused_computation.27 | convolution fusion | flops 1617428480 | bytes 6750208 | tf_op jit(solution)/shard_map/dot_general | solution.py:77
  328.0 0.0 copy-done
  328.0 3.9 %multiply_reduce_fusion = (f32[256]{0:T(256)S(1)}, f32[256,2048]{1,0:T(8,128)S(1)}) fusion(bf16[256,2048]{1,0:T(8,128)(2,1)S(1)} %copy-done, f32[2048]{0:T(1024)S(1)} %copy-done.5, f32[256,2048]{1,0:T(8,128)S(1)} %convolution_add_fusion, f32[257,2048]{1,0:T(8,128)S(1)} %copy-done.2, f32[512,257]{1,0:T(8,128)S(1)} %get-tuple-element.16, ...), kind=kOutput, calls=%fused_computation.31 | convolution fusion | flops 1621098240 | bytes 8856576 | tf_op jit(solution)/shard_map/dot_general | solution.py:78
  332.0 6.2 %psum.7 = f32[256]{0:T(256)S(1)} all-reduce(f32[256]{0:T(256)S(1)} %get-tuple-element.22), channel_id=1, replica_groups=mesh['tok'=8,'chan'=4] {'chan'}, use_global_device_ids=true, to_apply=%region_6.8 | all-reduce | flops 256 | bytes 2048 | tf_op jit(solution)/shard_map/psum | solution.py:81
  338.2 1.6 multiply_multiply_fusion
  (15 shorter events, 0.1 us)
Async XLA Ops:
  6.5 130.7 %all-gather.5.cloned.1.call-start = ((), (), s32[]{:S(2)}) async-start(), calls=%async_computation.1 | async-start | bytes 9437184 | tf_op jit(solution)/shard_map/all_gather | solution.py:60
  9.5 253.0 %all-gather.3.cloned.1.call-start = ((), (), s32[]{:S(2)}) async-start(), calls=%async_computation | async-start | bytes 9437184 | tf_op jit(solution)/shard_map/all_gather | solution.py:64
  313.9 10.5 %copy-start.1 = (f32[257,2048]{1,0:T(8,128)S(1)}, f32[257,2048]{1,0:T(8,128)}, u32[]{:S(2)}) copy-start(f32[257,2048]{1,0:T(8,128)} %get-tuple-element.7) | copy-start | bytes 6316036
  313.9 14.1 %copy-start = (bf16[256,2048]{1,0:T(8,128)(2,1)S(1)}, bf16[256,2048]{1,0:T(8,128)(2,1)}, u32[]{:S(2)}) copy-start(bf16[256,2048]{1,0:T(8,128)(2,1)} %multiply_convert_fusion) | copy-start | bytes 3145732
  313.9 14.1 %copy-start.2 = (f32[257,2048]{1,0:T(8,128)S(1)}, f32[257,2048]{1,0:T(8,128)}, u32[]{:S(2)}) copy-start(f32[257,2048]{1,0:T(8,128)} %get-tuple-element.6) | copy-start | bytes 6316036
  313.9 14.1 %copy-start.3 = (bf16[256,2048]{1,0:T(8,128)(2,1)S(1)}, bf16[256,2048]{1,0:T(8,128)(2,1)}, u32[]{:S(2)}) copy-start(bf16[256,2048]{1,0:T(8,128)(2,1)} %param.9) | copy-start | bytes 3145732
  313.9 14.1 %copy-start.5 = (f32[2048]{0:T(1024)S(1)}, f32[2048]{0:T(1024)}, u32[]{:S(2)}) copy-start(f32[2048]{0:T(1024)} %param.14) | copy-start | bytes 24580
  324.4 13.8 %copy-start.4 = (f32[2048]{0:T(1024)S(1)}, f32[2048]{0:T(1024)}, u32[]{:S(2)}) copy-start(f32[2048]{0:T(1024)} %param.15) | copy-start | bytes 24580
Sparse Core Ops, SparseCore 0:
  9.6 127.6 all-gather.4
  139.4 123.1 all-gather.2
where the time goes:
time: 351 us; the launch traced here: 347 us
  waiting for transfers between devices  157 us (45%)
  matrix products  106 us (30%)
  local copies, waits for them, and re-layouts  56.1 us (16%)
  between operations  13.9 us (4%)
  other arithmetic  8.4 us (2%)
  blocking collectives  6.17 us (2%)
    all_gather x1, waiting for transfers between devices, local(): every_input = lax.all_gather(gated, 'tok', axis=0, tiled=True)  123 us
    dot_general x2, matrix products, spectra(): real_part = jnp.einsum('fp,kpc->kfc', cos_tab, blocks, precision=THREE_PASS)  56.8 us
    all_gather x1, waiting for transfers between devices, local(): lax.all_gather(filter_store, 'tok', axis=0, tiled=True).astype(jnp.float32)  32.8 us
    dot_general x2, matrix products, spectra(): jnp.einsum('fp,kpc->kfc', sin_tab, blocks, precision=THREE_PASS)  31 us
    gather x2, local copies, waits for them, and re-layouts, accumulate(): src_im = jnp.take(in_im, picked, axis=0)  28.4 us
    gather x2, local copies, waits for them, and re-layouts, accumulate(): src_re = jnp.take(in_re, picked, axis=0)  27.7 us
  transfers between devices with their start and end apart: 2, of which 2 were waited for; matrix products, arithmetic and copies ran while one was open for 28% of the time, Pallas kernels for 0%

commit v1 on v0

v1 whole, which is shorter than its diff:
```python
import functools
import math

import jax
import jax.numpy as jnp
import ml_dtypes
import numpy as np
from jax import lax
from jax.experimental import pallas as pl
from jax.experimental.pallas import tpu as pltpu
from jax.sharding import PartitionSpec as P


def split_bf16(table):
    high = table.astype(ml_dtypes.bfloat16)
    low = (table - high.astype(np.float64)).astype(ml_dtypes.bfloat16)
    return high, low


def tables(width):
    freq = np.concatenate([np.arange(0, width, 2), np.arange(1, width, 2)])
    place = np.arange(width)
    steps = ((2 * freq[:, None] + 1) * place[None, :]) % (4 * width)
    angle = math.pi / (2 * width) * steps
    forward = np.concatenate([np.cos(angle), -np.sin(angle)], axis=0)
    inverse = forward.T / width
    return split_bf16(forward) + split_bf16(inverse)


def conv_kernel(count, width, lag_ref, f_ref, g_ref, fh_ref, fl_ref, ih_ref, il_ref, out_ref, fs, gs, ss):
    dot = functools.partial(jnp.dot, preferred_element_type=jnp.float32)
    for i in range(count):
        fs[lag_ref[i]] = dot(fh_ref[...], f_ref[i]) + dot(fl_ref[...], f_ref[i])
        gs[i] = dot(fh_ref[...], g_ref[i]) + dot(fl_ref[...], g_ref[i])
    columns = f_ref.shape[2]
    lane = min(128, columns)

    def products(row, sign):
        re_rows = pl.ds(pl.multiple_of(row * 8, 8), 8)
        im_rows = pl.ds(pl.multiple_of(row * 8 + width, 8), 8)
        for at in range(0, columns, lane):
            lanes = pl.ds(at, lane)
            f_re = [fs[i, re_rows, lanes] for i in range(count)]
            f_im = [fs[i, im_rows, lanes] for i in range(count)]
            h_re, h_im = [], []
            for i in range(count):
                g_re, g_im = gs[i, re_rows, lanes], gs[i, im_rows, lanes]
                if i == 0:
                    h_re.append(g_re)
                    h_im.append(g_im)
                elif sign > 0:
                    h_re.append(g_re - last_im)
                    h_im.append(g_im + last_re)
                else:
                    h_re.append(g_re + last_im)
                    h_im.append(g_im - last_re)
                last_re, last_im = g_re, g_im
            for j in range(count):
                s_re = f_re[0] * h_re[j] - f_im[0] * h_im[j]
                s_im = f_re[0] * h_im[j] + f_im[0] * h_re[j]
                for i in range(1, j + 1):
                    s_re = s_re + f_re[i] * h_re[j - i] - f_im[i] * h_im[j - i]
                    s_im = s_im + f_re[i] * h_im[j - i] + f_im[i] * h_re[j - i]
                ss[j, re_rows, lanes] = s_re
                ss[j, im_rows, lanes] = s_im

    half = width // 16

    @pl.loop(0, half)
    def _(row):
        products(row, 1)

    @pl.loop(half, 2 * half)
    def _(row):
        products(row, -1)

    for j in range(count):
        total = ss[j]
        high = total.astype(jnp.bfloat16)
        low = (total - high.astype(jnp.float32)).astype(jnp.bfloat16)
        out_ref[j] = (dot(ih_ref[...], high) + dot(ih_ref[...], low) + dot(il_ref[...], high)).astype(jnp.bfloat16)


def block_conv(lag_of_block, filt, gated):
    count, width, columns = filt.shape
    tabs = [jnp.asarray(t) for t in tables(width)]
    whole = pl.BlockSpec(memory_space=pltpu.VMEM)
    spectra = pltpu.VMEM((count, 2 * width, columns), jnp.float32)
    return pl.pallas_call(
        functools.partial(conv_kernel, count, width),
        out_shape=jax.ShapeDtypeStruct((count, width, columns), jnp.bfloat16),
        in_specs=[pl.BlockSpec(memory_space=pltpu.SMEM)] + [whole] * 6,
        out_specs=whole,
        scratch_shapes=[spectra, spectra, spectra],
        compiler_params=pltpu.CompilerParams(vmem_limit_bytes=40 * 1024 * 1024),
        cost_estimate=pl.CostEstimate(
            flops=2 * count * width * 2 * width * columns * 7,
            bytes_accessed=6 * count * width * columns,
            transcendentals=0,
        ),
    )(lag_of_block, filt, gated, *tabs)


def local(query, key_in, value_in, filter_store, lag_of_block, skip, out_gain):
    width, columns = query.shape
    count = lax.axis_size("tok")
    part = columns // count

    def to_channels(x):
        return lax.all_to_all(x.reshape(width, count, part).transpose(1, 0, 2), "tok", 0, 0, tiled=True)

    filt_all = to_channels(filter_store)
    gated = (key_in.astype(jnp.float32) * value_in.astype(jnp.float32)).astype(jnp.bfloat16)
    gated_all = to_channels(gated)
    conv_all = block_conv(lag_of_block, filt_all, gated_all)
    conv = lax.all_to_all(conv_all, "tok", 0, 0, tiled=True).transpose(1, 0, 2).reshape(width, columns)
    pre = query.astype(jnp.float32) * (conv.astype(jnp.float32) + skip[None, :] * gated.astype(jnp.float32))
    total = lax.psum(jnp.sum(pre * pre, axis=1), "chan")
    mean_sq = total / (columns * lax.axis_size("chan"))
    return out_gain[None, :] * pre * lax.rsqrt(mean_sq + 1e-06)[:, None]


def solution(mesh):
    in_specs = (
        P("tok", "chan"),
        P("tok", "chan"),
        P("tok", "chan"),
        P("tok", "chan"),
        P(),
        P("chan"),
        P("chan"),
    )
    return jax.shard_map(local, mesh=mesh, in_specs=in_specs, out_specs=P("tok", "chan"), check_vma=False)
```

time: 351 us -> 121 us (0.34); the launches traced: 347 us -> 121 us
  waiting for transfers between devices: 157 us -> 46.3 us
  matrix products: 106 us -> 0 us
  local copies, waits for them, and re-layouts: 56.1 us -> 13.3 us
  blocking collectives: 6.17 us -> 35.2 us
  between operations: 13.9 us -> 0.12 us
  starting transfers between devices: 0.04 us -> 11 us
  Pallas kernels: 0 us -> 8.47 us
    all_gather x2 -> x0, waiting for transfers between devices: 156 us -> none  [the longest x1 123 us: local(): every_input = lax.all_gather(gated, 'tok', axis=0, tiled=True)]
    dot_general x8 -> x0, matrix products: 106 us -> none  [the longest x2 56.8 us: spectra(): real_part = jnp.einsum('fp,kpc->kfc', cos_tab, blocks, precision=THREE_PASS)]
    gather x4 -> x0, local copies, waits for them, and re-layouts: 56.1 us -> none  [the longest x2 28.4 us: accumulate(): src_im = jnp.take(in_im, picked, axis=0)]
    all_to_all x0 -> x2, waiting for transfers between devices: none -> 46.3 us  [the longest x1 24.3 us: local(): lax.all_to_all(conv_all, 'tok', 0, 0, tiled=True).transpose(1, 0, 2)]
    all_to_all x0 -> x1, blocking collectives: none -> 29.5 us  [to_channels(): lax.all_to_all(x.reshape(width, count, part).transpose(1, 0, 2), 'tok', 0...]
    all_to_all x0 -> x2, starting transfers between devices: none -> 11 us  [the longest x1 7.25 us: to_channels(): lax.all_to_all(x.reshape(width, count, part).transpose(1, 0, 2), 'tok', 0...]
    pallas_call x0 -> x1, Pallas kernels: none -> 8.47 us  [block_conv(): pl.pallas_call(functools.partial(conv_kernel, count, width), out_shape=ja...]
    unnamed x12 -> x24, local copies, waits for them, and re-layouts: 0.02 us -> 4.76 us
  transfers between devices with their start and end apart: 2 -> 2, of which waited for: 2 -> 2; matrix products, arithmetic and copies ran while one was open for 28% -> 4% of each run, Pallas kernels for 0% -> 0%
where the time goes in v1:
time: 121 us
  waiting for transfers between devices  46.3 us (38%)
  blocking collectives  35.2 us (29%)
  local copies, waits for them, and re-layouts  13.3 us (11%)
  starting transfers between devices  11 us (9%)
  Pallas kernels  8.47 us (7%)
  other arithmetic  6.66 us (6%)
    all_to_all x1, blocking collectives, to_channels(): lax.all_to_all(x.reshape(width, count, part).transpose(1, 0, 2), 'tok', 0...  29.5 us
    all_to_all x1, waiting for transfers between devices, local(): lax.all_to_all(conv_all, 'tok', 0, 0, tiled=True).transpose(1, 0, 2)  24.3 us
    all_to_all x1, waiting for transfers between devices, to_channels(): lax.all_to_all(x.reshape(width, count, part).transpose(1, 0, 2), 'tok', 0...  22.1 us
    pallas_call x1, Pallas kernels, block_conv(): pl.pallas_call(functools.partial(conv_kernel, count, width), out_shape=ja...  8.47 us
    all_to_all x1, starting transfers between devices, to_channels(): lax.all_to_all(x.reshape(width, count, part).transpose(1, 0, 2), 'tok', 0...  7.25 us
    psum x1, blocking collectives, local(): total = lax.psum(jnp.sum(pre * pre, axis=1), 'chan')  5.67 us
    unnamed x24, local copies, waits for them, and re-layouts  4.76 us
    all_to_all x1, starting transfers between devices, local(): lax.all_to_all(conv_all, 'tok', 0, 0, tiled=True).transpose(1, 0, 2)  3.77 us
  transfers between devices with their start and end apart: 2, of which 2 were waited for; matrix products, arithmetic and copies ran while one was open for 4% of the time, Pallas kernels for 0%

profile of v1, /device:TPU:0, one launch (start us, length us, event | category | flops | bytes accessed | tf_op | source)
XLA Modules:
  0.0 121.0 jit_solution(13543638380596093252)
XLA Ops:
  0.0 1.6 %copy.15 = bf16[256,2048]{0,1:T(8,128)(2,1)S(1)} copy(bf16[256,2048]{1,0:T(8,128)(2,1)} %param.12) | data formatting | bytes 2097152 | tf_op args[1]
  1.6 0.0 copy-done.5
  1.6 0.5 copy.16
  2.1 0.3 multiply_convert_fusion
  2.4 0.0 copy-start.6
  2.4 1.3 %copy.17 = bf16[256,8,256]{2,0,1:T(8,128)(2,1)} copy(bf16[256,8,256]{0,2,1:T(8,128)(2,1)S(1)} %bitcast.14) | data formatting | bytes 2097152 | tf_op jit(solution)/shard_map/reshape | solution.py:110
  3.7 7.3 %all-to-all-start.1 = ((bf16[8,256,256]{2,1,0:T(8,128)(2,1)}), bf16[8,256,256]{2,1,0:T(8,128)(2,1)S(1)}, u32[]{:S(2)}, u32[]{:S(2)}) async-start(bf16[8,256,256]{2,1,0:T(8,128)(2,1)} %bitcast.3), calls=%async_computation.1 | async-start | bytes 2097152 | tf_op jit(solution)/shard_map/all_to_all | solution.py:110
  11.0 1.3 %copy.13 = bf16[256,2048]{0,1:T(8,128)(2,1)} copy(bf16[256,2048]{1,0:T(8,128)(2,1)S(1)} %copy-done.6) | data formatting | bytes 2097152 | tf_op args[3]
  12.3 0.0 copy-start.4
  12.3 2.4 %copy.14 = bf16[256,8,256]{2,0,1:T(8,128)(2,1)} copy(bf16[256,8,256]{0,2,1:T(8,128)(2,1)} %bitcast.16) | data formatting | bytes 2097152 | tf_op jit(solution)/shard_map/reshape | solution.py:110
  14.7 22.1 %all-to-all-done.1.g_ref = bf16[8,256,256]{2,1,0:T(8,128)(2,1)S(1)} async-done(((bf16[8,256,256]{2,1,0:T(8,128)(2,1)}), bf16[8,256,256]{2,1,0:T(8,128)(2,1)S(1)}, u32[]{:S(2)}, u32[]{:S(2)}) %all-to-all-start.1) | async-done | bytes 1048608 | tf_op jit(solution)/shard_map/all_to_all | solution.py:110
  36.8 29.5 %all_to_all.15.f_ref = bf16[8,256,256]{2,1,0:T(8,128)(2,1)S(1)} all-to-all(bf16[8,256,256]{2,1,0:T(8,128)(2,1)} %bitcast.15), channel_id=1, replica_groups=mesh['tok'=8,'chan'=4] {'tok'}, dimensions={0} | all-to-all | bytes 2097152 | tf_op jit(solution)/shard_map/all_to_all | solution.py:110
  66.2 0.0 copy-done.1
  66.3 8.5 %shard_map.109 = bf16[8,256,256]{2,1,0:T(8,128)(2,1)} custom-call(s32[8]{0:T(128)S(1)} %copy-done, bf16[8,256,256]{2,1,0:T(8,128)(2,1)S(1)} %all_to_all.15.f_ref, bf16[8,256,256]{2,1,0:T(8,128)(2,1)S(1)} %all-to-all-done.1.g_ref, bf16[512,256]{1,0:T(8,128)(2,1)S(1)} %copy-done.4, bf16[512,256]{1,0:T(8,128)(2,1)S(1)} %copy-done.3, ...), custom_call_target="tpu_custom_call" | custom-call | flops 3758096384 | bytes 3145728 | tf_op jit(solution)/shard_map/pallas_call | solution.py:89
  74.7 3.8 %all-to-all-start.2 = ((bf16[8,256,256]{2,1,0:T(8,128)(2,1)}), bf16[8,256,256]{2,1,0:T(8,128)(2,1)S(1)}, u32[]{:S(2)}, u32[]{:S(2)}) async-start(bf16[8,256,256]{2,1,0:T(8,128)(2,1)} %shard_map.109), calls=%async_computation.2 | async-start | bytes 2097152 | tf_op jit(solution)/shard_map/all_to_all | solution.py:116
  78.5 1.3 %copy.12 = bf16[256,2048]{0,1:T(8,128)(2,1)} copy(bf16[256,2048]{1,0:T(8,128)(2,1)S(1)} %copy-done.7) | data formatting | bytes 2097152 | tf_op args[0]
  79.8 24.3 %all-to-all-done.2 = bf16[8,256,256]{2,1,0:T(8,128)(2,1)S(1)} async-done(((bf16[8,256,256]{2,1,0:T(8,128)(2,1)}), bf16[8,256,256]{2,1,0:T(8,128)(2,1)S(1)}, u32[]{:S(2)}, u32[]{:S(2)}) %all-to-all-start.2) | async-done | bytes 1048608 | tf_op jit(solution)/shard_map/all_to_all | solution.py:116
  104.1 1.5 %convert_bitcast_fusion = f32[256,8,256]{2,0,1:T(8,128)} fusion(bf16[8,256,256]{2,1,0:T(8,128)(2,1)S(1)} %all-to-all-done.2), kind=kLoop, calls=%fused_computation.2 | loop fusion | flops 524288 | bytes 3145728 | tf_op jit(solution)/shard_map/convert_element_type | solution.py:117
  105.6 1.9 %copy.18 = f32[256,8,256]{0,2,1:T(8,128)S(1)} copy(f32[256,8,256]{2,0,1:T(8,128)} %convert_bitcast_fusion) | data formatting | bytes 4194304 | tf_op jit(solution)/shard_map/convert_element_type | solution.py:117
  107.6 0.0 copy-start.9
  107.6 2.0 %multiply_reduce_fusion = f32[256]{0:T(256)S(1)} fusion(bf16[256,2048]{0,1:T(8,128)(2,1)S(1)} %multiply_convert_fusion, f32[2048]{0:T(1024)S(1)} %copy-done.8, f32[256,8,256]{0,2,1:T(8,128)S(1)} %copy.18, bf16[256,2048]{0,1:T(8,128)(2,1)} %copy.12), kind=kLoop, calls=%fused_computation.3 | loop fusion | flops 3669760 | bytes 4203520 | tf_op jit(solution)/shard_map/reduce_sum | solution.py:118
  109.6 5.7 %psum.7 = f32[256]{0:T(256)S(1)} all-reduce(f32[256]{0:T(256)S(1)} %multiply_reduce_fusion), channel_id=1, replica_groups=mesh['tok'=8,'chan'=4] {'chan'}, use_global_device_ids=true, to_apply=%region_1.0 | all-reduce | flops 256 | bytes 2048 | tf_op jit(solution)/shard_map/psum | solution.py:118
  115.3 2.8 %multiply_multiply_fusion = f32[256,2048]{0,1:T(8,128)} fusion(f32[256]{0:T(256)S(1)} %add_rsqrt_fusion, f32[2048]{0:T(1024)S(1)} %copy-done.9, bf16[256,2048]{0,1:T(8,128)(2,1)S(1)} %multiply_convert_fusion, f32[2048]{0:T(1024)S(1)} %copy-done.8, f32[256,8,256]{0,2,1:T(8,128)S(1)} %copy.18, bf16[256,2048]{0,1:T(8,128)(2,1)} %copy.12), kind=kLoop, calls=%fused_computation.4 | loop fusion | flops 3670016 | bytes 6308864 | tf_op jit(solution)/shard_map/mul | solution.py:120
  118.1 2.9 %copy.19 = f32[256,2048]{1,0:T(8,128)} copy(f32[256,2048]{0,1:T(8,128)} %multiply_multiply_fusion) | data formatting | bytes 4194304 | tf_op jit(solution)/shard_map/mul | solution.py:120
  (16 shorter events, 0.0 us)
Async XLA Ops:
  0.0 1.6 %copy-start.5 = (bf16[256,2048]{1,0:T(8,128)(2,1)S(1)}, bf16[256,2048]{1,0:T(8,128)(2,1)}, u32[]{:S(2)}) copy-start(bf16[256,2048]{1,0:T(8,128)(2,1)} %param.13) | copy-start | bytes 3145732
  2.4 8.6 %copy-start.6 = (bf16[256,2048]{1,0:T(8,128)(2,1)S(1)}, bf16[256,2048]{1,0:T(8,128)(2,1)}, u32[]{:S(2)}) copy-start(bf16[256,2048]{1,0:T(8,128)(2,1)} %param.14) | copy-start | bytes 3145732
  3.7 33.0 %all-to-all-start.1 = ((bf16[8,256,256]{2,1,0:T(8,128)(2,1)}), bf16[8,256,256]{2,1,0:T(8,128)(2,1)S(1)}, u32[]{:S(2)}, u32[]{:S(2)}) async-start(bf16[8,256,256]{2,1,0:T(8,128)(2,1)} %bitcast.3), calls=%async_computation.1 | async-start | bytes 2097152 | tf_op jit(solution)/shard_map/all_to_all | solution.py:110
  12.3 53.9 %copy-start = (s32[8]{0:T(128)S(1)}, s32[8]{0:T(128)}, u32[]{:S(2)}) copy-start(s32[8]{0:T(128)} %lag_ref.1) | copy-start | bytes 100
  12.3 53.9 %copy-start.1 = (bf16[256,512]{1,0:T(8,128)(2,1)S(1)}, bf16[256,512]{1,0:T(8,128)(2,1)}, u32[]{:S(2)}) copy-start(bf16[256,512]{1,0:T(8,128)(2,1)} %constant.18.clone.il_ref) | copy-start | bytes 786436
  12.3 53.9 %copy-start.2 = (bf16[256,512]{1,0:T(8,128)(2,1)S(1)}, bf16[256,512]{1,0:T(8,128)(2,1)}, u32[]{:S(2)}) copy-start(bf16[256,512]{1,0:T(8,128)(2,1)} %constant.17.clone.ih_ref) | copy-start | bytes 786436
  12.3 54.0 %copy-start.3 = (bf16[512,256]{1,0:T(8,128)(2,1)S(1)}, bf16[512,256]{1,0:T(8,128)(2,1)}, u32[]{:S(2)}) copy-start(bf16[512,256]{1,0:T(8,128)(2,1)} %constant.16.clone.fl_ref) | copy-start | bytes 786436
  12.3 54.0 %copy-start.4 = (bf16[512,256]{1,0:T(8,128)(2,1)S(1)}, bf16[512,256]{1,0:T(8,128)(2,1)}, u32[]{:S(2)}) copy-start(bf16[512,256]{1,0:T(8,128)(2,1)} %constant.15.clone.fh_ref) | copy-start | bytes 786436
  74.7 3.8 %copy-start.7 = (bf16[256,2048]{1,0:T(8,128)(2,1)S(1)}, bf16[256,2048]{1,0:T(8,128)(2,1)}, u32[]{:S(2)}) copy-start(bf16[256,2048]{1,0:T(8,128)(2,1)} %param.11) | copy-start | bytes 3145732
  74.7 29.4 %all-to-all-start.2 = ((bf16[8,256,256]{2,1,0:T(8,128)(2,1)}), bf16[8,256,256]{2,1,0:T(8,128)(2,1)S(1)}, u32[]{:S(2)}, u32[]{:S(2)}) async-start(bf16[8,256,256]{2,1,0:T(8,128)(2,1)} %shard_map.109), calls=%async_computation.2 | async-start | bytes 2097152 | tf_op jit(solution)/shard_map/all_to_all | solution.py:116
  105.6 1.9 %copy-start.8 = (f32[2048]{0:T(1024)S(1)}, f32[2048]{0:T(1024)}, u32[]{:S(2)}) copy-start(f32[2048]{0:T(1024)} %param.16) | copy-start | bytes 24580
  107.6 7.7 %copy-start.9 = (f32[2048]{0:T(1024)S(1)}, f32[2048]{0:T(1024)}, u32[]{:S(2)}) copy-start(f32[2048]{0:T(1024)} %param.17) | copy-start | bytes 24580

commit v2 on v1

--- a/solution.py
+++ b/solution.py
@@ -10,6 +10,10 @@
 from jax.experimental.pallas import tpu as pltpu
 from jax.sharding import PartitionSpec as P
 
+MIB = 1024 * 1024
+WHOLE = pl.BlockSpec(memory_space=pltpu.VMEM)
+IN_HBM = pl.BlockSpec(memory_space=pltpu.HBM)
+
 
 def split_bf16(table):
     high = table.astype(ml_dtypes.bfloat16)
@@ -27,12 +31,59 @@
     return split_bf16(forward) + split_bf16(inverse)
 
 
-def conv_kernel(count, width, lag_ref, f_ref, g_ref, fh_ref, fl_ref, ih_ref, il_ref, out_ref, fs, gs, ss):
+def gate_kernel(count, part, key_ref, value_ref, filt_ref, out_ref, key_buf, value_buf, sems, filt_sems):
+    width = key_ref.shape[0]
+    copies = []
+    for j in range(count):
+        cols = pl.ds(j * part, part)
+        copies.append(
+            (
+                pltpu.make_async_copy(key_ref.at[:, cols], key_buf.at[j], sems.at[0, j]),
+                pltpu.make_async_copy(value_ref.at[:, cols], value_buf.at[j], sems.at[1, j]),
+            )
+        )
+        for copy in copies[-1]:
+            copy.start()
+    filts = []
+    for j in range(count):
+        cols = pl.ds(j * part, part)
+        filts.append(pltpu.make_async_copy(filt_ref.at[:, cols], out_ref.at[j, pl.ds(0, width), :], filt_sems.at[j]))
+        filts[-1].start()
+    for j in range(count):
+        for copy in copies[j]:
+            copy.wait()
+        product = key_buf[j].astype(jnp.float32) * value_buf[j].astype(jnp.float32)
+        out_ref[j, pl.ds(width, width), :] = product.astype(jnp.bfloat16)
+    for copy in filts:
+        copy.wait()
+
+
+def gate(count, key_in, value_in, filter_store):
+    width, columns = key_in.shape
+    part = columns // count
+    if part % 128:
+        gated = (key_in.astype(jnp.float32) * value_in.astype(jnp.float32)).astype(jnp.bfloat16)
+        both = jnp.concatenate([filter_store, gated], axis=0)
+        return both.reshape(2 * width, count, part).transpose(1, 0, 2)
+    block = pltpu.VMEM((count, width, part), jnp.bfloat16)
+    return pl.pallas_call(
+        functools.partial(gate_kernel, count, part),
+        out_shape=jax.ShapeDtypeStruct((count, 2 * width, part), jnp.bfloat16),
+        in_specs=[IN_HBM] * 3,
+        out_specs=WHOLE,
+        scratch_shapes=[block, block, pltpu.SemaphoreType.DMA((2, count)), pltpu.SemaphoreType.DMA((count,))],
+        compiler_params=pltpu.CompilerParams(vmem_limit_bytes=16 * MIB),
+        cost_estimate=pl.CostEstimate(flops=width * columns, bytes_accessed=10 * width * columns, transcendentals=0),
+    )(key_in, value_in, filter_store)
+
+
+def conv_kernel(count, width, lag_ref, fg_ref, fh_ref, fl_ref, ih_ref, il_ref, out_ref, fs, gs, ss):
     dot = functools.partial(jnp.dot, preferred_element_type=jnp.float32)
     for i in range(count):
-        fs[lag_ref[i]] = dot(fh_ref[...], f_ref[i]) + dot(fl_ref[...], f_ref[i])
-        gs[i] = dot(fh_ref[...], g_ref[i]) + dot(fl_ref[...], g_ref[i])
-    columns = f_ref.shape[2]
+        filt, gated = fg_ref[i, pl.ds(0, width), :], fg_ref[i, pl.ds(width, width), :]
+        fs[lag_ref[i]] = dot(fh_ref[...], filt) + dot(fl_ref[...], filt)
+        gs[i] = dot(fh_ref[...], gated) + dot(fl_ref[...], gated)
+    columns = fg_ref.shape[2]
     lane = min(128, columns)
 
     def products(row, sign):
@@ -81,43 +132,99 @@
         out_ref[j] = (dot(ih_ref[...], high) + dot(ih_ref[...], low) + dot(il_ref[...], high)).astype(jnp.bfloat16)
 
 
-def block_conv(lag_of_block, filt, gated):
-    count, width, columns = filt.shape
+def block_conv(lag_of_block, both):
+    count, twice, columns = both.shape
+    width = twice // 2
     tabs = [jnp.asarray(t) for t in tables(width)]
-    whole = pl.BlockSpec(memory_space=pltpu.VMEM)
     spectra = pltpu.VMEM((count, 2 * width, columns), jnp.float32)
     return pl.pallas_call(
         functools.partial(conv_kernel, count, width),
         out_shape=jax.ShapeDtypeStruct((count, width, columns), jnp.bfloat16),
-        in_specs=[pl.BlockSpec(memory_space=pltpu.SMEM)] + [whole] * 6,
-        out_specs=whole,
+        in_specs=[pl.BlockSpec(memory_space=pltpu.SMEM)] + [WHOLE] * 5,
+        out_specs=WHOLE,
         scratch_shapes=[spectra, spectra, spectra],
-        compiler_params=pltpu.CompilerParams(vmem_limit_bytes=40 * 1024 * 1024),
+        compiler_params=pltpu.CompilerParams(vmem_limit_bytes=32 * MIB),
         cost_estimate=pl.CostEstimate(
             flops=2 * count * width * 2 * width * columns * 7,
             bytes_accessed=6 * count * width * columns,
             transcendentals=0,
         ),
-    )(lag_of_block, filt, gated, *tabs)
+    )(lag_of_block, both, *tabs)
+
+
+def pre_kernel(query_ref, conv_ref, both_ref, skip_ref, pre_ref, square_ref):
+    count, width, part = conv_ref.shape
+    total = jnp.zeros((width, 128), jnp.float32)
+    for j in range(count):
+        for at in range(0, part, 128):
+            lanes, cols = pl.ds(at, 128), pl.ds(j * part + at, 128)
+            gated = both_ref[j, pl.ds(width, width), lanes].astype(jnp.float32)
+            conv = conv_ref[j, :, lanes].astype(jnp.float32)
+            pre = query_ref[:, cols].astype(jnp.float32) * (conv + skip_ref[:, cols] * gated)
+            pre_ref[:, cols] = pre
+            total = total + pre * pre
+    square_ref[...] = jnp.sum(total.T, axis=0, keepdims=True)
+
+
+def gated_output(query, conv, both, skip):
+    width, columns = query.shape
+    return pl.pallas_call(
+        pre_kernel,
+        out_shape=(
+            jax.ShapeDtypeStruct((width, columns), jnp.float32),
+            jax.ShapeDtypeStruct((1, width), jnp.float32),
+        ),
+        in_specs=[WHOLE] * 4,
+        out_specs=(WHOLE, WHOLE),
+        compiler_params=pltpu.CompilerParams(vmem_limit_bytes=16 * MIB),
+        cost_estimate=pl.CostEstimate(flops=6 * width * columns, bytes_accessed=10 * width * columns, transcendentals=0),
+    )(query, conv, both, skip)
+
+
+def scale_kernel(channels, steps, pre_ref, square_ref, gain_ref, out_ref, buf, sems):
+    width = pre_ref.shape[0]
+    rows = width // steps
+    scale = lax.rsqrt(square_ref[...] * (1.0 / channels) + 1e-06)
+    scale = jnp.broadcast_to(scale, (128, width)).T
+    copies = []
+    for s in range(steps):
+        for at in range(0, pre_ref.shape[1], 128):
+            cols = pl.ds(at, 128)
+            here = scale[s * rows : (s + 1) * rows, :]
+            buf[pl.ds(s * rows, rows), cols] = gain_ref[:, cols] * pre_ref[pl.ds(s * rows, rows), cols] * here
+        window = pl.ds(s * rows, rows)
+        copies.append(pltpu.make_async_copy(buf.at[window, :], out_ref.at[window, :], sems.at[s]))
+        copies[-1].start()
+    for copy in copies:
+        copy.wait()
+
+
+def scaled(channels, pre, square, out_gain):
+    width, columns = pre.shape
+    steps = 8
+    return pl.pallas_call(
+        functools.partial(scale_kernel, channels, steps),
+        out_shape=jax.ShapeDtypeStruct((width, columns), jnp.float32),
+        in_specs=[WHOLE] * 3,
+        out_specs=IN_HBM,
+        scratch_shapes=[pltpu.VMEM((width, columns), jnp.float32), pltpu.SemaphoreType.DMA((steps,))],
+        compiler_params=pltpu.CompilerParams(vmem_limit_bytes=16 * MIB),
+        cost_estimate=pl.CostEstimate(flops=2 * width * columns, bytes_accessed=8 * width * columns, transcendentals=0),
+    )(pre, square, out_gain)
 
 
 def local(query, key_in, value_in, filter_store, lag_of_block, skip, out_gain):
     width, columns = query.shape
     count = lax.axis_size("tok")
-    part = columns // count
-
-    def to_channels(x):
-        return lax.all_to_all(x.reshape(width, count, part).transpose(1, 0, 2), "tok", 0, 0, tiled=True)
-
-    filt_all = to_channels(filter_store)
-    gated = (key_in.astype(jnp.float32) * value_in.astype(jnp.float32)).astype(jnp.bfloat16)
-    gated_all = to_channels(gated)
-    conv_all = block_conv(lag_of_block, filt_all, gated_all)
-    conv = lax.all_to_all(conv_all, "tok", 0, 0, tiled=True).transpose(1, 0, 2).reshape(width, columns)
-    pre = query.astype(jnp.float32) * (conv.astype(jnp.float32) + skip[None, :] * gated.astype(jnp.float32))
-    total = lax.psum(jnp.sum(pre * pre, axis=1), "chan")
-    mean_sq = total / (columns * lax.axis_size("chan"))
-    return out_gain[None, :] * pre * lax.rsqrt(mean_sq + 1e-06)[:, None]
+    both = gate(count, key_in, value_in, filter_store)
+    everywhere = lax.all_to_all(both, "tok", 0, 0, tiled=True)
+    conv = lax.all_to_all(block_conv(lag_of_block, everywhere), "tok", 0, 0, tiled=True)
+    if conv.shape[2] % 128:
+        conv = conv.transpose(1, 0, 2).reshape(1, width, columns)
+        both = both.transpose(1, 0, 2).reshape(1, 2 * width, columns)
+    pre, square = gated_output(query, conv, both, skip[None, :])
+    square = lax.psum(square, "chan")
+    return scaled(columns * lax.axis_size("chan"), pre, square, out_gain[None, :])
 
 
 def solution(mesh):

time: 121 us -> 105 us (0.87)
  blocking collectives: 35.2 us -> 90.1 us
  waiting for transfers between devices: 46.3 us -> 0 us
  starting transfers between devices: 11 us -> 0 us
  local copies, waits for them, and re-layouts: 13.3 us -> 3.72 us
  other arithmetic: 6.66 us -> 0 us
  Pallas kernels: 8.47 us -> 10.8 us
    all_to_all x1 -> x2, blocking collectives: 29.5 us -> 84.4 us  [the longest x1 55.4 us: local(): everywhere = lax.all_to_all(both, 'tok', 0, 0, tiled=True)]
    all_to_all x2 -> x0, waiting for transfers between devices: 46.3 us -> none  [the longest x1 24.3 us: local(): lax.all_to_all(conv_all, 'tok', 0, 0, tiled=True).transpose(1, 0, 2)]
    all_to_all x2 -> x0, starting transfers between devices: 11 us -> none  [the longest x1 7.25 us: to_channels(): lax.all_to_all(x.reshape(width, count, part).transpose(1, 0, 2), 'tok', 0...]
    reshape x2 -> x0, local copies, waits for them, and re-layouts: 3.68 us -> none  [to_channels(): x.reshape(width, count, part).transpose(1, 0, 2)]
    pallas_call x0 -> x3, Pallas kernels: none -> 3.21 us  [the longest x1 1.51 us: scaled(): pl.pallas_call(functools.partial(scale_kernel, channels, steps), out_shap...]
    mul x1 -> x0, local copies, waits for them, and re-layouts: 2.88 us -> none  [local(): return out_gain[None, :] * pre * lax.rsqrt(mean_sq + 1e-06)[:, None]]
    mul x1 -> x0, other arithmetic: 2.85 us -> none  [local(): return out_gain[None, :] * pre * lax.rsqrt(mean_sq + 1e-06)[:, None]]
    reduce_sum x1 -> x0, other arithmetic: 2.03 us -> none  [local(): total = lax.psum(jnp.sum(pre * pre, axis=1), 'chan')]
  transfers between devices with their start and end apart: 2 -> 0, of which waited for: 2 -> 0; matrix products, arithmetic and copies ran while one was open for 4% -> 0% of each run, Pallas kernels for 0% -> 0%
where the time goes in v2:
time: 105 us
  blocking collectives  90.1 us (86%)
  Pallas kernels  10.8 us (10%)
  local copies, waits for them, and re-layouts  3.72 us (4%)
    all_to_all x1, blocking collectives, local(): everywhere = lax.all_to_all(both, 'tok', 0, 0, tiled=True)  55.4 us
    all_to_all x1, blocking collectives, local(): lax.all_to_all(block_conv(lag_of_block, everywhere), 'tok', 0, 0, tiled=T...  29 us
    pallas_call x1, Pallas kernels, block_conv(): pl.pallas_call(functools.partial(conv_kernel, count, width), out_shape=ja...  7.57 us
    psum x1, blocking collectives, local(): square = lax.psum(square, 'chan')  5.67 us
    unnamed x22, local copies, waits for them, and re-layouts  3.72 us

profile of v2, /device:TPU:0, one launch (start us, length us, event | category | flops | bytes accessed | tf_op | source)
XLA Modules:
  0.0 104.7 jit_solution(4281627342719194466)
XLA Ops:
  0.0 1.2 %copy-done = bf16[256,2048]{1,0:T(8,128)(2,1)S(1)} copy-done((bf16[256,2048]{1,0:T(8,128)(2,1)S(1)}, bf16[256,2048]{1,0:T(8,128)(2,1)}, u32[]{:S(2)}) %copy-start) | copy-done | bytes 1048600
  1.2 1.2 %copy-done.1 = bf16[256,2048]{1,0:T(8,128)(2,1)S(1)} copy-done((bf16[256,2048]{1,0:T(8,128)(2,1)S(1)}, bf16[256,2048]{1,0:T(8,128)(2,1)}, u32[]{:S(2)}) %copy-start.1) | copy-done | bytes 1048600
  2.5 1.2 %copy-done.2 = bf16[256,2048]{1,0:T(8,128)(2,1)S(1)} copy-done((bf16[256,2048]{1,0:T(8,128)(2,1)S(1)}, bf16[256,2048]{1,0:T(8,128)(2,1)}, u32[]{:S(2)}) %copy-start.2) | copy-done | bytes 1048600
  3.7 1.0 shard_map.109.both_ref
  4.6 0.0 copy-start.6
  4.7 0.0 copy-start.7
  4.7 0.0 copy-start.8
  4.7 0.0 copy-start.9
  4.7 0.0 copy-start.10
  4.7 55.4 %all_to_all.10.fg_ref = bf16[8,512,256]{2,1,0:T(8,128)(2,1)S(1)} all-to-all(bf16[8,512,256]{2,1,0:T(8,128)(2,1)S(1)} %shard_map.109.both_ref), channel_id=1, replica_groups=mesh['tok'=8,'chan'=4] {'tok'}, dimensions={0} | all-to-all | bytes 4194304 | tf_op jit(solution)/shard_map/all_to_all | solution.py:220
  60.1 0.0 copy-done.6
  60.1 0.0 copy-done.7
  60.1 0.0 copy-done.8
  60.1 0.0 copy-done.9
  60.1 0.0 copy-done.10
  60.2 7.6 %shard_map.110 = bf16[8,256,256]{2,1,0:T(8,128)(2,1)S(1)} custom-call(s32[8]{0:T(128)S(1)} %copy-done.6, bf16[8,512,256]{2,1,0:T(8,128)(2,1)S(1)} %all_to_all.10.fg_ref, bf16[512,256]{1,0:T(8,128)(2,1)S(1)} %copy-done.10, bf16[512,256]{1,0:T(8,128)(2,1)S(1)} %copy-done.9, bf16[256,512]{1,0:T(8,128)(2,1)S(1)} %copy-done.8, bf16[256,512]{1,0:T(8,128)(2,1)S(1)} %copy-done.7), custom_call_target="tpu_custom_call" | custom-call | flops 3758096384 | bytes 3145728 | tf_op jit(solution)/shard_map/pallas_call | solution.py:140
  67.7 0.0 copy-start.3
  67.7 0.0 copy-start.4
  67.8 29.0 %all_to_all.11.conv_ref = bf16[8,256,256]{2,1,0:T(8,128)(2,1)S(1)} all-to-all(bf16[8,256,256]{2,1,0:T(8,128)(2,1)S(1)} %shard_map.110), channel_id=1, replica_groups=mesh['tok'=8,'chan'=4] {'tok'}, dimensions={0} | all-to-all | bytes 2097152 | tf_op jit(solution)/shard_map/all_to_all | solution.py:221
  96.7 0.0 copy-done.3
  96.7 0.0 copy-done.4
  96.7 0.8 shard_map.111
  97.5 5.7 %psum.7.square_ref = f32[1,256]{1,0:T(1,128)S(1)} all-reduce(f32[1,256]{1,0:T(1,128)S(1)} %get-tuple-element.8), channel_id=1, replica_groups=mesh['tok'=8,'chan'=4] {'chan'}, use_global_device_ids=true, to_apply=%region_0.0 | all-reduce | flops 256 | bytes 2048 | tf_op jit(solution)/shard_map/psum | solution.py:226
  103.2 1.5 %shard_map.112 = f32[256,2048]{1,0:T(8,128)} custom-call(f32[256,2048]{1,0:T(8,128)S(1)} %get-tuple-element.7.pre_ref, f32[1,256]{1,0:T(1,128)S(1)} %psum.7.square_ref, f32[1,2048]{1,0:T(1,128)S(1)} %bitcast.3), custom_call_target="tpu_custom_call" | custom-call | flops 1048576 | bytes 4194304 | tf_op jit(solution)/shard_map/pallas_call | solution.py:205
  (5 shorter events, 0.0 us)
Async XLA Ops:
  0.0 1.2 %copy-start = (bf16[256,2048]{1,0:T(8,128)(2,1)S(1)}, bf16[256,2048]{1,0:T(8,128)(2,1)}, u32[]{:S(2)}) copy-start(bf16[256,2048]{1,0:T(8,128)(2,1)} %key_ref.1) | copy-start | bytes 3145732
  1.2 1.2 %copy-start.1 = (bf16[256,2048]{1,0:T(8,128)(2,1)S(1)}, bf16[256,2048]{1,0:T(8,128)(2,1)}, u32[]{:S(2)}) copy-start(bf16[256,2048]{1,0:T(8,128)(2,1)} %value_ref.1) | copy-start | bytes 3145732
  2.5 1.2 %copy-start.2 = (bf16[256,2048]{1,0:T(8,128)(2,1)S(1)}, bf16[256,2048]{1,0:T(8,128)(2,1)}, u32[]{:S(2)}) copy-start(bf16[256,2048]{1,0:T(8,128)(2,1)} %filt_ref.1) | copy-start | bytes 3145732
  4.6 55.5 %copy-start.6 = (s32[8]{0:T(128)S(1)}, s32[8]{0:T(128)}, u32[]{:S(2)}) copy-start(s32[8]{0:T(128)} %lag_ref.1) | copy-start | bytes 100
  4.7 55.5 %copy-start.7 = (bf16[256,512]{1,0:T(8,128)(2,1)S(1)}, bf16[256,512]{1,0:T(8,128)(2,1)}, u32[]{:S(2)}) copy-start(bf16[256,512]{1,0:T(8,128)(2,1)} %constant.11.clone.il_ref) | copy-start | bytes 786436
  4.7 55.5 %copy-start.8 = (bf16[256,512]{1,0:T(8,128)(2,1)S(1)}, bf16[256,512]{1,0:T(8,128)(2,1)}, u32[]{:S(2)}) copy-start(bf16[256,512]{1,0:T(8,128)(2,1)} %constant.10.clone.ih_ref) | copy-start | bytes 786436
  4.7 55.5 %copy-start.9 = (bf16[512,256]{1,0:T(8,128)(2,1)S(1)}, bf16[512,256]{1,0:T(8,128)(2,1)}, u32[]{:S(2)}) copy-start(bf16[512,256]{1,0:T(8,128)(2,1)} %constant.9.clone.fl_ref) | copy-start | bytes 786436
  4.7 55.5 %copy-start.10 = (bf16[512,256]{1,0:T(8,128)(2,1)S(1)}, bf16[512,256]{1,0:T(8,128)(2,1)}, u32[]{:S(2)}) copy-start(bf16[512,256]{1,0:T(8,128)(2,1)} %constant.8.clone.fh_ref) | copy-start | bytes 786436
  67.7 29.0 %copy-start.3 = (bf16[256,2048]{1,0:T(8,128)(2,1)S(1)}, bf16[256,2048]{1,0:T(8,128)(2,1)}, u32[]{:S(2)}) copy-start(bf16[256,2048]{1,0:T(8,128)(2,1)} %query_ref.1) | copy-start | bytes 3145732
  67.7 29.0 %copy-start.4 = (f32[2048]{0:T(1024)S(1)}, f32[2048]{0:T(1024)}, u32[]{:S(2)}) copy-start(f32[2048]{0:T(1024)} %param.16) | copy-start | bytes 24580
  96.7 6.4 %copy-start.5 = (f32[2048]{0:T(1024)S(1)}, f32[2048]{0:T(1024)}, u32[]{:S(2)}) copy-start(f32[2048]{0:T(1024)} %param.17) | copy-start | bytes 24580

commit v3 on v2

--- a/solution.py
+++ b/solution.py
@@ -11,6 +11,7 @@
 from jax.sharding import PartitionSpec as P
 
 MIB = 1024 * 1024
+BIG = 48 * MIB
 WHOLE = pl.BlockSpec(memory_space=pltpu.VMEM)
 IN_HBM = pl.BlockSpec(memory_space=pltpu.HBM)
 
@@ -31,59 +32,98 @@
     return split_bf16(forward) + split_bf16(inverse)
 
 
-def gate_kernel(count, part, key_ref, value_ref, filt_ref, out_ref, key_buf, value_buf, sems, filt_sems):
-    width = key_ref.shape[0]
+def partner(step):
+    return lax.axis_index("tok") ^ step
+
+
+def exchange(blocks):
+    count = len(blocks)
+    return [blocks[0]] + [
+        lax.ppermute(blocks[k], "tok", [(d, d ^ k) for d in range(count)]) for k in range(1, count)
+    ]
+
+
+def columns_of(step, part):
+    return pl.ds(pl.multiple_of(partner(step) * part, 128), part)
+
+
+def split_kernel(count, part, filt_ref, *refs):
+    outs, sems = refs[:count], refs[count]
     copies = []
-    for j in range(count):
-        cols = pl.ds(j * part, part)
+    for k in range(count):
+        copies.append(pltpu.make_async_copy(filt_ref.at[:, columns_of(k, part)], outs[k], sems.at[k]))
+        copies[-1].start()
+    for copy in copies:
+        copy.wait()
+
+
+def gate_kernel(count, part, key_ref, value_ref, *refs):
+    outs, (key_buf, value_buf, sems) = refs[:count], refs[count:]
+    copies = []
+    for k in range(count):
+        cols = columns_of(k, part)
         copies.append(
             (
-                pltpu.make_async_copy(key_ref.at[:, cols], key_buf.at[j], sems.at[0, j]),
-                pltpu.make_async_copy(value_ref.at[:, cols], value_buf.at[j], sems.at[1, j]),
+                pltpu.make_async_copy(key_ref.at[:, cols], key_buf.at[k], sems.at[0, k]),
+                pltpu.make_async_copy(value_ref.at[:, cols], value_buf.at[k], sems.at[1, k]),
             )
         )
         for copy in copies[-1]:
             copy.start()
-    filts = []
-    for j in range(count):
-        cols = pl.ds(j * part, part)
-        filts.append(pltpu.make_async_copy(filt_ref.at[:, cols], out_ref.at[j, pl.ds(0, width), :], filt_sems.at[j]))
-        filts[-1].start()
-    for j in range(count):
-        for copy in copies[j]:
+    for k in range(count):
+        for copy in copies[k]:
             copy.wait()
-        product = key_buf[j].astype(jnp.float32) * value_buf[j].astype(jnp.float32)
-        out_ref[j, pl.ds(width, width), :] = product.astype(jnp.bfloat16)
-    for copy in filts:
-        copy.wait()
-
-
-def gate(count, key_in, value_in, filter_store):
+        product = key_buf[k].astype(jnp.float32) * value_buf[k].astype(jnp.float32)
+        outs[k][...] = product.astype(jnp.bfloat16)
+
+
+def pieces(x, count):
+    part = x.shape[1] // count
+    return [lax.dynamic_slice_in_dim(x, partner(k) * part, part, axis=1) for k in range(count)]
+
+
+def split(count, filter_store):
+    width, columns = filter_store.shape
+    part = columns // count
+    if part % 128:
+        return pieces(filter_store, count)
+    return pl.pallas_call(
+        functools.partial(split_kernel, count, part),
+        out_shape=[jax.ShapeDtypeStruct((width, part), jnp.bfloat16)] * count,
+        in_specs=[IN_HBM],
+        out_specs=[WHOLE] * count,
+        scratch_shapes=[pltpu.SemaphoreType.DMA((count,))],
+        compiler_params=pltpu.CompilerParams(vmem_limit_bytes=BIG),
+        cost_estimate=pl.CostEstimate(flops=0, bytes_accessed=4 * width * columns, transcendentals=0),
+    )(filter_store)
+
+
+def gate(count, key_in, value_in):
     width, columns = key_in.shape
     part = columns // count
     if part % 128:
         gated = (key_in.astype(jnp.float32) * value_in.astype(jnp.float32)).astype(jnp.bfloat16)
-        both = jnp.concatenate([filter_store, gated], axis=0)
-        return both.reshape(2 * width, count, part).transpose(1, 0, 2)
+        return pieces(gated, count)
     block = pltpu.VMEM((count, width, part), jnp.bfloat16)
     return pl.pallas_call(
         functools.partial(gate_kernel, count, part),
-        out_shape=jax.ShapeDtypeStruct((count, 2 * width, part), jnp.bfloat16),
-        in_specs=[IN_HBM] * 3,
-        out_specs=WHOLE,
-        scratch_shapes=[block, block, pltpu.SemaphoreType.DMA((2, count)), pltpu.SemaphoreType.DMA((count,))],
-        compiler_params=pltpu.CompilerParams(vmem_limit_bytes=16 * MIB),
-        cost_estimate=pl.CostEstimate(flops=width * columns, bytes_accessed=10 * width * columns, transcendentals=0),
-    )(key_in, value_in, filter_store)
-
-
-def conv_kernel(count, width, lag_ref, fg_ref, fh_ref, fl_ref, ih_ref, il_ref, out_ref, fs, gs, ss):
+        out_shape=[jax.ShapeDtypeStruct((width, part), jnp.bfloat16)] * count,
+        in_specs=[IN_HBM] * 2,
+        out_specs=[WHOLE] * count,
+        scratch_shapes=[block, block, pltpu.SemaphoreType.DMA((2, count))],
+        compiler_params=pltpu.CompilerParams(vmem_limit_bytes=BIG),
+        cost_estimate=pl.CostEstimate(flops=width * columns, bytes_accessed=6 * width * columns, transcendentals=0),
+    )(key_in, value_in)
+
+
+def conv_kernel(count, width, lag_ref, fh_ref, fl_ref, ih_ref, il_ref, *refs):
+    filts, gates, outs, (fs, gs, ss) = refs[:count], refs[count : 2 * count], refs[2 * count : 3 * count], refs[3 * count :]
     dot = functools.partial(jnp.dot, preferred_element_type=jnp.float32)
-    for i in range(count):
-        filt, gated = fg_ref[i, pl.ds(0, width), :], fg_ref[i, pl.ds(width, width), :]
-        fs[lag_ref[i]] = dot(fh_ref[...], filt) + dot(fl_ref[...], filt)
-        gs[i] = dot(fh_ref[...], gated) + dot(fl_ref[...], gated)
-    columns = fg_ref.shape[2]
+    for k in range(count):
+        filt, gated = filts[k][...], gates[k][...]
+        fs[lag_ref[partner(k)]] = dot(fh_ref[...], filt) + dot(fl_ref[...], filt)
+        gs[partner(k)] = dot(fh_ref[...], gated) + dot(fl_ref[...], gated)
+    columns = filts[0].shape[1]
     lane = min(128, columns)
 
     def products(row, sign):
@@ -125,23 +165,23 @@
     def _(row):
         products(row, -1)
 
-    for j in range(count):
-        total = ss[j]
+    for k in range(count):
+        total = ss[partner(k)]
         high = total.astype(jnp.bfloat16)
         low = (total - high.astype(jnp.float32)).astype(jnp.bfloat16)
-        out_ref[j] = (dot(ih_ref[...], high) + dot(ih_ref[...], low) + dot(il_ref[...], high)).astype(jnp.bfloat16)
-
-
-def block_conv(lag_of_block, both):
-    count, twice, columns = both.shape
-    width = twice // 2
+        outs[k][...] = (dot(ih_ref[...], high) + dot(ih_ref[...], low) + dot(il_ref[...], high)).astype(jnp.bfloat16)
+
+
+def block_conv(lag_of_block, filts, gates):
+    count = len(filts)
+    width, columns = filts[0].shape
     tabs = [jnp.asarray(t) for t in tables(width)]
     spectra = pltpu.VMEM((count, 2 * width, columns), jnp.float32)
     return pl.pallas_call(
         functools.partial(conv_kernel, count, width),
-        out_shape=jax.ShapeDtypeStruct((count, width, columns), jnp.bfloat16),
-        in_specs=[pl.BlockSpec(memory_space=pltpu.SMEM)] + [WHOLE] * 5,
-        out_specs=WHOLE,
+        out_shape=[jax.ShapeDtypeStruct((width, columns), jnp.bfloat16)] * count,
+        in_specs=[pl.BlockSpec(memory_space=pltpu.SMEM)] + [WHOLE] * (4 + 2 * count),
+        out_specs=[WHOLE] * count,
         scratch_shapes=[spectra, spectra, spectra],
         compiler_params=pltpu.CompilerParams(vmem_limit_bytes=32 * MIB),
         cost_estimate=pl.CostEstimate(
@@ -149,36 +189,48 @@
             bytes_accessed=6 * count * width * columns,
             transcendentals=0,
         ),
-    )(lag_of_block, both, *tabs)
-
-
-def pre_kernel(query_ref, conv_ref, both_ref, skip_ref, pre_ref, square_ref):
-    count, width, part = conv_ref.shape
+    )(lag_of_block, *tabs, *filts, *gates)
+
+
+def pre_kernel(count, query_ref, skip_ref, *refs):
+    convs, gates, (pre_ref, square_ref) = refs[:count], refs[count : 2 * count], refs[2 * count :]
+    width, part = convs[0].shape
     total = jnp.zeros((width, 128), jnp.float32)
-    for j in range(count):
+    for k in range(count):
+        start = partner(k) * part if count > 1 else 0
         for at in range(0, part, 128):
-            lanes, cols = pl.ds(at, 128), pl.ds(j * part + at, 128)
-            gated = both_ref[j, pl.ds(width, width), lanes].astype(jnp.float32)
-            conv = conv_ref[j, :, lanes].astype(jnp.float32)
+            lanes, cols = pl.ds(at, 128), pl.ds(pl.multiple_of(start + at, 128), 128)
+            gated = gates[k][:, lanes].astype(jnp.float32)
+            conv = convs[k][:, lanes].astype(jnp.float32)
             pre = query_ref[:, cols].astype(jnp.float32) * (conv + skip_ref[:, cols] * gated)
             pre_ref[:, cols] = pre
             total = total + pre * pre
     square_ref[...] = jnp.sum(total.T, axis=0, keepdims=True)
 
 
-def gated_output(query, conv, both, skip):
+def together(blocks):
+    count = len(blocks)
+    order = jnp.arange(count, dtype=jnp.int32) ^ lax.axis_index("tok")
+    stacked = jnp.take(jnp.stack(blocks), order, axis=0)
+    return [stacked.transpose(1, 0, 2).reshape(blocks[0].shape[0], -1)]
+
+
+def gated_output(query, skip, convs, gates):
     width, columns = query.shape
-    return pl.pallas_call(
-        pre_kernel,
+    if convs[0].shape[1] % 128:
+        convs, gates = together(convs), together(gates)
+    count = len(convs)
+    return pl.pallas_call(
+        functools.partial(pre_kernel, count),
         out_shape=(
             jax.ShapeDtypeStruct((width, columns), jnp.float32),
             jax.ShapeDtypeStruct((1, width), jnp.float32),
         ),
-        in_specs=[WHOLE] * 4,
+        in_specs=[WHOLE] * (2 + 2 * count),
         out_specs=(WHOLE, WHOLE),
         compiler_params=pltpu.CompilerParams(vmem_limit_bytes=16 * MIB),
         cost_estimate=pl.CostEstimate(flops=6 * width * columns, bytes_accessed=10 * width * columns, transcendentals=0),
-    )(query, conv, both, skip)
+    )(query, skip, *convs, *gates)
 
 
 def scale_kernel(channels, steps, pre_ref, square_ref, gain_ref, out_ref, buf, sems):
@@ -216,13 +268,10 @@
 def local(query, key_in, value_in, filter_store, lag_of_block, skip, out_gain):
     width, columns = query.shape
     count = lax.axis_size("tok")
-    both = gate(count, key_in, value_in, filter_store)
-    everywhere = lax.all_to_all(both, "tok", 0, 0, tiled=True)
-    conv = lax.all_to_all(block_conv(lag_of_block, everywhere), "tok", 0, 0, tiled=True)
-    if conv.shape[2] % 128:
-        conv = conv.transpose(1, 0, 2).reshape(1, width, columns)
-        both = both.transpose(1, 0, 2).reshape(1, 2 * width, columns)
-    pre, square = gated_output(query, conv, both, skip[None, :])
+    filts = exchange(split(count, filter_store))
+    mine = gate(count, key_in, value_in)
+    convs = exchange(block_conv(lag_of_block, filts, exchange(mine)))
+    pre, square = gated_output(query, skip[None, :], convs, mine)
     square = lax.psum(square, "chan")
     return scaled(columns * lax.axis_size("chan"), pre, square, out_gain[None, :])
 

time: 105 us -> 99.2 us (0.945)
  the two profiles are of different devices: /device:TPU:0 before, /device:TPU:12 now
where the time goes in v3:
time: 99.2 us; the launch traced here: 99 us
  waiting for transfers between devices  50.8 us (51%)
  starting transfers between devices  28.8 us (29%)
  Pallas kernels  10.9 us (11%)
  blocking collectives  5.88 us (6%)
  local copies, waits for them, and re-layouts  2.5 us (3%)
    ppermute x21, waiting for transfers between devices, exchange(): lax.ppermute(blocks[k], 'tok', [(d, d ^ k) for d in range(count)])  50.8 us
    ppermute x21, starting transfers between devices, exchange(): lax.ppermute(blocks[k], 'tok', [(d, d ^ k) for d in range(count)])  28.8 us
    pallas_call x1, Pallas kernels, block_conv(): pl.pallas_call(functools.partial(conv_kernel, count, width), out_shape=[j...  7.58 us
    psum x1, blocking collectives, local(): square = lax.psum(square, 'chan')  5.88 us
    unnamed x22, local copies, waits for them, and re-layouts  2.5 us
  transfers between devices with their start and end apart: 21, of which 14 were waited for; matrix products, arithmetic and copies ran while one was open for 0% of the time, Pallas kernels for 0%

profile of v3, /device:TPU:12, one launch (start us, length us, event | category | flops | bytes accessed | tf_op | source)
XLA Modules:
  0.0 99.0 jit_solution(9059820736111708681)
XLA Ops:
  3.2 1.6 %collective-permute-start.7 = (bf16[256,256]{1,0:T(8,128)(2,1)S(1)}, bf16[256,256]{1,0:T(8,128)(2,1)S(1)}, u32[]{:S(2)}, u32[]{:S(2)}) collective-permute-start(bf16[256,256]{1,0:T(8,128)(2,1)S(1)} %get-tuple-element.40.refs_9_), channel_id=1, source_target_pairs={{0,4},{4,0},{8,12},{12,8},{16,20},{20,16},{24,28},{28,24},{1,5},{5... | collective-permute-start | bytes 393224 | tf_op jit(solution)/shard_map/ppermute | solution.py:42
  5.3 1.5 %collective-permute-start.9 = (bf16[256,256]{1,0:T(8,128)(2,1)S(1)}, bf16[256,256]{1,0:T(8,128)(2,1)S(1)}, u32[]{:S(2)}, u32[]{:S(2)}) collective-permute-start(bf16[256,256]{1,0:T(8,128)(2,1)S(1)} %get-tuple-element.42.refs_11_), channel_id=1, source_target_pairs={{0,12},{4,8},{8,4},{12,0},{16,28},{20,24},{24,20},{28,16},{1,13},{... | collective-permute-start | bytes 393224 | tf_op jit(solution)/shard_map/ppermute | solution.py:42
  6.8 2.6 %collective-permute-start.10 = (bf16[256,256]{1,0:T(8,128)(2,1)S(1)}, bf16[256,256]{1,0:T(8,128)(2,1)S(1)}, u32[]{:S(2)}, u32[]{:S(2)}) collective-permute-start(bf16[256,256]{1,0:T(8,128)(2,1)S(1)} %get-tuple-element.43.refs_12_), channel_id=1, source_target_pairs={{0,16},{4,20},{8,24},{12,28},{16,0},{20,4},{24,8},{28,12},{1,17},{... | collective-permute-start | bytes 393224 | tf_op jit(solution)/shard_map/ppermute | solution.py:42
  10.9 1.6 %collective-permute-start.12 = (bf16[256,256]{1,0:T(8,128)(2,1)S(1)}, bf16[256,256]{1,0:T(8,128)(2,1)S(1)}, u32[]{:S(2)}, u32[]{:S(2)}) collective-permute-start(bf16[256,256]{1,0:T(8,128)(2,1)S(1)} %get-tuple-element.45.refs_14_), channel_id=1, source_target_pairs={{0,24},{4,28},{8,16},{12,20},{16,8},{20,12},{24,0},{28,4},{1,25},{... | collective-permute-start | bytes 393224 | tf_op jit(solution)/shard_map/ppermute | solution.py:42
  13.5 1.6 %collective-permute-done.9.refs_11_ = bf16[256,256]{1,0:T(8,128)(2,1)S(1)} collective-permute-done((bf16[256,256]{1,0:T(8,128)(2,1)S(1)}, bf16[256,256]{1,0:T(8,128)(2,1)S(1)}, u32[]{:S(2)}, u32[]{:S(2)}) %collective-permute-start.9) | collective-permute-done | bytes 131104 | tf_op jit(solution)/shard_map/ppermute | solution.py:42
  16.5 7.6 %collective-permute-done.10.refs_12_ = bf16[256,256]{1,0:T(8,128)(2,1)S(1)} collective-permute-done((bf16[256,256]{1,0:T(8,128)(2,1)S(1)}, bf16[256,256]{1,0:T(8,128)(2,1)S(1)}, u32[]{:S(2)}, u32[]{:S(2)}) %collective-permute-start.10) | collective-permute-done | bytes 131104 | tf_op jit(solution)/shard_map/ppermute | solution.py:42
  24.0 3.2 %collective-permute-done.11.refs_13_ = bf16[256,256]{1,0:T(8,128)(2,1)S(1)} collective-permute-done((bf16[256,256]{1,0:T(8,128)(2,1)S(1)}, bf16[256,256]{1,0:T(8,128)(2,1)S(1)}, u32[]{:S(2)}, u32[]{:S(2)}) %collective-permute-start.11) | collective-permute-done | bytes 131104 | tf_op jit(solution)/shard_map/ppermute | solution.py:42
  27.2 2.2 %collective-permute-start.2 = (bf16[256,256]{1,0:T(8,128)(2,1)S(1)}, bf16[256,256]{1,0:T(8,128)(2,1)S(1)}, u32[]{:S(2)}, u32[]{:S(2)}) collective-permute-start(bf16[256,256]{1,0:T(8,128)(2,1)S(1)} %get-tuple-element.34), channel_id=1, source_target_pairs={{0,12},{4,8},{8,4},{12,0},{16,28},{20,24},{24,20},{28,16},{1,13},{... | collective-permute-start | bytes 393224 | tf_op jit(solution)/shard_map/ppermute | solution.py:42
  31.1 7.3 %collective-permute-done.13.refs_15_ = bf16[256,256]{1,0:T(8,128)(2,1)S(1)} collective-permute-done((bf16[256,256]{1,0:T(8,128)(2,1)S(1)}, bf16[256,256]{1,0:T(8,128)(2,1)S(1)}, u32[]{:S(2)}, u32[]{:S(2)}) %collective-permute-start.13) | collective-permute-done | bytes 131104 | tf_op jit(solution)/shard_map/ppermute | solution.py:42
  38.4 5.0 %collective-permute-start.6 = (bf16[256,256]{1,0:T(8,128)(2,1)S(1)}, bf16[256,256]{1,0:T(8,128)(2,1)S(1)}, u32[]{:S(2)}, u32[]{:S(2)}) collective-permute-start(bf16[256,256]{1,0:T(8,128)(2,1)S(1)} %get-tuple-element.38), channel_id=1, source_target_pairs={{0,28},{4,24},{8,20},{12,16},{16,12},{20,8},{24,4},{28,0},{1,29},{... | collective-permute-start | bytes 393224 | tf_op jit(solution)/shard_map/ppermute | solution.py:42
  43.4 2.1 %collective-permute-done.4.refs_5_ = bf16[256,256]{1,0:T(8,128)(2,1)S(1)} collective-permute-done((bf16[256,256]{1,0:T(8,128)(2,1)S(1)}, bf16[256,256]{1,0:T(8,128)(2,1)S(1)}, u32[]{:S(2)}, u32[]{:S(2)}) %collective-permute-start.4) | collective-permute-done | bytes 131104 | tf_op jit(solution)/shard_map/ppermute | solution.py:42
  45.5 7.0 %collective-permute-done.5.refs_6_ = bf16[256,256]{1,0:T(8,128)(2,1)S(1)} collective-permute-done((bf16[256,256]{1,0:T(8,128)(2,1)S(1)}, bf16[256,256]{1,0:T(8,128)(2,1)S(1)}, u32[]{:S(2)}, u32[]{:S(2)}) %collective-permute-start.5) | collective-permute-done | bytes 131104 | tf_op jit(solution)/shard_map/ppermute | solution.py:42
  52.5 2.3 %collective-permute-done.6.refs_7_ = bf16[256,256]{1,0:T(8,128)(2,1)S(1)} collective-permute-done((bf16[256,256]{1,0:T(8,128)(2,1)S(1)}, bf16[256,256]{1,0:T(8,128)(2,1)S(1)}, u32[]{:S(2)}, u32[]{:S(2)}) %collective-permute-start.6) | collective-permute-done | bytes 131104 | tf_op jit(solution)/shard_map/ppermute | solution.py:42
  54.9 7.6 %shard_map.111 = (bf16[256,256]{1,0:T(8,128)(2,1)S(1)}, bf16[256,256]{1,0:T(8,128)(2,1)S(1)}, bf16[256,256]{1,0:T(8,128)(2,1)S(1)}, bf16[256,256]{1,0:T(8,128)(2...) custom-call(s32[8]{0:T(128)S(1)} %copy-done.6, ...), custom_call_target="tpu_custom_call" | custom-call | flops 3758096384 | bytes 3145728 | tf_op jit(solution)/shard_map/pallas_call | solution.py:180
  63.1 2.9 %collective-permute-start.16 = (bf16[256,256]{1,0:T(8,128)(2,1)S(1)}, bf16[256,256]{1,0:T(8,128)(2,1)S(1)}, u32[]{:S(2)}, u32[]{:S(2)}) collective-permute-start(bf16[256,256]{1,0:T(8,128)(2,1)S(1)} %get-tuple-element.50), channel_id=1, source_target_pairs={{0,12},{4,8},{8,4},{12,0},{16,28},{20,24},{24,20},{28,16},{1,13},{... | collective-permute-start | bytes 393224 | tf_op jit(solution)/shard_map/ppermute | solution.py:42
  66.0 1.5 %collective-permute-start.17 = (bf16[256,256]{1,0:T(8,128)(2,1)S(1)}, bf16[256,256]{1,0:T(8,128)(2,1)S(1)}, u32[]{:S(2)}, u32[]{:S(2)}) collective-permute-start(bf16[256,256]{1,0:T(8,128)(2,1)S(1)} %get-tuple-element.51), channel_id=1, source_target_pairs={{0,16},{4,20},{8,24},{12,28},{16,0},{20,4},{24,8},{28,12},{1,17},{... | collective-permute-start | bytes 393224 | tf_op jit(solution)/shard_map/ppermute | solution.py:42
  68.9 2.1 %collective-permute-start.19 = (bf16[256,256]{1,0:T(8,128)(2,1)S(1)}, bf16[256,256]{1,0:T(8,128)(2,1)S(1)}, u32[]{:S(2)}, u32[]{:S(2)}) collective-permute-start(bf16[256,256]{1,0:T(8,128)(2,1)S(1)} %get-tuple-element.53), channel_id=1, source_target_pairs={{0,24},{4,28},{8,16},{12,20},{16,8},{20,12},{24,0},{28,4},{1,25},{... | collective-permute-start | bytes 393224 | tf_op jit(solution)/shard_map/ppermute | solution.py:42
  71.1 1.5 %collective-permute-start.20 = (bf16[256,256]{1,0:T(8,128)(2,1)S(1)}, bf16[256,256]{1,0:T(8,128)(2,1)S(1)}, u32[]{:S(2)}, u32[]{:S(2)}) collective-permute-start(bf16[256,256]{1,0:T(8,128)(2,1)S(1)} %get-tuple-element.54), channel_id=1, source_target_pairs={{0,28},{4,24},{8,20},{12,16},{16,12},{20,8},{24,4},{28,0},{1,29},{... | collective-permute-start | bytes 393224 | tf_op jit(solution)/shard_map/ppermute | solution.py:42
  72.9 9.1 %collective-permute-done.17.refs_4_ = bf16[256,256]{1,0:T(8,128)(2,1)S(1)} collective-permute-done((bf16[256,256]{1,0:T(8,128)(2,1)S(1)}, bf16[256,256]{1,0:T(8,128)(2,1)S(1)}, u32[]{:S(2)}, u32[]{:S(2)}) %collective-permute-start.17) | collective-permute-done | bytes 131104 | tf_op jit(solution)/shard_map/ppermute | solution.py:42
  82.0 2.8 %collective-permute-done.18.refs_5_ = bf16[256,256]{1,0:T(8,128)(2,1)S(1)} collective-permute-done((bf16[256,256]{1,0:T(8,128)(2,1)S(1)}, bf16[256,256]{1,0:T(8,128)(2,1)S(1)}, u32[]{:S(2)}, u32[]{:S(2)}) %collective-permute-start.18) | collective-permute-done | bytes 131104 | tf_op jit(solution)/shard_map/ppermute | solution.py:42
  84.8 3.6 %collective-permute-done.19.refs_6_ = bf16[256,256]{1,0:T(8,128)(2,1)S(1)} collective-permute-done((bf16[256,256]{1,0:T(8,128)(2,1)S(1)}, bf16[256,256]{1,0:T(8,128)(2,1)S(1)}, u32[]{:S(2)}, u32[]{:S(2)}) %collective-permute-start.19) | collective-permute-done | bytes 131104 | tf_op jit(solution)/shard_map/ppermute | solution.py:42
  88.4 2.4 %collective-permute-done.20.refs_7_ = bf16[256,256]{1,0:T(8,128)(2,1)S(1)} collective-permute-done((bf16[256,256]{1,0:T(8,128)(2,1)S(1)}, bf16[256,256]{1,0:T(8,128)(2,1)S(1)}, u32[]{:S(2)}, u32[]{:S(2)}) %collective-permute-start.20) | collective-permute-done | bytes 131104 | tf_op jit(solution)/shard_map/ppermute | solution.py:42
  91.6 5.9 %psum.7.square_ref = f32[1,256]{1,0:T(1,128)S(1)} all-reduce(f32[1,256]{1,0:T(1,128)S(1)} %get-tuple-element.56), channel_id=1, replica_groups=mesh['tok'=8,'chan'=4] {'chan'}, use_global_device_ids=true, to_apply=%region_0.0 | all-reduce | flops 256 | bytes 2048 | tf_op jit(solution)/shard_map/psum | solution.py:275
  97.5 1.5 %shard_map.113 = f32[256,2048]{1,0:T(8,128)} custom-call(f32[256,2048]{1,0:T(8,128)S(1)} %get-tuple-element.55.pre_ref, f32[1,256]{1,0:T(1,128)S(1)} %psum.7.square_ref, f32[1,2048]{1,0:T(1,128)S(1)} %bitcast.3), custom_call_target="tpu_custom_call" | custom-call | flops 1048576 | bytes 4194304 | tf_op jit(solution)/shard_map/pallas_call | solution.py:257
  (46 shorter events, 12.3 us)
Async XLA Ops:
  2.5 52.4 %copy-start.7 = (bf16[256,512]{1,0:T(8,128)(2,1)S(1)}, bf16[256,512]{1,0:T(8,128)(2,1)}, u32[]{:S(2)}) copy-start(bf16[256,512]{1,0:T(8,128)(2,1)} %constant.11.clone.il_ref) | copy-start | bytes 786436
  2.5 52.4 %copy-start.8 = (bf16[256,512]{1,0:T(8,128)(2,1)S(1)}, bf16[256,512]{1,0:T(8,128)(2,1)}, u32[]{:S(2)}) copy-start(bf16[256,512]{1,0:T(8,128)(2,1)} %constant.10.clone.ih_ref) | copy-start | bytes 786436
  2.5 52.4 %copy-start.9 = (bf16[512,256]{1,0:T(8,128)(2,1)S(1)}, bf16[512,256]{1,0:T(8,128)(2,1)}, u32[]{:S(2)}) copy-start(bf16[512,256]{1,0:T(8,128)(2,1)} %constant.9.clone.fl_ref) | copy-start | bytes 786436
  3.2 7.7 %collective-permute-start.7 = (bf16[256,256]{1,0:T(8,128)(2,1)S(1)}, bf16[256,256]{1,0:T(8,128)(2,1)S(1)}, u32[]{:S(2)}, u32[]{:S(2)}) collective-permute-start(bf16[256,256]{1,0:T(8,128)(2,1)S(1)} %get-tuple-element.40.refs_9_), channel_id=1, source_target_pairs={{0,4},{4,0},{8,12},{12,8},{16,20},{20,16},{24,28},{28,24},{1,5},{5... | collective-permute-start | bytes 393224 | tf_op jit(solution)/shard_map/ppermute | solution.py:42
  4.8 8.7 %collective-permute-start.8 = (bf16[256,256]{1,0:T(8,128)(2,1)S(1)}, bf16[256,256]{1,0:T(8,128)(2,1)S(1)}, u32[]{:S(2)}, u32[]{:S(2)}) collective-permute-start(bf16[256,256]{1,0:T(8,128)(2,1)S(1)} %get-tuple-element.41.refs_10_), channel_id=1, source_target_pairs={{0,8},{4,12},{8,0},{12,4},{16,24},{20,28},{24,16},{28,20},{1,9},{5... | collective-permute-start | bytes 393224 | tf_op jit(solution)/shard_map/ppermute | solution.py:42
  5.3 9.8 %collective-permute-start.9 = (bf16[256,256]{1,0:T(8,128)(2,1)S(1)}, bf16[256,256]{1,0:T(8,128)(2,1)S(1)}, u32[]{:S(2)}, u32[]{:S(2)}) collective-permute-start(bf16[256,256]{1,0:T(8,128)(2,1)S(1)} %get-tuple-element.42.refs_11_), channel_id=1, source_target_pairs={{0,12},{4,8},{8,4},{12,0},{16,28},{20,24},{24,20},{28,16},{1,13},{... | collective-permute-start | bytes 393224 | tf_op jit(solution)/shard_map/ppermute | solution.py:42
  6.8 17.2 %collective-permute-start.10 = (bf16[256,256]{1,0:T(8,128)(2,1)S(1)}, bf16[256,256]{1,0:T(8,128)(2,1)S(1)}, u32[]{:S(2)}, u32[]{:S(2)}) collective-permute-start(bf16[256,256]{1,0:T(8,128)(2,1)S(1)} %get-tuple-element.43.refs_12_), channel_id=1, source_target_pairs={{0,16},{4,20},{8,24},{12,28},{16,0},{20,4},{24,8},{28,12},{1,17},{... | collective-permute-start | bytes 393224 | tf_op jit(solution)/shard_map/ppermute | solution.py:42
  9.4 17.8 %collective-permute-start.11 = (bf16[256,256]{1,0:T(8,128)(2,1)S(1)}, bf16[256,256]{1,0:T(8,128)(2,1)S(1)}, u32[]{:S(2)}, u32[]{:S(2)}) collective-permute-start(bf16[256,256]{1,0:T(8,128)(2,1)S(1)} %get-tuple-element.44.refs_13_), channel_id=1, source_target_pairs={{0,20},{4,16},{8,28},{12,24},{16,4},{20,0},{24,12},{28,8},{1,21},{... | collective-permute-start | bytes 393224 | tf_op jit(solution)/shard_map/ppermute | solution.py:42
  10.9 19.1 %collective-permute-start.12 = (bf16[256,256]{1,0:T(8,128)(2,1)S(1)}, bf16[256,256]{1,0:T(8,128)(2,1)S(1)}, u32[]{:S(2)}, u32[]{:S(2)}) collective-permute-start(bf16[256,256]{1,0:T(8,128)(2,1)S(1)} %get-tuple-element.45.refs_14_), channel_id=1, source_target_pairs={{0,24},{4,28},{8,16},{12,20},{16,8},{20,12},{24,0},{28,4},{1,25},{... | collective-permute-start | bytes 393224 | tf_op jit(solution)/shard_map/ppermute | solution.py:42
  13.5 24.9 %collective-permute-start.13 = (bf16[256,256]{1,0:T(8,128)(2,1)S(1)}, bf16[256,256]{1,0:T(8,128)(2,1)S(1)}, u32[]{:S(2)}, u32[]{:S(2)}) collective-permute-start(bf16[256,256]{1,0:T(8,128)(2,1)S(1)} %get-tuple-element.46.refs_15_), channel_id=1, source_target_pairs={{0,28},{4,24},{8,20},{12,16},{16,12},{20,8},{24,4},{28,0},{1,29},{... | collective-permute-start | bytes 393224 | tf_op jit(solution)/shard_map/ppermute | solution.py:42
  15.1 23.2 %collective-permute-start = (bf16[256,256]{1,0:T(8,128)(2,1)S(1)}, bf16[256,256]{1,0:T(8,128)(2,1)S(1)}, u32[]{:S(2)}, u32[]{:S(2)}) collective-permute-start(bf16[256,256]{1,0:T(8,128)(2,1)S(1)} %get-tuple-element.32), channel_id=1, source_target_pairs={{0,4},{4,0},{8,12},{12,8},{16,20},{20,16},{24,28},{28,24},{1,5},{5... | collective-permute-start | bytes 393224 | tf_op jit(solution)/shard_map/ppermute | solution.py:42
  24.0 14.3 %collective-permute-start.1 = (bf16[256,256]{1,0:T(8,128)(2,1)S(1)}, bf16[256,256]{1,0:T(8,128)(2,1)S(1)}, u32[]{:S(2)}, u32[]{:S(2)}) collective-permute-start(bf16[256,256]{1,0:T(8,128)(2,1)S(1)} %get-tuple-element.33), channel_id=1, source_target_pairs={{0,8},{4,12},{8,0},{12,4},{16,24},{20,28},{24,16},{28,20},{1,9},{5... | collective-permute-start | bytes 393224 | tf_op jit(solution)/shard_map/ppermute | solution.py:42
  27.2 16.1 %collective-permute-start.2 = (bf16[256,256]{1,0:T(8,128)(2,1)S(1)}, bf16[256,256]{1,0:T(8,128)(2,1)S(1)}, u32[]{:S(2)}, u32[]{:S(2)}) collective-permute-start(bf16[256,256]{1,0:T(8,128)(2,1)S(1)} %get-tuple-element.34), channel_id=1, source_target_pairs={{0,12},{4,8},{8,4},{12,0},{16,28},{20,24},{24,20},{28,16},{1,13},{... | collective-permute-start | bytes 393224 | tf_op jit(solution)/shard_map/ppermute | solution.py:42
  30.0 13.4 %collective-permute-start.3 = (bf16[256,256]{1,0:T(8,128)(2,1)S(1)}, bf16[256,256]{1,0:T(8,128)(2,1)S(1)}, u32[]{:S(2)}, u32[]{:S(2)}) collective-permute-start(bf16[256,256]{1,0:T(8,128)(2,1)S(1)} %get-tuple-element.35), channel_id=1, source_target_pairs={{0,16},{4,20},{8,24},{12,28},{16,0},{20,4},{24,8},{28,12},{1,17},{... | collective-permute-start | bytes 393224 | tf_op jit(solution)/shard_map/ppermute | solution.py:42
  38.3 7.1 %collective-permute-start.4 = (bf16[256,256]{1,0:T(8,128)(2,1)S(1)}, bf16[256,256]{1,0:T(8,128)(2,1)S(1)}, u32[]{:S(2)}, u32[]{:S(2)}) collective-permute-start(bf16[256,256]{1,0:T(8,128)(2,1)S(1)} %get-tuple-element.36), channel_id=1, source_target_pairs={{0,20},{4,16},{8,28},{12,24},{16,4},{20,0},{24,12},{28,8},{1,21},{... | collective-permute-start | bytes 393224 | tf_op jit(solution)/shard_map/ppermute | solution.py:42
  38.3 14.1 %collective-permute-start.5 = (bf16[256,256]{1,0:T(8,128)(2,1)S(1)}, bf16[256,256]{1,0:T(8,128)(2,1)S(1)}, u32[]{:S(2)}, u32[]{:S(2)}) collective-permute-start(bf16[256,256]{1,0:T(8,128)(2,1)S(1)} %get-tuple-element.37), channel_id=1, source_target_pairs={{0,24},{4,28},{8,16},{12,20},{16,8},{20,12},{24,0},{28,4},{1,25},{... | collective-permute-start | bytes 393224 | tf_op jit(solution)/shard_map/ppermute | solution.py:42
  38.4 16.5 %collective-permute-start.6 = (bf16[256,256]{1,0:T(8,128)(2,1)S(1)}, bf16[256,256]{1,0:T(8,128)(2,1)S(1)}, u32[]{:S(2)}, u32[]{:S(2)}) collective-permute-start(bf16[256,256]{1,0:T(8,128)(2,1)S(1)} %get-tuple-element.38), channel_id=1, source_target_pairs={{0,28},{4,24},{8,20},{12,16},{16,12},{20,8},{24,4},{28,0},{1,29},{... | collective-permute-start | bytes 393224 | tf_op jit(solution)/shard_map/ppermute | solution.py:42
  62.5 6.5 %collective-permute-start.14 = (bf16[256,256]{1,0:T(8,128)(2,1)S(1)}, bf16[256,256]{1,0:T(8,128)(2,1)S(1)}, u32[]{:S(2)}, u32[]{:S(2)}) collective-permute-start(bf16[256,256]{1,0:T(8,128)(2,1)S(1)} %get-tuple-element.48), channel_id=1, source_target_pairs={{0,4},{4,0},{8,12},{12,8},{16,20},{20,16},{24,28},{28,24},{1,5},{5... | collective-permute-start | bytes 393224 | tf_op jit(solution)/shard_map/ppermute | solution.py:42
  63.1 8.0 %collective-permute-start.15 = (bf16[256,256]{1,0:T(8,128)(2,1)S(1)}, bf16[256,256]{1,0:T(8,128)(2,1)S(1)}, u32[]{:S(2)}, u32[]{:S(2)}) collective-permute-start(bf16[256,256]{1,0:T(8,128)(2,1)S(1)} %get-tuple-element.49), channel_id=1, source_target_pairs={{0,8},{4,12},{8,0},{12,4},{16,24},{20,28},{24,16},{28,20},{1,9},{5... | collective-permute-start | bytes 393224 | tf_op jit(solution)/shard_map/ppermute | solution.py:42
  63.1 9.8 %collective-permute-start.16 = (bf16[256,256]{1,0:T(8,128)(2,1)S(1)}, bf16[256,256]{1,0:T(8,128)(2,1)S(1)}, u32[]{:S(2)}, u32[]{:S(2)}) collective-permute-start(bf16[256,256]{1,0:T(8,128)(2,1)S(1)} %get-tuple-element.50), channel_id=1, source_target_pairs={{0,12},{4,8},{8,4},{12,0},{16,28},{20,24},{24,20},{28,16},{1,13},{... | collective-permute-start | bytes 393224 | tf_op jit(solution)/shard_map/ppermute | solution.py:42
  66.0 15.9 %collective-permute-start.17 = (bf16[256,256]{1,0:T(8,128)(2,1)S(1)}, bf16[256,256]{1,0:T(8,128)(2,1)S(1)}, u32[]{:S(2)}, u32[]{:S(2)}) collective-permute-start(bf16[256,256]{1,0:T(8,128)(2,1)S(1)} %get-tuple-element.51), channel_id=1, source_target_pairs={{0,16},{4,20},{8,24},{12,28},{16,0},{20,4},{24,8},{28,12},{1,17},{... | collective-permute-start | bytes 393224 | tf_op jit(solution)/shard_map/ppermute | solution.py:42
  67.5 17.2 %collective-permute-start.18 = (bf16[256,256]{1,0:T(8,128)(2,1)S(1)}, bf16[256,256]{1,0:T(8,128)(2,1)S(1)}, u32[]{:S(2)}, u32[]{:S(2)}) collective-permute-start(bf16[256,256]{1,0:T(8,128)(2,1)S(1)} %get-tuple-element.52), channel_id=1, source_target_pairs={{0,20},{4,16},{8,28},{12,24},{16,4},{20,0},{24,12},{28,8},{1,21},{... | collective-permute-start | bytes 393224 | tf_op jit(solution)/shard_map/ppermute | solution.py:42
  68.9 19.4 %collective-permute-start.19 = (bf16[256,256]{1,0:T(8,128)(2,1)S(1)}, bf16[256,256]{1,0:T(8,128)(2,1)S(1)}, u32[]{:S(2)}, u32[]{:S(2)}) collective-permute-start(bf16[256,256]{1,0:T(8,128)(2,1)S(1)} %get-tuple-element.53), channel_id=1, source_target_pairs={{0,24},{4,28},{8,16},{12,20},{16,8},{20,12},{24,0},{28,4},{1,25},{... | collective-permute-start | bytes 393224 | tf_op jit(solution)/shard_map/ppermute | solution.py:42
  71.1 19.7 %collective-permute-start.20 = (bf16[256,256]{1,0:T(8,128)(2,1)S(1)}, bf16[256,256]{1,0:T(8,128)(2,1)S(1)}, u32[]{:S(2)}, u32[]{:S(2)}) collective-permute-start(bf16[256,256]{1,0:T(8,128)(2,1)S(1)} %get-tuple-element.54), channel_id=1, source_target_pairs={{0,28},{4,24},{8,20},{12,16},{16,12},{20,8},{24,4},{28,0},{1,29},{... | collective-permute-start | bytes 393224 | tf_op jit(solution)/shard_map/ppermute | solution.py:42
  (8 other events, 222.2 us)

commit v4 on v3

--- a/solution.py
+++ b/solution.py
@@ -36,11 +36,15 @@
     return lax.axis_index("tok") ^ step
 
 
-def exchange(blocks):
-    count = len(blocks)
-    return [blocks[0]] + [
-        lax.ppermute(blocks[k], "tok", [(d, d ^ k) for d in range(count)]) for k in range(1, count)
-    ]
+def send(block, step, count):
+    return lax.ppermute(block, "tok", [(d, d ^ step) for d in range(count)])
+
+
+def far_first(count):
+    half = count // 2
+    far = list(range(half, count, 2)) + list(range(half + 1, count, 2))
+    near = list(range(2, half)) + [1]
+    return far, near
 
 
 def columns_of(step, part):
@@ -116,14 +120,69 @@
     )(key_in, value_in)
 
 
-def conv_kernel(count, width, lag_ref, fh_ref, fl_ref, ih_ref, il_ref, *refs):
-    filts, gates, outs, (fs, gs, ss) = refs[:count], refs[count : 2 * count], refs[2 * count : 3 * count], refs[3 * count :]
-    dot = functools.partial(jnp.dot, preferred_element_type=jnp.float32)
-    for k in range(count):
-        filt, gated = filts[k][...], gates[k][...]
-        fs[lag_ref[partner(k)]] = dot(fh_ref[...], filt) + dot(fl_ref[...], filt)
-        gs[partner(k)] = dot(fh_ref[...], gated) + dot(fl_ref[...], gated)
-    columns = filts[0].shape[1]
+def dot(x, y):
+    return jnp.dot(x, y, preferred_element_type=jnp.float32)
+
+
+def transform(high, low, block):
+    return dot(high, block) + dot(low, block)
+
+
+def filter_kernel(steps, lag_ref, high_ref, low_ref, *refs):
+    blocks, out = refs[:-1], refs[-1]
+    for k, block in zip(steps, blocks):
+        out[lag_ref[partner(k)]] = transform(high_ref[...], low_ref[...], block[...])
+
+
+def gated_kernel(steps, high_ref, low_ref, *refs):
+    blocks, out = refs[:-1], refs[-1]
+    for k, block in zip(steps, blocks):
+        out[partner(k)] = transform(high_ref[...], low_ref[...], block[...])
+
+
+def spectra_shape(count, block):
+    width, columns = block.shape
+    return jax.ShapeDtypeStruct((count, 2 * width, columns), jnp.float32)
+
+
+def transform_cost(count, block, passes):
+    width, columns = block.shape
+    return pl.CostEstimate(
+        flops=4 * passes * count * width * width * columns,
+        bytes_accessed=10 * count * width * columns,
+        transcendentals=0,
+    )
+
+
+def filter_spectra(lag_of_block, high, low, blocks):
+    steps = list(blocks)
+    return pl.pallas_call(
+        functools.partial(filter_kernel, steps),
+        out_shape=spectra_shape(len(steps), blocks[steps[0]]),
+        in_specs=[pl.BlockSpec(memory_space=pltpu.SMEM)] + [WHOLE] * (2 + len(steps)),
+        out_specs=WHOLE,
+        compiler_params=pltpu.CompilerParams(vmem_limit_bytes=16 * MIB),
+        cost_estimate=transform_cost(len(steps), blocks[steps[0]], 2),
+    )(lag_of_block, high, low, *[blocks[k] for k in steps])
+
+
+def gated_spectra(count, high, low, blocks):
+    steps = list(blocks)
+    return pl.pallas_call(
+        functools.partial(gated_kernel, steps),
+        out_shape=spectra_shape(count, blocks[steps[0]]),
+        in_specs=[WHOLE] * (2 + len(steps)),
+        out_specs=WHOLE,
+        compiler_params=pltpu.CompilerParams(vmem_limit_bytes=16 * MIB),
+        cost_estimate=transform_cost(len(steps), blocks[steps[0]], 2),
+    )(high, low, *[blocks[k] for k in steps])
+
+
+def product_kernel(count, steps, first, fh_ref, fl_ref, ih_ref, il_ref, fs, gs, *refs):
+    blocks, (gs, sh, sl), outs, ss = refs[: len(steps)], refs[len(steps) : len(steps) + 3], refs[len(steps) + 3 : -1], refs[-1]
+    width, columns = outs[0].shape
+    for k, block in zip(steps, blocks):
+        gs[partner(k)] = transform(fh_ref[...], fl_ref[...], block[...])
     lane = min(128, columns)
 
     def products(row, sign):
@@ -165,43 +224,69 @@
     def _(row):
         products(row, -1)
 
-    for k in range(count):
+    for at, k in enumerate(first + [k for k in range(count) if k not in first]):
         total = ss[partner(k)]
         high = total.astype(jnp.bfloat16)
         low = (total - high.astype(jnp.float32)).astype(jnp.bfloat16)
-        outs[k][...] = (dot(ih_ref[...], high) + dot(ih_ref[...], low) + dot(il_ref[...], high)).astype(jnp.bfloat16)
-
-
-def block_conv(lag_of_block, filts, gates):
-    count = len(filts)
-    width, columns = filts[0].shape
-    tabs = [jnp.asarray(t) for t in tables(width)]
-    spectra = pltpu.VMEM((count, 2 * width, columns), jnp.float32)
-    return pl.pallas_call(
-        functools.partial(conv_kernel, count, width),
-        out_shape=[jax.ShapeDtypeStruct((width, columns), jnp.bfloat16)] * count,
-        in_specs=[pl.BlockSpec(memory_space=pltpu.SMEM)] + [WHOLE] * (4 + 2 * count),
-        out_specs=[WHOLE] * count,
-        scratch_shapes=[spectra, spectra, spectra],
-        compiler_params=pltpu.CompilerParams(vmem_limit_bytes=32 * MIB),
-        cost_estimate=pl.CostEstimate(
-            flops=2 * count * width * 2 * width * columns * 7,
-            bytes_accessed=6 * count * width * columns,
-            transcendentals=0,
-        ),
-    )(lag_of_block, *tabs, *filts, *gates)
-
-
-def pre_kernel(count, query_ref, skip_ref, *refs):
+        if k in first:
+            outs[at][...] = inverse(ih_ref[...], il_ref[...], high, low)
+        else:
+            sh[partner(k)] = high
+            sl[partner(k)] = low
+
+
+def inverse(table_high, table_low, high, low):
+    return (dot(table_high, high) + dot(table_high, low) + dot(table_low, high)).astype(jnp.bfloat16)
+
+
+def products(count, first, tabs, filt, gated, blocks):
+    steps = list(blocks)
+    width, columns = blocks[steps[0]].shape
+    half = jax.ShapeDtypeStruct((count, 2 * width, columns), jnp.bfloat16)
+    found = pl.pallas_call(
+        functools.partial(product_kernel, count, steps, first),
+        out_shape=[jax.ShapeDtypeStruct(gated.shape, jnp.float32), half, half]
+        + [jax.ShapeDtypeStruct((width, columns), jnp.bfloat16)] * len(first),
+        in_specs=[WHOLE] * (6 + len(steps)),
+        out_specs=[WHOLE] * (3 + len(first)),
+        scratch_shapes=[pltpu.VMEM(gated.shape, jnp.float32)],
+        input_output_aliases={5: 0},
+        compiler_params=pltpu.CompilerParams(vmem_limit_bytes=20 * MIB),
+        cost_estimate=transform_cost(count, blocks[steps[0]], 7),
+    )(*tabs, filt, gated, *[blocks[k] for k in steps])
+    return found[1], found[2], dict(zip(first, found[3:]))
+
+
+def inverse_kernel(steps, ih_ref, il_ref, sh, sl, *outs):
+    for k, out in zip(steps, outs):
+        out[...] = inverse(ih_ref[...], il_ref[...], sh[partner(k)], sl[partner(k)])
+
+
+def inverses(steps, tabs, high, low):
+    count, twice, columns = high.shape
+    block = jax.ShapeDtypeStruct((twice // 2, columns), jnp.bfloat16)
+    found = pl.pallas_call(
+        functools.partial(inverse_kernel, steps),
+        out_shape=[block] * len(steps),
+        in_specs=[WHOLE] * 4,
+        out_specs=[WHOLE] * len(steps),
+        compiler_params=pltpu.CompilerParams(vmem_limit_bytes=16 * MIB),
+        cost_estimate=transform_cost(len(steps), block, 3),
+    )(*tabs[2:], high, low)
+    return dict(zip(steps, found))
+
+
+def pre_kernel(steps, query_ref, skip_ref, *refs):
+    count = len(steps)
     convs, gates, (pre_ref, square_ref) = refs[:count], refs[count : 2 * count], refs[2 * count :]
     width, part = convs[0].shape
     total = jnp.zeros((width, 128), jnp.float32)
-    for k in range(count):
+    for at_k, k in enumerate(steps):
         start = partner(k) * part if count > 1 else 0
         for at in range(0, part, 128):
             lanes, cols = pl.ds(at, 128), pl.ds(pl.multiple_of(start + at, 128), 128)
-            gated = gates[k][:, lanes].astype(jnp.float32)
-            conv = convs[k][:, lanes].astype(jnp.float32)
+            gated = gates[at_k][:, lanes].astype(jnp.float32)
+            conv = convs[at_k][:, lanes].astype(jnp.float32)
             pre = query_ref[:, cols].astype(jnp.float32) * (conv + skip_ref[:, cols] * gated)
             pre_ref[:, cols] = pre
             total = total + pre * pre
@@ -209,19 +294,21 @@
 
 
 def together(blocks):
+    blocks = [blocks[k] for k in range(len(blocks))]
     count = len(blocks)
     order = jnp.arange(count, dtype=jnp.int32) ^ lax.axis_index("tok")
     stacked = jnp.take(jnp.stack(blocks), order, axis=0)
-    return [stacked.transpose(1, 0, 2).reshape(blocks[0].shape[0], -1)]
+    return {0: stacked.transpose(1, 0, 2).reshape(blocks[0].shape[0], -1)}
 
 
 def gated_output(query, skip, convs, gates):
     width, columns = query.shape
+    steps = list(convs)
     if convs[0].shape[1] % 128:
-        convs, gates = together(convs), together(gates)
-    count = len(convs)
-    return pl.pallas_call(
-        functools.partial(pre_kernel, count),
+        convs, gates, steps = together(convs), together(gates), [0]
+    count = len(steps)
+    return pl.pallas_call(
+        functools.partial(pre_kernel, steps),
         out_shape=(
             jax.ShapeDtypeStruct((width, columns), jnp.float32),
             jax.ShapeDtypeStruct((1, width), jnp.float32),
@@ -230,7 +317,7 @@
         out_specs=(WHOLE, WHOLE),
         compiler_params=pltpu.CompilerParams(vmem_limit_bytes=16 * MIB),
         cost_estimate=pl.CostEstimate(flops=6 * width * columns, bytes_accessed=10 * width * columns, transcendentals=0),
-    )(query, skip, *convs, *gates)
+    )(query, skip, *[convs[k] for k in steps], *[gates[k] for k in steps])
 
 
 def scale_kernel(channels, steps, pre_ref, square_ref, gain_ref, out_ref, buf, sems):
@@ -268,9 +355,30 @@
 def local(query, key_in, value_in, filter_store, lag_of_block, skip, out_gain):
     width, columns = query.shape
     count = lax.axis_size("tok")
-    filts = exchange(split(count, filter_store))
+    tabs = [jnp.asarray(t) for t in tables(width)]
+    own = split(count, filter_store)
+    held, key_in, value_in = lax.optimization_barrier((own[0], key_in, value_in))
     mine = gate(count, key_in, value_in)
-    convs = exchange(block_conv(lag_of_block, filts, exchange(mine)))
+    far, near = far_first(count)
+    filts, gates, convs = {}, {}, {}
+    for k in far + near:
+        filts[k] = send(own[k], k, count)
+    gated_order = []
+    for at in range(max(len(far), len(near))):
+        gated_order += far[at : at + 1] + near[at : at + 1]
+    for k in gated_order:
+        gates[k] = send(mine[k], k, count)
+    filts[0], gates[0] = held, mine[0]
+    filt = filter_spectra(lag_of_block, *tabs[:2], filts)
+    early = gated_order[: count // 2] + [0]
+    gated = gated_spectra(count, *tabs[:2], {k: gates[k] for k in early})
+    first = far[:2]
+    high, low, found = products(count, first, tabs, filt, gated, {k: gates[k] for k in gates if k not in early})
+    rest = [k for k in far + near if k not in first] + [0]
+    found.update(inverses(rest, tabs, high, low))
+    for k in far + near:
+        convs[k] = send(found[k], k, count)
+    convs[0] = found[0]
     pre, square = gated_output(query, skip[None, :], convs, mine)
     square = lax.psum(square, "chan")
     return scaled(columns * lax.axis_size("chan"), pre, square, out_gain[None, :])

time: 99.2 us -> 95 us (0.958)
  the two profiles are of different devices: /device:TPU:12 before, /device:TPU:0 now
where the time goes in v4:
time: 95 us; the launch traced here: 94.5 us
  waiting for transfers between devices  37 us (39%)
  starting transfers between devices  35 us (37%)
  Pallas kernels  12.3 us (13%)
  blocking collectives  6.38 us (7%)
  local copies, waits for them, and re-layouts  3.71 us (4%)
    ppermute x21, waiting for transfers between devices, send(): return lax.ppermute(block, 'tok', [(d, d ^ step) for d in range(count)])  37 us
    ppermute x21, starting transfers between devices, send(): return lax.ppermute(block, 'tok', [(d, d ^ step) for d in range(count)])  35 us
    psum x1, blocking collectives, local(): square = lax.psum(square, 'chan')  6.38 us
    pallas_call x1, Pallas kernels, products(): pl.pallas_call(functools.partial(product_kernel, count, steps, first), ou...  4.72 us
    unnamed x22, local copies, waits for them, and re-layouts  3.71 us
    pallas_call x1, Pallas kernels, filter_spectra(): pl.pallas_call(functools.partial(filter_kernel, steps), out_shape=spectra...  1.93 us
  transfers between devices with their start and end apart: 21, of which 9 were waited for; matrix products, arithmetic and copies ran while one was open for 0% of the time, Pallas kernels for 5%

profile of v4, /device:TPU:0, one launch (start us, length us, event | category | flops | bytes accessed | tf_op | source)
XLA Modules:
  0.0 94.5 jit_solution(11033966033183727275)
XLA Ops:
  1.5 4.1 %collective-permute-start = (bf16[256,256]{1,0:T(8,128)(2,1)S(1)}, bf16[256,256]{1,0:T(8,128)(2,1)S(1)}, u32[]{:S(2)}, u32[]{:S(2)}) collective-permute-start(bf16[256,256]{1,0:T(8,128)(2,1)S(1)} %get-tuple-element.36), channel_id=1, source_target_pairs={{0,16},{4,20},{8,24},{12,28},{16,0},{20,4},{24,8},{28,12},{1,17},{... | collective-permute-start | bytes 393224 | tf_op jit(solution)/shard_map/ppermute | solution.py:40
  6.9 2.6 %collective-permute-start.2 = (bf16[256,256]{1,0:T(8,128)(2,1)S(1)}, bf16[256,256]{1,0:T(8,128)(2,1)S(1)}, u32[]{:S(2)}, u32[]{:S(2)}) collective-permute-start(bf16[256,256]{1,0:T(8,128)(2,1)S(1)} %get-tuple-element.38), channel_id=1, source_target_pairs={{0,20},{4,16},{8,28},{12,24},{16,4},{20,0},{24,12},{28,8},{1,21},{... | collective-permute-start | bytes 393224 | tf_op jit(solution)/shard_map/ppermute | solution.py:40
  14.5 6.6 %collective-permute-done.refs_0_ = bf16[256,256]{1,0:T(8,128)(2,1)S(1)} collective-permute-done((bf16[256,256]{1,0:T(8,128)(2,1)S(1)}, bf16[256,256]{1,0:T(8,128)(2,1)S(1)}, u32[]{:S(2)}, u32[]{:S(2)}) %collective-permute-start) | collective-permute-done | bytes 131104 | tf_op jit(solution)/shard_map/ppermute | solution.py:40
  21.1 5.6 %collective-permute-start.8 = (bf16[256,256]{1,0:T(8,128)(2,1)S(1)}, bf16[256,256]{1,0:T(8,128)(2,1)S(1)}, u32[]{:S(2)}, u32[]{:S(2)}) collective-permute-start(bf16[256,256]{1,0:T(8,128)(2,1)S(1)} %get-tuple-element.48.refs_12_), channel_id=1, source_target_pairs={{0,8},{4,12},{8,0},{12,4},{16,24},{20,28},{24,16},{28,20},{1,9},{5... | collective-permute-start | bytes 393224 | tf_op jit(solution)/shard_map/ppermute | solution.py:40
  26.8 4.1 %collective-permute-done.2.refs_2_ = bf16[256,256]{1,0:T(8,128)(2,1)S(1)} collective-permute-done((bf16[256,256]{1,0:T(8,128)(2,1)S(1)}, bf16[256,256]{1,0:T(8,128)(2,1)S(1)}, u32[]{:S(2)}, u32[]{:S(2)}) %collective-permute-start.2) | collective-permute-done | bytes 131104 | tf_op jit(solution)/shard_map/ppermute | solution.py:40
  30.8 2.5 %collective-permute-start.9 = (bf16[256,256]{1,0:T(8,128)(2,1)S(1)}, bf16[256,256]{1,0:T(8,128)(2,1)S(1)}, u32[]{:S(2)}, u32[]{:S(2)}) collective-permute-start(bf16[256,256]{1,0:T(8,128)(2,1)S(1)} %get-tuple-element.49.refs_9_), channel_id=1, source_target_pairs={{0,24},{4,28},{8,16},{12,20},{16,8},{20,12},{24,0},{28,4},{1,25},{... | collective-permute-start | bytes 393224 | tf_op jit(solution)/shard_map/ppermute | solution.py:40
  33.8 2.4 %collective-permute-start.5 = (bf16[256,256]{1,0:T(8,128)(2,1)S(1)}, bf16[256,256]{1,0:T(8,128)(2,1)S(1)}, u32[]{:S(2)}, u32[]{:S(2)}) collective-permute-start(bf16[256,256]{1,0:T(8,128)(2,1)S(1)} %get-tuple-element.41), channel_id=1, source_target_pairs={{0,12},{4,8},{8,4},{12,0},{16,28},{20,24},{24,20},{28,16},{1,13},{... | collective-permute-start | bytes 393224 | tf_op jit(solution)/shard_map/ppermute | solution.py:40
  36.3 1.6 %collective-permute-done.7.refs_0_ = bf16[256,256]{1,0:T(8,128)(2,1)S(1)} collective-permute-done((bf16[256,256]{1,0:T(8,128)(2,1)S(1)}, bf16[256,256]{1,0:T(8,128)(2,1)S(1)}, u32[]{:S(2)}, u32[]{:S(2)}) %collective-permute-start.7) | collective-permute-done | bytes 131104 | tf_op jit(solution)/shard_map/ppermute | solution.py:40
  37.9 1.9 %collective-permute-start.6 = (bf16[256,256]{1,0:T(8,128)(2,1)S(1)}, bf16[256,256]{1,0:T(8,128)(2,1)S(1)}, u32[]{:S(2)}, u32[]{:S(2)}) collective-permute-start(bf16[256,256]{1,0:T(8,128)(2,1)S(1)} %get-tuple-element.42), channel_id=1, source_target_pairs={{0,4},{4,0},{8,12},{12,8},{16,20},{20,16},{24,28},{28,24},{1,5},{5... | collective-permute-start | bytes 393224 | tf_op jit(solution)/shard_map/ppermute | solution.py:40
  40.8 2.0 %collective-permute-done.10.refs_3_ = bf16[256,256]{1,0:T(8,128)(2,1)S(1)} collective-permute-done((bf16[256,256]{1,0:T(8,128)(2,1)S(1)}, bf16[256,256]{1,0:T(8,128)(2,1)S(1)}, u32[]{:S(2)}, u32[]{:S(2)}) %collective-permute-start.10) | collective-permute-done | bytes 131104 | tf_op jit(solution)/shard_map/ppermute | solution.py:40
  42.9 1.7 %collective-permute-start.13 = (bf16[256,256]{1,0:T(8,128)(2,1)S(1)}, bf16[256,256]{1,0:T(8,128)(2,1)S(1)}, u32[]{:S(2)}, u32[]{:S(2)}) collective-permute-start(bf16[256,256]{1,0:T(8,128)(2,1)S(1)} %get-tuple-element.54.refs_11_), channel_id=1, source_target_pairs={{0,28},{4,24},{8,20},{12,16},{16,12},{20,8},{24,4},{28,0},{1,29},{... | collective-permute-start | bytes 393224 | tf_op jit(solution)/shard_map/ppermute | solution.py:40
  45.5 7.0 %collective-permute-done.6.refs_6_ = bf16[256,256]{1,0:T(8,128)(2,1)S(1)} collective-permute-done((bf16[256,256]{1,0:T(8,128)(2,1)S(1)}, bf16[256,256]{1,0:T(8,128)(2,1)S(1)}, u32[]{:S(2)}, u32[]{:S(2)}) %collective-permute-start.6) | collective-permute-done | bytes 131104 | tf_op jit(solution)/shard_map/ppermute | solution.py:40
  52.5 1.9 %shard_map.110.fs = f32[8,512,256]{2,1,0:T(8,128)S(1)} custom-call(s32[8]{0:T(128)S(1)} %copy-done.10, bf16[512,256]{1,0:T(8,128)(2,1)S(1)} %copy-done.5, bf16[512,256]{1,0:T(8,128)(2,1)S(1)} %copy-done.4, bf16[256,256]{1,0:T(8,128)(2,1)S(1)} %collective-permute-done.refs_0_, bf16[256,256]{1,0:T(8,128)(2,1)S(1)} %collective-permute-done.1.refs_1_, ...), custom_call_target="tpu_custom_call" | custom-call | flops 1073741824 | bytes 5242880 | tf_op jit(solution)/shard_map/pallas_call | solution.py:159
  54.5 4.7 %shard_map.113 = (f32[8,512,256]{2,1,0:T(8,128)S(1)}, bf16[8,512,256]{2,1,0:T(8,128)(2,1)S(1)}, bf16[8,512,256]{2,1,0:T(8,128)(2,1)S(1)}, bf16[256,256]{1,0:T(8,128)(2,1)S(1)}, bf16[256,256]{1,0:T(8,128)(2,1)S(1)}) custom-call(bf16[512,256]{1,0:T(8,128)(2,1)S(1)} %copy-done.5, bf16[512,256]{1,0:T(8,128)(2,1)S(1)} %copy-done.4, ...), custom_call_target="tpu_custom_call", output_to_operand_aliasing={{0}: (5, {})} | custom-call | flops 3758096384 | bytes 5242880 | tf_op jit(solution)/shard_map/pallas_call | solution.py:246
  59.2 1.7 %collective-permute-start.14 = (bf16[256,256]{1,0:T(8,128)(2,1)S(1)}, bf16[256,256]{1,0:T(8,128)(2,1)S(1)}, u32[]{:S(2)}, u32[]{:S(2)}) collective-permute-start(bf16[256,256]{1,0:T(8,128)(2,1)S(1)} %get-tuple-element.55), channel_id=1, source_target_pairs={{0,16},{4,20},{8,24},{12,28},{16,0},{20,4},{24,8},{28,12},{1,17},{... | collective-permute-start | bytes 393224 | tf_op jit(solution)/shard_map/ppermute | solution.py:40
  60.9 2.5 %collective-permute-start.15 = (bf16[256,256]{1,0:T(8,128)(2,1)S(1)}, bf16[256,256]{1,0:T(8,128)(2,1)S(1)}, u32[]{:S(2)}, u32[]{:S(2)}) collective-permute-start(bf16[256,256]{1,0:T(8,128)(2,1)S(1)} %get-tuple-element.56), channel_id=1, source_target_pairs={{0,24},{4,28},{8,16},{12,20},{16,8},{20,12},{24,0},{28,4},{1,25},{... | collective-permute-start | bytes 393224 | tf_op jit(solution)/shard_map/ppermute | solution.py:40
  63.4 1.4 %shard_map.114 = (bf16[256,256]{1,0:T(8,128)(2,1)S(1)}, bf16[256,256]{1,0:T(8,128)(2,1)S(1)}, bf16[256,256]{1,0:T(8,128)(2,1)S(1)}, bf16[256,256]{1,0:T(8,128)(2...) custom-call(bf16[256,512]{1,0:T(8,128)(2,1)S(1)} %copy-done.7, bf16[256,512]{1,0:T(8,128)(2,1)S(1)} %copy-done.6, ...), custom_call_target="tpu_custom_call" | custom-call | flops 1207959552 | bytes 3932160 | tf_op jit(solution)/shard_map/pallas_call | solution.py:268
  64.8 2.0 %collective-permute-start.16 = (bf16[256,256]{1,0:T(8,128)(2,1)S(1)}, bf16[256,256]{1,0:T(8,128)(2,1)S(1)}, u32[]{:S(2)}, u32[]{:S(2)}) collective-permute-start(bf16[256,256]{1,0:T(8,128)(2,1)S(1)} %get-tuple-element.59), channel_id=1, source_target_pairs={{0,20},{4,16},{8,28},{12,24},{16,4},{20,0},{24,12},{28,8},{1,21},{... | collective-permute-start | bytes 393224 | tf_op jit(solution)/shard_map/ppermute | solution.py:40
  66.8 1.8 %collective-permute-start.17 = (bf16[256,256]{1,0:T(8,128)(2,1)S(1)}, bf16[256,256]{1,0:T(8,128)(2,1)S(1)}, u32[]{:S(2)}, u32[]{:S(2)}) collective-permute-start(bf16[256,256]{1,0:T(8,128)(2,1)S(1)} %get-tuple-element.60), channel_id=1, source_target_pairs={{0,28},{4,24},{8,20},{12,16},{16,12},{20,8},{24,4},{28,0},{1,29},{... | collective-permute-start | bytes 393224 | tf_op jit(solution)/shard_map/ppermute | solution.py:40
  69.3 7.9 %collective-permute-done.14.refs_0_ = bf16[256,256]{1,0:T(8,128)(2,1)S(1)} collective-permute-done((bf16[256,256]{1,0:T(8,128)(2,1)S(1)}, bf16[256,256]{1,0:T(8,128)(2,1)S(1)}, u32[]{:S(2)}, u32[]{:S(2)}) %collective-permute-start.14) | collective-permute-done | bytes 131104 | tf_op jit(solution)/shard_map/ppermute | solution.py:40
  78.0 5.1 %collective-permute-done.16.refs_2_ = bf16[256,256]{1,0:T(8,128)(2,1)S(1)} collective-permute-done((bf16[256,256]{1,0:T(8,128)(2,1)S(1)}, bf16[256,256]{1,0:T(8,128)(2,1)S(1)}, u32[]{:S(2)}, u32[]{:S(2)}) %collective-permute-start.16) | collective-permute-done | bytes 131104 | tf_op jit(solution)/shard_map/ppermute | solution.py:40
  83.8 1.9 %collective-permute-done.20.refs_6_ = bf16[256,256]{1,0:T(8,128)(2,1)S(1)} collective-permute-done((bf16[256,256]{1,0:T(8,128)(2,1)S(1)}, bf16[256,256]{1,0:T(8,128)(2,1)S(1)}, u32[]{:S(2)}, u32[]{:S(2)}) %collective-permute-start.20) | collective-permute-done | bytes 131104 | tf_op jit(solution)/shard_map/ppermute | solution.py:40
  86.6 6.4 %psum.7.square_ref = f32[1,256]{1,0:T(1,128)S(1)} all-reduce(f32[1,256]{1,0:T(1,128)S(1)} %get-tuple-element.66), channel_id=1, replica_groups=mesh['tok'=8,'chan'=4] {'chan'}, use_global_device_ids=true, to_apply=%region_0.0 | all-reduce | flops 256 | bytes 2048 | tf_op jit(solution)/shard_map/psum | solution.py:383
  93.0 1.5 %shard_map.116 = f32[256,2048]{1,0:T(8,128)} custom-call(f32[256,2048]{1,0:T(8,128)S(1)} %get-tuple-element.65.pre_ref, f32[1,256]{1,0:T(1,128)S(1)} %psum.7.square_ref, f32[1,2048]{1,0:T(1,128)S(1)} %bitcast.3), custom_call_target="tpu_custom_call" | custom-call | flops 1048576 | bytes 4194304 | tf_op jit(solution)/shard_map/pallas_call | solution.py:344
  (49 shorter events, 13.3 us)
Async XLA Ops:
  1.2 43.3 %copy-start.4 = (bf16[512,256]{1,0:T(8,128)(2,1)S(1)}, bf16[512,256]{1,0:T(8,128)(2,1)}, u32[]{:S(2)}) copy-start(bf16[512,256]{1,0:T(8,128)(2,1)} %constant.9.clone.low_ref.fl_ref) | copy-start | bytes 786436
  1.2 43.3 %copy-start.5 = (bf16[512,256]{1,0:T(8,128)(2,1)S(1)}, bf16[512,256]{1,0:T(8,128)(2,1)}, u32[]{:S(2)}) copy-start(bf16[512,256]{1,0:T(8,128)(2,1)} %constant.8.clone.high_ref.fh_ref) | copy-start | bytes 786436
  1.5 19.7 %collective-permute-start = (bf16[256,256]{1,0:T(8,128)(2,1)S(1)}, bf16[256,256]{1,0:T(8,128)(2,1)S(1)}, u32[]{:S(2)}, u32[]{:S(2)}) collective-permute-start(bf16[256,256]{1,0:T(8,128)(2,1)S(1)} %get-tuple-element.36), channel_id=1, source_target_pairs={{0,16},{4,20},{8,24},{12,28},{16,0},{20,4},{24,8},{28,12},{1,17},{... | collective-permute-start | bytes 393224 | tf_op jit(solution)/shard_map/ppermute | solution.py:40
  5.6 15.6 %collective-permute-start.1 = (bf16[256,256]{1,0:T(8,128)(2,1)S(1)}, bf16[256,256]{1,0:T(8,128)(2,1)S(1)}, u32[]{:S(2)}, u32[]{:S(2)}) collective-permute-start(bf16[256,256]{1,0:T(8,128)(2,1)S(1)} %get-tuple-element.37), channel_id=1, source_target_pairs={{0,24},{4,28},{8,16},{12,20},{16,8},{20,12},{24,0},{28,4},{1,25},{... | collective-permute-start | bytes 393224 | tf_op jit(solution)/shard_map/ppermute | solution.py:40
  6.9 23.9 %collective-permute-start.2 = (bf16[256,256]{1,0:T(8,128)(2,1)S(1)}, bf16[256,256]{1,0:T(8,128)(2,1)S(1)}, u32[]{:S(2)}, u32[]{:S(2)}) collective-permute-start(bf16[256,256]{1,0:T(8,128)(2,1)S(1)} %get-tuple-element.38), channel_id=1, source_target_pairs={{0,20},{4,16},{8,28},{12,24},{16,4},{20,0},{24,12},{28,8},{1,21},{... | collective-permute-start | bytes 393224 | tf_op jit(solution)/shard_map/ppermute | solution.py:40
  9.5 23.8 %collective-permute-start.3 = (bf16[256,256]{1,0:T(8,128)(2,1)S(1)}, bf16[256,256]{1,0:T(8,128)(2,1)S(1)}, u32[]{:S(2)}, u32[]{:S(2)}) collective-permute-start(bf16[256,256]{1,0:T(8,128)(2,1)S(1)} %get-tuple-element.39), channel_id=1, source_target_pairs={{0,28},{4,24},{8,20},{12,16},{16,12},{20,8},{24,4},{28,0},{1,29},{... | collective-permute-start | bytes 393224 | tf_op jit(solution)/shard_map/ppermute | solution.py:40
  10.4 23.4 %collective-permute-start.4 = (bf16[256,256]{1,0:T(8,128)(2,1)S(1)}, bf16[256,256]{1,0:T(8,128)(2,1)S(1)}, u32[]{:S(2)}, u32[]{:S(2)}) collective-permute-start(bf16[256,256]{1,0:T(8,128)(2,1)S(1)} %get-tuple-element.40), channel_id=1, source_target_pairs={{0,8},{4,12},{8,0},{12,4},{16,24},{20,28},{24,16},{28,20},{1,9},{5... | collective-permute-start | bytes 393224 | tf_op jit(solution)/shard_map/ppermute | solution.py:40
  21.1 16.7 %collective-permute-start.7 = (bf16[256,256]{1,0:T(8,128)(2,1)S(1)}, bf16[256,256]{1,0:T(8,128)(2,1)S(1)}, u32[]{:S(2)}, u32[]{:S(2)}) collective-permute-start(bf16[256,256]{1,0:T(8,128)(2,1)S(1)} %get-tuple-element.47.refs_8_), channel_id=1, source_target_pairs={{0,16},{4,20},{8,24},{12,28},{16,0},{20,4},{24,8},{28,12},{1,17},{... | collective-permute-start | bytes 393224 | tf_op jit(solution)/shard_map/ppermute | solution.py:40
  21.1 18.7 %collective-permute-start.8 = (bf16[256,256]{1,0:T(8,128)(2,1)S(1)}, bf16[256,256]{1,0:T(8,128)(2,1)S(1)}, u32[]{:S(2)}, u32[]{:S(2)}) collective-permute-start(bf16[256,256]{1,0:T(8,128)(2,1)S(1)} %get-tuple-element.48.refs_12_), channel_id=1, source_target_pairs={{0,8},{4,12},{8,0},{12,4},{16,24},{20,28},{24,16},{28,20},{1,9},{5... | collective-permute-start | bytes 393224 | tf_op jit(solution)/shard_map/ppermute | solution.py:40
  30.8 9.0 %collective-permute-start.9 = (bf16[256,256]{1,0:T(8,128)(2,1)S(1)}, bf16[256,256]{1,0:T(8,128)(2,1)S(1)}, u32[]{:S(2)}, u32[]{:S(2)}) collective-permute-start(bf16[256,256]{1,0:T(8,128)(2,1)S(1)} %get-tuple-element.49.refs_9_), channel_id=1, source_target_pairs={{0,24},{4,28},{8,16},{12,20},{16,8},{20,12},{24,0},{28,4},{1,25},{... | collective-permute-start | bytes 393224 | tf_op jit(solution)/shard_map/ppermute | solution.py:40
  33.4 9.5 %collective-permute-start.10 = (bf16[256,256]{1,0:T(8,128)(2,1)S(1)}, bf16[256,256]{1,0:T(8,128)(2,1)S(1)}, u32[]{:S(2)}, u32[]{:S(2)}) collective-permute-start(bf16[256,256]{1,0:T(8,128)(2,1)S(1)} %get-tuple-element.50.refs_13_), channel_id=1, source_target_pairs={{0,12},{4,8},{8,4},{12,0},{16,28},{20,24},{24,20},{28,16},{1,13},{... | collective-permute-start | bytes 393224 | tf_op jit(solution)/shard_map/ppermute | solution.py:40
  33.8 11.6 %collective-permute-start.5 = (bf16[256,256]{1,0:T(8,128)(2,1)S(1)}, bf16[256,256]{1,0:T(8,128)(2,1)S(1)}, u32[]{:S(2)}, u32[]{:S(2)}) collective-permute-start(bf16[256,256]{1,0:T(8,128)(2,1)S(1)} %get-tuple-element.41), channel_id=1, source_target_pairs={{0,12},{4,8},{8,4},{12,0},{16,28},{20,24},{24,20},{28,16},{1,13},{... | collective-permute-start | bytes 393224 | tf_op jit(solution)/shard_map/ppermute | solution.py:40
  37.9 14.6 %collective-permute-start.6 = (bf16[256,256]{1,0:T(8,128)(2,1)S(1)}, bf16[256,256]{1,0:T(8,128)(2,1)S(1)}, u32[]{:S(2)}, u32[]{:S(2)}) collective-permute-start(bf16[256,256]{1,0:T(8,128)(2,1)S(1)} %get-tuple-element.42), channel_id=1, source_target_pairs={{0,4},{4,0},{8,12},{12,8},{16,20},{20,16},{24,28},{28,24},{1,5},{5... | collective-permute-start | bytes 393224 | tf_op jit(solution)/shard_map/ppermute | solution.py:40
  39.8 14.6 %collective-permute-start.11 = (bf16[256,256]{1,0:T(8,128)(2,1)S(1)}, bf16[256,256]{1,0:T(8,128)(2,1)S(1)}, u32[]{:S(2)}, u32[]{:S(2)}) collective-permute-start(bf16[256,256]{1,0:T(8,128)(2,1)S(1)} %get-tuple-element.52.refs_10_), channel_id=1, source_target_pairs={{0,20},{4,16},{8,28},{12,24},{16,4},{20,0},{24,12},{28,8},{1,21},{... | collective-permute-start | bytes 393224 | tf_op jit(solution)/shard_map/ppermute | solution.py:40
  39.8 14.6 %collective-permute-start.12 = (bf16[256,256]{1,0:T(8,128)(2,1)S(1)}, bf16[256,256]{1,0:T(8,128)(2,1)S(1)}, u32[]{:S(2)}, u32[]{:S(2)}) collective-permute-start(bf16[256,256]{1,0:T(8,128)(2,1)S(1)} %get-tuple-element.53.refs_14_), channel_id=1, source_target_pairs={{0,4},{4,0},{8,12},{12,8},{16,20},{20,16},{24,28},{28,24},{1,5},{5... | collective-permute-start | bytes 393224 | tf_op jit(solution)/shard_map/ppermute | solution.py:40
  42.9 11.6 %collective-permute-start.13 = (bf16[256,256]{1,0:T(8,128)(2,1)S(1)}, bf16[256,256]{1,0:T(8,128)(2,1)S(1)}, u32[]{:S(2)}, u32[]{:S(2)}) collective-permute-start(bf16[256,256]{1,0:T(8,128)(2,1)S(1)} %get-tuple-element.54.refs_11_), channel_id=1, source_target_pairs={{0,28},{4,24},{8,20},{12,16},{16,12},{20,8},{24,4},{28,0},{1,29},{... | collective-permute-start | bytes 393224 | tf_op jit(solution)/shard_map/ppermute | solution.py:40
  59.2 18.0 %collective-permute-start.14 = (bf16[256,256]{1,0:T(8,128)(2,1)S(1)}, bf16[256,256]{1,0:T(8,128)(2,1)S(1)}, u32[]{:S(2)}, u32[]{:S(2)}) collective-permute-start(bf16[256,256]{1,0:T(8,128)(2,1)S(1)} %get-tuple-element.55), channel_id=1, source_target_pairs={{0,16},{4,20},{8,24},{12,28},{16,0},{20,4},{24,8},{28,12},{1,17},{... | collective-permute-start | bytes 393224 | tf_op jit(solution)/shard_map/ppermute | solution.py:40
  60.9 16.3 %collective-permute-start.15 = (bf16[256,256]{1,0:T(8,128)(2,1)S(1)}, bf16[256,256]{1,0:T(8,128)(2,1)S(1)}, u32[]{:S(2)}, u32[]{:S(2)}) collective-permute-start(bf16[256,256]{1,0:T(8,128)(2,1)S(1)} %get-tuple-element.56), channel_id=1, source_target_pairs={{0,24},{4,28},{8,16},{12,20},{16,8},{20,12},{24,0},{28,4},{1,25},{... | collective-permute-start | bytes 393224 | tf_op jit(solution)/shard_map/ppermute | solution.py:40
  64.8 28.2 %copy-start.9 = (f32[2048]{0:T(1024)S(1)}, f32[2048]{0:T(1024)}, u32[]{:S(2)}) copy-start(f32[2048]{0:T(1024)} %param.17) | copy-start | bytes 24580
  64.8 18.2 %collective-permute-start.16 = (bf16[256,256]{1,0:T(8,128)(2,1)S(1)}, bf16[256,256]{1,0:T(8,128)(2,1)S(1)}, u32[]{:S(2)}, u32[]{:S(2)}) collective-permute-start(bf16[256,256]{1,0:T(8,128)(2,1)S(1)} %get-tuple-element.59), channel_id=1, source_target_pairs={{0,20},{4,16},{8,28},{12,24},{16,4},{20,0},{24,12},{28,8},{1,21},{... | collective-permute-start | bytes 393224 | tf_op jit(solution)/shard_map/ppermute | solution.py:40
  66.8 16.3 %collective-permute-start.17 = (bf16[256,256]{1,0:T(8,128)(2,1)S(1)}, bf16[256,256]{1,0:T(8,128)(2,1)S(1)}, u32[]{:S(2)}, u32[]{:S(2)}) collective-permute-start(bf16[256,256]{1,0:T(8,128)(2,1)S(1)} %get-tuple-element.60), channel_id=1, source_target_pairs={{0,28},{4,24},{8,20},{12,16},{16,12},{20,8},{24,4},{28,0},{1,29},{... | collective-permute-start | bytes 393224 | tf_op jit(solution)/shard_map/ppermute | solution.py:40
  68.6 14.4 %collective-permute-start.18 = (bf16[256,256]{1,0:T(8,128)(2,1)S(1)}, bf16[256,256]{1,0:T(8,128)(2,1)S(1)}, u32[]{:S(2)}, u32[]{:S(2)}) collective-permute-start(bf16[256,256]{1,0:T(8,128)(2,1)S(1)} %get-tuple-element.61), channel_id=1, source_target_pairs={{0,8},{4,12},{8,0},{12,4},{16,24},{20,28},{24,16},{28,20},{1,9},{5... | collective-permute-start | bytes 393224 | tf_op jit(solution)/shard_map/ppermute | solution.py:40
  77.2 6.6 %collective-permute-start.19 = (bf16[256,256]{1,0:T(8,128)(2,1)S(1)}, bf16[256,256]{1,0:T(8,128)(2,1)S(1)}, u32[]{:S(2)}, u32[]{:S(2)}) collective-permute-start(bf16[256,256]{1,0:T(8,128)(2,1)S(1)} %get-tuple-element.62), channel_id=1, source_target_pairs={{0,12},{4,8},{8,4},{12,0},{16,28},{20,24},{24,20},{28,16},{1,13},{... | collective-permute-start | bytes 393224 | tf_op jit(solution)/shard_map/ppermute | solution.py:40
  77.2 8.5 %collective-permute-start.20 = (bf16[256,256]{1,0:T(8,128)(2,1)S(1)}, bf16[256,256]{1,0:T(8,128)(2,1)S(1)}, u32[]{:S(2)}, u32[]{:S(2)}) collective-permute-start(bf16[256,256]{1,0:T(8,128)(2,1)S(1)} %get-tuple-element.63), channel_id=1, source_target_pairs={{0,4},{4,0},{8,12},{12,8},{16,20},{20,16},{24,28},{28,24},{1,5},{5... | collective-permute-start | bytes 393224 | tf_op jit(solution)/shard_map/ppermute | solution.py:40
  (8 other events, 74.3 us)

commit v5 on v4

--- a/solution.py
+++ b/solution.py
@@ -40,11 +40,14 @@
     return lax.ppermute(block, "tok", [(d, d ^ step) for d in range(count)])
 
 
-def far_first(count):
+def sending_order(count):
     half = count // 2
     far = list(range(half, count, 2)) + list(range(half + 1, count, 2))
     near = list(range(2, half)) + [1]
-    return far, near
+    order = []
+    for at in range(half - 1):
+        order += [far[at], near[at]]
+    return order[:-1] + far[-1:] + order[-1:]
 
 
 def columns_of(step, part):
@@ -359,24 +362,21 @@
     own = split(count, filter_store)
     held, key_in, value_in = lax.optimization_barrier((own[0], key_in, value_in))
     mine = gate(count, key_in, value_in)
-    far, near = far_first(count)
+    order = sending_order(count)
     filts, gates, convs = {}, {}, {}
-    for k in far + near:
+    for k in order:
         filts[k] = send(own[k], k, count)
-    gated_order = []
-    for at in range(max(len(far), len(near))):
-        gated_order += far[at : at + 1] + near[at : at + 1]
-    for k in gated_order:
+    for k in order:
         gates[k] = send(mine[k], k, count)
     filts[0], gates[0] = held, mine[0]
     filt = filter_spectra(lag_of_block, *tabs[:2], filts)
-    early = gated_order[: count // 2] + [0]
+    early = order[: count // 2] + [0]
     gated = gated_spectra(count, *tabs[:2], {k: gates[k] for k in early})
-    first = far[:2]
+    first = order[:2]
     high, low, found = products(count, first, tabs, filt, gated, {k: gates[k] for k in gates if k not in early})
-    rest = [k for k in far + near if k not in first] + [0]
+    rest = order[2:] + [0]
     found.update(inverses(rest, tabs, high, low))
-    for k in far + near:
+    for k in order:
         convs[k] = send(found[k], k, count)
     convs[0] = found[0]
     pre, square = gated_output(query, skip[None, :], convs, mine)

time: 95 us -> 89.5 us (0.942)
  waiting for transfers between devices: 37 us -> 24.5 us
  starting transfers between devices: 35 us -> 42.5 us
    ppermute x21, waiting for transfers between devices: 37 us -> 24.5 us  [send(): return lax.ppermute(block, 'tok', [(d, d ^ step) for d in range(count)])]
    ppermute x21, starting transfers between devices: 35 us -> 42.5 us  [send(): return lax.ppermute(block, 'tok', [(d, d ^ step) for d in range(count)])]
  transfers between devices with their start and end apart: 21 -> 21, of which waited for: 9 -> 8; matrix products, arithmetic and copies ran while one was open for 0% -> 0% of each run, Pallas kernels for 5% -> 6%
where the time goes in v5:
time: 89.5 us; the launch traced here: 88.9 us
  starting transfers between devices  42.5 us (47%)
  waiting for transfers between devices  24.5 us (27%)
  Pallas kernels  12.3 us (14%)
  blocking collectives  5.71 us (6%)
  local copies, waits for them, and re-layouts  3.71 us (4%)
    ppermute x21, starting transfers between devices, send(): return lax.ppermute(block, 'tok', [(d, d ^ step) for d in range(count)])  42.5 us
    ppermute x21, waiting for transfers between devices, send(): return lax.ppermute(block, 'tok', [(d, d ^ step) for d in range(count)])  24.5 us
    psum x1, blocking collectives, local(): square = lax.psum(square, 'chan')  5.71 us
    pallas_call x1, Pallas kernels, products(): pl.pallas_call(functools.partial(product_kernel, count, steps, first), ou...  4.72 us
    unnamed x22, local copies, waits for them, and re-layouts  3.71 us
    pallas_call x1, Pallas kernels, filter_spectra(): pl.pallas_call(functools.partial(filter_kernel, steps), out_shape=spectra...  1.94 us
  transfers between devices with their start and end apart: 21, of which 8 were waited for; matrix products, arithmetic and copies ran while one was open for 0% of the time, Pallas kernels for 6%

profile of v5, /device:TPU:0, one launch (start us, length us, event | category | flops | bytes accessed | tf_op | source)
XLA Modules:
  0.0 88.9 jit_solution(14764787504710024632)
XLA Ops:
  0.0 1.2 %copy-done.1 = bf16[256,2048]{1,0:T(8,128)(2,1)S(1)} copy-done((bf16[256,2048]{1,0:T(8,128)(2,1)S(1)}, bf16[256,2048]{1,0:T(8,128)(2,1)}, u32[]{:S(2)}) %copy-start.1) | copy-done | bytes 1048600
  1.5 4.1 %collective-permute-start = (bf16[256,256]{1,0:T(8,128)(2,1)S(1)}, bf16[256,256]{1,0:T(8,128)(2,1)S(1)}, u32[]{:S(2)}, u32[]{:S(2)}) collective-permute-start(bf16[256,256]{1,0:T(8,128)(2,1)S(1)} %get-tuple-element.36), channel_id=1, source_target_pairs={{0,16},{4,20},{8,24},{12,28},{16,0},{20,4},{24,8},{28,12},{1,17},{... | collective-permute-start | bytes 393224 | tf_op jit(solution)/shard_map/ppermute | solution.py:40
  5.6 1.6 %collective-permute-start.1 = (bf16[256,256]{1,0:T(8,128)(2,1)S(1)}, bf16[256,256]{1,0:T(8,128)(2,1)S(1)}, u32[]{:S(2)}, u32[]{:S(2)}) collective-permute-start(bf16[256,256]{1,0:T(8,128)(2,1)S(1)} %get-tuple-element.37), channel_id=1, source_target_pairs={{0,8},{4,12},{8,0},{12,4},{16,24},{20,28},{24,16},{28,20},{1,9},{5... | collective-permute-start | bytes 393224 | tf_op jit(solution)/shard_map/ppermute | solution.py:40
  7.2 1.8 %collective-permute-start.3 = (bf16[256,256]{1,0:T(8,128)(2,1)S(1)}, bf16[256,256]{1,0:T(8,128)(2,1)S(1)}, u32[]{:S(2)}, u32[]{:S(2)}) collective-permute-start(bf16[256,256]{1,0:T(8,128)(2,1)S(1)} %get-tuple-element.39), channel_id=1, source_target_pairs={{0,12},{4,8},{8,4},{12,0},{16,28},{20,24},{24,20},{28,16},{1,13},{... | collective-permute-start | bytes 393224 | tf_op jit(solution)/shard_map/ppermute | solution.py:40
  9.0 3.5 %collective-permute-start.4 = (bf16[256,256]{1,0:T(8,128)(2,1)S(1)}, bf16[256,256]{1,0:T(8,128)(2,1)S(1)}, u32[]{:S(2)}, u32[]{:S(2)}) collective-permute-start(bf16[256,256]{1,0:T(8,128)(2,1)S(1)} %get-tuple-element.40), channel_id=1, source_target_pairs={{0,20},{4,16},{8,28},{12,24},{16,4},{20,0},{24,12},{28,8},{1,21},{... | collective-permute-start | bytes 393224 | tf_op jit(solution)/shard_map/ppermute | solution.py:40
  15.8 2.2 %collective-permute-start.8 = (bf16[256,256]{1,0:T(8,128)(2,1)S(1)}, bf16[256,256]{1,0:T(8,128)(2,1)S(1)}, u32[]{:S(2)}, u32[]{:S(2)}) collective-permute-start(bf16[256,256]{1,0:T(8,128)(2,1)S(1)} %get-tuple-element.48.refs_9_), channel_id=1, source_target_pairs={{0,8},{4,12},{8,0},{12,4},{16,24},{20,28},{24,16},{28,20},{1,9},{5... | collective-permute-start | bytes 393224 | tf_op jit(solution)/shard_map/ppermute | solution.py:40
  17.9 2.2 %collective-permute-start.9 = (bf16[256,256]{1,0:T(8,128)(2,1)S(1)}, bf16[256,256]{1,0:T(8,128)(2,1)S(1)}, u32[]{:S(2)}, u32[]{:S(2)}) collective-permute-start(bf16[256,256]{1,0:T(8,128)(2,1)S(1)} %get-tuple-element.49.refs_10_), channel_id=1, source_target_pairs={{0,24},{4,28},{8,16},{12,20},{16,8},{20,12},{24,0},{28,4},{1,25},{... | collective-permute-start | bytes 393224 | tf_op jit(solution)/shard_map/ppermute | solution.py:40
  20.5 5.8 %collective-permute-start.10 = (bf16[256,256]{1,0:T(8,128)(2,1)S(1)}, bf16[256,256]{1,0:T(8,128)(2,1)S(1)}, u32[]{:S(2)}, u32[]{:S(2)}) collective-permute-start(bf16[256,256]{1,0:T(8,128)(2,1)S(1)} %get-tuple-element.50.refs_11_), channel_id=1, source_target_pairs={{0,12},{4,8},{8,4},{12,0},{16,28},{20,24},{24,20},{28,16},{1,13},{... | collective-permute-start | bytes 393224 | tf_op jit(solution)/shard_map/ppermute | solution.py:40
  26.3 2.9 %collective-permute-done.4.refs_4_ = bf16[256,256]{1,0:T(8,128)(2,1)S(1)} collective-permute-done((bf16[256,256]{1,0:T(8,128)(2,1)S(1)}, bf16[256,256]{1,0:T(8,128)(2,1)S(1)}, u32[]{:S(2)}, u32[]{:S(2)}) %collective-permute-start.4) | collective-permute-done | bytes 131104 | tf_op jit(solution)/shard_map/ppermute | solution.py:40
  29.2 3.1 %collective-permute-start.5 = (bf16[256,256]{1,0:T(8,128)(2,1)S(1)}, bf16[256,256]{1,0:T(8,128)(2,1)S(1)}, u32[]{:S(2)}, u32[]{:S(2)}) collective-permute-start(bf16[256,256]{1,0:T(8,128)(2,1)S(1)} %get-tuple-element.41), channel_id=1, source_target_pairs={{0,28},{4,24},{8,20},{12,16},{16,12},{20,8},{24,4},{28,0},{1,29},{... | collective-permute-start | bytes 393224 | tf_op jit(solution)/shard_map/ppermute | solution.py:40
  32.4 3.0 %collective-permute-start.6 = (bf16[256,256]{1,0:T(8,128)(2,1)S(1)}, bf16[256,256]{1,0:T(8,128)(2,1)S(1)}, u32[]{:S(2)}, u32[]{:S(2)}) collective-permute-start(bf16[256,256]{1,0:T(8,128)(2,1)S(1)} %get-tuple-element.42), channel_id=1, source_target_pairs={{0,4},{4,0},{8,12},{12,8},{16,20},{20,16},{24,28},{28,24},{1,5},{5... | collective-permute-start | bytes 393224 | tf_op jit(solution)/shard_map/ppermute | solution.py:40
  35.4 1.8 %collective-permute-start.12 = (bf16[256,256]{1,0:T(8,128)(2,1)S(1)}, bf16[256,256]{1,0:T(8,128)(2,1)S(1)}, u32[]{:S(2)}, u32[]{:S(2)}) collective-permute-start(bf16[256,256]{1,0:T(8,128)(2,1)S(1)} %get-tuple-element.53.refs_13_), channel_id=1, source_target_pairs={{0,28},{4,24},{8,20},{12,16},{16,12},{20,8},{24,4},{28,0},{1,29},{... | collective-permute-start | bytes 393224 | tf_op jit(solution)/shard_map/ppermute | solution.py:40
  40.3 1.9 %shard_map.110.fs = f32[8,512,256]{2,1,0:T(8,128)S(1)} custom-call(s32[8]{0:T(128)S(1)} %copy-done.10, bf16[512,256]{1,0:T(8,128)(2,1)S(1)} %copy-done.5, bf16[512,256]{1,0:T(8,128)(2,1)S(1)} %copy-done.4, bf16[256,256]{1,0:T(8,128)(2,1)S(1)} %collective-permute-done.refs_0_, bf16[256,256]{1,0:T(8,128)(2,1)S(1)} %collective-permute-done.1.refs_1_, ...), custom_call_target="tpu_custom_call" | custom-call | flops 1073741824 | bytes 5242880 | tf_op jit(solution)/shard_map/pallas_call | solution.py:162
  42.2 8.3 %collective-permute-done.11.refs_0_ = bf16[256,256]{1,0:T(8,128)(2,1)S(1)} collective-permute-done((bf16[256,256]{1,0:T(8,128)(2,1)S(1)}, bf16[256,256]{1,0:T(8,128)(2,1)S(1)}, u32[]{:S(2)}, u32[]{:S(2)}) %collective-permute-start.11) | collective-permute-done | bytes 131104 | tf_op jit(solution)/shard_map/ppermute | solution.py:40
  50.6 4.7 %shard_map.113 = (f32[8,512,256]{2,1,0:T(8,128)S(1)}, bf16[8,512,256]{2,1,0:T(8,128)(2,1)S(1)}, bf16[8,512,256]{2,1,0:T(8,128)(2,1)S(1)}, bf16[256,256]{1,0:T(8,128)(2,1)S(1)}, bf16[256,256]{1,0:T(8,128)(2,1)S(1)}) custom-call(bf16[512,256]{1,0:T(8,128)(2,1)S(1)} %copy-done.5, bf16[512,256]{1,0:T(8,128)(2,1)S(1)} %copy-done.4, ...), custom_call_target="tpu_custom_call", output_to_operand_aliasing={{0}: (5, {})} | custom-call | flops 3758096384 | bytes 5242880 | tf_op jit(solution)/shard_map/pallas_call | solution.py:249
  55.3 4.4 %collective-permute-start.14 = (bf16[256,256]{1,0:T(8,128)(2,1)S(1)}, bf16[256,256]{1,0:T(8,128)(2,1)S(1)}, u32[]{:S(2)}, u32[]{:S(2)}) collective-permute-start(bf16[256,256]{1,0:T(8,128)(2,1)S(1)} %get-tuple-element.55), channel_id=1, source_target_pairs={{0,16},{4,20},{8,24},{12,28},{16,0},{20,4},{24,8},{28,12},{1,17},{... | collective-permute-start | bytes 393224 | tf_op jit(solution)/shard_map/ppermute | solution.py:40
  59.7 1.4 %shard_map.114 = (bf16[256,256]{1,0:T(8,128)(2,1)S(1)}, bf16[256,256]{1,0:T(8,128)(2,1)S(1)}, bf16[256,256]{1,0:T(8,128)(2,1)S(1)}, bf16[256,256]{1,0:T(8,128)(2...) custom-call(bf16[256,512]{1,0:T(8,128)(2,1)S(1)} %copy-done.7, bf16[256,512]{1,0:T(8,128)(2,1)S(1)} %copy-done.6, ...), custom_call_target="tpu_custom_call" | custom-call | flops 1207959552 | bytes 3932160 | tf_op jit(solution)/shard_map/pallas_call | solution.py:271
  61.1 2.3 %collective-permute-start.16 = (bf16[256,256]{1,0:T(8,128)(2,1)S(1)}, bf16[256,256]{1,0:T(8,128)(2,1)S(1)}, u32[]{:S(2)}, u32[]{:S(2)}) collective-permute-start(bf16[256,256]{1,0:T(8,128)(2,1)S(1)} %get-tuple-element.59), channel_id=1, source_target_pairs={{0,24},{4,28},{8,16},{12,20},{16,8},{20,12},{24,0},{28,4},{1,25},{... | collective-permute-start | bytes 393224 | tf_op jit(solution)/shard_map/ppermute | solution.py:40
  64.6 1.9 %collective-permute-start.18 = (bf16[256,256]{1,0:T(8,128)(2,1)S(1)}, bf16[256,256]{1,0:T(8,128)(2,1)S(1)}, u32[]{:S(2)}, u32[]{:S(2)}) collective-permute-start(bf16[256,256]{1,0:T(8,128)(2,1)S(1)} %get-tuple-element.61), channel_id=1, source_target_pairs={{0,20},{4,16},{8,28},{12,24},{16,4},{20,0},{24,12},{28,8},{1,21},{... | collective-permute-start | bytes 393224 | tf_op jit(solution)/shard_map/ppermute | solution.py:40
  68.7 1.4 %collective-permute-start.20 = (bf16[256,256]{1,0:T(8,128)(2,1)S(1)}, bf16[256,256]{1,0:T(8,128)(2,1)S(1)}, u32[]{:S(2)}, u32[]{:S(2)}) collective-permute-start(bf16[256,256]{1,0:T(8,128)(2,1)S(1)} %get-tuple-element.63), channel_id=1, source_target_pairs={{0,4},{4,0},{8,12},{12,8},{16,20},{20,16},{24,28},{28,24},{1,5},{5... | collective-permute-start | bytes 393224 | tf_op jit(solution)/shard_map/ppermute | solution.py:40
  70.1 1.8 %collective-permute-done.16.refs_2_ = bf16[256,256]{1,0:T(8,128)(2,1)S(1)} collective-permute-done((bf16[256,256]{1,0:T(8,128)(2,1)S(1)}, bf16[256,256]{1,0:T(8,128)(2,1)S(1)}, u32[]{:S(2)}, u32[]{:S(2)}) %collective-permute-start.16) | collective-permute-done | bytes 131104 | tf_op jit(solution)/shard_map/ppermute | solution.py:40
  72.2 8.6 %collective-permute-done.18.refs_4_ = bf16[256,256]{1,0:T(8,128)(2,1)S(1)} collective-permute-done((bf16[256,256]{1,0:T(8,128)(2,1)S(1)}, bf16[256,256]{1,0:T(8,128)(2,1)S(1)}, u32[]{:S(2)}, u32[]{:S(2)}) %collective-permute-start.18) | collective-permute-done | bytes 131104 | tf_op jit(solution)/shard_map/ppermute | solution.py:40
  81.7 5.7 %psum.7.square_ref = f32[1,256]{1,0:T(1,128)S(1)} all-reduce(f32[1,256]{1,0:T(1,128)S(1)} %get-tuple-element.66), channel_id=1, replica_groups=mesh['tok'=8,'chan'=4] {'chan'}, use_global_device_ids=true, to_apply=%region_0.0 | all-reduce | flops 256 | bytes 2048 | tf_op jit(solution)/shard_map/psum | solution.py:383
  87.4 1.5 %shard_map.116 = f32[256,2048]{1,0:T(8,128)} custom-call(f32[256,2048]{1,0:T(8,128)S(1)} %get-tuple-element.65.pre_ref, f32[1,256]{1,0:T(1,128)S(1)} %psum.7.square_ref, f32[1,2048]{1,0:T(1,128)S(1)} %bitcast.3), custom_call_target="tpu_custom_call" | custom-call | flops 1048576 | bytes 4194304 | tf_op jit(solution)/shard_map/pallas_call | solution.py:347
  (49 shorter events, 11.7 us)
Async XLA Ops:
  1.2 37.1 %copy-start.4 = (bf16[512,256]{1,0:T(8,128)(2,1)S(1)}, bf16[512,256]{1,0:T(8,128)(2,1)}, u32[]{:S(2)}) copy-start(bf16[512,256]{1,0:T(8,128)(2,1)} %constant.9.clone.low_ref.fl_ref) | copy-start | bytes 786436
  1.2 37.1 %copy-start.5 = (bf16[512,256]{1,0:T(8,128)(2,1)S(1)}, bf16[512,256]{1,0:T(8,128)(2,1)}, u32[]{:S(2)}) copy-start(bf16[512,256]{1,0:T(8,128)(2,1)} %constant.8.clone.high_ref.fh_ref) | copy-start | bytes 786436
  1.5 14.2 %collective-permute-start = (bf16[256,256]{1,0:T(8,128)(2,1)S(1)}, bf16[256,256]{1,0:T(8,128)(2,1)S(1)}, u32[]{:S(2)}, u32[]{:S(2)}) collective-permute-start(bf16[256,256]{1,0:T(8,128)(2,1)S(1)} %get-tuple-element.36), channel_id=1, source_target_pairs={{0,16},{4,20},{8,24},{12,28},{16,0},{20,4},{24,8},{28,12},{1,17},{... | collective-permute-start | bytes 393224 | tf_op jit(solution)/shard_map/ppermute | solution.py:40
  5.6 10.2 %collective-permute-start.1 = (bf16[256,256]{1,0:T(8,128)(2,1)S(1)}, bf16[256,256]{1,0:T(8,128)(2,1)S(1)}, u32[]{:S(2)}, u32[]{:S(2)}) collective-permute-start(bf16[256,256]{1,0:T(8,128)(2,1)S(1)} %get-tuple-element.37), channel_id=1, source_target_pairs={{0,8},{4,12},{8,0},{12,4},{16,24},{20,28},{24,16},{28,20},{1,9},{5... | collective-permute-start | bytes 393224 | tf_op jit(solution)/shard_map/ppermute | solution.py:40
  7.2 10.8 %collective-permute-start.2 = (bf16[256,256]{1,0:T(8,128)(2,1)S(1)}, bf16[256,256]{1,0:T(8,128)(2,1)S(1)}, u32[]{:S(2)}, u32[]{:S(2)}) collective-permute-start(bf16[256,256]{1,0:T(8,128)(2,1)S(1)} %get-tuple-element.38), channel_id=1, source_target_pairs={{0,24},{4,28},{8,16},{12,20},{16,8},{20,12},{24,0},{28,4},{1,25},{... | collective-permute-start | bytes 393224 | tf_op jit(solution)/shard_map/ppermute | solution.py:40
  7.2 13.3 %collective-permute-start.3 = (bf16[256,256]{1,0:T(8,128)(2,1)S(1)}, bf16[256,256]{1,0:T(8,128)(2,1)S(1)}, u32[]{:S(2)}, u32[]{:S(2)}) collective-permute-start(bf16[256,256]{1,0:T(8,128)(2,1)S(1)} %get-tuple-element.39), channel_id=1, source_target_pairs={{0,12},{4,8},{8,4},{12,0},{16,28},{20,24},{24,20},{28,16},{1,13},{... | collective-permute-start | bytes 393224 | tf_op jit(solution)/shard_map/ppermute | solution.py:40
  9.0 20.3 %collective-permute-start.4 = (bf16[256,256]{1,0:T(8,128)(2,1)S(1)}, bf16[256,256]{1,0:T(8,128)(2,1)S(1)}, u32[]{:S(2)}, u32[]{:S(2)}) collective-permute-start(bf16[256,256]{1,0:T(8,128)(2,1)S(1)} %get-tuple-element.40), channel_id=1, source_target_pairs={{0,20},{4,16},{8,28},{12,24},{16,4},{20,0},{24,12},{28,8},{1,21},{... | collective-permute-start | bytes 393224 | tf_op jit(solution)/shard_map/ppermute | solution.py:40
  15.7 16.8 %collective-permute-start.7 = (bf16[256,256]{1,0:T(8,128)(2,1)S(1)}, bf16[256,256]{1,0:T(8,128)(2,1)S(1)}, u32[]{:S(2)}, u32[]{:S(2)}) collective-permute-start(bf16[256,256]{1,0:T(8,128)(2,1)S(1)} %get-tuple-element.47.refs_8_), channel_id=1, source_target_pairs={{0,16},{4,20},{8,24},{12,28},{16,0},{20,4},{24,8},{28,12},{1,17},{... | collective-permute-start | bytes 393224 | tf_op jit(solution)/shard_map/ppermute | solution.py:40
  15.8 19.6 %collective-permute-start.8 = (bf16[256,256]{1,0:T(8,128)(2,1)S(1)}, bf16[256,256]{1,0:T(8,128)(2,1)S(1)}, u32[]{:S(2)}, u32[]{:S(2)}) collective-permute-start(bf16[256,256]{1,0:T(8,128)(2,1)S(1)} %get-tuple-element.48.refs_9_), channel_id=1, source_target_pairs={{0,8},{4,12},{8,0},{12,4},{16,24},{20,28},{24,16},{28,20},{1,9},{5... | collective-permute-start | bytes 393224 | tf_op jit(solution)/shard_map/ppermute | solution.py:40
  17.9 17.5 %collective-permute-start.9 = (bf16[256,256]{1,0:T(8,128)(2,1)S(1)}, bf16[256,256]{1,0:T(8,128)(2,1)S(1)}, u32[]{:S(2)}, u32[]{:S(2)}) collective-permute-start(bf16[256,256]{1,0:T(8,128)(2,1)S(1)} %get-tuple-element.49.refs_10_), channel_id=1, source_target_pairs={{0,24},{4,28},{8,16},{12,20},{16,8},{20,12},{24,0},{28,4},{1,25},{... | collective-permute-start | bytes 393224 | tf_op jit(solution)/shard_map/ppermute | solution.py:40
  20.5 16.7 %collective-permute-start.10 = (bf16[256,256]{1,0:T(8,128)(2,1)S(1)}, bf16[256,256]{1,0:T(8,128)(2,1)S(1)}, u32[]{:S(2)}, u32[]{:S(2)}) collective-permute-start(bf16[256,256]{1,0:T(8,128)(2,1)S(1)} %get-tuple-element.50.refs_11_), channel_id=1, source_target_pairs={{0,12},{4,8},{8,4},{12,0},{16,28},{20,24},{24,20},{28,16},{1,13},{... | collective-permute-start | bytes 393224 | tf_op jit(solution)/shard_map/ppermute | solution.py:40
  29.2 10.0 %collective-permute-start.5 = (bf16[256,256]{1,0:T(8,128)(2,1)S(1)}, bf16[256,256]{1,0:T(8,128)(2,1)S(1)}, u32[]{:S(2)}, u32[]{:S(2)}) collective-permute-start(bf16[256,256]{1,0:T(8,128)(2,1)S(1)} %get-tuple-element.41), channel_id=1, source_target_pairs={{0,28},{4,24},{8,20},{12,16},{16,12},{20,8},{24,4},{28,0},{1,29},{... | collective-permute-start | bytes 393224 | tf_op jit(solution)/shard_map/ppermute | solution.py:40
  32.4 7.9 %collective-permute-start.6 = (bf16[256,256]{1,0:T(8,128)(2,1)S(1)}, bf16[256,256]{1,0:T(8,128)(2,1)S(1)}, u32[]{:S(2)}, u32[]{:S(2)}) collective-permute-start(bf16[256,256]{1,0:T(8,128)(2,1)S(1)} %get-tuple-element.42), channel_id=1, source_target_pairs={{0,4},{4,0},{8,12},{12,8},{16,20},{20,16},{24,28},{28,24},{1,5},{5... | collective-permute-start | bytes 393224 | tf_op jit(solution)/shard_map/ppermute | solution.py:40
  35.4 15.2 %collective-permute-start.11 = (bf16[256,256]{1,0:T(8,128)(2,1)S(1)}, bf16[256,256]{1,0:T(8,128)(2,1)S(1)}, u32[]{:S(2)}, u32[]{:S(2)}) collective-permute-start(bf16[256,256]{1,0:T(8,128)(2,1)S(1)} %get-tuple-element.52.refs_12_), channel_id=1, source_target_pairs={{0,20},{4,16},{8,28},{12,24},{16,4},{20,0},{24,12},{28,8},{1,21},{... | collective-permute-start | bytes 393224 | tf_op jit(solution)/shard_map/ppermute | solution.py:40
  35.4 15.2 %collective-permute-start.12 = (bf16[256,256]{1,0:T(8,128)(2,1)S(1)}, bf16[256,256]{1,0:T(8,128)(2,1)S(1)}, u32[]{:S(2)}, u32[]{:S(2)}) collective-permute-start(bf16[256,256]{1,0:T(8,128)(2,1)S(1)} %get-tuple-element.53.refs_13_), channel_id=1, source_target_pairs={{0,28},{4,24},{8,20},{12,16},{16,12},{20,8},{24,4},{28,0},{1,29},{... | collective-permute-start | bytes 393224 | tf_op jit(solution)/shard_map/ppermute | solution.py:40
  37.2 13.3 %collective-permute-start.13 = (bf16[256,256]{1,0:T(8,128)(2,1)S(1)}, bf16[256,256]{1,0:T(8,128)(2,1)S(1)}, u32[]{:S(2)}, u32[]{:S(2)}) collective-permute-start(bf16[256,256]{1,0:T(8,128)(2,1)S(1)} %get-tuple-element.54.refs_14_), channel_id=1, source_target_pairs={{0,4},{4,0},{8,12},{12,8},{16,20},{20,16},{24,28},{28,24},{1,5},{5... | collective-permute-start | bytes 393224 | tf_op jit(solution)/shard_map/ppermute | solution.py:40
  55.3 12.3 %collective-permute-start.14 = (bf16[256,256]{1,0:T(8,128)(2,1)S(1)}, bf16[256,256]{1,0:T(8,128)(2,1)S(1)}, u32[]{:S(2)}, u32[]{:S(2)}) collective-permute-start(bf16[256,256]{1,0:T(8,128)(2,1)S(1)} %get-tuple-element.55), channel_id=1, source_target_pairs={{0,16},{4,20},{8,24},{12,28},{16,0},{20,4},{24,8},{28,12},{1,17},{... | collective-permute-start | bytes 393224 | tf_op jit(solution)/shard_map/ppermute | solution.py:40
  59.7 9.1 %collective-permute-start.15 = (bf16[256,256]{1,0:T(8,128)(2,1)S(1)}, bf16[256,256]{1,0:T(8,128)(2,1)S(1)}, u32[]{:S(2)}, u32[]{:S(2)}) collective-permute-start(bf16[256,256]{1,0:T(8,128)(2,1)S(1)} %get-tuple-element.56), channel_id=1, source_target_pairs={{0,8},{4,12},{8,0},{12,4},{16,24},{20,28},{24,16},{28,20},{1,9},{5... | collective-permute-start | bytes 393224 | tf_op jit(solution)/shard_map/ppermute | solution.py:40
  61.1 26.3 %copy-start.9 = (f32[2048]{0:T(1024)S(1)}, f32[2048]{0:T(1024)}, u32[]{:S(2)}) copy-start(f32[2048]{0:T(1024)} %param.17) | copy-start | bytes 24580
  61.1 10.8 %collective-permute-start.16 = (bf16[256,256]{1,0:T(8,128)(2,1)S(1)}, bf16[256,256]{1,0:T(8,128)(2,1)S(1)}, u32[]{:S(2)}, u32[]{:S(2)}) collective-permute-start(bf16[256,256]{1,0:T(8,128)(2,1)S(1)} %get-tuple-element.59), channel_id=1, source_target_pairs={{0,24},{4,28},{8,16},{12,20},{16,8},{20,12},{24,0},{28,4},{1,25},{... | collective-permute-start | bytes 393224 | tf_op jit(solution)/shard_map/ppermute | solution.py:40
  63.4 8.8 %collective-permute-start.17 = (bf16[256,256]{1,0:T(8,128)(2,1)S(1)}, bf16[256,256]{1,0:T(8,128)(2,1)S(1)}, u32[]{:S(2)}, u32[]{:S(2)}) collective-permute-start(bf16[256,256]{1,0:T(8,128)(2,1)S(1)} %get-tuple-element.60), channel_id=1, source_target_pairs={{0,12},{4,8},{8,4},{12,0},{16,28},{20,24},{24,20},{28,16},{1,13},{... | collective-permute-start | bytes 393224 | tf_op jit(solution)/shard_map/ppermute | solution.py:40
  64.6 16.2 %collective-permute-start.18 = (bf16[256,256]{1,0:T(8,128)(2,1)S(1)}, bf16[256,256]{1,0:T(8,128)(2,1)S(1)}, u32[]{:S(2)}, u32[]{:S(2)}) collective-permute-start(bf16[256,256]{1,0:T(8,128)(2,1)S(1)} %get-tuple-element.61), channel_id=1, source_target_pairs={{0,20},{4,16},{8,28},{12,24},{16,4},{20,0},{24,12},{28,8},{1,21},{... | collective-permute-start | bytes 393224 | tf_op jit(solution)/shard_map/ppermute | solution.py:40
  67.6 13.1 %collective-permute-start.19 = (bf16[256,256]{1,0:T(8,128)(2,1)S(1)}, bf16[256,256]{1,0:T(8,128)(2,1)S(1)}, u32[]{:S(2)}, u32[]{:S(2)}) collective-permute-start(bf16[256,256]{1,0:T(8,128)(2,1)S(1)} %get-tuple-element.62), channel_id=1, source_target_pairs={{0,28},{4,24},{8,20},{12,16},{16,12},{20,8},{24,4},{28,0},{1,29},{... | collective-permute-start | bytes 393224 | tf_op jit(solution)/shard_map/ppermute | solution.py:40
  68.7 12.0 %collective-permute-start.20 = (bf16[256,256]{1,0:T(8,128)(2,1)S(1)}, bf16[256,256]{1,0:T(8,128)(2,1)S(1)}, u32[]{:S(2)}, u32[]{:S(2)}) collective-permute-start(bf16[256,256]{1,0:T(8,128)(2,1)S(1)} %get-tuple-element.63), channel_id=1, source_target_pairs={{0,4},{4,0},{8,12},{12,8},{16,20},{20,16},{24,28},{28,24},{1,5},{5... | collective-permute-start | bytes 393224 | tf_op jit(solution)/shard_map/ppermute | solution.py:40
  (8 other events, 70.4 us)

commit v6 on v3

--- a/solution.py
+++ b/solution.py
@@ -11,7 +11,6 @@
 from jax.sharding import PartitionSpec as P
 
 MIB = 1024 * 1024
-BIG = 48 * MIB
 WHOLE = pl.BlockSpec(memory_space=pltpu.VMEM)
 IN_HBM = pl.BlockSpec(memory_space=pltpu.HBM)
 
@@ -36,11 +35,30 @@
     return lax.axis_index("tok") ^ step
 
 
-def exchange(blocks):
-    count = len(blocks)
-    return [blocks[0]] + [
-        lax.ppermute(blocks[k], "tok", [(d, d ^ k) for d in range(count)]) for k in range(1, count)
-    ]
+class Window:
+    def __init__(self, count, size):
+        self.count, self.size, self.arrived = count, size, []
+
+    def send(self, block, step, after=None):
+        if after is None:
+            after = [len(self.arrived) - self.size] if len(self.arrived) >= self.size else []
+        if after:
+            held = lax.optimization_barrier((block, *[self.arrived[i] for i in after]))
+            block = held[0]
+            for i, value in zip(after, held[1:]):
+                self.arrived[i] = value
+        self.arrived.append(lax.ppermute(block, "tok", [(d, d ^ step) for d in range(self.count)]))
+        return len(self.arrived) - 1
+
+
+def sending_order(count):
+    half = count // 2
+    far = list(range(half, count, 2)) + list(range(half + 1, count, 2))
+    near = list(range(2, half)) + [1]
+    order = []
+    for at in range(half - 1):
+        order += [far[at], near[at]]
+    return order[:-1] + far[-1:] + order[-1:]
 
 
 def columns_of(step, part):
@@ -57,8 +75,21 @@
         copy.wait()
 
 
+def chunks_of(part):
+    return 2 if part % 256 == 0 else 1
+
+
+def is_far(step, count):
+    return step >= count // 2
+
+
+def place(step, count, part):
+    parts = chunks_of(part) if is_far(step, count) else 1
+    return [(c * (part // parts), part // parts) for c in range(parts)]
+
+
 def gate_kernel(count, part, key_ref, value_ref, *refs):
-    outs, (key_buf, value_buf, sems) = refs[:count], refs[count:]
+    outs, (key_buf, value_buf, sems) = list(refs[:-3]), refs[-3:]
     copies = []
     for k in range(count):
         cols = columns_of(k, part)
@@ -74,7 +105,9 @@
         for copy in copies[k]:
             copy.wait()
         product = key_buf[k].astype(jnp.float32) * value_buf[k].astype(jnp.float32)
-        outs[k][...] = product.astype(jnp.bfloat16)
+        product = product.astype(jnp.bfloat16)
+        for at, size in place(k, count, part):
+            outs.pop(0)[...] = product[:, at : at + size]
 
 
 def pieces(x, count):
@@ -93,7 +126,7 @@
         in_specs=[IN_HBM],
         out_specs=[WHOLE] * count,
         scratch_shapes=[pltpu.SemaphoreType.DMA((count,))],
-        compiler_params=pltpu.CompilerParams(vmem_limit_bytes=BIG),
+        compiler_params=pltpu.CompilerParams(vmem_limit_bytes=16 * MIB),
         cost_estimate=pl.CostEstimate(flops=0, bytes_accessed=4 * width * columns, transcendentals=0),
     )(filter_store)
 
@@ -103,30 +136,66 @@
     part = columns // count
     if part % 128:
         gated = (key_in.astype(jnp.float32) * value_in.astype(jnp.float32)).astype(jnp.bfloat16)
-        return pieces(gated, count)
+        return [[piece] for piece in pieces(gated, count)]
     block = pltpu.VMEM((count, width, part), jnp.bfloat16)
+    places = [place(k, count, part) for k in range(count)]
+    shapes = [jax.ShapeDtypeStruct((width, size), jnp.bfloat16) for sizes in places for _, size in sizes]
+    found = list(
+        pl.pallas_call(
+            functools.partial(gate_kernel, count, part),
+            out_shape=shapes,
+            in_specs=[IN_HBM] * 2,
+            out_specs=[WHOLE] * len(shapes),
+            scratch_shapes=[block, block, pltpu.SemaphoreType.DMA((2, count))],
+            compiler_params=pltpu.CompilerParams(vmem_limit_bytes=16 * MIB),
+            cost_estimate=pl.CostEstimate(
+                flops=width * columns, bytes_accessed=6 * width * columns, transcendentals=0
+            ),
+        )(key_in, value_in)
+    )
+    return [[found.pop(0) for _ in sizes] for sizes in places]
+
+
+def dot(x, y):
+    return jnp.dot(x, y, preferred_element_type=jnp.float32)
+
+
+def transform(high, low, block):
+    return dot(high, block) + dot(low, block)
+
+
+def filter_kernel(steps, lag_ref, high_ref, low_ref, *refs):
+    blocks, outs = refs[: len(steps)], refs[len(steps) :]
+    chunk = outs[0].shape[2]
+    for k, block in zip(steps, blocks):
+        spectrum = transform(high_ref[...], low_ref[...], block[...])
+        for c, out in enumerate(outs):
+            out[lag_ref[partner(k)]] = spectrum[:, c * chunk : (c + 1) * chunk]
+
+
+def filter_spectra(lag_of_block, high, low, blocks):
+    steps = list(blocks)
+    width, part = blocks[0].shape
+    chunks = chunks_of(part)
+    shape = jax.ShapeDtypeStruct((len(steps), 2 * width, part // chunks), jnp.float32)
     return pl.pallas_call(
-        functools.partial(gate_kernel, count, part),
-        out_shape=[jax.ShapeDtypeStruct((width, part), jnp.bfloat16)] * count,
-        in_specs=[IN_HBM] * 2,
-        out_specs=[WHOLE] * count,
-        scratch_shapes=[block, block, pltpu.SemaphoreType.DMA((2, count))],
-        compiler_params=pltpu.CompilerParams(vmem_limit_bytes=BIG),
-        cost_estimate=pl.CostEstimate(flops=width * columns, bytes_accessed=6 * width * columns, transcendentals=0),
-    )(key_in, value_in)
-
-
-def conv_kernel(count, width, lag_ref, fh_ref, fl_ref, ih_ref, il_ref, *refs):
-    filts, gates, outs, (fs, gs, ss) = refs[:count], refs[count : 2 * count], refs[2 * count : 3 * count], refs[3 * count :]
-    dot = functools.partial(jnp.dot, preferred_element_type=jnp.float32)
-    for k in range(count):
-        filt, gated = filts[k][...], gates[k][...]
-        fs[lag_ref[partner(k)]] = dot(fh_ref[...], filt) + dot(fl_ref[...], filt)
-        gs[partner(k)] = dot(fh_ref[...], gated) + dot(fl_ref[...], gated)
-    columns = filts[0].shape[1]
+        functools.partial(filter_kernel, steps),
+        out_shape=[shape] * chunks,
+        in_specs=[pl.BlockSpec(memory_space=pltpu.SMEM)] + [WHOLE] * (2 + len(steps)),
+        out_specs=[WHOLE] * chunks,
+        compiler_params=pltpu.CompilerParams(vmem_limit_bytes=16 * MIB),
+        cost_estimate=pl.CostEstimate(
+            flops=8 * len(steps) * width * width * part,
+            bytes_accessed=10 * len(steps) * width * part,
+            transcendentals=0,
+        ),
+    )(lag_of_block, high, low, *[blocks[k] for k in steps])
+
+
+def multiply_spectra(count, width, columns, fs, gs, ss):
     lane = min(128, columns)
 
-    def products(row, sign):
+    def tile(row, sign):
         re_rows = pl.ds(pl.multiple_of(row * 8, 8), 8)
         im_rows = pl.ds(pl.multiple_of(row * 8 + width, 8), 8)
         for at in range(0, columns, lane):
@@ -159,49 +228,89 @@
 
     @pl.loop(0, half)
     def _(row):
-        products(row, 1)
+        tile(row, 1)
 
     @pl.loop(half, 2 * half)
     def _(row):
-        products(row, -1)
-
-    for k in range(count):
-        total = ss[partner(k)]
+        tile(row, -1)
+
+
+def pairs(items, columns):
+    size = 2 if columns == 128 else 1
+    return [items[at : at + size] for at in range(0, len(items), size)]
+
+
+def conv_kernel(count, chunk, chunks, steps, ends, fh_ref, fl_ref, ih_ref, il_ref, fs, *refs):
+    blocks, earlier, outs, (gs, ss) = (
+        dict(zip(steps, refs[:count])),
+        refs[count : count + ends[0]],
+        refs[count + ends[0] : -2],
+        refs[-2:],
+    )
+    width, columns = gs.shape[1] // 2, gs.shape[2]
+    here = pl.ds(chunk * columns, columns)
+
+    def block(k):
+        ref = blocks[k]
+        return ref[...] if ref.shape[1] == columns else ref[:, here]
+
+    for group in pairs(steps, columns):
+        found = transform(fh_ref[...], fl_ref[...], jnp.concatenate([block(k) for k in group], axis=1))
+        for at, k in enumerate(group):
+            gs[partner(k)] = found[:, at * columns : (at + 1) * columns]
+    multiply_spectra(count, width, columns, fs, gs, ss)
+    earlier = list(earlier)
+    outs = dict(zip(steps, outs))
+    for group in pairs(steps, columns):
+        total = jnp.concatenate([ss[partner(k)] for k in group], axis=1)
         high = total.astype(jnp.bfloat16)
         low = (total - high.astype(jnp.float32)).astype(jnp.bfloat16)
-        outs[k][...] = (dot(ih_ref[...], high) + dot(ih_ref[...], low) + dot(il_ref[...], high)).astype(jnp.bfloat16)
-
-
-def block_conv(lag_of_block, filts, gates):
-    count = len(filts)
-    width, columns = filts[0].shape
-    tabs = [jnp.asarray(t) for t in tables(width)]
-    spectra = pltpu.VMEM((count, 2 * width, columns), jnp.float32)
-    return pl.pallas_call(
-        functools.partial(conv_kernel, count, width),
-        out_shape=[jax.ShapeDtypeStruct((width, columns), jnp.bfloat16)] * count,
-        in_specs=[pl.BlockSpec(memory_space=pltpu.SMEM)] + [WHOLE] * (4 + 2 * count),
+        conv = dot(ih_ref[...], high) + dot(ih_ref[...], low) + dot(il_ref[...], high)
+        conv = conv.astype(jnp.bfloat16)
+        for at, k in enumerate(group):
+            found = conv[:, at * columns : (at + 1) * columns]
+            if outs[k].shape[1] == columns:
+                outs[k][...] = found
+            else:
+                outs[k][:, : chunk * columns] = earlier.pop(0)[...]
+                outs[k][:, here] = found
+
+
+def block_conv(chunk, chunks, tabs, filt, blocks, earlier):
+    count, twice, columns = filt.shape
+    width = twice // 2
+    steps = list(blocks)
+    whole = [k for k in steps if not is_far(k, count)] if chunk == chunks - 1 else []
+    before = [earlier[k] for k in whole] if earlier else []
+    spectra = pltpu.VMEM((count, twice, columns), jnp.float32)
+    sizes = [columns * chunks if k in whole else columns for k in steps]
+    found = pl.pallas_call(
+        functools.partial(conv_kernel, count, chunk, chunks, steps, [len(before)]),
+        out_shape=[jax.ShapeDtypeStruct((width, size), jnp.bfloat16) for size in sizes],
+        in_specs=[WHOLE] * (5 + count + len(before)),
         out_specs=[WHOLE] * count,
-        scratch_shapes=[spectra, spectra, spectra],
-        compiler_params=pltpu.CompilerParams(vmem_limit_bytes=32 * MIB),
+        scratch_shapes=[spectra, spectra],
+        compiler_params=pltpu.CompilerParams(vmem_limit_bytes=20 * MIB),
         cost_estimate=pl.CostEstimate(
-            flops=2 * count * width * 2 * width * columns * 7,
-            bytes_accessed=6 * count * width * columns,
+            flops=24 * count * width * width * columns,
+            bytes_accessed=14 * count * width * columns,
             transcendentals=0,
         ),
-    )(lag_of_block, *tabs, *filts, *gates)
-
-
-def pre_kernel(count, query_ref, skip_ref, *refs):
+    )(*tabs, filt, *[blocks[k] for k in steps], *before)
+    return dict(zip(steps, found))
+
+
+def pre_kernel(where, part, query_ref, skip_ref, *refs):
+    count = len(where)
     convs, gates, (pre_ref, square_ref) = refs[:count], refs[count : 2 * count], refs[2 * count :]
-    width, part = convs[0].shape
+    width = query_ref.shape[0]
     total = jnp.zeros((width, 128), jnp.float32)
-    for k in range(count):
-        start = partner(k) * part if count > 1 else 0
-        for at in range(0, part, 128):
+    for (k, start), conv_ref, gated_ref in zip(where, convs, gates):
+        start = partner(k) * part + start if part else start
+        for at in range(0, conv_ref.shape[1], 128):
             lanes, cols = pl.ds(at, 128), pl.ds(pl.multiple_of(start + at, 128), 128)
-            gated = gates[k][:, lanes].astype(jnp.float32)
-            conv = convs[k][:, lanes].astype(jnp.float32)
+            gated = gated_ref[:, lanes].astype(jnp.float32)
+            conv = conv_ref[:, lanes].astype(jnp.float32)
             pre = query_ref[:, cols].astype(jnp.float32) * (conv + skip_ref[:, cols] * gated)
             pre_ref[:, cols] = pre
             total = total + pre * pre
@@ -211,26 +320,28 @@
 def together(blocks):
     count = len(blocks)
     order = jnp.arange(count, dtype=jnp.int32) ^ lax.axis_index("tok")
-    stacked = jnp.take(jnp.stack(blocks), order, axis=0)
-    return [stacked.transpose(1, 0, 2).reshape(blocks[0].shape[0], -1)]
-
-
-def gated_output(query, skip, convs, gates):
+    stacked = jnp.take(jnp.stack([blocks[k] for k in range(count)]), order, axis=0)
+    return stacked.transpose(1, 0, 2).reshape(blocks[0].shape[0], -1)
+
+
+def gated_output(query, skip, part, convs, gates):
     width, columns = query.shape
-    if convs[0].shape[1] % 128:
-        convs, gates = together(convs), together(gates)
-    count = len(convs)
+    where = list(convs)
+    if part % 128:
+        convs = {(0, 0): together({k: piece for (k, _), piece in convs.items()})}
+        gates = {(0, 0): together({k: piece for (k, _), piece in gates.items()})}
+        where, part = [(0, 0)], 0
     return pl.pallas_call(
-        functools.partial(pre_kernel, count),
+        functools.partial(pre_kernel, where, part),
         out_shape=(
             jax.ShapeDtypeStruct((width, columns), jnp.float32),
             jax.ShapeDtypeStruct((1, width), jnp.float32),
         ),
-        in_specs=[WHOLE] * (2 + 2 * count),
+        in_specs=[WHOLE] * (2 + 2 * len(where)),
         out_specs=(WHOLE, WHOLE),
         compiler_params=pltpu.CompilerParams(vmem_limit_bytes=16 * MIB),
         cost_estimate=pl.CostEstimate(flops=6 * width * columns, bytes_accessed=10 * width * columns, transcendentals=0),
-    )(query, skip, *convs, *gates)
+    )(query, skip, *[convs[w] for w in where], *[gates[w] for w in where])
 
 
 def scale_kernel(channels, steps, pre_ref, square_ref, gain_ref, out_ref, buf, sems):
@@ -268,10 +379,41 @@
 def local(query, key_in, value_in, filter_store, lag_of_block, skip, out_gain):
     width, columns = query.shape
     count = lax.axis_size("tok")
-    filts = exchange(split(count, filter_store))
+    tabs = [jnp.asarray(t) for t in tables(width)]
+    own = split(count, filter_store)
+    held, key_in, value_in = lax.optimization_barrier((own[0], key_in, value_in))
     mine = gate(count, key_in, value_in)
-    convs = exchange(block_conv(lag_of_block, filts, exchange(mine)))
-    pre, square = gated_output(query, skip[None, :], convs, mine)
+    order = sending_order(count)
+    part = columns // count
+    chunks = chunks_of(part)
+    window = Window(count, 5)
+    filts = {k: window.send(own[k], k) for k in order}
+    arrived = {}
+    for c in range(chunks):
+        for k in order:
+            if c == 0 or is_far(k, count):
+                arrived[k, c] = window.send(mine[k][c], k)
+    filts = {k: window.arrived[i] for k, i in filts.items()}
+    filts[0] = held
+    filt = filter_spectra(lag_of_block, *tabs[:2], filts)
+    convs, done = {}, {}
+    for c in range(chunks):
+        blocks = {k: window.arrived[arrived[k, c if is_far(k, count) else 0]] for k in order}
+        blocks[0] = mine[0][0]
+        done = block_conv(c, chunks, tabs, filt[c], blocks, done)
+        begin = len(window.arrived)
+        for k in order:
+            if is_far(k, count) or c == chunks - 1:
+                at = c * (part // chunks) if is_far(k, count) else 0
+                sent = len(window.arrived)
+                after = [sent - 5]
+                if c and sent < begin + 3:
+                    after = [begin - 4, begin - 3, begin - 2]
+                convs[k, at] = window.send(done[k], k, after)
+    convs = {w: window.arrived[i] for w, i in convs.items()}
+    convs[0, 0] = done[0]
+    gates = {(k, at): mine[k][c] for k in range(count) for c, (at, _) in enumerate(place(k, count, part))}
+    pre, square = gated_output(query, skip[None, :], part, convs, gates)
     square = lax.psum(square, "chan")
     return scaled(columns * lax.axis_size("chan"), pre, square, out_gain[None, :])
 

time: 99.2 us -> 92.9 us (0.936)
  the two profiles are of different devices: /device:TPU:12 before, /device:TPU:0 now
where the time goes in v6:
time: 92.9 us; the launch traced here: 92.7 us
  starting transfers between devices  53 us (57%)
  waiting for transfers between devices  17.9 us (19%)
  Pallas kernels  12.3 us (13%)
  blocking collectives  5.67 us (6%)
  local copies, waits for them, and re-layouts  3.72 us (4%)
    ppermute x29, starting transfers between devices, send(): lax.ppermute(block, 'tok', [(d, d ^ step) for d in range(self.count)])  53 us
    ppermute x29, waiting for transfers between devices, send(): lax.ppermute(block, 'tok', [(d, d ^ step) for d in range(self.count)])  17.9 us
    pallas_call x2, Pallas kernels, block_conv(): pl.pallas_call(functools.partial(conv_kernel, count, chunk, chunks, steps...  6.94 us
    psum x1, blocking collectives, local(): square = lax.psum(square, 'chan')  5.67 us
    unnamed x22, local copies, waits for them, and re-layouts  3.72 us
    pallas_call x1, Pallas kernels, filter_spectra(): pl.pallas_call(functools.partial(filter_kernel, steps), out_shape=[shape]...  1.92 us
  transfers between devices with their start and end apart: 29, of which 9 were waited for; matrix products, arithmetic and copies ran while one was open for 0% of the time, Pallas kernels for 10%

profile of v6, /device:TPU:0, one launch (start us, length us, event | category | flops | bytes accessed | tf_op | source)
XLA Modules:
  0.0 92.7 jit_solution(16549320718916962303)
XLA Ops:
  1.5 4.1 %collective-permute-start = (bf16[256,256]{1,0:T(8,128)(2,1)S(1)}, bf16[256,256]{1,0:T(8,128)(2,1)S(1)}, u32[]{:S(2)}, u32[]{:S(2)}) collective-permute-start(bf16[256,256]{1,0:T(8,128)(2,1)S(1)} %get-tuple-element.103), channel_id=1, source_target_pairs={{0,16},{4,20},{8,24},{12,28},{16,0},{20,4},{24,8},{28,12},{1,17},{... | collective-permute-start | bytes 393224 | tf_op jit(solution)/shard_map/ppermute | solution.py:50
  5.6 2.5 %collective-permute-start.3 = (bf16[256,256]{1,0:T(8,128)(2,1)S(1)}, bf16[256,256]{1,0:T(8,128)(2,1)S(1)}, u32[]{:S(2)}, u32[]{:S(2)}) collective-permute-start(bf16[256,256]{1,0:T(8,128)(2,1)S(1)} %get-tuple-element.115), channel_id=1, source_target_pairs={{0,12},{4,8},{8,4},{12,0},{16,28},{20,24},{24,20},{28,16},{1,13},{... | collective-permute-start | bytes 393224 | tf_op jit(solution)/shard_map/ppermute | solution.py:50
  9.9 1.7 %collective-permute-start.4 = (bf16[256,256]{1,0:T(8,128)(2,1)S(1)}, bf16[256,256]{1,0:T(8,128)(2,1)S(1)}, u32[]{:S(2)}, u32[]{:S(2)}) collective-permute-start(bf16[256,256]{1,0:T(8,128)(2,1)S(1)} %get-tuple-element.118), channel_id=1, source_target_pairs={{0,20},{4,16},{8,28},{12,24},{16,4},{20,0},{24,12},{28,8},{1,21},{... | collective-permute-start | bytes 393224 | tf_op jit(solution)/shard_map/ppermute | solution.py:50
  14.8 1.9 %collective-permute-start.5 = (bf16[256,256]{1,0:T(8,128)(2,1)S(1)}, bf16[256,256]{1,0:T(8,128)(2,1)S(1)}, u32[]{:S(2)}, u32[]{:S(2)}) collective-permute-start(bf16[256,256]{1,0:T(8,128)(2,1)S(1)} %get-tuple-element.121), channel_id=1, source_target_pairs={{0,28},{4,24},{8,20},{12,16},{16,12},{20,8},{24,4},{28,0},{1,29},{... | collective-permute-start | bytes 393224 | tf_op jit(solution)/shard_map/ppermute | solution.py:50
  17.6 3.2 %collective-permute-done.1.refs_1_ = bf16[256,256]{1,0:T(8,128)(2,1)S(1)} collective-permute-done((bf16[256,256]{1,0:T(8,128)(2,1)S(1)}, bf16[256,256]{1,0:T(8,128)(2,1)S(1)}, u32[]{:S(2)}, u32[]{:S(2)}) %collective-permute-start.1) | collective-permute-done | bytes 131104 | tf_op jit(solution)/shard_map/ppermute | solution.py:50
  21.3 5.0 %collective-permute-start.7 = (bf16[256,128]{1,0:T(8,128)(2,1)S(1)}, bf16[256,128]{1,0:T(8,128)(2,1)S(1)}, u32[]{:S(2)}, u32[]{:S(2)}) collective-permute-start(bf16[256,128]{1,0:T(8,128)(2,1)S(1)} %get-tuple-element.130.refs_12_), channel_id=1, source_target_pairs={{0,16},{4,20},{8,24},{12,28},{16,0},{20,4},{24,8},{28,12},{1,17},{... | collective-permute-start | bytes 196616 | tf_op jit(solution)/shard_map/ppermute | solution.py:50
  26.3 2.5 %collective-permute-done.4.refs_4_ = bf16[256,256]{1,0:T(8,128)(2,1)S(1)} collective-permute-done((bf16[256,256]{1,0:T(8,128)(2,1)S(1)}, bf16[256,256]{1,0:T(8,128)(2,1)S(1)}, u32[]{:S(2)}, u32[]{:S(2)}) %collective-permute-start.4) | collective-permute-done | bytes 131104 | tf_op jit(solution)/shard_map/ppermute | solution.py:50
  28.8 2.5 %collective-permute-start.9 = (bf16[256,128]{1,0:T(8,128)(2,1)S(1)}, bf16[256,128]{1,0:T(8,128)(2,1)S(1)}, u32[]{:S(2)}, u32[]{:S(2)}) collective-permute-start(bf16[256,128]{1,0:T(8,128)(2,1)S(1)} %get-tuple-element.136.refs_13_), channel_id=1, source_target_pairs={{0,24},{4,28},{8,16},{12,20},{16,8},{20,12},{24,0},{28,4},{1,25},{... | collective-permute-start | bytes 196616 | tf_op jit(solution)/shard_map/ppermute | solution.py:50
  31.3 1.7 %collective-permute-done.7.refs_0_ = bf16[256,128]{1,0:T(8,128)(2,1)S(1)} collective-permute-done((bf16[256,128]{1,0:T(8,128)(2,1)S(1)}, bf16[256,128]{1,0:T(8,128)(2,1)S(1)}, u32[]{:S(2)}, u32[]{:S(2)}) %collective-permute-start.7) | collective-permute-done | bytes 65568 | tf_op jit(solution)/shard_map/ppermute | solution.py:50
  33.0 4.6 %collective-permute-start.12 = (bf16[256,128]{1,0:T(8,128)(2,1)S(1)}, bf16[256,128]{1,0:T(8,128)(2,1)S(1)}, u32[]{:S(2)}, u32[]{:S(2)}) collective-permute-start(bf16[256,128]{1,0:T(8,128)(2,1)S(1)} %get-tuple-element.145.refs_15_), channel_id=1, source_target_pairs={{0,28},{4,24},{8,20},{12,16},{16,12},{20,8},{24,4},{28,0},{1,29},{... | collective-permute-start | bytes 196616 | tf_op jit(solution)/shard_map/ppermute | solution.py:50
  37.7 2.2 %collective-permute-start.14 = (bf16[256,128]{1,0:T(8,128)(2,1)S(1)}, bf16[256,128]{1,0:T(8,128)(2,1)S(1)}, u32[]{:S(2)}, u32[]{:S(2)}) collective-permute-start(bf16[256,128]{1,0:T(8,128)(2,1)S(1)} %get-tuple-element.150.refs_16_), channel_id=1, source_target_pairs={{0,16},{4,20},{8,24},{12,28},{16,0},{20,4},{24,8},{28,12},{1,17},{... | collective-permute-start | bytes 196616 | tf_op jit(solution)/shard_map/ppermute | solution.py:50
  39.8 2.2 %collective-permute-start.11 = (bf16[256,128]{1,0:T(8,128)(2,1)S(1)}, bf16[256,128]{1,0:T(8,128)(2,1)S(1)}, u32[]{:S(2)}, u32[]{:S(2)}) collective-permute-start(bf16[256,128]{1,0:T(8,128)(2,1)S(1)} %get-tuple-element.142.refs_14_), channel_id=1, source_target_pairs={{0,20},{4,16},{8,28},{12,24},{16,4},{20,0},{24,12},{28,8},{1,21},{... | collective-permute-start | bytes 196616 | tf_op jit(solution)/shard_map/ppermute | solution.py:50
  42.0 3.2 %collective-permute-start.17 = (bf16[256,128]{1,0:T(8,128)(2,1)S(1)}, bf16[256,128]{1,0:T(8,128)(2,1)S(1)}, u32[]{:S(2)}, u32[]{:S(2)}) collective-permute-start(bf16[256,128]{1,0:T(8,128)(2,1)S(1)} %get-tuple-element.158.refs_21_), channel_id=1, source_target_pairs={{0,28},{4,24},{8,20},{12,16},{16,12},{20,8},{24,4},{28,0},{1,29},{... | collective-permute-start | bytes 196616 | tf_op jit(solution)/shard_map/ppermute | solution.py:50
  45.2 1.9 %shard_map.111 = (f32[8,512,128]{2,1,0:T(8,128)S(1)}, f32[8,512,128]{2,1,0:T(8,128)S(1)}) custom-call(s32[8]{0:T(128)S(1)} %copy-done.6, bf16[512,256]{1,0:T(8,128)(2,1)S(1)} %copy-done.7, bf16[512,256]{1,0:T(8,128)(2,1)S(1)} %copy-done.8, bf16[256,256]{1,0:T(8,128)(2,1)S(1)} %collective-permute-done.refs_0_, ...), custom_call_target="tpu_custom_call" | custom-call | flops 1073741824 | bytes 5242880 | tf_op jit(solution)/shard_map/pallas_call | solution.py:181
  47.2 2.5 %collective-permute-done.11.refs_4_ = bf16[256,128]{1,0:T(8,128)(2,1)S(1)} collective-permute-done((bf16[256,128]{1,0:T(8,128)(2,1)S(1)}, bf16[256,128]{1,0:T(8,128)(2,1)S(1)}, u32[]{:S(2)}, u32[]{:S(2)}) %collective-permute-start.11) | collective-permute-done | bytes 65568 | tf_op jit(solution)/shard_map/ppermute | solution.py:50
  51.0 3.5 %shard_map.112 = (bf16[256,128]{1,0:T(8,128)(2,1)S(1)}, bf16[256,128]{1,0:T(8,128)(2,1)S(1)}, bf16[256,128]{1,0:T(8,128)(2,1)S(1)}, bf16[256,128]{1,0:T(8,128)(2...) custom-call(bf16[512,256]{1,0:T(8,128)(2,1)S(1)} %copy-done.7, ...), custom_call_target="tpu_custom_call" | custom-call | flops 1610612736 | bytes 3670016 | tf_op jit(solution)/shard_map/pallas_call | solution.py:287
  54.5 3.9 %collective-permute-start.18 = (bf16[256,128]{1,0:T(8,128)(2,1)S(1)}, bf16[256,128]{1,0:T(8,128)(2,1)S(1)}, u32[]{:S(2)}, u32[]{:S(2)}) collective-permute-start(bf16[256,128]{1,0:T(8,128)(2,1)S(1)} %get-tuple-element.168), channel_id=1, source_target_pairs={{0,16},{4,20},{8,24},{12,28},{16,0},{20,4},{24,8},{28,12},{1,17},{... | collective-permute-start | bytes 196616 | tf_op jit(solution)/shard_map/ppermute | solution.py:50
  59.6 3.5 %shard_map.113 = (bf16[256,128]{1,0:T(8,128)(2,1)S(1)}, bf16[256,256]{1,0:T(8,128)(2,1)S(1)}, bf16[256,128]{1,0:T(8,128)(2,1)S(1)}, bf16[256,256]{1,0:T(8,128)(2...) custom-call(bf16[512,256]{1,0:T(8,128)(2,1)S(1)} %copy-done.7, ...), custom_call_target="tpu_custom_call" | custom-call | flops 1610612736 | bytes 3670016 | tf_op jit(solution)/shard_map/pallas_call | solution.py:287
  66.0 2.8 %collective-permute-start.21 = (bf16[256,128]{1,0:T(8,128)(2,1)S(1)}, bf16[256,128]{1,0:T(8,128)(2,1)S(1)}, u32[]{:S(2)}, u32[]{:S(2)}) collective-permute-start(bf16[256,128]{1,0:T(8,128)(2,1)S(1)} %get-tuple-element.183), channel_id=1, source_target_pairs={{0,28},{4,24},{8,20},{12,16},{16,12},{20,8},{24,4},{28,0},{1,29},{... | collective-permute-start | bytes 196616 | tf_op jit(solution)/shard_map/ppermute | solution.py:50
  71.6 4.8 %collective-permute-start.28 = (bf16[256,256]{1,0:T(8,128)(2,1)S(1)}, bf16[256,256]{1,0:T(8,128)(2,1)S(1)}, u32[]{:S(2)}, u32[]{:S(2)}) collective-permute-start(bf16[256,256]{1,0:T(8,128)(2,1)S(1)} %get-tuple-element.195), channel_id=1, source_target_pairs={{0,4},{4,0},{8,12},{12,8},{16,20},{20,16},{24,28},{28,24},{1,5},{5... | collective-permute-start | bytes 393224 | tf_op jit(solution)/shard_map/ppermute | solution.py:50
  77.5 2.4 %collective-permute-start.27 = (bf16[256,128]{1,0:T(8,128)(2,1)S(1)}, bf16[256,128]{1,0:T(8,128)(2,1)S(1)}, u32[]{:S(2)}, u32[]{:S(2)}) collective-permute-start(bf16[256,128]{1,0:T(8,128)(2,1)S(1)} %get-tuple-element.194), channel_id=1, source_target_pairs={{0,28},{4,24},{8,20},{12,16},{16,12},{20,8},{24,4},{28,0},{1,29},{... | collective-permute-start | bytes 196616 | tf_op jit(solution)/shard_map/ppermute | solution.py:50
  79.9 2.9 %collective-permute-done.26.refs_8_ = bf16[256,128]{1,0:T(8,128)(2,1)S(1)} collective-permute-done((bf16[256,128]{1,0:T(8,128)(2,1)S(1)}, bf16[256,128]{1,0:T(8,128)(2,1)S(1)}, u32[]{:S(2)}, u32[]{:S(2)}) %collective-permute-start.26) | collective-permute-done | bytes 65568 | tf_op jit(solution)/shard_map/ppermute | solution.py:50
  82.8 1.7 %collective-permute-done.27.refs_9_ = bf16[256,128]{1,0:T(8,128)(2,1)S(1)} collective-permute-done((bf16[256,128]{1,0:T(8,128)(2,1)S(1)}, bf16[256,128]{1,0:T(8,128)(2,1)S(1)}, u32[]{:S(2)}, u32[]{:S(2)}) %collective-permute-start.27) | collective-permute-done | bytes 65568 | tf_op jit(solution)/shard_map/ppermute | solution.py:50
  85.5 5.7 %psum.7.square_ref = f32[1,256]{1,0:T(1,128)S(1)} all-reduce(f32[1,256]{1,0:T(1,128)S(1)} %get-tuple-element.198), channel_id=1, replica_groups=mesh['tok'=8,'chan'=4] {'chan'}, use_global_device_ids=true, to_apply=%region_0.0 | all-reduce | flops 256 | bytes 2048 | tf_op jit(solution)/shard_map/psum | solution.py:417
  (64 shorter events, 19.7 us)
Async XLA Ops:
  1.5 13.3 %collective-permute-start = (bf16[256,256]{1,0:T(8,128)(2,1)S(1)}, bf16[256,256]{1,0:T(8,128)(2,1)S(1)}, u32[]{:S(2)}, u32[]{:S(2)}) collective-permute-start(bf16[256,256]{1,0:T(8,128)(2,1)S(1)} %get-tuple-element.103), channel_id=1, source_target_pairs={{0,16},{4,20},{8,24},{12,28},{16,0},{20,4},{24,8},{28,12},{1,17},{... | collective-permute-start | bytes 393224 | tf_op jit(solution)/shard_map/ppermute | solution.py:50
  5.6 11.1 %collective-permute-start.3 = (bf16[256,256]{1,0:T(8,128)(2,1)S(1)}, bf16[256,256]{1,0:T(8,128)(2,1)S(1)}, u32[]{:S(2)}, u32[]{:S(2)}) collective-permute-start(bf16[256,256]{1,0:T(8,128)(2,1)S(1)} %get-tuple-element.115), channel_id=1, source_target_pairs={{0,12},{4,8},{8,4},{12,0},{16,28},{20,24},{24,20},{28,16},{1,13},{... | collective-permute-start | bytes 393224 | tf_op jit(solution)/shard_map/ppermute | solution.py:50
  8.1 12.7 %collective-permute-start.1 = (bf16[256,256]{1,0:T(8,128)(2,1)S(1)}, bf16[256,256]{1,0:T(8,128)(2,1)S(1)}, u32[]{:S(2)}, u32[]{:S(2)}) collective-permute-start(bf16[256,256]{1,0:T(8,128)(2,1)S(1)} %get-tuple-element.106), channel_id=1, source_target_pairs={{0,8},{4,12},{8,0},{12,4},{16,24},{20,28},{24,16},{28,20},{1,9},{5... | collective-permute-start | bytes 393224 | tf_op jit(solution)/shard_map/ppermute | solution.py:50
  8.5 12.3 %collective-permute-start.2 = (bf16[256,256]{1,0:T(8,128)(2,1)S(1)}, bf16[256,256]{1,0:T(8,128)(2,1)S(1)}, u32[]{:S(2)}, u32[]{:S(2)}) collective-permute-start(bf16[256,256]{1,0:T(8,128)(2,1)S(1)} %get-tuple-element.112), channel_id=1, source_target_pairs={{0,24},{4,28},{8,16},{12,20},{16,8},{20,12},{24,0},{28,4},{1,25},{... | collective-permute-start | bytes 393224 | tf_op jit(solution)/shard_map/ppermute | solution.py:50
  9.9 18.9 %collective-permute-start.4 = (bf16[256,256]{1,0:T(8,128)(2,1)S(1)}, bf16[256,256]{1,0:T(8,128)(2,1)S(1)}, u32[]{:S(2)}, u32[]{:S(2)}) collective-permute-start(bf16[256,256]{1,0:T(8,128)(2,1)S(1)} %get-tuple-element.118), channel_id=1, source_target_pairs={{0,20},{4,16},{8,28},{12,24},{16,4},{20,0},{24,12},{28,8},{1,21},{... | collective-permute-start | bytes 393224 | tf_op jit(solution)/shard_map/ppermute | solution.py:50
  14.8 22.8 %collective-permute-start.5 = (bf16[256,256]{1,0:T(8,128)(2,1)S(1)}, bf16[256,256]{1,0:T(8,128)(2,1)S(1)}, u32[]{:S(2)}, u32[]{:S(2)}) collective-permute-start(bf16[256,256]{1,0:T(8,128)(2,1)S(1)} %get-tuple-element.121), channel_id=1, source_target_pairs={{0,28},{4,24},{8,20},{12,16},{16,12},{20,8},{24,4},{28,0},{1,29},{... | collective-permute-start | bytes 393224 | tf_op jit(solution)/shard_map/ppermute | solution.py:50
  16.7 20.9 %collective-permute-start.8 = (bf16[256,256]{1,0:T(8,128)(2,1)S(1)}, bf16[256,256]{1,0:T(8,128)(2,1)S(1)}, u32[]{:S(2)}, u32[]{:S(2)}) collective-permute-start(bf16[256,256]{1,0:T(8,128)(2,1)S(1)} %get-tuple-element.133.refs_17_), channel_id=1, source_target_pairs={{0,8},{4,12},{8,0},{12,4},{16,24},{20,28},{24,16},{28,20},{1,9},{5... | collective-permute-start | bytes 393224 | tf_op jit(solution)/shard_map/ppermute | solution.py:50
  20.8 19.0 %collective-permute-start.6 = (bf16[256,256]{1,0:T(8,128)(2,1)S(1)}, bf16[256,256]{1,0:T(8,128)(2,1)S(1)}, u32[]{:S(2)}, u32[]{:S(2)}) collective-permute-start(bf16[256,256]{1,0:T(8,128)(2,1)S(1)} %get-tuple-element.124), channel_id=1, source_target_pairs={{0,4},{4,0},{8,12},{12,8},{16,20},{20,16},{24,28},{28,24},{1,5},{5... | collective-permute-start | bytes 393224 | tf_op jit(solution)/shard_map/ppermute | solution.py:50
  21.3 11.6 %collective-permute-start.7 = (bf16[256,128]{1,0:T(8,128)(2,1)S(1)}, bf16[256,128]{1,0:T(8,128)(2,1)S(1)}, u32[]{:S(2)}, u32[]{:S(2)}) collective-permute-start(bf16[256,128]{1,0:T(8,128)(2,1)S(1)} %get-tuple-element.130.refs_12_), channel_id=1, source_target_pairs={{0,16},{4,20},{8,24},{12,28},{16,0},{20,4},{24,8},{28,12},{1,17},{... | collective-permute-start | bytes 196616 | tf_op jit(solution)/shard_map/ppermute | solution.py:50
  28.8 8.9 %collective-permute-start.9 = (bf16[256,128]{1,0:T(8,128)(2,1)S(1)}, bf16[256,128]{1,0:T(8,128)(2,1)S(1)}, u32[]{:S(2)}, u32[]{:S(2)}) collective-permute-start(bf16[256,128]{1,0:T(8,128)(2,1)S(1)} %get-tuple-element.136.refs_13_), channel_id=1, source_target_pairs={{0,24},{4,28},{8,16},{12,20},{16,8},{20,12},{24,0},{28,4},{1,25},{... | collective-permute-start | bytes 196616 | tf_op jit(solution)/shard_map/ppermute | solution.py:50
  33.0 9.1 %collective-permute-start.12 = (bf16[256,128]{1,0:T(8,128)(2,1)S(1)}, bf16[256,128]{1,0:T(8,128)(2,1)S(1)}, u32[]{:S(2)}, u32[]{:S(2)}) collective-permute-start(bf16[256,128]{1,0:T(8,128)(2,1)S(1)} %get-tuple-element.145.refs_15_), channel_id=1, source_target_pairs={{0,28},{4,24},{8,20},{12,16},{16,12},{20,8},{24,4},{28,0},{1,29},{... | collective-permute-start | bytes 196616 | tf_op jit(solution)/shard_map/ppermute | solution.py:50
  37.6 12.1 %collective-permute-start.10 = (bf16[256,256]{1,0:T(8,128)(2,1)S(1)}, bf16[256,256]{1,0:T(8,128)(2,1)S(1)}, u32[]{:S(2)}, u32[]{:S(2)}) collective-permute-start(bf16[256,256]{1,0:T(8,128)(2,1)S(1)} %get-tuple-element.139.refs_19_), channel_id=1, source_target_pairs={{0,12},{4,8},{8,4},{12,0},{16,28},{20,24},{24,20},{28,16},{1,13},{... | collective-permute-start | bytes 393224 | tf_op jit(solution)/shard_map/ppermute | solution.py:50
  37.6 13.4 %collective-permute-start.13 = (bf16[256,256]{1,0:T(8,128)(2,1)S(1)}, bf16[256,256]{1,0:T(8,128)(2,1)S(1)}, u32[]{:S(2)}, u32[]{:S(2)}) collective-permute-start(bf16[256,256]{1,0:T(8,128)(2,1)S(1)} %get-tuple-element.147.refs_22_), channel_id=1, source_target_pairs={{0,4},{4,0},{8,12},{12,8},{16,20},{20,16},{24,28},{28,24},{1,5},{5... | collective-permute-start | bytes 393224 | tf_op jit(solution)/shard_map/ppermute | solution.py:50
  37.7 16.8 %collective-permute-start.14 = (bf16[256,128]{1,0:T(8,128)(2,1)S(1)}, bf16[256,128]{1,0:T(8,128)(2,1)S(1)}, u32[]{:S(2)}, u32[]{:S(2)}) collective-permute-start(bf16[256,128]{1,0:T(8,128)(2,1)S(1)} %get-tuple-element.150.refs_16_), channel_id=1, source_target_pairs={{0,16},{4,20},{8,24},{12,28},{16,0},{20,4},{24,8},{28,12},{1,17},{... | collective-permute-start | bytes 196616 | tf_op jit(solution)/shard_map/ppermute | solution.py:50
  39.8 9.8 %collective-permute-start.11 = (bf16[256,128]{1,0:T(8,128)(2,1)S(1)}, bf16[256,128]{1,0:T(8,128)(2,1)S(1)}, u32[]{:S(2)}, u32[]{:S(2)}) collective-permute-start(bf16[256,128]{1,0:T(8,128)(2,1)S(1)} %get-tuple-element.142.refs_14_), channel_id=1, source_target_pairs={{0,20},{4,16},{8,28},{12,24},{16,4},{20,0},{24,12},{28,8},{1,21},{... | collective-permute-start | bytes 196616 | tf_op jit(solution)/shard_map/ppermute | solution.py:50
  42.0 17.5 %collective-permute-start.17 = (bf16[256,128]{1,0:T(8,128)(2,1)S(1)}, bf16[256,128]{1,0:T(8,128)(2,1)S(1)}, u32[]{:S(2)}, u32[]{:S(2)}) collective-permute-start(bf16[256,128]{1,0:T(8,128)(2,1)S(1)} %get-tuple-element.158.refs_21_), channel_id=1, source_target_pairs={{0,28},{4,24},{8,20},{12,16},{16,12},{20,8},{24,4},{28,0},{1,29},{... | collective-permute-start | bytes 196616 | tf_op jit(solution)/shard_map/ppermute | solution.py:50
  49.7 9.8 %collective-permute-start.16 = (bf16[256,128]{1,0:T(8,128)(2,1)S(1)}, bf16[256,128]{1,0:T(8,128)(2,1)S(1)}, u32[]{:S(2)}, u32[]{:S(2)}) collective-permute-start(bf16[256,128]{1,0:T(8,128)(2,1)S(1)} %get-tuple-element.156.refs_20_), channel_id=1, source_target_pairs={{0,20},{4,16},{8,28},{12,24},{16,4},{20,0},{24,12},{28,8},{1,21},{... | collective-permute-start | bytes 196616 | tf_op jit(solution)/shard_map/ppermute | solution.py:50
  49.7 9.8 %collective-permute-start.15 = (bf16[256,128]{1,0:T(8,128)(2,1)S(1)}, bf16[256,128]{1,0:T(8,128)(2,1)S(1)}, u32[]{:S(2)}, u32[]{:S(2)}) collective-permute-start(bf16[256,128]{1,0:T(8,128)(2,1)S(1)} %get-tuple-element.153.refs_18_), channel_id=1, source_target_pairs={{0,24},{4,28},{8,16},{12,20},{16,8},{20,12},{24,0},{28,4},{1,25},{... | collective-permute-start | bytes 196616 | tf_op jit(solution)/shard_map/ppermute | solution.py:50
  54.5 8.6 %collective-permute-start.18 = (bf16[256,128]{1,0:T(8,128)(2,1)S(1)}, bf16[256,128]{1,0:T(8,128)(2,1)S(1)}, u32[]{:S(2)}, u32[]{:S(2)}) collective-permute-start(bf16[256,128]{1,0:T(8,128)(2,1)S(1)} %get-tuple-element.168), channel_id=1, source_target_pairs={{0,16},{4,20},{8,24},{12,28},{16,0},{20,4},{24,8},{28,12},{1,17},{... | collective-permute-start | bytes 196616 | tf_op jit(solution)/shard_map/ppermute | solution.py:50
  66.0 10.5 %collective-permute-start.21 = (bf16[256,128]{1,0:T(8,128)(2,1)S(1)}, bf16[256,128]{1,0:T(8,128)(2,1)S(1)}, u32[]{:S(2)}, u32[]{:S(2)}) collective-permute-start(bf16[256,128]{1,0:T(8,128)(2,1)S(1)} %get-tuple-element.183), channel_id=1, source_target_pairs={{0,28},{4,24},{8,20},{12,16},{16,12},{20,8},{24,4},{28,0},{1,29},{... | collective-permute-start | bytes 196616 | tf_op jit(solution)/shard_map/ppermute | solution.py:50
  68.8 8.7 %collective-permute-start.22 = (bf16[256,128]{1,0:T(8,128)(2,1)S(1)}, bf16[256,128]{1,0:T(8,128)(2,1)S(1)}, u32[]{:S(2)}, u32[]{:S(2)}) collective-permute-start(bf16[256,128]{1,0:T(8,128)(2,1)S(1)} %get-tuple-element.186), channel_id=1, source_target_pairs={{0,16},{4,20},{8,24},{12,28},{16,0},{20,4},{24,8},{28,12},{1,17},{... | collective-permute-start | bytes 196616 | tf_op jit(solution)/shard_map/ppermute | solution.py:50
  70.2 14.3 %collective-permute-start.25 = (bf16[256,256]{1,0:T(8,128)(2,1)S(1)}, bf16[256,256]{1,0:T(8,128)(2,1)S(1)}, u32[]{:S(2)}, u32[]{:S(2)}) collective-permute-start(bf16[256,256]{1,0:T(8,128)(2,1)S(1)} %get-tuple-element.192), channel_id=1, source_target_pairs={{0,12},{4,8},{8,4},{12,0},{16,28},{20,24},{24,20},{28,16},{1,13},{... | collective-permute-start | bytes 393224 | tf_op jit(solution)/shard_map/ppermute | solution.py:50
  71.6 12.9 %collective-permute-start.28 = (bf16[256,256]{1,0:T(8,128)(2,1)S(1)}, bf16[256,256]{1,0:T(8,128)(2,1)S(1)}, u32[]{:S(2)}, u32[]{:S(2)}) collective-permute-start(bf16[256,256]{1,0:T(8,128)(2,1)S(1)} %get-tuple-element.195), channel_id=1, source_target_pairs={{0,4},{4,0},{8,12},{12,8},{16,20},{20,16},{24,28},{28,24},{1,5},{5... | collective-permute-start | bytes 393224 | tf_op jit(solution)/shard_map/ppermute | solution.py:50
  77.5 7.1 %collective-permute-start.27 = (bf16[256,128]{1,0:T(8,128)(2,1)S(1)}, bf16[256,128]{1,0:T(8,128)(2,1)S(1)}, u32[]{:S(2)}, u32[]{:S(2)}) collective-permute-start(bf16[256,128]{1,0:T(8,128)(2,1)S(1)} %get-tuple-element.194), channel_id=1, source_target_pairs={{0,28},{4,24},{8,20},{12,16},{16,12},{20,8},{24,4},{28,0},{1,29},{... | collective-permute-start | bytes 196616 | tf_op jit(solution)/shard_map/ppermute | solution.py:50
  (16 other events, 317.1 us)

commit v7 on v3

--- a/solution.py
+++ b/solution.py
@@ -11,7 +11,7 @@
 from jax.sharding import PartitionSpec as P
 
 MIB = 1024 * 1024
-BIG = 48 * MIB
+EARLY = 3
 WHOLE = pl.BlockSpec(memory_space=pltpu.VMEM)
 IN_HBM = pl.BlockSpec(memory_space=pltpu.HBM)
 
@@ -36,29 +36,48 @@
     return lax.axis_index("tok") ^ step
 
 
-def exchange(blocks):
-    count = len(blocks)
-    return [blocks[0]] + [
-        lax.ppermute(blocks[k], "tok", [(d, d ^ k) for d in range(count)]) for k in range(1, count)
-    ]
+def after(value, *earlier):
+    held = lax.optimization_barrier((value, *earlier))
+    return held[0], list(held[1:])
+
+
+def send(block, step, count):
+    return lax.ppermute(block, "tok", [(d, d ^ step) for d in range(count)])
+
+
+def spread(blocks):
+    return lax.all_to_all(blocks, "tok", 0, 0, tiled=True)
+
+
+def sending_order(count):
+    half = count // 2
+    far = list(range(half, count, 2)) + list(range(half + 1, count, 2))
+    near = list(range(2, half)) + [1]
+    order = []
+    for at in range(half - 1):
+        order += [far[at], near[at]]
+    return order[:-1] + far[-1:] + order[-1:]
 
 
 def columns_of(step, part):
     return pl.ds(pl.multiple_of(partner(step) * part, 128), part)
 
 
-def split_kernel(count, part, filt_ref, *refs):
-    outs, sems = refs[:count], refs[count]
+def split_kernel(count, part, filt_ref, out_ref, sems):
     copies = []
-    for k in range(count):
-        copies.append(pltpu.make_async_copy(filt_ref.at[:, columns_of(k, part)], outs[k], sems.at[k]))
+    for j in range(count):
+        copies.append(pltpu.make_async_copy(filt_ref.at[:, pl.ds(j * part, part)], out_ref.at[j], sems.at[j]))
         copies[-1].start()
     for copy in copies:
         copy.wait()
 
 
+def chunks_of(part):
+    return 2 if part % 256 == 0 else 1
+
+
 def gate_kernel(count, part, key_ref, value_ref, *refs):
-    outs, (key_buf, value_buf, sems) = refs[:count], refs[count:]
+    firsts, lasts, (key_buf, value_buf, sems) = refs[:count], refs[count:-3], refs[-3:]
     copies = []
     for k in range(count):
         cols = columns_of(k, part)
@@ -74,7 +93,11 @@
         for copy in copies[k]:
             copy.wait()
         product = key_buf[k].astype(jnp.float32) * value_buf[k].astype(jnp.float32)
-        outs[k][...] = product.astype(jnp.bfloat16)
+        product = product.astype(jnp.bfloat16)
+        size = firsts[k].shape[1]
+        firsts[k][...] = product[:, :size]
+        if lasts:
+            lasts[0][partner(k)] = product[:, size:]
 
 
 def pieces(x, count):
@@ -86,14 +109,14 @@
     width, columns = filter_store.shape
     part = columns // count
     if part % 128:
-        return pieces(filter_store, count)
+        return filter_store.reshape(width, count, part).transpose(1, 0, 2)
     return pl.pallas_call(
         functools.partial(split_kernel, count, part),
-        out_shape=[jax.ShapeDtypeStruct((width, part), jnp.bfloat16)] * count,
+        out_shape=jax.ShapeDtypeStruct((count, width, part), jnp.bfloat16),
         in_specs=[IN_HBM],
-        out_specs=[WHOLE] * count,
+        out_specs=WHOLE,
         scratch_shapes=[pltpu.SemaphoreType.DMA((count,))],
-        compiler_params=pltpu.CompilerParams(vmem_limit_bytes=BIG),
+        compiler_params=pltpu.CompilerParams(vmem_limit_bytes=16 * MIB),
         cost_estimate=pl.CostEstimate(flops=0, bytes_accessed=4 * width * columns, transcendentals=0),
     )(filter_store)
 
@@ -103,30 +126,62 @@
     part = columns // count
     if part % 128:
         gated = (key_in.astype(jnp.float32) * value_in.astype(jnp.float32)).astype(jnp.bfloat16)
-        return pieces(gated, count)
+        return pieces(gated, count), []
+    chunks = chunks_of(part)
+    size = part // chunks
     block = pltpu.VMEM((count, width, part), jnp.bfloat16)
-    return pl.pallas_call(
+    shapes = [jax.ShapeDtypeStruct((width, size), jnp.bfloat16)] * count
+    shapes += [jax.ShapeDtypeStruct((count, width, size), jnp.bfloat16)] * (chunks - 1)
+    found = pl.pallas_call(
         functools.partial(gate_kernel, count, part),
-        out_shape=[jax.ShapeDtypeStruct((width, part), jnp.bfloat16)] * count,
+        out_shape=shapes,
         in_specs=[IN_HBM] * 2,
-        out_specs=[WHOLE] * count,
+        out_specs=[WHOLE] * len(shapes),
         scratch_shapes=[block, block, pltpu.SemaphoreType.DMA((2, count))],
-        compiler_params=pltpu.CompilerParams(vmem_limit_bytes=BIG),
+        compiler_params=pltpu.CompilerParams(vmem_limit_bytes=16 * MIB),
         cost_estimate=pl.CostEstimate(flops=width * columns, bytes_accessed=6 * width * columns, transcendentals=0),
     )(key_in, value_in)
-
-
-def conv_kernel(count, width, lag_ref, fh_ref, fl_ref, ih_ref, il_ref, *refs):
-    filts, gates, outs, (fs, gs, ss) = refs[:count], refs[count : 2 * count], refs[2 * count : 3 * count], refs[3 * count :]
-    dot = functools.partial(jnp.dot, preferred_element_type=jnp.float32)
-    for k in range(count):
-        filt, gated = filts[k][...], gates[k][...]
-        fs[lag_ref[partner(k)]] = dot(fh_ref[...], filt) + dot(fl_ref[...], filt)
-        gs[partner(k)] = dot(fh_ref[...], gated) + dot(fl_ref[...], gated)
-    columns = filts[0].shape[1]
+    return found[:count], found[count:]
+
+
+def dot(x, y):
+    return jnp.dot(x, y, preferred_element_type=jnp.float32)
+
+
+def transform(high, low, block):
+    return dot(high, block) + dot(low, block)
+
+
+def filter_kernel(lag_ref, high_ref, low_ref, blocks, *outs):
+    chunk = outs[0].shape[2]
+    for i in range(blocks.shape[0]):
+        spectrum = transform(high_ref[...], low_ref[...], blocks[i])
+        for c, out in enumerate(outs):
+            out[lag_ref[i]] = spectrum[:, c * chunk : (c + 1) * chunk]
+
+
+def filter_spectra(lag_of_block, high, low, blocks):
+    count, width, part = blocks.shape
+    chunks = chunks_of(part)
+    shape = jax.ShapeDtypeStruct((count, 2 * width, part // chunks), jnp.float32)
+    return pl.pallas_call(
+        filter_kernel,
+        out_shape=[shape] * chunks,
+        in_specs=[pl.BlockSpec(memory_space=pltpu.SMEM)] + [WHOLE] * 3,
+        out_specs=[WHOLE] * chunks,
+        compiler_params=pltpu.CompilerParams(vmem_limit_bytes=16 * MIB),
+        cost_estimate=pl.CostEstimate(
+            flops=8 * count * width * width * part,
+            bytes_accessed=10 * count * width * part,
+            transcendentals=0,
+        ),
+    )(lag_of_block, high, low, blocks)
+
+
+def multiply_spectra(count, width, columns, fs, gs, ss):
     lane = min(128, columns)
 
-    def products(row, sign):
+    def tile(row, sign):
         re_rows = pl.ds(pl.multiple_of(row * 8, 8), 8)
         im_rows = pl.ds(pl.multiple_of(row * 8 + width, 8), 8)
         for at in range(0, columns, lane):
@@ -159,74 +214,109 @@
 
     @pl.loop(0, half)
     def _(row):
-        products(row, 1)
+        tile(row, 1)
 
     @pl.loop(half, 2 * half)
     def _(row):
-        products(row, -1)
-
-    for k in range(count):
-        total = ss[partner(k)]
+        tile(row, -1)
+
+
+def pairs(items, columns):
+    size = 2 if columns == 128 else 1
+    return [items[at : at + size] for at in range(0, len(items), size)]
+
+
+def conv_kernel(steps, fh_ref, fl_ref, ih_ref, il_ref, fs, *refs):
+    gs, ss = refs[-2:]
+    count, columns = gs.shape[0], gs.shape[2]
+    width = gs.shape[1] // 2
+    if steps:
+        blocks, outs = dict(zip(steps, refs[:count])), dict(zip(steps, refs[count:-2]))
+        where = partner
+    else:
+        steps = list(range(count))
+        blocks, outs = ({k: ref.at[k] for k in steps} for ref in refs[:2])
+        where = int
+    for group in pairs(steps, columns):
+        found = transform(fh_ref[...], fl_ref[...], jnp.concatenate([blocks[k][...] for k in group], axis=1))
+        for at, k in enumerate(group):
+            gs[where(k)] = found[:, at * columns : (at + 1) * columns]
+    multiply_spectra(count, width, columns, fs, gs, ss)
+    for group in pairs(steps, columns):
+        total = jnp.concatenate([ss[where(k)] for k in group], axis=1)
         high = total.astype(jnp.bfloat16)
         low = (total - high.astype(jnp.float32)).astype(jnp.bfloat16)
-        outs[k][...] = (dot(ih_ref[...], high) + dot(ih_ref[...], low) + dot(il_ref[...], high)).astype(jnp.bfloat16)
-
-
-def block_conv(lag_of_block, filts, gates):
-    count = len(filts)
-    width, columns = filts[0].shape
-    tabs = [jnp.asarray(t) for t in tables(width)]
-    spectra = pltpu.VMEM((count, 2 * width, columns), jnp.float32)
-    return pl.pallas_call(
-        functools.partial(conv_kernel, count, width),
-        out_shape=[jax.ShapeDtypeStruct((width, columns), jnp.bfloat16)] * count,
-        in_specs=[pl.BlockSpec(memory_space=pltpu.SMEM)] + [WHOLE] * (4 + 2 * count),
-        out_specs=[WHOLE] * count,
-        scratch_shapes=[spectra, spectra, spectra],
-        compiler_params=pltpu.CompilerParams(vmem_limit_bytes=32 * MIB),
+        conv = dot(ih_ref[...], high) + dot(ih_ref[...], low) + dot(il_ref[...], high)
+        conv = conv.astype(jnp.bfloat16)
+        for at, k in enumerate(group):
+            outs[k][...] = conv[:, at * columns : (at + 1) * columns]
+
+
+def block_conv(tabs, filt, steps, blocks):
+    count, twice, columns = filt.shape
+    width = twice // 2
+    spectra = pltpu.VMEM((count, twice, columns), jnp.float32)
+    return pl.pallas_call(
+        functools.partial(conv_kernel, steps),
+        out_shape=[jax.ShapeDtypeStruct(block.shape, jnp.bfloat16) for block in blocks],
+        in_specs=[WHOLE] * (5 + len(blocks)),
+        out_specs=[WHOLE] * len(blocks),
+        scratch_shapes=[spectra, spectra],
+        compiler_params=pltpu.CompilerParams(vmem_limit_bytes=20 * MIB),
         cost_estimate=pl.CostEstimate(
-            flops=2 * count * width * 2 * width * columns * 7,
-            bytes_accessed=6 * count * width * columns,
+            flops=24 * count * width * width * columns,
+            bytes_accessed=14 * count * width * columns,
             transcendentals=0,
         ),
-    )(lag_of_block, *tabs, *filts, *gates)
-
-
-def pre_kernel(count, query_ref, skip_ref, *refs):
-    convs, gates, (pre_ref, square_ref) = refs[:count], refs[count : 2 * count], refs[2 * count :]
-    width, part = convs[0].shape
+    )(*tabs, filt, *blocks)
+
+
+def pre_kernel(steps, part, query_ref, skip_ref, *refs):
+    count = len(steps)
+    pieces = len(refs) // 2 - 1
+    convs, gates, (pre_ref, square_ref) = refs[:pieces], refs[pieces : 2 * pieces], refs[-2:]
+    width = query_ref.shape[0]
     total = jnp.zeros((width, 128), jnp.float32)
-    for k in range(count):
-        start = partner(k) * part if count > 1 else 0
-        for at in range(0, part, 128):
+
+    def add(total, start, conv_ref, gated_ref):
+        for at in range(0, conv_ref.shape[1], 128):
             lanes, cols = pl.ds(at, 128), pl.ds(pl.multiple_of(start + at, 128), 128)
-            gated = gates[k][:, lanes].astype(jnp.float32)
-            conv = convs[k][:, lanes].astype(jnp.float32)
+            gated = gated_ref[:, lanes].astype(jnp.float32)
+            conv = conv_ref[:, lanes].astype(jnp.float32)
             pre = query_ref[:, cols].astype(jnp.float32) * (conv + skip_ref[:, cols] * gated)
             pre_ref[:, cols] = pre
             total = total + pre * pre
+        return total
+
+    for k, conv_ref, gated_ref in zip(steps, convs, gates):
+        total = add(total, partner(k) * part if count > 1 else 0, conv_ref, gated_ref)
+    if pieces > count:
+        size = convs[-1].shape[2]
+        for j in range(count):
+            total = add(total, j * part + part - size, convs[-1].at[j], gates[-1].at[j])
     square_ref[...] = jnp.sum(total.T, axis=0, keepdims=True)
 
 
 def together(blocks):
     count = len(blocks)
     order = jnp.arange(count, dtype=jnp.int32) ^ lax.axis_index("tok")
-    stacked = jnp.take(jnp.stack(blocks), order, axis=0)
-    return [stacked.transpose(1, 0, 2).reshape(blocks[0].shape[0], -1)]
-
-
-def gated_output(query, skip, convs, gates):
+    stacked = jnp.take(jnp.stack([blocks[k] for k in range(count)]), order, axis=0)
+    return stacked.transpose(1, 0, 2).reshape(blocks[0].shape[0], -1)
+
+
+def gated_output(query, skip, steps, convs, gates):
     width, columns = query.shape
-    if convs[0].shape[1] % 128:
-        convs, gates = together(convs), together(gates)
-    count = len(convs)
-    return pl.pallas_call(
-        functools.partial(pre_kernel, count),
+    part = columns // len(steps)
+    if part % 128:
+        convs, gates = ([together(dict(zip(steps, blocks)))] for blocks in (convs, gates))
+        steps = [0]
+    return pl.pallas_call(
+        functools.partial(pre_kernel, steps, part),
         out_shape=(
             jax.ShapeDtypeStruct((width, columns), jnp.float32),
             jax.ShapeDtypeStruct((1, width), jnp.float32),
         ),
-        in_specs=[WHOLE] * (2 + 2 * count),
+        in_specs=[WHOLE] * (2 + 2 * len(convs)),
         out_specs=(WHOLE, WHOLE),
         compiler_params=pltpu.CompilerParams(vmem_limit_bytes=16 * MIB),
         cost_estimate=pl.CostEstimate(flops=6 * width * columns, bytes_accessed=10 * width * columns, transcendentals=0),
@@ -268,10 +358,23 @@
 def local(query, key_in, value_in, filter_store, lag_of_block, skip, out_gain):
     width, columns = query.shape
     count = lax.axis_size("tok")
-    filts = exchange(split(count, filter_store))
-    mine = gate(count, key_in, value_in)
-    convs = exchange(block_conv(lag_of_block, filts, exchange(mine)))
-    pre, square = gated_output(query, skip[None, :], convs, mine)
+    tabs = [jnp.asarray(t) for t in tables(width)]
+    own = split(count, filter_store)
+    own, (key_in, value_in) = after(own, key_in, value_in)
+    firsts, lasts = gate(count, key_in, value_in)
+    order = sending_order(count)
+    steps = order + [0]
+    filt = filter_spectra(lag_of_block, *tabs[:2], spread(own))
+    blocks = [send(firsts[k], k, count) for k in order] + [firsts[0]]
+    lasts_all = [spread(last) for last in lasts]
+    done = block_conv(tabs, filt[0], steps, blocks)
+    convs = [send(done[at], k, count) for at, k in enumerate(order)] + [done[-1]]
+    for filt_last, last in zip(filt[1:], lasts_all):
+        (done,) = block_conv(tabs, filt_last, [], [last])
+        done, convs[:EARLY] = after(done, *convs[:EARLY])
+        convs.append(spread(done))
+    gates = [firsts[k] for k in steps] + list(lasts)
+    pre, square = gated_output(query, skip[None, :], steps, convs, gates)
     square = lax.psum(square, "chan")
     return scaled(columns * lax.axis_size("chan"), pre, square, out_gain[None, :])
 

time: 99.2 us -> 118 us (1.19)
  the two profiles are of different devices: /device:TPU:12 before, /device:TPU:0 now
where the time goes in v7:
time: 118 us
  waiting for transfers between devices  45.1 us (38%)
  starting transfers between devices  39.1 us (33%)
  Pallas kernels  15.6 us (13%)
  local copies, waits for them, and re-layouts  12 us (10%)
  blocking collectives  5.76 us (5%)
    all_to_all x3, waiting for transfers between devices, spread(): return lax.all_to_all(blocks, 'tok', 0, 0, tiled=True)  23 us
    ppermute x14, starting transfers between devices, send(): return lax.ppermute(block, 'tok', [(d, d ^ step) for d in range(count)])  22.8 us
    ppermute x14, waiting for transfers between devices, send(): return lax.ppermute(block, 'tok', [(d, d ^ step) for d in range(count)])  22.1 us
    all_to_all x3, starting transfers between devices, spread(): return lax.all_to_all(blocks, 'tok', 0, 0, tiled=True)  16.3 us
    unnamed x48, local copies, waits for them, and re-layouts  12 us
    pallas_call x2, Pallas kernels, block_conv(): pl.pallas_call(functools.partial(conv_kernel, steps), out_shape=[jax.Shap...  7.55 us
    psum x1, blocking collectives, local(): square = lax.psum(square, 'chan')  5.76 us
  transfers between devices with their start and end apart: 17, of which 5 were waited for; matrix products, arithmetic and copies ran while one was open for 0% of the time, Pallas kernels for 9%

profile of v7, /device:TPU:0, one launch (start us, length us, event | category | flops | bytes accessed | tf_op | source)
XLA Modules:
  0.0 117.7 jit_solution(9594168020220928892)
XLA Ops:
  2.4 7.3 %all-to-all-start = ((bf16[8,256,256]{2,1,0:T(8,128)(2,1)}), bf16[8,256,256]{2,1,0:T(8,128)(2,1)S(1)}, u32[]{:S(2)}, u32[]{:S(2)}) async-start(bf16[8,256,256]{2,1,0:T(8,128)(2,1)} %shard_map.109), calls=%async_computation | async-start | bytes 2097152 | tf_op jit(solution)/shard_map/all_to_all | solution.py:49
  9.7 1.5 %shard_map.111 = (bf16[256,128]{1,0:T(8,128)(2,1)S(1)}, bf16[256,128]{1,0:T(8,128)(2,1)S(1)}, bf16[256,128]{1,0:T(8,128)(2,1)S(1)}, bf16[256,128]{1,0:T(8,128)(2...) custom-call(bf16[256,2048]{1,0:T(8,128)(2,1)S(1)} %copy-done.2, ...), custom_call_target="tpu_custom_call" | custom-call | flops 524288 | bytes 3145728 | tf_op jit(solution)/shard_map/pallas_call | solution.py:135
  12.5 23.0 %all-to-all-done.blocks = bf16[8,256,256]{2,1,0:T(8,128)(2,1)S(1)} async-done(((bf16[8,256,256]{2,1,0:T(8,128)(2,1)}), bf16[8,256,256]{2,1,0:T(8,128)(2,1)S(1)}, u32[]{:S(2)}, u32[]{:S(2)}) %all-to-all-start) | async-done | bytes 1048608 | tf_op jit(solution)/shard_map/all_to_all | solution.py:49
  35.5 3.7 %all-to-all-start.1 = ((bf16[8,256,128]{2,1,0:T(8,128)(2,1)}), bf16[8,256,128]{2,1,0:T(8,128)(2,1)S(1)}, u32[]{:S(2)}, u32[]{:S(2)}) async-start(bf16[8,256,128]{2,1,0:T(8,128)(2,1)} %get-tuple-element.37.refs_17_), calls=%async_computation.1 | async-start | bytes 1048576 | tf_op jit(solution)/shard_map/all_to_all | solution.py:49
  39.2 2.9 %collective-permute-start = (bf16[256,128]{1,0:T(8,128)(2,1)S(1)}, bf16[256,128]{1,0:T(8,128)(2,1)S(1)}, u32[]{:S(2)}, u32[]{:S(2)}) collective-permute-start(bf16[256,128]{1,0:T(8,128)(2,1)S(1)} %get-tuple-element.39.refs_9_), channel_id=1, source_target_pairs={{0,16},{4,20},{8,24},{12,28},{16,0},{20,4},{24,8},{28,12},{1,17},{... | collective-permute-start | bytes 196616 | tf_op jit(solution)/shard_map/ppermute | solution.py:45
  42.1 1.5 %collective-permute-start.1 = (bf16[256,128]{1,0:T(8,128)(2,1)S(1)}, bf16[256,128]{1,0:T(8,128)(2,1)S(1)}, u32[]{:S(2)}, u32[]{:S(2)}) collective-permute-start(bf16[256,128]{1,0:T(8,128)(2,1)S(1)} %get-tuple-element.40.refs_10_), channel_id=1, source_target_pairs={{0,8},{4,12},{8,0},{12,4},{16,24},{20,28},{24,16},{28,20},{1,9},{5... | collective-permute-start | bytes 196616 | tf_op jit(solution)/shard_map/ppermute | solution.py:45
  43.6 2.0 %collective-permute-start.3 = (bf16[256,128]{1,0:T(8,128)(2,1)S(1)}, bf16[256,128]{1,0:T(8,128)(2,1)S(1)}, u32[]{:S(2)}, u32[]{:S(2)}) collective-permute-start(bf16[256,128]{1,0:T(8,128)(2,1)S(1)} %get-tuple-element.42.refs_12_), channel_id=1, source_target_pairs={{0,12},{4,8},{8,4},{12,0},{16,28},{20,24},{24,20},{28,16},{1,13},{... | collective-permute-start | bytes 196616 | tf_op jit(solution)/shard_map/ppermute | solution.py:45
  45.6 3.3 %collective-permute-start.4 = (bf16[256,128]{1,0:T(8,128)(2,1)S(1)}, bf16[256,128]{1,0:T(8,128)(2,1)S(1)}, u32[]{:S(2)}, u32[]{:S(2)}) collective-permute-start(bf16[256,128]{1,0:T(8,128)(2,1)S(1)} %get-tuple-element.43.refs_13_), channel_id=1, source_target_pairs={{0,20},{4,16},{8,28},{12,24},{16,4},{20,0},{24,12},{28,8},{1,21},{... | collective-permute-start | bytes 196616 | tf_op jit(solution)/shard_map/ppermute | solution.py:45
  48.9 11.9 %collective-permute-done.refs_0_ = bf16[256,128]{1,0:T(8,128)(2,1)S(1)} collective-permute-done((bf16[256,128]{1,0:T(8,128)(2,1)S(1)}, bf16[256,128]{1,0:T(8,128)(2,1)S(1)}, u32[]{:S(2)}, u32[]{:S(2)}) %collective-permute-start) | collective-permute-done | bytes 65568 | tf_op jit(solution)/shard_map/ppermute | solution.py:45
  64.6 1.9 %shard_map.110 = (f32[8,512,128]{2,1,0:T(8,128)S(1)}, f32[8,512,128]{2,1,0:T(8,128)S(1)}) custom-call(s32[8]{0:T(128)S(1)} %copy-done.15, bf16[512,256]{1,0:T(8,128)(2,1)S(1)} %copy-done.16, bf16[512,256]{1,0:T(8,128)(2,1)S(1)} %copy-done.18, bf16[8,256,256]{2,1,0:T(8,128)(2,1)S(1)} %all-to-all-done.blocks), custom_call_target="tpu_custom_call" | custom-call | flops 1073741824 | bytes 5242880 | tf_op jit(solution)/shard_map/pallas_call | solution.py:167
  66.5 1.3 %copy-done.22 = f32[8,512,128]{2,1,0:T(8,128)} copy-done((f32[8,512,128]{2,1,0:T(8,128)}, f32[8,512,128]{2,1,0:T(8,128)S(1)}, u32[]{:S(2)}) %copy-start.22) | copy-done | bytes 2097176
  68.0 3.5 %shard_map.113 = (bf16[256,128]{1,0:T(8,128)(2,1)S(1)}, bf16[256,128]{1,0:T(8,128)(2,1)S(1)}, bf16[256,128]{1,0:T(8,128)(2,1)S(1)}, bf16[256,128]{1,0:T(8,128)(2...) custom-call(bf16[512,256]{1,0:T(8,128)(2,1)S(1)} %copy-done.17, ...), custom_call_target="tpu_custom_call" | custom-call | flops 1610612736 | bytes 3670016 | tf_op jit(solution)/shard_map/pallas_call | solution.py:259
  71.5 3.9 %collective-permute-start.8 = (bf16[256,128]{1,0:T(8,128)(2,1)S(1)}, bf16[256,128]{1,0:T(8,128)(2,1)S(1)}, u32[]{:S(2)}, u32[]{:S(2)}) collective-permute-start(bf16[256,128]{1,0:T(8,128)(2,1)S(1)} %get-tuple-element.48), channel_id=1, source_target_pairs={{0,8},{4,12},{8,0},{12,4},{16,24},{20,28},{24,16},{28,20},{1,9},{5... | collective-permute-start | bytes 196616 | tf_op jit(solution)/shard_map/ppermute | solution.py:45
  75.9 1.6 %copy-done.23 = f32[8,512,128]{2,1,0:T(8,128)S(1)} copy-done((f32[8,512,128]{2,1,0:T(8,128)S(1)}, f32[8,512,128]{2,1,0:T(8,128)}, u32[]{:S(2)}) %copy-start.23) | copy-done | bytes 2097176
  77.5 4.1 %shard_map.112 = bf16[8,256,128]{2,1,0:T(8,128)(2,1)} custom-call(bf16[512,256]{1,0:T(8,128)(2,1)S(1)} %copy-done.17, bf16[512,256]{1,0:T(8,128)(2,1)S(1)} %copy-done.19, bf16[256,512]{1,0:T(8,128)(2,1)S(1)} %copy-done.20, bf16[256,512]{1,0:T(8,128)(2,1)S(1)} %copy-done.21, f32[8,512,128]{2,1,0:T(8,128)S(1)} %copy-done.23, ...), custom_call_target="tpu_custom_call" | custom-call | flops 1610612736 | bytes 3670016 | tf_op jit(solution)/shard_map/pallas_call | solution.py:259
  81.6 5.3 %all-to-all-start.2 = ((bf16[8,256,128]{2,1,0:T(8,128)(2,1)}), bf16[8,256,128]{2,1,0:T(8,128)(2,1)S(1)}, u32[]{:S(2)}, u32[]{:S(2)}) async-start(bf16[8,256,128]{2,1,0:T(8,128)(2,1)} %shard_map.112), calls=%async_computation.2 | async-start | bytes 1048576 | tf_op jit(solution)/shard_map/all_to_all | solution.py:49
  86.9 2.9 %collective-permute-start.10 = (bf16[256,128]{1,0:T(8,128)(2,1)S(1)}, bf16[256,128]{1,0:T(8,128)(2,1)S(1)}, u32[]{:S(2)}, u32[]{:S(2)}) collective-permute-start(bf16[256,128]{1,0:T(8,128)(2,1)S(1)} %get-tuple-element.53), channel_id=1, source_target_pairs={{0,12},{4,8},{8,4},{12,0},{16,28},{20,24},{24,20},{28,16},{1,13},{... | collective-permute-start | bytes 196616 | tf_op jit(solution)/shard_map/ppermute | solution.py:45
  89.8 2.4 %collective-permute-start.11 = (bf16[256,128]{1,0:T(8,128)(2,1)S(1)}, bf16[256,128]{1,0:T(8,128)(2,1)S(1)}, u32[]{:S(2)}, u32[]{:S(2)}) collective-permute-start(bf16[256,128]{1,0:T(8,128)(2,1)S(1)} %get-tuple-element.54), channel_id=1, source_target_pairs={{0,20},{4,16},{8,28},{12,24},{16,4},{20,0},{24,12},{28,8},{1,21},{... | collective-permute-start | bytes 196616 | tf_op jit(solution)/shard_map/ppermute | solution.py:45
  92.1 1.5 %collective-permute-start.12 = (bf16[256,128]{1,0:T(8,128)(2,1)S(1)}, bf16[256,128]{1,0:T(8,128)(2,1)S(1)}, u32[]{:S(2)}, u32[]{:S(2)}) collective-permute-start(bf16[256,128]{1,0:T(8,128)(2,1)S(1)} %get-tuple-element.55), channel_id=1, source_target_pairs={{0,28},{4,24},{8,20},{12,16},{16,12},{20,8},{24,4},{28,0},{1,29},{... | collective-permute-start | bytes 196616 | tf_op jit(solution)/shard_map/ppermute | solution.py:45
  93.6 1.5 %collective-permute-done.10.refs_3_ = bf16[256,128]{1,0:T(8,128)(2,1)S(1)} collective-permute-done((bf16[256,128]{1,0:T(8,128)(2,1)S(1)}, bf16[256,128]{1,0:T(8,128)(2,1)S(1)}, u32[]{:S(2)}, u32[]{:S(2)}) %collective-permute-start.10) | collective-permute-done | bytes 65568 | tf_op jit(solution)/shard_map/ppermute | solution.py:45
  95.1 8.7 %collective-permute-done.11.refs_4_ = bf16[256,128]{1,0:T(8,128)(2,1)S(1)} collective-permute-done((bf16[256,128]{1,0:T(8,128)(2,1)S(1)}, bf16[256,128]{1,0:T(8,128)(2,1)S(1)}, u32[]{:S(2)}, u32[]{:S(2)}) %collective-permute-start.11) | collective-permute-done | bytes 65568 | tf_op jit(solution)/shard_map/ppermute | solution.py:45
  108.0 1.9 %shard_map.114 = (f32[256,2048]{1,0:T(8,128)S(1)}, f32[1,256]{1,0:T(1,128)S(1)}) custom-call(bf16[256,2048]{1,0:T(8,128)(2,1)S(1)} %copy-done, f32[1,2048]{1,0:T(1,128)S(1)} %bitcast.2, bf16[256,128]{1,0:T(8,128)(2,1)S(1)} %collective-permute-done.7.refs_0_, bf16[256,128]{1,0:T(8,128)(2,1)S(1)} %collective-permute-done.8.refs_1_, ...), custom_call_target="tpu_custom_call" | custom-call | flops 3145728 | bytes 5242880 | tf_op jit(solution)/shard_map/pallas_call | solution.py:313
  110.5 5.8 %psum.7.square_ref = f32[1,256]{1,0:T(1,128)S(1)} all-reduce(f32[1,256]{1,0:T(1,128)} %copy-done.14), channel_id=1, replica_groups=mesh['tok'=8,'chan'=4] {'chan'}, use_global_device_ids=true, to_apply=%region_0.0 | all-reduce | flops 256 | bytes 2048 | tf_op jit(solution)/shard_map/psum | solution.py:378
  116.2 1.5 %shard_map.115 = f32[256,2048]{1,0:T(8,128)} custom-call(f32[256,2048]{1,0:T(8,128)S(1)} %get-tuple-element.59.pre_ref, f32[1,256]{1,0:T(1,128)S(1)} %psum.7.square_ref, f32[1,2048]{1,0:T(1,128)S(1)} %bitcast.3), custom_call_target="tpu_custom_call" | custom-call | flops 1048576 | bytes 4194304 | tf_op jit(solution)/shard_map/pallas_call | solution.py:347
  (66 shorter events, 13.0 us)
Async XLA Ops:
  2.4 33.0 %all-to-all-start = ((bf16[8,256,256]{2,1,0:T(8,128)(2,1)}), bf16[8,256,256]{2,1,0:T(8,128)(2,1)S(1)}, u32[]{:S(2)}, u32[]{:S(2)}) async-start(bf16[8,256,256]{2,1,0:T(8,128)(2,1)} %shard_map.109), calls=%async_computation | async-start | bytes 2097152 | tf_op jit(solution)/shard_map/all_to_all | solution.py:49
  9.7 53.0 %copy-start.15 = (s32[8]{0:T(128)S(1)}, s32[8]{0:T(128)}, u32[]{:S(2)}) copy-start(s32[8]{0:T(128)} %lag_ref.1) | copy-start | bytes 100
  35.5 32.5 %copy-start.17 = (bf16[512,256]{1,0:T(8,128)(2,1)S(1)}, bf16[512,256]{1,0:T(8,128)(2,1)}, u32[]{:S(2)}) copy-start(bf16[512,256]{1,0:T(8,128)(2,1)} %constant.8.clone.high_ref.fh_ref) | copy-start | bytes 786436
  35.5 32.5 %copy-start.19 = (bf16[512,256]{1,0:T(8,128)(2,1)S(1)}, bf16[512,256]{1,0:T(8,128)(2,1)}, u32[]{:S(2)}) copy-start(bf16[512,256]{1,0:T(8,128)(2,1)} %constant.9.clone.low_ref.fl_ref) | copy-start | bytes 786436
  35.5 32.5 %copy-start.20 = (bf16[256,512]{1,0:T(8,128)(2,1)S(1)}, bf16[256,512]{1,0:T(8,128)(2,1)}, u32[]{:S(2)}) copy-start(bf16[256,512]{1,0:T(8,128)(2,1)} %constant.10.clone.ih_ref) | copy-start | bytes 786436
  35.5 32.5 %copy-start.21 = (bf16[256,512]{1,0:T(8,128)(2,1)S(1)}, bf16[256,512]{1,0:T(8,128)(2,1)}, u32[]{:S(2)}) copy-start(bf16[256,512]{1,0:T(8,128)(2,1)} %constant.11.clone.il_ref) | copy-start | bytes 786436
  35.5 40.4 %all-to-all-start.1 = ((bf16[8,256,128]{2,1,0:T(8,128)(2,1)}), bf16[8,256,128]{2,1,0:T(8,128)(2,1)S(1)}, u32[]{:S(2)}, u32[]{:S(2)}) async-start(bf16[8,256,128]{2,1,0:T(8,128)(2,1)} %get-tuple-element.37.refs_17_), calls=%async_computation.1 | async-start | bytes 1048576 | tf_op jit(solution)/shard_map/all_to_all | solution.py:49
  39.2 21.5 %collective-permute-start = (bf16[256,128]{1,0:T(8,128)(2,1)S(1)}, bf16[256,128]{1,0:T(8,128)(2,1)S(1)}, u32[]{:S(2)}, u32[]{:S(2)}) collective-permute-start(bf16[256,128]{1,0:T(8,128)(2,1)S(1)} %get-tuple-element.39.refs_9_), channel_id=1, source_target_pairs={{0,16},{4,20},{8,24},{12,28},{16,0},{20,4},{24,8},{28,12},{1,17},{... | collective-permute-start | bytes 196616 | tf_op jit(solution)/shard_map/ppermute | solution.py:45
  42.1 19.8 %collective-permute-start.1 = (bf16[256,128]{1,0:T(8,128)(2,1)S(1)}, bf16[256,128]{1,0:T(8,128)(2,1)S(1)}, u32[]{:S(2)}, u32[]{:S(2)}) collective-permute-start(bf16[256,128]{1,0:T(8,128)(2,1)S(1)} %get-tuple-element.40.refs_10_), channel_id=1, source_target_pairs={{0,8},{4,12},{8,0},{12,4},{16,24},{20,28},{24,16},{28,20},{1,9},{5... | collective-permute-start | bytes 196616 | tf_op jit(solution)/shard_map/ppermute | solution.py:45
  43.6 24.2 %collective-permute-start.2 = (bf16[256,128]{1,0:T(8,128)(2,1)}, bf16[256,128]{1,0:T(8,128)(2,1)S(1)}, u32[]{:S(2)}, u32[]{:S(2)}) collective-permute-start(bf16[256,128]{1,0:T(8,128)(2,1)} %copy-done.4), channel_id=1, source_target_pairs={{0,24},{4,28},{8,16},{12,20},{16,8},{20,12},{24,0},{28,4},{1,25},{... | collective-permute-start | bytes 196616 | tf_op jit(solution)/shard_map/ppermute | solution.py:45
  43.6 24.2 %collective-permute-start.3 = (bf16[256,128]{1,0:T(8,128)(2,1)S(1)}, bf16[256,128]{1,0:T(8,128)(2,1)S(1)}, u32[]{:S(2)}, u32[]{:S(2)}) collective-permute-start(bf16[256,128]{1,0:T(8,128)(2,1)S(1)} %get-tuple-element.42.refs_12_), channel_id=1, source_target_pairs={{0,12},{4,8},{8,4},{12,0},{16,28},{20,24},{24,20},{28,16},{1,13},{... | collective-permute-start | bytes 196616 | tf_op jit(solution)/shard_map/ppermute | solution.py:45
  45.6 22.2 %collective-permute-start.4 = (bf16[256,128]{1,0:T(8,128)(2,1)S(1)}, bf16[256,128]{1,0:T(8,128)(2,1)S(1)}, u32[]{:S(2)}, u32[]{:S(2)}) collective-permute-start(bf16[256,128]{1,0:T(8,128)(2,1)S(1)} %get-tuple-element.43.refs_13_), channel_id=1, source_target_pairs={{0,20},{4,16},{8,28},{12,24},{16,4},{20,0},{24,12},{28,8},{1,21},{... | collective-permute-start | bytes 196616 | tf_op jit(solution)/shard_map/ppermute | solution.py:45
  60.8 7.2 %collective-permute-start.5 = (bf16[256,128]{1,0:T(8,128)(2,1)}, bf16[256,128]{1,0:T(8,128)(2,1)S(1)}, u32[]{:S(2)}, u32[]{:S(2)}) collective-permute-start(bf16[256,128]{1,0:T(8,128)(2,1)} %copy-done.6), channel_id=1, source_target_pairs={{0,28},{4,24},{8,20},{12,16},{16,12},{20,8},{24,4},{28,0},{1,29},{... | collective-permute-start | bytes 196616 | tf_op jit(solution)/shard_map/ppermute | solution.py:45
  62.0 6.0 %collective-permute-start.6 = (bf16[256,128]{1,0:T(8,128)(2,1)S(1)}, bf16[256,128]{1,0:T(8,128)(2,1)S(1)}, u32[]{:S(2)}, u32[]{:S(2)}) collective-permute-start(bf16[256,128]{1,0:T(8,128)(2,1)S(1)} %get-tuple-element.45.refs_15_), channel_id=1, source_target_pairs={{0,4},{4,0},{8,12},{12,8},{16,20},{20,16},{24,28},{28,24},{1,5},{5... | collective-permute-start | bytes 196616 | tf_op jit(solution)/shard_map/ppermute | solution.py:45
  71.4 10.2 %collective-permute-start.7 = (bf16[256,128]{1,0:T(8,128)(2,1)S(1)}, bf16[256,128]{1,0:T(8,128)(2,1)S(1)}, u32[]{:S(2)}, u32[]{:S(2)}) collective-permute-start(bf16[256,128]{1,0:T(8,128)(2,1)S(1)} %get-tuple-element.47), channel_id=1, source_target_pairs={{0,16},{4,20},{8,24},{12,28},{16,0},{20,4},{24,8},{28,12},{1,17},{... | collective-permute-start | bytes 196616 | tf_op jit(solution)/shard_map/ppermute | solution.py:45
  71.5 10.1 %collective-permute-start.8 = (bf16[256,128]{1,0:T(8,128)(2,1)S(1)}, bf16[256,128]{1,0:T(8,128)(2,1)S(1)}, u32[]{:S(2)}, u32[]{:S(2)}) collective-permute-start(bf16[256,128]{1,0:T(8,128)(2,1)S(1)} %get-tuple-element.48), channel_id=1, source_target_pairs={{0,8},{4,12},{8,0},{12,4},{16,24},{20,28},{24,16},{28,20},{1,9},{5... | collective-permute-start | bytes 196616 | tf_op jit(solution)/shard_map/ppermute | solution.py:45
  75.4 6.2 %collective-permute-start.9 = (bf16[256,128]{1,0:T(8,128)(2,1)S(1)}, bf16[256,128]{1,0:T(8,128)(2,1)S(1)}, u32[]{:S(2)}, u32[]{:S(2)}) collective-permute-start(bf16[256,128]{1,0:T(8,128)(2,1)S(1)} %get-tuple-element.49), channel_id=1, source_target_pairs={{0,24},{4,28},{8,16},{12,20},{16,8},{20,12},{24,0},{28,4},{1,25},{... | collective-permute-start | bytes 196616 | tf_op jit(solution)/shard_map/ppermute | solution.py:45
  77.5 27.6 %copy-start.12 = (f32[2048]{0:T(1024)S(1)}, f32[2048]{0:T(1024)}, u32[]{:S(2)}) copy-start(f32[2048]{0:T(1024)} %param.16) | copy-start | bytes 24580
  81.6 34.6 %copy-start.13 = (f32[2048]{0:T(1024)S(1)}, f32[2048]{0:T(1024)}, u32[]{:S(2)}) copy-start(f32[2048]{0:T(1024)} %param.17) | copy-start | bytes 24580
  81.6 23.4 %all-to-all-start.2 = ((bf16[8,256,128]{2,1,0:T(8,128)(2,1)}), bf16[8,256,128]{2,1,0:T(8,128)(2,1)S(1)}, u32[]{:S(2)}, u32[]{:S(2)}) async-start(bf16[8,256,128]{2,1,0:T(8,128)(2,1)} %shard_map.112), calls=%async_computation.2 | async-start | bytes 1048576 | tf_op jit(solution)/shard_map/all_to_all | solution.py:49
  86.9 8.2 %collective-permute-start.10 = (bf16[256,128]{1,0:T(8,128)(2,1)S(1)}, bf16[256,128]{1,0:T(8,128)(2,1)S(1)}, u32[]{:S(2)}, u32[]{:S(2)}) collective-permute-start(bf16[256,128]{1,0:T(8,128)(2,1)S(1)} %get-tuple-element.53), channel_id=1, source_target_pairs={{0,12},{4,8},{8,4},{12,0},{16,28},{20,24},{24,20},{28,16},{1,13},{... | collective-permute-start | bytes 196616 | tf_op jit(solution)/shard_map/ppermute | solution.py:45
  89.8 14.0 %collective-permute-start.11 = (bf16[256,128]{1,0:T(8,128)(2,1)S(1)}, bf16[256,128]{1,0:T(8,128)(2,1)S(1)}, u32[]{:S(2)}, u32[]{:S(2)}) collective-permute-start(bf16[256,128]{1,0:T(8,128)(2,1)S(1)} %get-tuple-element.54), channel_id=1, source_target_pairs={{0,20},{4,16},{8,28},{12,24},{16,4},{20,0},{24,12},{28,8},{1,21},{... | collective-permute-start | bytes 196616 | tf_op jit(solution)/shard_map/ppermute | solution.py:45
  92.1 11.7 %collective-permute-start.12 = (bf16[256,128]{1,0:T(8,128)(2,1)S(1)}, bf16[256,128]{1,0:T(8,128)(2,1)S(1)}, u32[]{:S(2)}, u32[]{:S(2)}) collective-permute-start(bf16[256,128]{1,0:T(8,128)(2,1)S(1)} %get-tuple-element.55), channel_id=1, source_target_pairs={{0,28},{4,24},{8,20},{12,16},{16,12},{20,8},{24,4},{28,0},{1,29},{... | collective-permute-start | bytes 196616 | tf_op jit(solution)/shard_map/ppermute | solution.py:45
  93.6 10.8 %collective-permute-start.13 = (bf16[256,128]{1,0:T(8,128)(2,1)S(1)}, bf16[256,128]{1,0:T(8,128)(2,1)S(1)}, u32[]{:S(2)}, u32[]{:S(2)}) collective-permute-start(bf16[256,128]{1,0:T(8,128)(2,1)S(1)} %get-tuple-element.56), channel_id=1, source_target_pairs={{0,4},{4,0},{8,12},{12,8},{16,20},{20,16},{24,28},{28,24},{1,5},{5... | collective-permute-start | bytes 196616 | tf_op jit(solution)/shard_map/ppermute | solution.py:45
  (17 other events, 84.1 us)

commit v8 on v7

--- a/solution.py
+++ b/solution.py
@@ -11,7 +11,6 @@
 from jax.sharding import PartitionSpec as P
 
 MIB = 1024 * 1024
-EARLY = 3
 WHOLE = pl.BlockSpec(memory_space=pltpu.VMEM)
 IN_HBM = pl.BlockSpec(memory_space=pltpu.HBM)
 
@@ -63,10 +62,11 @@
     return pl.ds(pl.multiple_of(partner(step) * part, 128), part)
 
 
-def split_kernel(count, part, filt_ref, out_ref, sems):
+def split_kernel(count, part, filt_ref, *refs):
+    outs, sems = refs[:count], refs[count]
     copies = []
-    for j in range(count):
-        copies.append(pltpu.make_async_copy(filt_ref.at[:, pl.ds(j * part, part)], out_ref.at[j], sems.at[j]))
+    for k in range(count):
+        copies.append(pltpu.make_async_copy(filt_ref.at[:, columns_of(k, part)], outs[k], sems.at[k]))
         copies[-1].start()
     for copy in copies:
         copy.wait()
@@ -77,7 +77,7 @@
 
 
 def gate_kernel(count, part, key_ref, value_ref, *refs):
-    firsts, lasts, (key_buf, value_buf, sems) = refs[:count], refs[count:-3], refs[-3:]
+    lasts, firsts, (key_buf, value_buf, sems) = refs[:count], refs[count:-3], refs[-3:]
     copies = []
     for k in range(count):
         cols = columns_of(k, part)
@@ -94,10 +94,10 @@
             copy.wait()
         product = key_buf[k].astype(jnp.float32) * value_buf[k].astype(jnp.float32)
         product = product.astype(jnp.bfloat16)
-        size = firsts[k].shape[1]
-        firsts[k][...] = product[:, :size]
-        if lasts:
-            lasts[0][partner(k)] = product[:, size:]
+        size = lasts[k].shape[1]
+        lasts[k][...] = product[:, part - size :]
+        if firsts:
+            firsts[0][partner(k)] = product[:, : part - size]
 
 
 def pieces(x, count):
@@ -109,12 +109,12 @@
     width, columns = filter_store.shape
     part = columns // count
     if part % 128:
-        return filter_store.reshape(width, count, part).transpose(1, 0, 2)
+        return pieces(filter_store, count)
     return pl.pallas_call(
         functools.partial(split_kernel, count, part),
-        out_shape=jax.ShapeDtypeStruct((count, width, part), jnp.bfloat16),
+        out_shape=[jax.ShapeDtypeStruct((width, part), jnp.bfloat16)] * count,
         in_specs=[IN_HBM],
-        out_specs=WHOLE,
+        out_specs=[WHOLE] * count,
         scratch_shapes=[pltpu.SemaphoreType.DMA((count,))],
         compiler_params=pltpu.CompilerParams(vmem_limit_bytes=16 * MIB),
         cost_estimate=pl.CostEstimate(flops=0, bytes_accessed=4 * width * columns, transcendentals=0),
@@ -152,30 +152,32 @@
     return dot(high, block) + dot(low, block)
 
 
-def filter_kernel(lag_ref, high_ref, low_ref, blocks, *outs):
+def filter_kernel(steps, lag_ref, high_ref, low_ref, *refs):
+    blocks, outs = refs[: len(steps)], refs[len(steps) :]
     chunk = outs[0].shape[2]
-    for i in range(blocks.shape[0]):
-        spectrum = transform(high_ref[...], low_ref[...], blocks[i])
+    for k, block in zip(steps, blocks):
+        spectrum = transform(high_ref[...], low_ref[...], block[...])
         for c, out in enumerate(outs):
-            out[lag_ref[i]] = spectrum[:, c * chunk : (c + 1) * chunk]
+            out[lag_ref[partner(k)]] = spectrum[:, c * chunk : (c + 1) * chunk]
 
 
 def filter_spectra(lag_of_block, high, low, blocks):
-    count, width, part = blocks.shape
+    steps = list(blocks)
+    width, part = blocks[0].shape
     chunks = chunks_of(part)
-    shape = jax.ShapeDtypeStruct((count, 2 * width, part // chunks), jnp.float32)
+    shape = jax.ShapeDtypeStruct((len(steps), 2 * width, part // chunks), jnp.float32)
     return pl.pallas_call(
-        filter_kernel,
+        functools.partial(filter_kernel, steps),
         out_shape=[shape] * chunks,
-        in_specs=[pl.BlockSpec(memory_space=pltpu.SMEM)] + [WHOLE] * 3,
+        in_specs=[pl.BlockSpec(memory_space=pltpu.SMEM)] + [WHOLE] * (2 + len(steps)),
         out_specs=[WHOLE] * chunks,
         compiler_params=pltpu.CompilerParams(vmem_limit_bytes=16 * MIB),
         cost_estimate=pl.CostEstimate(
-            flops=8 * count * width * width * part,
-            bytes_accessed=10 * count * width * part,
+            flops=8 * len(steps) * width * width * part,
+            bytes_accessed=10 * len(steps) * width * part,
             transcendentals=0,
         ),
-    )(lag_of_block, high, low, blocks)
+    )(lag_of_block, high, low, *[blocks[k] for k in steps])
 
 
 def multiply_spectra(count, width, columns, fs, gs, ss):
@@ -288,12 +290,12 @@
             total = total + pre * pre
         return total
 
+    if pieces > count:
+        for j in range(count):
+            total = add(total, j * part, convs[-1].at[j], gates[-1].at[j])
     for k, conv_ref, gated_ref in zip(steps, convs, gates):
-        total = add(total, partner(k) * part if count > 1 else 0, conv_ref, gated_ref)
-    if pieces > count:
-        size = convs[-1].shape[2]
-        for j in range(count):
-            total = add(total, j * part + part - size, convs[-1].at[j], gates[-1].at[j])
+        start = partner(k) * part + part - conv_ref.shape[1] if count > 1 else 0
+        total = add(total, start, conv_ref, gated_ref)
     square_ref[...] = jnp.sum(total.T, axis=0, keepdims=True)
 
 
@@ -359,22 +361,29 @@
     width, columns = query.shape
     count = lax.axis_size("tok")
     tabs = [jnp.asarray(t) for t in tables(width)]
-    own = split(count, filter_store)
-    own, (key_in, value_in) = after(own, key_in, value_in)
-    firsts, lasts = gate(count, key_in, value_in)
+    own = list(split(count, filter_store))
+    own[0], (key_in, value_in) = after(own[0], key_in, value_in)
+    lasts, firsts = gate(count, key_in, value_in)
     order = sending_order(count)
     steps = order + [0]
-    filt = filter_spectra(lag_of_block, *tabs[:2], spread(own))
-    blocks = [send(firsts[k], k, count) for k in order] + [firsts[0]]
-    lasts_all = [spread(last) for last in lasts]
-    done = block_conv(tabs, filt[0], steps, blocks)
+    filts = [send(own[k], k, count) for k in order]
+    blocks = []
+    for at, k in enumerate(order):
+        block = lasts[k]
+        if at + 2 < len(order):
+            block, (filts[at + 2],) = after(block, filts[at + 2])
+        blocks.append(send(block, k, count))
+    filt = filter_spectra(lag_of_block, *tabs[:2], dict(zip(steps, filts + own[:1])))
+    own_last = lasts[0]
+    spread_convs = []
+    for filt_first, first in zip(filt[:-1], firsts):
+        (done,) = block_conv(tabs, filt_first, [], [spread(first)])
+        own_last, (done,) = after(own_last, done)
+        spread_convs.append(spread(done))
+    done = block_conv(tabs, filt[-1], steps, blocks + [own_last])
     convs = [send(done[at], k, count) for at, k in enumerate(order)] + [done[-1]]
-    for filt_last, last in zip(filt[1:], lasts_all):
-        (done,) = block_conv(tabs, filt_last, [], [last])
-        done, convs[:EARLY] = after(done, *convs[:EARLY])
-        convs.append(spread(done))
-    gates = [firsts[k] for k in steps] + list(lasts)
-    pre, square = gated_output(query, skip[None, :], steps, convs, gates)
+    gates = [lasts[k] for k in steps] + list(firsts)
+    pre, square = gated_output(query, skip[None, :], steps, convs + spread_convs, gates)
     square = lax.psum(square, "chan")
     return scaled(columns * lax.axis_size("chan"), pre, square, out_gain[None, :])
 

time: 118 us -> 126 us (1.068)
  starting transfers between devices: 39.1 us -> 62.2 us
  waiting for transfers between devices: 45.1 us -> 28.3 us
  local copies, waits for them, and re-layouts: 12 us -> 14.2 us
    ppermute x14 -> x21, starting transfers between devices: 22.8 us -> 51.2 us  [send(): return lax.ppermute(block, 'tok', [(d, d ^ step) for d in range(count)])]
    all_to_all x3 -> x2, waiting for transfers between devices: 23 us -> 0.01 us  [spread(): return lax.all_to_all(blocks, 'tok', 0, 0, tiled=True)]
    ppermute x14 -> x21, waiting for transfers between devices: 22.1 us -> 28.3 us  [send(): return lax.ppermute(block, 'tok', [(d, d ^ step) for d in range(count)])]
    all_to_all x3 -> x2, starting transfers between devices: 16.3 us -> 11 us  [spread(): return lax.all_to_all(blocks, 'tok', 0, 0, tiled=True)]
    unnamed x48 -> x40, local copies, waits for them, and re-layouts: 12 us -> 14.2 us
  transfers between devices with their start and end apart: 17 -> 23, of which waited for: 5 -> 10; matrix products, arithmetic and copies ran while one was open for 0% -> 0% of each run, Pallas kernels for 9% -> 4%
where the time goes in v8:
time: 126 us; the launch traced here: 125 us
  starting transfers between devices  62.2 us (49%)
  waiting for transfers between devices  28.3 us (22%)
  Pallas kernels  14.6 us (12%)
  local copies, waits for them, and re-layouts  14.2 us (11%)
  blocking collectives  5.76 us (5%)
    ppermute x21, starting transfers between devices, send(): return lax.ppermute(block, 'tok', [(d, d ^ step) for d in range(count)])  51.2 us
    ppermute x21, waiting for transfers between devices, send(): return lax.ppermute(block, 'tok', [(d, d ^ step) for d in range(count)])  28.3 us
    unnamed x40, local copies, waits for them, and re-layouts  14.2 us
    all_to_all x2, starting transfers between devices, spread(): return lax.all_to_all(blocks, 'tok', 0, 0, tiled=True)  11 us
    pallas_call x2, Pallas kernels, block_conv(): pl.pallas_call(functools.partial(conv_kernel, steps), out_shape=[jax.Shap...  7.61 us
    psum x1, blocking collectives, local(): square = lax.psum(square, 'chan')  5.76 us
  transfers between devices with their start and end apart: 23, of which 10 were waited for; matrix products, arithmetic and copies ran while one was open for 0% of the time, Pallas kernels for 4%

profile of v8, /device:TPU:0, one launch (start us, length us, event | category | flops | bytes accessed | tf_op | source)
XLA Modules:
  0.0 125.3 jit_solution(7417162283191759812)
XLA Ops:
  5.5 7.3 %all-to-all-start = ((bf16[8,256,128]{2,1,0:T(8,128)(2,1)}), bf16[8,256,128]{2,1,0:T(8,128)(2,1)S(1)}, u32[]{:S(2)}, u32[]{:S(2)}) async-start(bf16[8,256,128]{2,1,0:T(8,128)(2,1)} %get-tuple-element.80.refs_17_), calls=%async_computation | async-start | bytes 1048576 | tf_op jit(solution)/shard_map/all_to_all | solution.py:48
  12.8 2.0 %collective-permute-start.6 = (bf16[256,256]{1,0:T(8,128)(2,1)S(1)}, bf16[256,256]{1,0:T(8,128)(2,1)S(1)}, u32[]{:S(2)}, u32[]{:S(2)}) collective-permute-start(bf16[256,256]{1,0:T(8,128)(2,1)S(1)} %get-tuple-element.67), channel_id=1, source_target_pairs={{0,4},{4,0},{8,12},{12,8},{16,20},{20,16},{24,28},{28,24},{1,5},{5... | collective-permute-start | bytes 393224 | tf_op jit(solution)/shard_map/ppermute | solution.py:44
  14.8 3.3 %collective-permute-start.5 = (bf16[256,256]{1,0:T(8,128)(2,1)S(1)}, bf16[256,256]{1,0:T(8,128)(2,1)S(1)}, u32[]{:S(2)}, u32[]{:S(2)}) collective-permute-start(bf16[256,256]{1,0:T(8,128)(2,1)S(1)} %get-tuple-element.64), channel_id=1, source_target_pairs={{0,28},{4,24},{8,20},{12,16},{16,12},{20,8},{24,4},{28,0},{1,29},{... | collective-permute-start | bytes 393224 | tf_op jit(solution)/shard_map/ppermute | solution.py:44
  19.6 3.7 %collective-permute-start.2 = (bf16[256,256]{1,0:T(8,128)(2,1)S(1)}, bf16[256,256]{1,0:T(8,128)(2,1)S(1)}, u32[]{:S(2)}, u32[]{:S(2)}) collective-permute-start(bf16[256,256]{1,0:T(8,128)(2,1)S(1)} %get-tuple-element.55), channel_id=1, source_target_pairs={{0,24},{4,28},{8,16},{12,20},{16,8},{20,12},{24,0},{28,4},{1,25},{... | collective-permute-start | bytes 393224 | tf_op jit(solution)/shard_map/ppermute | solution.py:44
  23.3 4.4 %collective-permute-done.6.refs_6_ = bf16[256,256]{1,0:T(8,128)(2,1)S(1)} collective-permute-done((bf16[256,256]{1,0:T(8,128)(2,1)S(1)}, bf16[256,256]{1,0:T(8,128)(2,1)S(1)}, u32[]{:S(2)}, u32[]{:S(2)}) %collective-permute-start.6) | collective-permute-done | bytes 131104 | tf_op jit(solution)/shard_map/ppermute | solution.py:44
  27.7 2.9 %collective-permute-done.5.refs_5_ = bf16[256,256]{1,0:T(8,128)(2,1)S(1)} collective-permute-done((bf16[256,256]{1,0:T(8,128)(2,1)S(1)}, bf16[256,256]{1,0:T(8,128)(2,1)S(1)}, u32[]{:S(2)}, u32[]{:S(2)}) %collective-permute-start.5) | collective-permute-done | bytes 131104 | tf_op jit(solution)/shard_map/ppermute | solution.py:44
  30.6 13.5 %collective-permute-start.1 = (bf16[256,256]{1,0:T(8,128)(2,1)S(1)}, bf16[256,256]{1,0:T(8,128)(2,1)S(1)}, u32[]{:S(2)}, u32[]{:S(2)}) collective-permute-start(bf16[256,256]{1,0:T(8,128)(2,1)S(1)} %get-tuple-element.50), channel_id=1, source_target_pairs={{0,8},{4,12},{8,0},{12,4},{16,24},{20,28},{24,16},{28,20},{1,9},{5... | collective-permute-start | bytes 393224 | tf_op jit(solution)/shard_map/ppermute | solution.py:44
  44.1 2.2 %collective-permute-done.4.refs_4_ = bf16[256,256]{1,0:T(8,128)(2,1)S(1)} collective-permute-done((bf16[256,256]{1,0:T(8,128)(2,1)S(1)}, bf16[256,256]{1,0:T(8,128)(2,1)S(1)}, u32[]{:S(2)}, u32[]{:S(2)}) %collective-permute-start.4) | collective-permute-done | bytes 131104 | tf_op jit(solution)/shard_map/ppermute | solution.py:44
  46.3 3.5 %collective-permute-done.refs_0_ = bf16[256,256]{1,0:T(8,128)(2,1)S(1)} collective-permute-done((bf16[256,256]{1,0:T(8,128)(2,1)S(1)}, bf16[256,256]{1,0:T(8,128)(2,1)S(1)}, u32[]{:S(2)}, u32[]{:S(2)}) %collective-permute-start) | collective-permute-done | bytes 131104 | tf_op jit(solution)/shard_map/ppermute | solution.py:44
  49.9 1.9 %shard_map.111 = (f32[8,512,128]{2,1,0:T(8,128)S(1)}, f32[8,512,128]{2,1,0:T(8,128)S(1)}) custom-call(s32[8]{0:T(128)S(1)} %copy-done.11, bf16[512,256]{1,0:T(8,128)(2,1)S(1)} %copy-done.12, bf16[512,256]{1,0:T(8,128)(2,1)S(1)} %copy-done.13, bf16[256,256]{1,0:T(8,128)(2,1)S(1)} %collective-permute-done.refs_0_, ...), custom_call_target="tpu_custom_call" | custom-call | flops 1073741824 | bytes 5242880 | tf_op jit(solution)/shard_map/pallas_call | solution.py:169
  56.1 4.1 %shard_map.112 = bf16[8,256,128]{2,1,0:T(8,128)(2,1)} custom-call(bf16[512,256]{1,0:T(8,128)(2,1)S(1)} %copy-done.12, bf16[512,256]{1,0:T(8,128)(2,1)S(1)} %copy-done.13, bf16[256,512]{1,0:T(8,128)(2,1)S(1)} %copy-done.14, bf16[256,512]{1,0:T(8,128)(2,1)S(1)} %copy-done.15, f32[8,512,128]{2,1,0:T(8,128)S(1)} %copy-done.17, ...), custom_call_target="tpu_custom_call" | custom-call | flops 1610612736 | bytes 3670016 | tf_op jit(solution)/shard_map/pallas_call | solution.py:261
  60.2 3.8 %all-to-all-start.1 = ((bf16[8,256,128]{2,1,0:T(8,128)(2,1)}), bf16[8,256,128]{2,1,0:T(8,128)(2,1)S(1)}, u32[]{:S(2)}, u32[]{:S(2)}) async-start(bf16[8,256,128]{2,1,0:T(8,128)(2,1)} %shard_map.112), calls=%async_computation.1 | async-start | bytes 1048576 | tf_op jit(solution)/shard_map/all_to_all | solution.py:48
  64.0 4.7 %collective-permute-start.12 = (bf16[256,128]{1,0:T(8,128)(2,1)S(1)}, bf16[256,128]{1,0:T(8,128)(2,1)S(1)}, u32[]{:S(2)}, u32[]{:S(2)}) collective-permute-start(bf16[256,128]{1,0:T(8,128)(2,1)S(1)} %get-tuple-element.76.refs_14_), channel_id=1, source_target_pairs={{0,28},{4,24},{8,20},{12,16},{16,12},{20,8},{24,4},{28,0},{1,29},{... | collective-permute-start | bytes 196616 | tf_op jit(solution)/shard_map/ppermute | solution.py:44
  70.8 3.8 %collective-permute-start.9 = (bf16[256,128]{1,0:T(8,128)(2,1)S(1)}, bf16[256,128]{1,0:T(8,128)(2,1)S(1)}, u32[]{:S(2)}, u32[]{:S(2)}) collective-permute-start(bf16[256,128]{1,0:T(8,128)(2,1)S(1)} %get-tuple-element.73.refs_11_), channel_id=1, source_target_pairs={{0,24},{4,28},{8,16},{12,20},{16,8},{20,12},{24,0},{28,4},{1,25},{... | collective-permute-start | bytes 196616 | tf_op jit(solution)/shard_map/ppermute | solution.py:44
  74.6 5.8 %collective-permute-done.12.refs_5_ = bf16[256,128]{1,0:T(8,128)(2,1)S(1)} collective-permute-done((bf16[256,128]{1,0:T(8,128)(2,1)S(1)}, bf16[256,128]{1,0:T(8,128)(2,1)S(1)}, u32[]{:S(2)}, u32[]{:S(2)}) %collective-permute-start.12) | collective-permute-done | bytes 65568 | tf_op jit(solution)/shard_map/ppermute | solution.py:44
  80.4 6.4 %collective-permute-start.8 = (bf16[256,128]{1,0:T(8,128)(2,1)S(1)}, bf16[256,128]{1,0:T(8,128)(2,1)S(1)}, u32[]{:S(2)}, u32[]{:S(2)}) collective-permute-start(bf16[256,128]{1,0:T(8,128)(2,1)S(1)} %get-tuple-element.72.refs_10_), channel_id=1, source_target_pairs={{0,8},{4,12},{8,0},{12,4},{16,24},{20,28},{24,16},{28,20},{1,9},{5... | collective-permute-start | bytes 196616 | tf_op jit(solution)/shard_map/ppermute | solution.py:44
  87.3 1.9 %collective-permute-done.8.refs_1_ = bf16[256,128]{1,0:T(8,128)(2,1)S(1)} collective-permute-done((bf16[256,128]{1,0:T(8,128)(2,1)S(1)}, bf16[256,128]{1,0:T(8,128)(2,1)S(1)}, u32[]{:S(2)}, u32[]{:S(2)}) %collective-permute-start.8) | collective-permute-done | bytes 65568 | tf_op jit(solution)/shard_map/ppermute | solution.py:44
  89.1 2.9 %collective-permute-done.7.refs_0_ = bf16[256,128]{1,0:T(8,128)(2,1)S(1)} collective-permute-done((bf16[256,128]{1,0:T(8,128)(2,1)S(1)}, bf16[256,128]{1,0:T(8,128)(2,1)S(1)}, u32[]{:S(2)}, u32[]{:S(2)}) %collective-permute-start.7) | collective-permute-done | bytes 65568 | tf_op jit(solution)/shard_map/ppermute | solution.py:44
  93.7 3.5 %shard_map.113 = (bf16[256,128]{1,0:T(8,128)(2,1)S(1)}, bf16[256,128]{1,0:T(8,128)(2,1)S(1)}, bf16[256,128]{1,0:T(8,128)(2,1)S(1)}, bf16[256,128]{1,0:T(8,128)(2...) custom-call(bf16[512,256]{1,0:T(8,128)(2,1)S(1)} %copy-done.12, ...), custom_call_target="tpu_custom_call" | custom-call | flops 1610612736 | bytes 3670016 | tf_op jit(solution)/shard_map/pallas_call | solution.py:261
  98.2 3.4 %collective-permute-start.16 = (bf16[256,128]{1,0:T(8,128)(2,1)S(1)}, bf16[256,128]{1,0:T(8,128)(2,1)S(1)}, u32[]{:S(2)}, u32[]{:S(2)}) collective-permute-start(bf16[256,128]{1,0:T(8,128)(2,1)S(1)} %get-tuple-element.84), channel_id=1, source_target_pairs={{0,24},{4,28},{8,16},{12,20},{16,8},{20,12},{24,0},{28,4},{1,25},{... | collective-permute-start | bytes 196616 | tf_op jit(solution)/shard_map/ppermute | solution.py:44
  101.6 1.8 %collective-permute-start.18 = (bf16[256,128]{1,0:T(8,128)(2,1)S(1)}, bf16[256,128]{1,0:T(8,128)(2,1)S(1)}, u32[]{:S(2)}, u32[]{:S(2)}) collective-permute-start(bf16[256,128]{1,0:T(8,128)(2,1)S(1)} %get-tuple-element.86), channel_id=1, source_target_pairs={{0,20},{4,16},{8,28},{12,24},{16,4},{20,0},{24,12},{28,8},{1,21},{... | collective-permute-start | bytes 196616 | tf_op jit(solution)/shard_map/ppermute | solution.py:44
  104.4 2.7 %collective-permute-start.19 = (bf16[256,128]{1,0:T(8,128)(2,1)S(1)}, bf16[256,128]{1,0:T(8,128)(2,1)S(1)}, u32[]{:S(2)}, u32[]{:S(2)}) collective-permute-start(bf16[256,128]{1,0:T(8,128)(2,1)S(1)} %get-tuple-element.87), channel_id=1, source_target_pairs={{0,28},{4,24},{8,20},{12,16},{16,12},{20,8},{24,4},{28,0},{1,29},{... | collective-permute-start | bytes 196616 | tf_op jit(solution)/shard_map/ppermute | solution.py:44
  108.4 3.1 %collective-permute-done.19.refs_5_ = bf16[256,128]{1,0:T(8,128)(2,1)S(1)} collective-permute-done((bf16[256,128]{1,0:T(8,128)(2,1)S(1)}, bf16[256,128]{1,0:T(8,128)(2,1)S(1)}, u32[]{:S(2)}, u32[]{:S(2)}) %collective-permute-start.19) | collective-permute-done | bytes 65568 | tf_op jit(solution)/shard_map/ppermute | solution.py:44
  118.0 5.8 %psum.7.square_ref = f32[1,256]{1,0:T(1,128)S(1)} all-reduce(f32[1,256]{1,0:T(1,128)} %copy-done.10), channel_id=1, replica_groups=mesh['tok'=8,'chan'=4] {'chan'}, use_global_device_ids=true, to_apply=%region_0.0 | all-reduce | flops 256 | bytes 2048 | tf_op jit(solution)/shard_map/psum | solution.py:387
  (70 shorter events, 26.7 us)
Async XLA Ops:
  1.2 48.7 %copy-start.13 = (bf16[512,256]{1,0:T(8,128)(2,1)S(1)}, bf16[512,256]{1,0:T(8,128)(2,1)}, u32[]{:S(2)}) copy-start(bf16[512,256]{1,0:T(8,128)(2,1)} %constant.9.clone.low_ref.fl_ref) | copy-start | bytes 786436
  5.5 49.0 %all-to-all-start = ((bf16[8,256,128]{2,1,0:T(8,128)(2,1)}), bf16[8,256,128]{2,1,0:T(8,128)(2,1)S(1)}, u32[]{:S(2)}, u32[]{:S(2)}) async-start(bf16[8,256,128]{2,1,0:T(8,128)(2,1)} %get-tuple-element.80.refs_17_), calls=%async_computation | async-start | bytes 1048576 | tf_op jit(solution)/shard_map/all_to_all | solution.py:48
  12.8 15.0 %collective-permute-start.6 = (bf16[256,256]{1,0:T(8,128)(2,1)S(1)}, bf16[256,256]{1,0:T(8,128)(2,1)S(1)}, u32[]{:S(2)}, u32[]{:S(2)}) collective-permute-start(bf16[256,256]{1,0:T(8,128)(2,1)S(1)} %get-tuple-element.67), channel_id=1, source_target_pairs={{0,4},{4,0},{8,12},{12,8},{16,20},{20,16},{24,28},{28,24},{1,5},{5... | collective-permute-start | bytes 393224 | tf_op jit(solution)/shard_map/ppermute | solution.py:44
  14.8 15.8 %collective-permute-start.5 = (bf16[256,256]{1,0:T(8,128)(2,1)S(1)}, bf16[256,256]{1,0:T(8,128)(2,1)S(1)}, u32[]{:S(2)}, u32[]{:S(2)}) collective-permute-start(bf16[256,256]{1,0:T(8,128)(2,1)S(1)} %get-tuple-element.64), channel_id=1, source_target_pairs={{0,28},{4,24},{8,20},{12,16},{16,12},{20,8},{24,4},{28,0},{1,29},{... | collective-permute-start | bytes 393224 | tf_op jit(solution)/shard_map/ppermute | solution.py:44
  18.0 28.3 %collective-permute-start.4 = (bf16[256,256]{1,0:T(8,128)(2,1)S(1)}, bf16[256,256]{1,0:T(8,128)(2,1)S(1)}, u32[]{:S(2)}, u32[]{:S(2)}) collective-permute-start(bf16[256,256]{1,0:T(8,128)(2,1)S(1)} %get-tuple-element.61), channel_id=1, source_target_pairs={{0,20},{4,16},{8,28},{12,24},{16,4},{20,0},{24,12},{28,8},{1,21},{... | collective-permute-start | bytes 393224 | tf_op jit(solution)/shard_map/ppermute | solution.py:44
  18.6 27.7 %collective-permute-start.3 = (bf16[256,256]{1,0:T(8,128)(2,1)S(1)}, bf16[256,256]{1,0:T(8,128)(2,1)S(1)}, u32[]{:S(2)}, u32[]{:S(2)}) collective-permute-start(bf16[256,256]{1,0:T(8,128)(2,1)S(1)} %get-tuple-element.58), channel_id=1, source_target_pairs={{0,12},{4,8},{8,4},{12,0},{16,28},{20,24},{24,20},{28,16},{1,13},{... | collective-permute-start | bytes 393224 | tf_op jit(solution)/shard_map/ppermute | solution.py:44
  19.6 26.7 %collective-permute-start.2 = (bf16[256,256]{1,0:T(8,128)(2,1)S(1)}, bf16[256,256]{1,0:T(8,128)(2,1)S(1)}, u32[]{:S(2)}, u32[]{:S(2)}) collective-permute-start(bf16[256,256]{1,0:T(8,128)(2,1)S(1)} %get-tuple-element.55), channel_id=1, source_target_pairs={{0,24},{4,28},{8,16},{12,20},{16,8},{20,12},{24,0},{28,4},{1,25},{... | collective-permute-start | bytes 393224 | tf_op jit(solution)/shard_map/ppermute | solution.py:44
  27.7 22.1 %collective-permute-start = (bf16[256,256]{1,0:T(8,128)(2,1)S(1)}, bf16[256,256]{1,0:T(8,128)(2,1)S(1)}, u32[]{:S(2)}, u32[]{:S(2)}) collective-permute-start(bf16[256,256]{1,0:T(8,128)(2,1)S(1)} %get-tuple-element.49), channel_id=1, source_target_pairs={{0,16},{4,20},{8,24},{12,28},{16,0},{20,4},{24,8},{28,12},{1,17},{... | collective-permute-start | bytes 393224 | tf_op jit(solution)/shard_map/ppermute | solution.py:44
  30.6 19.3 %collective-permute-start.1 = (bf16[256,256]{1,0:T(8,128)(2,1)S(1)}, bf16[256,256]{1,0:T(8,128)(2,1)S(1)}, u32[]{:S(2)}, u32[]{:S(2)}) collective-permute-start(bf16[256,256]{1,0:T(8,128)(2,1)S(1)} %get-tuple-element.50), channel_id=1, source_target_pairs={{0,8},{4,12},{8,0},{12,4},{16,24},{20,28},{24,16},{28,20},{1,9},{5... | collective-permute-start | bytes 393224 | tf_op jit(solution)/shard_map/ppermute | solution.py:44
  60.2 52.5 %all-to-all-start.1 = ((bf16[8,256,128]{2,1,0:T(8,128)(2,1)}), bf16[8,256,128]{2,1,0:T(8,128)(2,1)S(1)}, u32[]{:S(2)}, u32[]{:S(2)}) async-start(bf16[8,256,128]{2,1,0:T(8,128)(2,1)} %shard_map.112), calls=%async_computation.1 | async-start | bytes 1048576 | tf_op jit(solution)/shard_map/all_to_all | solution.py:48
  64.0 16.4 %collective-permute-start.12 = (bf16[256,128]{1,0:T(8,128)(2,1)S(1)}, bf16[256,128]{1,0:T(8,128)(2,1)S(1)}, u32[]{:S(2)}, u32[]{:S(2)}) collective-permute-start(bf16[256,128]{1,0:T(8,128)(2,1)S(1)} %get-tuple-element.76.refs_14_), channel_id=1, source_target_pairs={{0,28},{4,24},{8,20},{12,16},{16,12},{20,8},{24,4},{28,0},{1,29},{... | collective-permute-start | bytes 196616 | tf_op jit(solution)/shard_map/ppermute | solution.py:44
  68.7 18.1 %collective-permute-start.13 = (bf16[256,128]{1,0:T(8,128)(2,1)S(1)}, bf16[256,128]{1,0:T(8,128)(2,1)S(1)}, u32[]{:S(2)}, u32[]{:S(2)}) collective-permute-start(bf16[256,128]{1,0:T(8,128)(2,1)S(1)} %get-tuple-element.77.refs_15_), channel_id=1, source_target_pairs={{0,4},{4,0},{8,12},{12,8},{16,20},{20,16},{24,28},{28,24},{1,5},{5... | collective-permute-start | bytes 196616 | tf_op jit(solution)/shard_map/ppermute | solution.py:44
  69.3 18.0 %collective-permute-start.11 = (bf16[256,128]{1,0:T(8,128)(2,1)S(1)}, bf16[256,128]{1,0:T(8,128)(2,1)S(1)}, u32[]{:S(2)}, u32[]{:S(2)}) collective-permute-start(bf16[256,128]{1,0:T(8,128)(2,1)S(1)} %get-tuple-element.75.refs_13_), channel_id=1, source_target_pairs={{0,20},{4,16},{8,28},{12,24},{16,4},{20,0},{24,12},{28,8},{1,21},{... | collective-permute-start | bytes 196616 | tf_op jit(solution)/shard_map/ppermute | solution.py:44
  69.8 17.4 %collective-permute-start.10 = (bf16[256,128]{1,0:T(8,128)(2,1)S(1)}, bf16[256,128]{1,0:T(8,128)(2,1)S(1)}, u32[]{:S(2)}, u32[]{:S(2)}) collective-permute-start(bf16[256,128]{1,0:T(8,128)(2,1)S(1)} %get-tuple-element.74.refs_12_), channel_id=1, source_target_pairs={{0,12},{4,8},{8,4},{12,0},{16,28},{20,24},{24,20},{28,16},{1,13},{... | collective-permute-start | bytes 196616 | tf_op jit(solution)/shard_map/ppermute | solution.py:44
  70.8 16.5 %collective-permute-start.9 = (bf16[256,128]{1,0:T(8,128)(2,1)S(1)}, bf16[256,128]{1,0:T(8,128)(2,1)S(1)}, u32[]{:S(2)}, u32[]{:S(2)}) collective-permute-start(bf16[256,128]{1,0:T(8,128)(2,1)S(1)} %get-tuple-element.73.refs_11_), channel_id=1, source_target_pairs={{0,24},{4,28},{8,16},{12,20},{16,8},{20,12},{24,0},{28,4},{1,25},{... | collective-permute-start | bytes 196616 | tf_op jit(solution)/shard_map/ppermute | solution.py:44
  80.4 8.7 %collective-permute-start.8 = (bf16[256,128]{1,0:T(8,128)(2,1)S(1)}, bf16[256,128]{1,0:T(8,128)(2,1)S(1)}, u32[]{:S(2)}, u32[]{:S(2)}) collective-permute-start(bf16[256,128]{1,0:T(8,128)(2,1)S(1)} %get-tuple-element.72.refs_10_), channel_id=1, source_target_pairs={{0,8},{4,12},{8,0},{12,4},{16,24},{20,28},{24,16},{28,20},{1,9},{5... | collective-permute-start | bytes 196616 | tf_op jit(solution)/shard_map/ppermute | solution.py:44
  86.8 5.3 %collective-permute-start.7 = (bf16[256,128]{1,0:T(8,128)(2,1)S(1)}, bf16[256,128]{1,0:T(8,128)(2,1)S(1)}, u32[]{:S(2)}, u32[]{:S(2)}) collective-permute-start(bf16[256,128]{1,0:T(8,128)(2,1)S(1)} %get-tuple-element.71.refs_9_), channel_id=1, source_target_pairs={{0,16},{4,20},{8,24},{12,28},{16,0},{20,4},{24,8},{28,12},{1,17},{... | collective-permute-start | bytes 196616 | tf_op jit(solution)/shard_map/ppermute | solution.py:44
  97.2 7.3 %collective-permute-start.14 = (bf16[256,128]{1,0:T(8,128)(2,1)S(1)}, bf16[256,128]{1,0:T(8,128)(2,1)S(1)}, u32[]{:S(2)}, u32[]{:S(2)}) collective-permute-start(bf16[256,128]{1,0:T(8,128)(2,1)S(1)} %get-tuple-element.82), channel_id=1, source_target_pairs={{0,16},{4,20},{8,24},{12,28},{16,0},{20,4},{24,8},{28,12},{1,17},{... | collective-permute-start | bytes 196616 | tf_op jit(solution)/shard_map/ppermute | solution.py:44
  97.8 9.4 %collective-permute-start.15 = (bf16[256,128]{1,0:T(8,128)(2,1)S(1)}, bf16[256,128]{1,0:T(8,128)(2,1)S(1)}, u32[]{:S(2)}, u32[]{:S(2)}) collective-permute-start(bf16[256,128]{1,0:T(8,128)(2,1)S(1)} %get-tuple-element.83), channel_id=1, source_target_pairs={{0,8},{4,12},{8,0},{12,4},{16,24},{20,28},{24,16},{28,20},{1,9},{5... | collective-permute-start | bytes 196616 | tf_op jit(solution)/shard_map/ppermute | solution.py:44
  98.2 10.2 %collective-permute-start.16 = (bf16[256,128]{1,0:T(8,128)(2,1)S(1)}, bf16[256,128]{1,0:T(8,128)(2,1)S(1)}, u32[]{:S(2)}, u32[]{:S(2)}) collective-permute-start(bf16[256,128]{1,0:T(8,128)(2,1)S(1)} %get-tuple-element.84), channel_id=1, source_target_pairs={{0,24},{4,28},{8,16},{12,20},{16,8},{20,12},{24,0},{28,4},{1,25},{... | collective-permute-start | bytes 196616 | tf_op jit(solution)/shard_map/ppermute | solution.py:44
  101.6 6.8 %collective-permute-start.17 = (bf16[256,128]{1,0:T(8,128)(2,1)S(1)}, bf16[256,128]{1,0:T(8,128)(2,1)S(1)}, u32[]{:S(2)}, u32[]{:S(2)}) collective-permute-start(bf16[256,128]{1,0:T(8,128)(2,1)S(1)} %get-tuple-element.85), channel_id=1, source_target_pairs={{0,12},{4,8},{8,4},{12,0},{16,28},{20,24},{24,20},{28,16},{1,13},{... | collective-permute-start | bytes 196616 | tf_op jit(solution)/shard_map/ppermute | solution.py:44
  101.6 6.8 %collective-permute-start.18 = (bf16[256,128]{1,0:T(8,128)(2,1)S(1)}, bf16[256,128]{1,0:T(8,128)(2,1)S(1)}, u32[]{:S(2)}, u32[]{:S(2)}) collective-permute-start(bf16[256,128]{1,0:T(8,128)(2,1)S(1)} %get-tuple-element.86), channel_id=1, source_target_pairs={{0,20},{4,16},{8,28},{12,24},{16,4},{20,0},{24,12},{28,8},{1,21},{... | collective-permute-start | bytes 196616 | tf_op jit(solution)/shard_map/ppermute | solution.py:44
  104.4 7.0 %collective-permute-start.19 = (bf16[256,128]{1,0:T(8,128)(2,1)S(1)}, bf16[256,128]{1,0:T(8,128)(2,1)S(1)}, u32[]{:S(2)}, u32[]{:S(2)}) collective-permute-start(bf16[256,128]{1,0:T(8,128)(2,1)S(1)} %get-tuple-element.87), channel_id=1, source_target_pairs={{0,28},{4,24},{8,20},{12,16},{16,12},{20,8},{24,4},{28,0},{1,29},{... | collective-permute-start | bytes 196616 | tf_op jit(solution)/shard_map/ppermute | solution.py:44
  107.1 5.0 %collective-permute-start.20 = (bf16[256,128]{1,0:T(8,128)(2,1)S(1)}, bf16[256,128]{1,0:T(8,128)(2,1)S(1)}, u32[]{:S(2)}, u32[]{:S(2)}) collective-permute-start(bf16[256,128]{1,0:T(8,128)(2,1)S(1)} %get-tuple-element.88), channel_id=1, source_target_pairs={{0,4},{4,0},{8,12},{12,8},{16,20},{20,16},{24,28},{28,24},{1,5},{5... | collective-permute-start | bytes 196616 | tf_op jit(solution)/shard_map/ppermute | solution.py:44
  (19 other events, 240.7 us)

commit v9 on v5

v9 whole, which is shorter than its diff:
```python
import functools
import math

import jax
import jax.numpy as jnp
import ml_dtypes
import numpy as np
from jax import lax
from jax.experimental import pallas as pl
from jax.experimental.pallas import tpu as pltpu
from jax.sharding import PartitionSpec as P

MIB = 1024 * 1024
BIG = 48 * MIB
WHOLE = pl.BlockSpec(memory_space=pltpu.VMEM)
IN_HBM = pl.BlockSpec(memory_space=pltpu.HBM)


def split_bf16(table):
    high = table.astype(ml_dtypes.bfloat16)
    low = (table - high.astype(np.float64)).astype(ml_dtypes.bfloat16)
    return high, low


def tables(width):
    freq = np.concatenate([np.arange(0, width, 2), np.arange(1, width, 2)])
    place = np.arange(width)
    steps = ((2 * freq[:, None] + 1) * place[None, :]) % (4 * width)
    angle = math.pi / (2 * width) * steps
    forward = np.concatenate([np.cos(angle), -np.sin(angle)], axis=0)
    inverse = forward.T / width
    return split_bf16(forward) + split_bf16(inverse)


def partner(step):
    return lax.axis_index("tok") ^ step


def send(block, step, count):
    return lax.ppermute(block, "tok", [(d, d ^ step) for d in range(count)])


def sending_order(count):
    half = count // 2
    far = list(range(half, count, 2)) + list(range(half + 1, count, 2))
    near = list(range(2, half)) + [1]
    order = []
    for at in range(half - 1):
        order += [far[at], near[at]]
    return order[:-1] + far[-1:] + order[-1:]


def columns_of(step, part):
    return pl.ds(pl.multiple_of(partner(step) * part, 128), part)


def piece(x, step, part):
    return lax.dynamic_slice_in_dim(x, partner(step) * part, part, axis=1)


def gate_kernel(alone, paired, part, filt_ref, key_ref, value_ref, *refs):
    width = key_ref.shape[0]
    outs, (key_buf, value_buf, sems) = list(refs[:-3]), refs[-3:]
    filts, gates = dict(zip(alone, outs)), dict(zip(alone + paired, outs[len(alone) :]))
    copies, stores = {}, []
    for k in alone + paired:
        cols = columns_of(k, part)
        copies[k] = (
            pltpu.make_async_copy(key_ref.at[:, cols], key_buf.at[k], sems.at[0, k]),
            pltpu.make_async_copy(value_ref.at[:, cols], value_buf.at[k], sems.at[1, k]),
        )
        for copy in copies[k]:
            copy.start()
    for k in alone + paired:
        to = filts[k] if k in filts else gates[k].at[pl.ds(0, width), :]
        stores.append(pltpu.make_async_copy(filt_ref.at[:, columns_of(k, part)], to, sems.at[2, k]))
        stores[-1].start()
    for k in alone + paired:
        for copy in copies[k]:
            copy.wait()
        product = key_buf[k].astype(jnp.float32) * value_buf[k].astype(jnp.float32)
        gates[k][pl.ds(0 if k in filts else width, width), :] = product.astype(jnp.bfloat16)
    for copy in stores:
        copy.wait()


def gate(count, alone, paired, filter_store, key_in, value_in):
    width, columns = key_in.shape
    part = columns // count
    if part % 128:
        gated = (key_in.astype(jnp.float32) * value_in.astype(jnp.float32)).astype(jnp.bfloat16)
        filts, gates = ({k: piece(x, k, part) for k in alone + paired} for x in (filter_store, gated))
        for k in paired:
            gates[k] = jnp.concatenate([filts.pop(k), gates[k]], axis=0)
        return filts, gates
    block = pltpu.VMEM((count, width, part), jnp.bfloat16)
    shapes = [jax.ShapeDtypeStruct((width, part), jnp.bfloat16)] * (2 * len(alone))
    shapes += [jax.ShapeDtypeStruct((2 * width, part), jnp.bfloat16)] * len(paired)
    found = pl.pallas_call(
        functools.partial(gate_kernel, alone, paired, part),
        out_shape=shapes,
        in_specs=[IN_HBM] * 3,
        out_specs=[WHOLE] * len(shapes),
        scratch_shapes=[block, block, pltpu.SemaphoreType.DMA((3, count))],
        compiler_params=pltpu.CompilerParams(vmem_limit_bytes=16 * MIB),
        cost_estimate=pl.CostEstimate(flops=width * columns, bytes_accessed=10 * width * columns, transcendentals=0),
    )(filter_store, key_in, value_in)
    return dict(zip(alone, found)), dict(zip(alone + paired, found[len(alone) :]))


def dot(x, y):
    return jnp.dot(x, y, preferred_element_type=jnp.float32)


def transform(high, low, block):
    return dot(high, block) + dot(low, block)


def filter_kernel(steps, lag_ref, high_ref, low_ref, *refs):
    blocks, out = refs[:-1], refs[-1]
    for k, block in zip(steps, blocks):
        rows = pl.ds(0, out.shape[1] // 2)
        out[lag_ref[partner(k)]] = transform(high_ref[...], low_ref[...], block[rows, :])


def gated_rows(block, width):
    return block[pl.ds(block.shape[0] - width, width), :]


def gated_kernel(steps, high_ref, low_ref, *refs):
    blocks, out = refs[:-1], refs[-1]
    for k, block in zip(steps, blocks):
        rows = gated_rows(block, out.shape[1] // 2)
        out[partner(k)] = transform(high_ref[...], low_ref[...], rows)


def spectra_shape(count, width, columns):
    return jax.ShapeDtypeStruct((count, 2 * width, columns), jnp.float32)


def transform_cost(count, width, columns, passes):
    return pl.CostEstimate(
        flops=4 * passes * count * width * width * columns,
        bytes_accessed=10 * count * width * columns,
        transcendentals=0,
    )


def filter_spectra(lag_of_block, high, low, blocks):
    steps = list(blocks)
    width, columns = blocks[0].shape
    return pl.pallas_call(
        functools.partial(filter_kernel, steps),
        out_shape=spectra_shape(len(steps), width, columns),
        in_specs=[pl.BlockSpec(memory_space=pltpu.SMEM)] + [WHOLE] * (2 + len(steps)),
        out_specs=WHOLE,
        compiler_params=pltpu.CompilerParams(vmem_limit_bytes=16 * MIB),
        cost_estimate=transform_cost(len(steps), width, columns, 2),
    )(lag_of_block, high, low, *[blocks[k] for k in steps])


def gated_spectra(count, high, low, blocks):
    steps = list(blocks)
    width, columns = blocks[0].shape
    return pl.pallas_call(
        functools.partial(gated_kernel, steps),
        out_shape=spectra_shape(count, width, columns),
        in_specs=[WHOLE] * (2 + len(steps)),
        out_specs=WHOLE,
        compiler_params=pltpu.CompilerParams(vmem_limit_bytes=16 * MIB),
        cost_estimate=transform_cost(len(steps), width, columns, 2),
    )(high, low, *[blocks[k] for k in steps])


def product_kernel(count, steps, first, fh_ref, fl_ref, ih_ref, il_ref, fs, gs, *refs):
    blocks, (gs, ss), outs = refs[: len(steps)], refs[len(steps) : len(steps) + 2], refs[len(steps) + 2 :]
    width, columns = outs[0].shape
    for k, block in zip(steps, blocks):
        gs[partner(k)] = transform(fh_ref[...], fl_ref[...], gated_rows(block, width))
    lane = min(128, columns)

    def products(row, sign):
        re_rows = pl.ds(pl.multiple_of(row * 8, 8), 8)
        im_rows = pl.ds(pl.multiple_of(row * 8 + width, 8), 8)
        for at in range(0, columns, lane):
            lanes = pl.ds(at, lane)
            f_re = [fs[i, re_rows, lanes] for i in range(count)]
            f_im = [fs[i, im_rows, lanes] for i in range(count)]
            h_re, h_im = [], []
            for i in range(count):
                g_re, g_im = gs[i, re_rows, lanes], gs[i, im_rows, lanes]
                if i == 0:
                    h_re.append(g_re)
                    h_im.append(g_im)
                elif sign > 0:
                    h_re.append(g_re - last_im)
                    h_im.append(g_im + last_re)
                else:
                    h_re.append(g_re + last_im)
                    h_im.append(g_im - last_re)
                last_re, last_im = g_re, g_im
            for j in range(count):
                s_re = f_re[0] * h_re[j] - f_im[0] * h_im[j]
                s_im = f_re[0] * h_im[j] + f_im[0] * h_re[j]
                for i in range(1, j + 1):
                    s_re = s_re + f_re[i] * h_re[j - i] - f_im[i] * h_im[j - i]
                    s_im = s_im + f_re[i] * h_im[j - i] + f_im[i] * h_re[j - i]
                ss[j, re_rows, lanes] = s_re
                ss[j, im_rows, lanes] = s_im

    half = width // 16

    @pl.loop(0, half)
    def _(row):
        products(row, 1)

    @pl.loop(half, 2 * half)
    def _(row):
        products(row, -1)

    for k, out in zip(first, outs):
        out[...] = inverse(ih_ref[...], il_ref[...], ss[partner(k)])


def inverse(table_high, table_low, total):
    high = total.astype(jnp.bfloat16)
    low = (total - high.astype(jnp.float32)).astype(jnp.bfloat16)
    return (dot(table_high, high) + dot(table_high, low) + dot(table_low, high)).astype(jnp.bfloat16)


def products(first, tabs, filt, gated, blocks):
    steps = list(blocks)
    count, twice, columns = gated.shape
    width = twice // 2
    found = pl.pallas_call(
        functools.partial(product_kernel, count, steps, first),
        out_shape=[jax.ShapeDtypeStruct(gated.shape, jnp.float32)] * 2
        + [jax.ShapeDtypeStruct((width, columns), jnp.bfloat16)] * len(first),
        in_specs=[WHOLE] * (6 + len(steps)),
        out_specs=[WHOLE] * (2 + len(first)),
        input_output_aliases={5: 0},
        compiler_params=pltpu.CompilerParams(vmem_limit_bytes=20 * MIB),
        cost_estimate=transform_cost(count, width, columns, 7),
    )(*tabs, filt, gated, *[blocks[k] for k in steps])
    return found[1], dict(zip(first, found[2:]))


def inverse_kernel(steps, ih_ref, il_ref, ss, *outs):
    for k, out in zip(steps, outs):
        out[...] = inverse(ih_ref[...], il_ref[...], ss[partner(k)])


def inverses(steps, tabs, sums):
    count, twice, columns = sums.shape
    width = twice // 2
    found = pl.pallas_call(
        functools.partial(inverse_kernel, steps),
        out_shape=[jax.ShapeDtypeStruct((width, columns), jnp.bfloat16)] * len(steps),
        in_specs=[WHOLE] * 3,
        out_specs=[WHOLE] * len(steps),
        compiler_params=pltpu.CompilerParams(vmem_limit_bytes=16 * MIB),
        cost_estimate=transform_cost(len(steps), width, columns, 3),
    )(*tabs[2:], sums)
    return dict(zip(steps, found))


def pre_kernel(steps, query_ref, skip_ref, *refs):
    count = len(steps)
    convs, gates, (pre_ref, square_ref) = refs[:count], refs[count : 2 * count], refs[2 * count :]
    width, part = convs[0].shape
    total = jnp.zeros((width, 128), jnp.float32)
    for at_k, k in enumerate(steps):
        start = partner(k) * part if count > 1 else 0
        for at in range(0, part, 128):
            lanes, cols = pl.ds(at, 128), pl.ds(pl.multiple_of(start + at, 128), 128)
            gated = gates[at_k][pl.ds(gates[at_k].shape[0] - width, width), lanes].astype(jnp.float32)
            conv = convs[at_k][:, lanes].astype(jnp.float32)
            pre = query_ref[:, cols].astype(jnp.float32) * (conv + skip_ref[:, cols] * gated)
            pre_ref[:, cols] = pre
            total = total + pre * pre
    square_ref[...] = jnp.sum(total.T, axis=0, keepdims=True)


def together(blocks, width):
    count = len(blocks)
    order = jnp.arange(count, dtype=jnp.int32) ^ lax.axis_index("tok")
    stacked = jnp.take(jnp.stack([blocks[k][-width:] for k in range(count)]), order, axis=0)
    return {0: stacked.transpose(1, 0, 2).reshape(width, -1)}


def gated_output(query, skip, convs, gates):
    width, columns = query.shape
    steps = list(convs)
    if convs[0].shape[1] % 128:
        convs, gates, steps = together(convs, width), together(gates, width), [0]
    count = len(steps)
    return pl.pallas_call(
        functools.partial(pre_kernel, steps),
        out_shape=(
            jax.ShapeDtypeStruct((width, columns), jnp.float32),
            jax.ShapeDtypeStruct((1, width), jnp.float32),
        ),
        in_specs=[WHOLE] * (2 + 2 * count),
        out_specs=(WHOLE, WHOLE),
        compiler_params=pltpu.CompilerParams(vmem_limit_bytes=16 * MIB),
        cost_estimate=pl.CostEstimate(flops=6 * width * columns, bytes_accessed=10 * width * columns, transcendentals=0),
    )(query, skip, *[convs[k] for k in steps], *[gates[k] for k in steps])


def scale_kernel(channels, steps, pre_ref, gain_ref, *refs):
    squares, (out_ref, buf, sems) = refs[:-3], refs[-3:]
    width = pre_ref.shape[0]
    rows = width // steps
    total = squares[0][...]
    for square in squares[1:]:
        total = total + square[...]
    scale = lax.rsqrt(total * (1.0 / channels) + 1e-06)
    scale = jnp.broadcast_to(scale, (128, width)).T
    copies = []
    for s in range(steps):
        for at in range(0, pre_ref.shape[1], 128):
            cols = pl.ds(at, 128)
            here = scale[s * rows : (s + 1) * rows, :]
            buf[pl.ds(s * rows, rows), cols] = gain_ref[:, cols] * pre_ref[pl.ds(s * rows, rows), cols] * here
        window = pl.ds(s * rows, rows)
        copies.append(pltpu.make_async_copy(buf.at[window, :], out_ref.at[window, :], sems.at[s]))
        copies[-1].start()
    for copy in copies:
        copy.wait()


def scaled(channels, pre, squares, out_gain):
    width, columns = pre.shape
    steps = 8
    return pl.pallas_call(
        functools.partial(scale_kernel, channels, steps),
        out_shape=jax.ShapeDtypeStruct((width, columns), jnp.float32),
        in_specs=[WHOLE] * (2 + len(squares)),
        out_specs=IN_HBM,
        scratch_shapes=[pltpu.VMEM((width, columns), jnp.float32), pltpu.SemaphoreType.DMA((steps,))],
        compiler_params=pltpu.CompilerParams(vmem_limit_bytes=16 * MIB),
        cost_estimate=pl.CostEstimate(flops=2 * width * columns, bytes_accessed=8 * width * columns, transcendentals=0),
    )(pre, out_gain, *squares)


def local(query, key_in, value_in, filter_store, lag_of_block, skip, out_gain):
    width, columns = query.shape
    count = lax.axis_size("tok")
    tabs = [jnp.asarray(t) for t in tables(width)]
    part = columns // count
    order = sending_order(count)
    at = count // 2
    ahead, alone, paired = order[:1], order[1:at], order[at:]
    filts = {k: send(piece(filter_store, k, part), k, count) for k in ahead}
    own_filts, mine = gate(count, alone + [0] + ahead, paired, filter_store, key_in, value_in)
    gates = {}
    for k in alone:
        filts[k] = send(own_filts[k], k, count)
    for k in paired:
        filts[k] = gates[k] = send(mine[k], k, count)
    for k in ahead + alone:
        gates[k] = send(mine[k], k, count)
    filts[0], gates[0] = own_filts[0], mine[0]
    late = (ahead + alone)[1:]
    early = paired + [ahead[0], 0]
    filt = filter_spectra(lag_of_block, *tabs[:2], filts)
    gated = gated_spectra(count, *tabs[:2], {k: gates[k] for k in early})
    first = order[:1]
    sums, found = products(first, tabs, filt, gated, {k: gates[k] for k in late})
    found.update(inverses(order[1:] + [0], tabs, sums))
    convs = {k: send(found[k], k, count) for k in order}
    convs[0] = found[0]
    pre, square = gated_output(query, skip[None, :], convs, mine)
    others = lax.axis_size("chan")
    squares = [square] + [
        lax.ppermute(square, "chan", [(d, d ^ step) for d in range(others)]) for step in reversed(range(1, others))
    ]
    return scaled(columns * others, pre, squares, out_gain[None, :])


def solution(mesh):
    in_specs = (
        P("tok", "chan"),
        P("tok", "chan"),
        P("tok", "chan"),
        P("tok", "chan"),
        P(),
        P("chan"),
        P("chan"),
    )
    return jax.shard_map(local, mesh=mesh, in_specs=in_specs, out_specs=P("tok", "chan"), check_vma=False)
```

time: 89.5 us -> 93.2 us (1.041)
  waiting for transfers between devices: 24.5 us -> 43.8 us
  starting transfers between devices: 42.5 us -> 29.8 us
  blocking collectives: 5.71 us -> 0 us
  local copies, waits for them, and re-layouts: 3.71 us -> 6.53 us
    ppermute x21 -> x18, waiting for transfers between devices: 24.5 us -> 41.1 us  [send(): return lax.ppermute(block, 'tok', [(d, d ^ step) for d in range(count)])]
    ppermute x21 -> x18, starting transfers between devices: 42.5 us -> 27.9 us  [send(): return lax.ppermute(block, 'tok', [(d, d ^ step) for d in range(count)])]
    psum x1 -> x0, blocking collectives: 5.71 us -> none  [local(): square = lax.psum(square, 'chan')]
    ppermute x0 -> x3, waiting for transfers between devices: none -> 2.72 us  [local(): lax.ppermute(square, 'chan', [(d, d ^ step) for d in range(others)])]
    ppermute x0 -> x3, starting transfers between devices: none -> 1.93 us  [local(): lax.ppermute(square, 'chan', [(d, d ^ step) for d in range(others)])]
    unnamed x22 -> x26, local copies, waits for them, and re-layouts: 3.71 us -> 5.61 us
    pallas_call x3 -> x2, Pallas kernels: 2.36 us -> 3.23 us  [the longest x1 1.62 us: gate(): pl.pallas_call(functools.partial(gate_kernel, alone, paired, part), out_s...]
  transfers between devices with their start and end apart: 21 -> 21, of which waited for: 8 -> 11; matrix products, arithmetic and copies ran while one was open for 0% -> 0% of each run, Pallas kernels for 6% -> 7%
where the time goes in v9:
time: 93.2 us; the launch traced here: 92.9 us
  waiting for transfers between devices  43.8 us (47%)
  starting transfers between devices  29.8 us (32%)
  Pallas kernels  12.6 us (14%)
  local copies, waits for them, and re-layouts  6.53 us (7%)
    ppermute x18, waiting for transfers between devices, send(): return lax.ppermute(block, 'tok', [(d, d ^ step) for d in range(count)])  41.1 us
    ppermute x18, starting transfers between devices, send(): return lax.ppermute(block, 'tok', [(d, d ^ step) for d in range(count)])  27.9 us
    unnamed x26, local copies, waits for them, and re-layouts  5.61 us
    pallas_call x1, Pallas kernels, products(): pl.pallas_call(functools.partial(product_kernel, count, steps, first), ou...  4.1 us
    ppermute x3, waiting for transfers between devices, local(): lax.ppermute(square, 'chan', [(d, d ^ step) for d in range(others)])  2.72 us
    ppermute x3, starting transfers between devices, local(): lax.ppermute(square, 'chan', [(d, d ^ step) for d in range(others)])  1.93 us
    pallas_call x1, Pallas kernels, filter_spectra(): pl.pallas_call(functools.partial(filter_kernel, steps), out_shape=spectra...  1.93 us
  transfers between devices with their start and end apart: 21, of which 11 were waited for; matrix products, arithmetic and copies ran while one was open for 0% of the time, Pallas kernels for 7%

profile of v9, /device:TPU:0, one launch (start us, length us, event | category | flops | bytes accessed | tf_op | source)
XLA Modules:
  0.0 92.9 jit_solution(5518261971927996207)
XLA Ops:
  0.9 4.1 %collective-permute-start = (bf16[256,256]{1,0:T(8,128)(2,1)S(1)}, bf16[256,256]{1,0:T(8,128)(2,1)S(1)}, u32[]{:S(2)}, u32[]{:S(2)}) collective-permute-start(bf16[256,256]{1,0:T(8,128)(2,1)S(1)} %constant_dynamic-slice_fusion), channel_id=1, source_target_pairs={{0,16},{4,20},{8,24},{12,28},{16,0},{20,4},{24,8},{28,12},{1,17},{... | collective-permute-start | bytes 393224 | tf_op jit(solution)/shard_map/ppermute | solution.py:40
  5.0 1.2 %copy-done = bf16[256,2048]{1,0:T(8,128)(2,1)S(1)} copy-done((bf16[256,2048]{1,0:T(8,128)(2,1)S(1)}, bf16[256,2048]{1,0:T(8,128)(2,1)}, u32[]{:S(2)}) %copy-start) | copy-done | bytes 1048600
  8.7 1.6 %shard_map.109 = (bf16[256,256]{1,0:T(8,128)(2,1)S(1)}, bf16[256,256]{1,0:T(8,128)(2,1)S(1)}, bf16[256,256]{1,0:T(8,128)(2,1)S(1)}, bf16[256,256]{1,0:T(8,128)(2...) custom-call(bf16[256,2048]{1,0:T(8,128)(2,1)S(1)} %copy-done, ...), custom_call_target="tpu_custom_call" | custom-call | flops 524288 | bytes 5242880 | tf_op jit(solution)/shard_map/pallas_call | solution.py:99
  10.3 1.3 %collective-permute-start.4 = (bf16[512,256]{1,0:T(8,128)(2,1)S(1)}, bf16[512,256]{1,0:T(8,128)(2,1)S(1)}, u32[]{:S(2)}, u32[]{:S(2)}) collective-permute-start(bf16[512,256]{1,0:T(8,128)(2,1)S(1)} %get-tuple-element.31.refs_12_), channel_id=1, source_target_pairs={{0,20},{4,16},{8,28},{12,24},{16,4},{20,0},{24,12},{28,8},{1,21},{... | collective-permute-start | bytes 786440 | tf_op jit(solution)/shard_map/ppermute | solution.py:40
  11.7 3.6 %collective-permute-start.5 = (bf16[512,256]{1,0:T(8,128)(2,1)S(1)}, bf16[512,256]{1,0:T(8,128)(2,1)S(1)}, u32[]{:S(2)}, u32[]{:S(2)}) collective-permute-start(bf16[512,256]{1,0:T(8,128)(2,1)S(1)} %get-tuple-element.32.refs_13_), channel_id=1, source_target_pairs={{0,28},{4,24},{8,20},{12,16},{16,12},{20,8},{24,4},{28,0},{1,29},{... | collective-permute-start | bytes 786440 | tf_op jit(solution)/shard_map/ppermute | solution.py:40
  15.2 1.5 %collective-permute-start.6 = (bf16[512,256]{1,0:T(8,128)(2,1)S(1)}, bf16[512,256]{1,0:T(8,128)(2,1)S(1)}, u32[]{:S(2)}, u32[]{:S(2)}) collective-permute-start(bf16[512,256]{1,0:T(8,128)(2,1)S(1)} %get-tuple-element.33.refs_14_), channel_id=1, source_target_pairs={{0,4},{4,0},{8,12},{12,8},{16,20},{20,16},{24,28},{28,24},{1,5},{5... | collective-permute-start | bytes 786440 | tf_op jit(solution)/shard_map/ppermute | solution.py:40
  17.5 11.1 %collective-permute-done.1.refs_1_ = bf16[256,256]{1,0:T(8,128)(2,1)S(1)} collective-permute-done((bf16[256,256]{1,0:T(8,128)(2,1)S(1)}, bf16[256,256]{1,0:T(8,128)(2,1)S(1)}, u32[]{:S(2)}, u32[]{:S(2)}) %collective-permute-start.1) | collective-permute-done | bytes 131104 | tf_op jit(solution)/shard_map/ppermute | solution.py:40
  28.6 2.0 %collective-permute-start.2 = (bf16[256,256]{1,0:T(8,128)(2,1)S(1)}, bf16[256,256]{1,0:T(8,128)(2,1)S(1)}, u32[]{:S(2)}, u32[]{:S(2)}) collective-permute-start(bf16[256,256]{1,0:T(8,128)(2,1)S(1)} %get-tuple-element.29), channel_id=1, source_target_pairs={{0,24},{4,28},{8,16},{12,20},{16,8},{20,12},{24,0},{28,4},{1,25},{... | collective-permute-start | bytes 393224 | tf_op jit(solution)/shard_map/ppermute | solution.py:40
  30.5 15.9 %collective-permute-done.7.refs_3_ = bf16[256,256]{1,0:T(8,128)(2,1)S(1)} collective-permute-done((bf16[256,256]{1,0:T(8,128)(2,1)S(1)}, bf16[256,256]{1,0:T(8,128)(2,1)S(1)}, u32[]{:S(2)}, u32[]{:S(2)}) %collective-permute-start.7) | collective-permute-done | bytes 131104 | tf_op jit(solution)/shard_map/ppermute | solution.py:40
  46.5 2.0 %collective-permute-start.8 = (bf16[256,256]{1,0:T(8,128)(2,1)S(1)}, bf16[256,256]{1,0:T(8,128)(2,1)S(1)}, u32[]{:S(2)}, u32[]{:S(2)}) collective-permute-start(bf16[256,256]{1,0:T(8,128)(2,1)S(1)} %get-tuple-element.37.refs_9_), channel_id=1, source_target_pairs={{0,8},{4,12},{8,0},{12,4},{16,24},{20,28},{24,16},{28,20},{1,9},{5... | collective-permute-start | bytes 393224 | tf_op jit(solution)/shard_map/ppermute | solution.py:40
  52.4 1.7 %collective-permute-done.3.refs_3_ = bf16[256,256]{1,0:T(8,128)(2,1)S(1)} collective-permute-done((bf16[256,256]{1,0:T(8,128)(2,1)S(1)}, bf16[256,256]{1,0:T(8,128)(2,1)S(1)}, u32[]{:S(2)}, u32[]{:S(2)}) %collective-permute-start.3) | collective-permute-done | bytes 131104 | tf_op jit(solution)/shard_map/ppermute | solution.py:40
  54.2 1.9 %shard_map.110.fs = f32[8,512,256]{2,1,0:T(8,128)S(1)} custom-call(s32[8]{0:T(128)S(1)} %copy-done.10, bf16[512,256]{1,0:T(8,128)(2,1)S(1)} %copy-done.7, bf16[512,256]{1,0:T(8,128)(2,1)S(1)} %copy-done.5, bf16[256,256]{1,0:T(8,128)(2,1)S(1)} %collective-permute-done.refs_0_, bf16[256,256]{1,0:T(8,128)(2,1)S(1)} %collective-permute-done.1.refs_1_, ...), custom_call_target="tpu_custom_call" | custom-call | flops 1073741824 | bytes 5242880 | tf_op jit(solution)/shard_map/pallas_call | solution.py:152
  57.3 2.0 %collective-permute-done.10.refs_2_ = bf16[256,256]{1,0:T(8,128)(2,1)S(1)} collective-permute-done((bf16[256,256]{1,0:T(8,128)(2,1)S(1)}, bf16[256,256]{1,0:T(8,128)(2,1)S(1)}, u32[]{:S(2)}, u32[]{:S(2)}) %collective-permute-start.10) | collective-permute-done | bytes 131104 | tf_op jit(solution)/shard_map/ppermute | solution.py:40
  59.4 4.1 %shard_map.112 = (f32[8,512,256]{2,1,0:T(8,128)S(1)}, f32[8,512,256]{2,1,0:T(8,128)S(1)}, bf16[256,256]{1,0:T(8,128)(2,1)S(1)}) custom-call(bf16[512,256]{1,0:T(8,128)(2,1)S(1)} %copy-done.7, bf16[512,256]{1,0:T(8,128)(2,1)S(1)} %copy-done.5, bf16[256,512]{1,0:T(8,128)(2,1)S(1)} %copy-done.12, ...), custom_call_target="tpu_custom_call", output_to_operand_aliasing={{0}: (5, {})} | custom-call | flops 3758096384 | bytes 5242880 | tf_op jit(solution)/shard_map/pallas_call | solution.py:235
  64.4 1.6 %shard_map.113 = (bf16[256,256]{1,0:T(8,128)(2,1)S(1)}, bf16[256,256]{1,0:T(8,128)(2,1)S(1)}, bf16[256,256]{1,0:T(8,128)(2,1)S(1)}, bf16[256,256]{1,0:T(8,128)(2...) custom-call(bf16[256,512]{1,0:T(8,128)(2,1)S(1)} %copy-done.12, ...), custom_call_target="tpu_custom_call" | custom-call | flops 1409286144 | bytes 4587520 | tf_op jit(solution)/shard_map/pallas_call | solution.py:256
  66.0 1.7 %collective-permute-start.12 = (bf16[256,256]{1,0:T(8,128)(2,1)S(1)}, bf16[256,256]{1,0:T(8,128)(2,1)S(1)}, u32[]{:S(2)}, u32[]{:S(2)}) collective-permute-start(bf16[256,256]{1,0:T(8,128)(2,1)S(1)} %get-tuple-element.42), channel_id=1, source_target_pairs={{0,8},{4,12},{8,0},{12,4},{16,24},{20,28},{24,16},{28,20},{1,9},{5... | collective-permute-start | bytes 393224 | tf_op jit(solution)/shard_map/ppermute | solution.py:40
  67.7 1.9 %collective-permute-start.13 = (bf16[256,256]{1,0:T(8,128)(2,1)S(1)}, bf16[256,256]{1,0:T(8,128)(2,1)S(1)}, u32[]{:S(2)}, u32[]{:S(2)}) collective-permute-start(bf16[256,256]{1,0:T(8,128)(2,1)S(1)} %get-tuple-element.43), channel_id=1, source_target_pairs={{0,24},{4,28},{8,16},{12,20},{16,8},{20,12},{24,0},{28,4},{1,25},{... | collective-permute-start | bytes 393224 | tf_op jit(solution)/shard_map/ppermute | solution.py:40
  69.6 3.4 %collective-permute-start.15 = (bf16[256,256]{1,0:T(8,128)(2,1)S(1)}, bf16[256,256]{1,0:T(8,128)(2,1)S(1)}, u32[]{:S(2)}, u32[]{:S(2)}) collective-permute-start(bf16[256,256]{1,0:T(8,128)(2,1)S(1)} %get-tuple-element.45), channel_id=1, source_target_pairs={{0,20},{4,16},{8,28},{12,24},{16,4},{20,0},{24,12},{28,8},{1,21},{... | collective-permute-start | bytes 393224 | tf_op jit(solution)/shard_map/ppermute | solution.py:40
  73.0 2.6 %collective-permute-start.16 = (bf16[256,256]{1,0:T(8,128)(2,1)S(1)}, bf16[256,256]{1,0:T(8,128)(2,1)S(1)}, u32[]{:S(2)}, u32[]{:S(2)}) collective-permute-start(bf16[256,256]{1,0:T(8,128)(2,1)S(1)} %get-tuple-element.46), channel_id=1, source_target_pairs={{0,28},{4,24},{8,20},{12,16},{16,12},{20,8},{24,4},{28,0},{1,29},{... | collective-permute-start | bytes 393224 | tf_op jit(solution)/shard_map/ppermute | solution.py:40
  77.6 2.2 %collective-permute-done.14.refs_3_ = bf16[256,256]{1,0:T(8,128)(2,1)S(1)} collective-permute-done((bf16[256,256]{1,0:T(8,128)(2,1)S(1)}, bf16[256,256]{1,0:T(8,128)(2,1)S(1)}, u32[]{:S(2)}, u32[]{:S(2)}) %collective-permute-start.14) | collective-permute-done | bytes 131104 | tf_op jit(solution)/shard_map/ppermute | solution.py:40
  79.7 6.0 %collective-permute-done.15.refs_4_ = bf16[256,256]{1,0:T(8,128)(2,1)S(1)} collective-permute-done((bf16[256,256]{1,0:T(8,128)(2,1)S(1)}, bf16[256,256]{1,0:T(8,128)(2,1)S(1)}, u32[]{:S(2)}, u32[]{:S(2)}) %collective-permute-start.15) | collective-permute-done | bytes 131104 | tf_op jit(solution)/shard_map/ppermute | solution.py:40
  86.8 1.6 %collective-permute-start.19 = (f32[1,256]{1,0:T(1,128)S(1)}, f32[1,256]{1,0:T(1,128)S(1)}, u32[]{:S(2)}, u32[]{:S(2)}) collective-permute-start(f32[1,256]{1,0:T(1,128)S(1)} %get-tuple-element.50.refs_0_), channel_id=1, source_target_pairs={{0,2},{1,3},{2,0},{3,1},{4,6},{5,7},{6,4},{7,5},{8,10},{9,11},{10,... | collective-permute-start | bytes 3080 | tf_op jit(solution)/shard_map/ppermute | solution.py:376
  88.7 1.8 %collective-permute-done.19.refs_2_ = f32[1,256]{1,0:T(1,128)S(1)} collective-permute-done((f32[1,256]{1,0:T(1,128)S(1)}, f32[1,256]{1,0:T(1,128)S(1)}, u32[]{:S(2)}, u32[]{:S(2)}) %collective-permute-start.19) | collective-permute-done | bytes 1056 | tf_op jit(solution)/shard_map/ppermute | solution.py:376
  91.4 1.5 %shard_map.115 = f32[256,2048]{1,0:T(8,128)} custom-call(f32[256,2048]{1,0:T(8,128)S(1)} %get-tuple-element.49.pre_ref, f32[1,2048]{1,0:T(1,128)S(1)} %bitcast.3, f32[1,256]{1,0:T(1,128)S(1)} %get-tuple-element.50.refs_0_, f32[1,256]{1,0:T(1,128)S(1)} %collective-permute-done.18.refs_1_, f32[1,256]{1,0:T(1,128)S(1)} %collective-permute-done.19.refs_2_, ...), custom_call_target="tpu_custom_call" | custom-call | flops 1048576 | bytes 4194304 | tf_op jit(solution)/shard_map/pallas_call | solution.py:335
  (52 shorter events, 14.3 us)
Async XLA Ops:
  0.9 15.8 %collective-permute-start = (bf16[256,256]{1,0:T(8,128)(2,1)S(1)}, bf16[256,256]{1,0:T(8,128)(2,1)S(1)}, u32[]{:S(2)}, u32[]{:S(2)}) collective-permute-start(bf16[256,256]{1,0:T(8,128)(2,1)S(1)} %constant_dynamic-slice_fusion), channel_id=1, source_target_pairs={{0,16},{4,20},{8,24},{12,28},{16,0},{20,4},{24,8},{28,12},{1,17},{... | collective-permute-start | bytes 393224 | tf_op jit(solution)/shard_map/ppermute | solution.py:40
  8.7 45.5 %copy-start.5 = (bf16[512,256]{1,0:T(8,128)(2,1)S(1)}, bf16[512,256]{1,0:T(8,128)(2,1)}, u32[]{:S(2)}) copy-start(bf16[512,256]{1,0:T(8,128)(2,1)} %constant.23.clone.low_ref.fl_ref) | copy-start | bytes 786436
  8.7 45.5 %copy-start.7 = (bf16[512,256]{1,0:T(8,128)(2,1)S(1)}, bf16[512,256]{1,0:T(8,128)(2,1)}, u32[]{:S(2)}) copy-start(bf16[512,256]{1,0:T(8,128)(2,1)} %constant.22.clone.high_ref.fh_ref) | copy-start | bytes 786436
  8.7 45.5 %copy-start.10 = (s32[8]{0:T(128)S(1)}, s32[8]{0:T(128)}, u32[]{:S(2)}) copy-start(s32[8]{0:T(128)} %lag_ref.1) | copy-start | bytes 100
  10.3 36.1 %collective-permute-start.4 = (bf16[512,256]{1,0:T(8,128)(2,1)S(1)}, bf16[512,256]{1,0:T(8,128)(2,1)S(1)}, u32[]{:S(2)}, u32[]{:S(2)}) collective-permute-start(bf16[512,256]{1,0:T(8,128)(2,1)S(1)} %get-tuple-element.31.refs_12_), channel_id=1, source_target_pairs={{0,20},{4,16},{8,28},{12,24},{16,4},{20,0},{24,12},{28,8},{1,21},{... | collective-permute-start | bytes 786440 | tf_op jit(solution)/shard_map/ppermute | solution.py:40
  11.7 36.8 %collective-permute-start.5 = (bf16[512,256]{1,0:T(8,128)(2,1)S(1)}, bf16[512,256]{1,0:T(8,128)(2,1)S(1)}, u32[]{:S(2)}, u32[]{:S(2)}) collective-permute-start(bf16[512,256]{1,0:T(8,128)(2,1)S(1)} %get-tuple-element.32.refs_13_), channel_id=1, source_target_pairs={{0,28},{4,24},{8,20},{12,16},{16,12},{20,8},{24,4},{28,0},{1,29},{... | collective-permute-start | bytes 786440 | tf_op jit(solution)/shard_map/ppermute | solution.py:40
  15.2 33.6 %collective-permute-start.6 = (bf16[512,256]{1,0:T(8,128)(2,1)S(1)}, bf16[512,256]{1,0:T(8,128)(2,1)S(1)}, u32[]{:S(2)}, u32[]{:S(2)}) collective-permute-start(bf16[512,256]{1,0:T(8,128)(2,1)S(1)} %get-tuple-element.33.refs_14_), channel_id=1, source_target_pairs={{0,4},{4,0},{8,12},{12,8},{16,20},{20,16},{24,28},{28,24},{1,5},{5... | collective-permute-start | bytes 786440 | tf_op jit(solution)/shard_map/ppermute | solution.py:40
  16.7 11.8 %collective-permute-start.1 = (bf16[256,256]{1,0:T(8,128)(2,1)S(1)}, bf16[256,256]{1,0:T(8,128)(2,1)S(1)}, u32[]{:S(2)}, u32[]{:S(2)}) collective-permute-start(bf16[256,256]{1,0:T(8,128)(2,1)S(1)} %get-tuple-element.28), channel_id=1, source_target_pairs={{0,8},{4,12},{8,0},{12,4},{16,24},{20,28},{24,16},{28,20},{1,9},{5... | collective-permute-start | bytes 393224 | tf_op jit(solution)/shard_map/ppermute | solution.py:40
  16.7 29.7 %collective-permute-start.7 = (bf16[256,256]{1,0:T(8,128)(2,1)S(1)}, bf16[256,256]{1,0:T(8,128)(2,1)S(1)}, u32[]{:S(2)}, u32[]{:S(2)}) collective-permute-start(bf16[256,256]{1,0:T(8,128)(2,1)S(1)} %get-tuple-element.35.refs_8_), channel_id=1, source_target_pairs={{0,16},{4,20},{8,24},{12,28},{16,0},{20,4},{24,8},{28,12},{1,17},{... | collective-permute-start | bytes 393224 | tf_op jit(solution)/shard_map/ppermute | solution.py:40
  28.6 23.8 %collective-permute-start.2 = (bf16[256,256]{1,0:T(8,128)(2,1)S(1)}, bf16[256,256]{1,0:T(8,128)(2,1)S(1)}, u32[]{:S(2)}, u32[]{:S(2)}) collective-permute-start(bf16[256,256]{1,0:T(8,128)(2,1)S(1)} %get-tuple-element.29), channel_id=1, source_target_pairs={{0,24},{4,28},{8,16},{12,20},{16,8},{20,12},{24,0},{28,4},{1,25},{... | collective-permute-start | bytes 393224 | tf_op jit(solution)/shard_map/ppermute | solution.py:40
  46.5 7.7 %collective-permute-start.3 = (bf16[256,256]{1,0:T(8,128)(2,1)S(1)}, bf16[256,256]{1,0:T(8,128)(2,1)S(1)}, u32[]{:S(2)}, u32[]{:S(2)}) collective-permute-start(bf16[256,256]{1,0:T(8,128)(2,1)S(1)} %get-tuple-element.30), channel_id=1, source_target_pairs={{0,12},{4,8},{8,4},{12,0},{16,28},{20,24},{24,20},{28,16},{1,13},{... | collective-permute-start | bytes 393224 | tf_op jit(solution)/shard_map/ppermute | solution.py:40
  46.5 10.2 %collective-permute-start.8 = (bf16[256,256]{1,0:T(8,128)(2,1)S(1)}, bf16[256,256]{1,0:T(8,128)(2,1)S(1)}, u32[]{:S(2)}, u32[]{:S(2)}) collective-permute-start(bf16[256,256]{1,0:T(8,128)(2,1)S(1)} %get-tuple-element.37.refs_9_), channel_id=1, source_target_pairs={{0,8},{4,12},{8,0},{12,4},{16,24},{20,28},{24,16},{28,20},{1,9},{5... | collective-permute-start | bytes 393224 | tf_op jit(solution)/shard_map/ppermute | solution.py:40
  48.5 8.9 %collective-permute-start.9 = (bf16[256,256]{1,0:T(8,128)(2,1)S(1)}, bf16[256,256]{1,0:T(8,128)(2,1)S(1)}, u32[]{:S(2)}, u32[]{:S(2)}) collective-permute-start(bf16[256,256]{1,0:T(8,128)(2,1)S(1)} %get-tuple-element.38.refs_10_), channel_id=1, source_target_pairs={{0,24},{4,28},{8,16},{12,20},{16,8},{20,12},{24,0},{28,4},{1,25},{... | collective-permute-start | bytes 393224 | tf_op jit(solution)/shard_map/ppermute | solution.py:40
  48.9 10.5 %collective-permute-start.10 = (bf16[256,256]{1,0:T(8,128)(2,1)S(1)}, bf16[256,256]{1,0:T(8,128)(2,1)S(1)}, u32[]{:S(2)}, u32[]{:S(2)}) collective-permute-start(bf16[256,256]{1,0:T(8,128)(2,1)S(1)} %get-tuple-element.39.refs_11_), channel_id=1, source_target_pairs={{0,12},{4,8},{8,4},{12,0},{16,28},{20,24},{24,20},{28,16},{1,13},{... | collective-permute-start | bytes 393224 | tf_op jit(solution)/shard_map/ppermute | solution.py:40
  63.5 9.5 %collective-permute-start.11 = (bf16[256,256]{1,0:T(8,128)(2,1)S(1)}, bf16[256,256]{1,0:T(8,128)(2,1)S(1)}, u32[]{:S(2)}, u32[]{:S(2)}) collective-permute-start(bf16[256,256]{1,0:T(8,128)(2,1)S(1)} %get-tuple-element.40), channel_id=1, source_target_pairs={{0,16},{4,20},{8,24},{12,28},{16,0},{20,4},{24,8},{28,12},{1,17},{... | collective-permute-start | bytes 393224 | tf_op jit(solution)/shard_map/ppermute | solution.py:40
  66.0 10.5 %collective-permute-start.12 = (bf16[256,256]{1,0:T(8,128)(2,1)S(1)}, bf16[256,256]{1,0:T(8,128)(2,1)S(1)}, u32[]{:S(2)}, u32[]{:S(2)}) collective-permute-start(bf16[256,256]{1,0:T(8,128)(2,1)S(1)} %get-tuple-element.42), channel_id=1, source_target_pairs={{0,8},{4,12},{8,0},{12,4},{16,24},{20,28},{24,16},{28,20},{1,9},{5... | collective-permute-start | bytes 393224 | tf_op jit(solution)/shard_map/ppermute | solution.py:40
  67.7 9.8 %collective-permute-start.13 = (bf16[256,256]{1,0:T(8,128)(2,1)S(1)}, bf16[256,256]{1,0:T(8,128)(2,1)S(1)}, u32[]{:S(2)}, u32[]{:S(2)}) collective-permute-start(bf16[256,256]{1,0:T(8,128)(2,1)S(1)} %get-tuple-element.43), channel_id=1, source_target_pairs={{0,24},{4,28},{8,16},{12,20},{16,8},{20,12},{24,0},{28,4},{1,25},{... | collective-permute-start | bytes 393224 | tf_op jit(solution)/shard_map/ppermute | solution.py:40
  69.6 10.1 %collective-permute-start.14 = (bf16[256,256]{1,0:T(8,128)(2,1)S(1)}, bf16[256,256]{1,0:T(8,128)(2,1)S(1)}, u32[]{:S(2)}, u32[]{:S(2)}) collective-permute-start(bf16[256,256]{1,0:T(8,128)(2,1)S(1)} %get-tuple-element.44), channel_id=1, source_target_pairs={{0,12},{4,8},{8,4},{12,0},{16,28},{20,24},{24,20},{28,16},{1,13},{... | collective-permute-start | bytes 393224 | tf_op jit(solution)/shard_map/ppermute | solution.py:40
  69.6 16.1 %collective-permute-start.15 = (bf16[256,256]{1,0:T(8,128)(2,1)S(1)}, bf16[256,256]{1,0:T(8,128)(2,1)S(1)}, u32[]{:S(2)}, u32[]{:S(2)}) collective-permute-start(bf16[256,256]{1,0:T(8,128)(2,1)S(1)} %get-tuple-element.45), channel_id=1, source_target_pairs={{0,20},{4,16},{8,28},{12,24},{16,4},{20,0},{24,12},{28,8},{1,21},{... | collective-permute-start | bytes 393224 | tf_op jit(solution)/shard_map/ppermute | solution.py:40
  73.0 12.7 %collective-permute-start.16 = (bf16[256,256]{1,0:T(8,128)(2,1)S(1)}, bf16[256,256]{1,0:T(8,128)(2,1)S(1)}, u32[]{:S(2)}, u32[]{:S(2)}) collective-permute-start(bf16[256,256]{1,0:T(8,128)(2,1)S(1)} %get-tuple-element.46), channel_id=1, source_target_pairs={{0,28},{4,24},{8,20},{12,16},{16,12},{20,8},{24,4},{28,0},{1,29},{... | collective-permute-start | bytes 393224 | tf_op jit(solution)/shard_map/ppermute | solution.py:40
  76.5 9.3 %collective-permute-start.17 = (bf16[256,256]{1,0:T(8,128)(2,1)S(1)}, bf16[256,256]{1,0:T(8,128)(2,1)S(1)}, u32[]{:S(2)}, u32[]{:S(2)}) collective-permute-start(bf16[256,256]{1,0:T(8,128)(2,1)S(1)} %get-tuple-element.47), channel_id=1, source_target_pairs={{0,4},{4,0},{8,12},{12,8},{16,20},{20,16},{24,28},{28,24},{1,5},{5... | collective-permute-start | bytes 393224 | tf_op jit(solution)/shard_map/ppermute | solution.py:40
  86.7 1.9 %collective-permute-start.20 = (f32[1,256]{1,0:T(1,128)S(1)}, f32[1,256]{1,0:T(1,128)S(1)}, u32[]{:S(2)}, u32[]{:S(2)}) collective-permute-start(f32[1,256]{1,0:T(1,128)S(1)} %get-tuple-element.50.refs_0_), channel_id=1, source_target_pairs={{0,1},{1,0},{2,3},{3,2},{4,5},{5,4},{6,7},{7,6},{8,9},{9,8},{10,11... | collective-permute-start | bytes 3080 | tf_op jit(solution)/shard_map/ppermute | solution.py:376
  86.8 3.6 %collective-permute-start.19 = (f32[1,256]{1,0:T(1,128)S(1)}, f32[1,256]{1,0:T(1,128)S(1)}, u32[]{:S(2)}, u32[]{:S(2)}) collective-permute-start(f32[1,256]{1,0:T(1,128)S(1)} %get-tuple-element.50.refs_0_), channel_id=1, source_target_pairs={{0,2},{1,3},{2,0},{3,1},{4,6},{5,7},{6,4},{7,5},{8,10},{9,11},{10,... | collective-permute-start | bytes 3080 | tf_op jit(solution)/shard_map/ppermute | solution.py:376
  88.4 3.0 %collective-permute-start.18 = (f32[1,256]{1,0:T(1,128)S(1)}, f32[1,256]{1,0:T(1,128)S(1)}, u32[]{:S(2)}, u32[]{:S(2)}) collective-permute-start(f32[1,256]{1,0:T(1,128)S(1)} %get-tuple-element.50.refs_0_), channel_id=1, source_target_pairs={{0,3},{1,2},{2,1},{3,0},{4,7},{5,6},{6,5},{7,4},{8,11},{9,10},{10,... | collective-permute-start | bytes 3080 | tf_op jit(solution)/shard_map/ppermute | solution.py:376
  (10 other events, 91.1 us)

commit v10 on v9

v10 whole, which is shorter than its diff:
```python
import functools
import math

import jax
import jax.numpy as jnp
import ml_dtypes
import numpy as np
from jax import lax
from jax.experimental import pallas as pl
from jax.experimental.pallas import tpu as pltpu
from jax.sharding import PartitionSpec as P

MIB = 1024 * 1024
BIG = 48 * MIB
WHOLE = pl.BlockSpec(memory_space=pltpu.VMEM)
IN_HBM = pl.BlockSpec(memory_space=pltpu.HBM)


def split_bf16(table):
    high = table.astype(ml_dtypes.bfloat16)
    low = (table - high.astype(np.float64)).astype(ml_dtypes.bfloat16)
    return high, low


def tables(width):
    freq = np.concatenate([np.arange(0, width, 2), np.arange(1, width, 2)])
    place = np.arange(width)
    steps = ((2 * freq[:, None] + 1) * place[None, :]) % (4 * width)
    angle = math.pi / (2 * width) * steps
    forward = np.concatenate([np.cos(angle), -np.sin(angle)], axis=0)
    inverse = forward.T / width
    return split_bf16(forward) + split_bf16(inverse)


def partner(step):
    return lax.axis_index("tok") ^ step


def send(block, step, count):
    return lax.ppermute(block, "tok", [(d, d ^ step) for d in range(count)])


def sending_order(count):
    half = count // 2
    far = list(range(half, count, 2)) + list(range(half + 1, count, 2))
    near = list(range(2, half)) + [1]
    order = []
    for at in range(half - 1):
        order += [far[at], near[at]]
    return order[:-1] + far[-1:] + order[-1:]


def columns_of(step, part):
    return pl.ds(pl.multiple_of(partner(step) * part, 128), part)


def piece(x, step, part):
    return lax.dynamic_slice_in_dim(x, partner(step) * part, part, axis=1)


def split_kernel(steps, part, filt_ref, *refs):
    outs, sems = refs[:-1], refs[-1]
    copies = []
    for at, k in enumerate(steps):
        copies.append(pltpu.make_async_copy(filt_ref.at[:, columns_of(k, part)], outs[at], sems.at[at]))
        copies[-1].start()
    for copy in copies:
        copy.wait()


def split(count, steps, filter_store):
    width, columns = filter_store.shape
    part = columns // count
    if part % 128:
        return {k: piece(filter_store, k, part) for k in steps}
    found = pl.pallas_call(
        functools.partial(split_kernel, steps, part),
        out_shape=[jax.ShapeDtypeStruct((width, part), jnp.bfloat16)] * len(steps),
        in_specs=[IN_HBM],
        out_specs=[WHOLE] * len(steps),
        scratch_shapes=[pltpu.SemaphoreType.DMA((len(steps),))],
        compiler_params=pltpu.CompilerParams(vmem_limit_bytes=16 * MIB),
        cost_estimate=pl.CostEstimate(flops=0, bytes_accessed=4 * width * columns, transcendentals=0),
    )(filter_store)
    return dict(zip(steps, found))


def gate_kernel(count, part, key_ref, value_ref, *refs):
    outs, (key_buf, value_buf, sems) = refs[:count], refs[count:]
    copies = []
    for k in range(count):
        cols = columns_of(k, part)
        copies.append(
            (
                pltpu.make_async_copy(key_ref.at[:, cols], key_buf.at[k], sems.at[0, k]),
                pltpu.make_async_copy(value_ref.at[:, cols], value_buf.at[k], sems.at[1, k]),
            )
        )
        for copy in copies[-1]:
            copy.start()
    for k in range(count):
        for copy in copies[k]:
            copy.wait()
        product = key_buf[k].astype(jnp.float32) * value_buf[k].astype(jnp.float32)
        outs[k][...] = product.astype(jnp.bfloat16)


def gate(count, key_in, value_in):
    width, columns = key_in.shape
    part = columns // count
    if part % 128:
        gated = (key_in.astype(jnp.float32) * value_in.astype(jnp.float32)).astype(jnp.bfloat16)
        return [piece(gated, k, part) for k in range(count)]
    block = pltpu.VMEM((count, width, part), jnp.bfloat16)
    return pl.pallas_call(
        functools.partial(gate_kernel, count, part),
        out_shape=[jax.ShapeDtypeStruct((width, part), jnp.bfloat16)] * count,
        in_specs=[IN_HBM] * 2,
        out_specs=[WHOLE] * count,
        scratch_shapes=[block, block, pltpu.SemaphoreType.DMA((2, count))],
        compiler_params=pltpu.CompilerParams(vmem_limit_bytes=16 * MIB),
        cost_estimate=pl.CostEstimate(flops=width * columns, bytes_accessed=6 * width * columns, transcendentals=0),
    )(key_in, value_in)


def dot(x, y):
    return jnp.dot(x, y, preferred_element_type=jnp.float32)


def transform(high, low, block):
    return dot(high, block) + dot(low, block)


def filter_kernel(steps, lag_ref, high_ref, low_ref, *refs):
    blocks, out = refs[:-1], refs[-1]
    count = len(steps)
    for at, (k, block) in enumerate(zip(steps, blocks)):
        out[at] = jnp.zeros(out.shape[1:], jnp.float32)
        out[count + lag_ref[partner(k)]] = transform(high_ref[...], low_ref[...], block[...])


def transform_cost(count, width, columns, passes):
    return pl.CostEstimate(
        flops=4 * passes * count * width * width * columns,
        bytes_accessed=10 * count * width * columns,
        transcendentals=0,
    )


def filter_spectra(lag_of_block, high, low, blocks):
    steps = list(blocks)
    count = len(steps)
    width, columns = blocks[0].shape
    return pl.pallas_call(
        functools.partial(filter_kernel, steps),
        out_shape=jax.ShapeDtypeStruct((2 * count, 2 * width, columns), jnp.float32),
        in_specs=[pl.BlockSpec(memory_space=pltpu.SMEM)] + [WHOLE] * (2 + count),
        out_specs=WHOLE,
        compiler_params=pltpu.CompilerParams(vmem_limit_bytes=16 * MIB),
        cost_estimate=transform_cost(count, width, columns, 2),
    )(lag_of_block, high, low, *[blocks[k] for k in steps])


def tiles(width, columns, tile):
    half = width // 16
    lane = min(128, columns)

    def run(row, sign):
        re_rows = pl.ds(pl.multiple_of(row * 8, 8), 8)
        im_rows = pl.ds(pl.multiple_of(row * 8 + width, 8), 8)
        for at in range(0, columns, lane):
            tile(re_rows, im_rows, pl.ds(at, lane), sign)

    @pl.loop(0, half)
    def _(row):
        run(row, 1)

    @pl.loop(half, 2 * half)
    def _(row):
        run(row, -1)


def early_kernel(count, steps, fh_ref, fl_ref, fs, *refs):
    blocks, (ss, gs) = refs[: len(steps)], refs[len(steps) :]
    width, columns = blocks[0].shape
    for k in range(count):
        if k not in steps:
            gs[partner(k)] = jnp.zeros(gs.shape[1:], jnp.float32)
    for k, block in zip(steps, blocks):
        gs[partner(k)] = transform(fh_ref[...], fl_ref[...], block[...])

    def tile(re_rows, im_rows, lanes, sign):
        f = [(fs[count + i, re_rows, lanes], fs[count + i, im_rows, lanes]) for i in range(count)]
        h, last = [], None
        for i in range(count):
            here = (gs[i, re_rows, lanes], gs[i, im_rows, lanes])
            if last is None:
                h.append(here)
            elif sign > 0:
                h.append((here[0] - last[1], here[1] + last[0]))
            else:
                h.append((here[0] + last[1], here[1] - last[0]))
            last = here
        for j in range(count):
            s_re = f[0][0] * h[j][0] - f[0][1] * h[j][1]
            s_im = f[0][0] * h[j][1] + f[0][1] * h[j][0]
            for i in range(1, j + 1):
                s_re = s_re + f[i][0] * h[j - i][0] - f[i][1] * h[j - i][1]
                s_im = s_im + f[i][0] * h[j - i][1] + f[i][1] * h[j - i][0]
            ss[j, re_rows, lanes] = s_re
            ss[j, im_rows, lanes] = s_im

    tiles(width, columns, tile)


def early_products(tabs, filt, blocks):
    steps = list(blocks)
    count = filt.shape[0] // 2
    width, columns = blocks[0].shape
    shape = (count, 2 * width, columns)
    return pl.pallas_call(
        functools.partial(early_kernel, count, steps),
        out_shape=jax.ShapeDtypeStruct(shape, jnp.float32),
        in_specs=[WHOLE] * (3 + len(steps)),
        out_specs=WHOLE,
        scratch_shapes=[pltpu.VMEM(shape, jnp.float32)],
        compiler_params=pltpu.CompilerParams(vmem_limit_bytes=16 * MIB),
        cost_estimate=transform_cost(count, width, columns, 4),
    )(*tabs[:2], filt, *[blocks[k] for k in steps])


def inverse(table_high, table_low, total):
    high = total.astype(jnp.bfloat16)
    low = (total - high.astype(jnp.float32)).astype(jnp.bfloat16)
    return (dot(table_high, high) + dot(table_high, low) + dot(table_low, high)).astype(jnp.bfloat16)


def late_kernel(count, steps, first, fh_ref, fl_ref, ih_ref, il_ref, fs, sums, *refs):
    blocks, ss, outs, gs = refs[: len(steps)], refs[len(steps)], refs[len(steps) + 1 : -1], refs[-1]
    width, columns = blocks[0].shape
    for at, block in enumerate(blocks):
        gs[at] = transform(fh_ref[...], fl_ref[...], block[...])
    starts = [count - partner(k) for k in steps]

    def tile(re_rows, im_rows, lanes, sign):
        g = [(gs[at, re_rows, lanes], gs[at, im_rows, lanes]) for at in range(len(steps))]
        last = None
        for j in range(count):
            d_re = d_im = None
            for start, (g_re, g_im) in zip(starts, g):
                f_re, f_im = fs[start + j, re_rows, lanes], fs[start + j, im_rows, lanes]
                p_re, p_im = f_re * g_re - f_im * g_im, f_re * g_im + f_im * g_re
                d_re, d_im = (p_re, p_im) if d_re is None else (d_re + p_re, d_im + p_im)
            s_re, s_im = ss[j, re_rows, lanes] + d_re, ss[j, im_rows, lanes] + d_im
            if last is not None and sign > 0:
                s_re, s_im = s_re - last[1], s_im + last[0]
            elif last is not None:
                s_re, s_im = s_re + last[1], s_im - last[0]
            ss[j, re_rows, lanes] = s_re
            ss[j, im_rows, lanes] = s_im
            last = (d_re, d_im)

    tiles(width, columns, tile)
    for k, out in zip(first, outs):
        out[...] = inverse(ih_ref[...], il_ref[...], ss[partner(k)])


def late_products(first, tabs, filt, sums, blocks):
    steps = list(blocks)
    count, twice, columns = sums.shape
    width = twice // 2
    found = pl.pallas_call(
        functools.partial(late_kernel, count, steps, first),
        out_shape=[jax.ShapeDtypeStruct(sums.shape, jnp.float32)]
        + [jax.ShapeDtypeStruct((width, columns), jnp.bfloat16)] * len(first),
        in_specs=[WHOLE] * (6 + len(steps)),
        out_specs=[WHOLE] * (1 + len(first)),
        scratch_shapes=[pltpu.VMEM((len(steps), twice, columns), jnp.float32)],
        input_output_aliases={5: 0},
        compiler_params=pltpu.CompilerParams(vmem_limit_bytes=16 * MIB),
        cost_estimate=transform_cost(count, width, columns, 3),
    )(*tabs, filt, sums, *[blocks[k] for k in steps])
    return found[0], dict(zip(first, found[1:]))


def inverse_kernel(steps, ih_ref, il_ref, ss, *outs):
    for k, out in zip(steps, outs):
        out[...] = inverse(ih_ref[...], il_ref[...], ss[partner(k)])


def inverses(steps, tabs, sums):
    count, twice, columns = sums.shape
    width = twice // 2
    found = pl.pallas_call(
        functools.partial(inverse_kernel, steps),
        out_shape=[jax.ShapeDtypeStruct((width, columns), jnp.bfloat16)] * len(steps),
        in_specs=[WHOLE] * 3,
        out_specs=[WHOLE] * len(steps),
        compiler_params=pltpu.CompilerParams(vmem_limit_bytes=16 * MIB),
        cost_estimate=transform_cost(len(steps), width, columns, 3),
    )(*tabs[2:], sums)
    return dict(zip(steps, found))


def pre_kernel(steps, before, after, query_ref, skip_ref, *refs):
    count = len(steps)
    refs = list(refs)
    total = jnp.zeros((query_ref.shape[0], 128), jnp.float32)
    if before:
        refs.pop(0)
        total = refs.pop(0)[...]
    convs, gates, (pre_ref, square_ref) = refs[:count], refs[count : 2 * count], refs[2 * count :]
    width, part = convs[0].shape
    for at_k, k in enumerate(steps):
        start = partner(k) * part if part < query_ref.shape[1] else 0
        for at in range(0, part, 128):
            lanes, cols = pl.ds(at, 128), pl.ds(pl.multiple_of(start + at, 128), 128)
            gated = gates[at_k][:, lanes].astype(jnp.float32)
            conv = convs[at_k][:, lanes].astype(jnp.float32)
            pre = query_ref[:, cols].astype(jnp.float32) * (conv + skip_ref[:, cols] * gated)
            pre_ref[:, cols] = pre
            total = total + pre * pre
    if after:
        square_ref[...] = total
    else:
        square_ref[...] = jnp.sum(total.T, axis=0, keepdims=True)


def together(blocks):
    count, width = len(blocks), blocks[0].shape[0]
    order = jnp.arange(count, dtype=jnp.int32) ^ lax.axis_index("tok")
    stacked = jnp.take(jnp.stack([blocks[k] for k in range(count)]), order, axis=0)
    return {0: stacked.transpose(1, 0, 2).reshape(width, -1)}


def gated_output(query, skip, early, convs, gates):
    width, columns = query.shape
    groups = [early, [k for k in convs if k not in early]]
    if convs[0].shape[1] % 128:
        convs, gates, groups = together(convs), together(gates), [[0]]
    found = []
    for at, steps in enumerate(groups):
        rest = at + 1 < len(groups)
        found = pl.pallas_call(
            functools.partial(pre_kernel, steps, at > 0, rest),
            out_shape=(
                jax.ShapeDtypeStruct((width, columns), jnp.float32),
                jax.ShapeDtypeStruct((width, 128) if rest else (1, width), jnp.float32),
            ),
            in_specs=[WHOLE] * (2 + len(found) + 2 * len(steps)),
            out_specs=(WHOLE, WHOLE),
            input_output_aliases={2: 0} if found else {},
            compiler_params=pltpu.CompilerParams(vmem_limit_bytes=16 * MIB),
            cost_estimate=pl.CostEstimate(
                flops=3 * width * columns, bytes_accessed=5 * width * columns, transcendentals=0
            ),
        )(query, skip, *found, *[convs[k] for k in steps], *[gates[k] for k in steps])
    return found


def scale_kernel(channels, steps, pre_ref, gain_ref, *refs):
    squares, (out_ref, buf, sems) = refs[:-3], refs[-3:]
    width = pre_ref.shape[0]
    rows = width // steps
    total = squares[0][...]
    for square in squares[1:]:
        total = total + square[...]
    scale = lax.rsqrt(total * (1.0 / channels) + 1e-06)
    scale = jnp.broadcast_to(scale, (128, width)).T
    copies = []
    for s in range(steps):
        for at in range(0, pre_ref.shape[1], 128):
            cols = pl.ds(at, 128)
            here = scale[s * rows : (s + 1) * rows, :]
            buf[pl.ds(s * rows, rows), cols] = gain_ref[:, cols] * pre_ref[pl.ds(s * rows, rows), cols] * here
        window = pl.ds(s * rows, rows)
        copies.append(pltpu.make_async_copy(buf.at[window, :], out_ref.at[window, :], sems.at[s]))
        copies[-1].start()
    for copy in copies:
        copy.wait()


def scaled(channels, pre, squares, out_gain):
    width, columns = pre.shape
    steps = 8
    return pl.pallas_call(
        functools.partial(scale_kernel, channels, steps),
        out_shape=jax.ShapeDtypeStruct((width, columns), jnp.float32),
        in_specs=[WHOLE] * (2 + len(squares)),
        out_specs=IN_HBM,
        scratch_shapes=[pltpu.VMEM((width, columns), jnp.float32), pltpu.SemaphoreType.DMA((steps,))],
        compiler_params=pltpu.CompilerParams(vmem_limit_bytes=16 * MIB),
        cost_estimate=pl.CostEstimate(flops=2 * width * columns, bytes_accessed=8 * width * columns, transcendentals=0),
    )(pre, out_gain, *squares)


def local(query, key_in, value_in, filter_store, lag_of_block, skip, out_gain):
    width, columns = query.shape
    count = lax.axis_size("tok")
    tabs = [jnp.asarray(t) for t in tables(width)]
    part = columns // count
    order = sending_order(count)
    gated_order = order[:-3] + order[-1:] + order[-3:-1]
    own = split(count, order[1:] + [0], filter_store)
    own[order[0]] = piece(filter_store, order[0], part)
    own[0], key_in, value_in = lax.optimization_barrier((own[0], key_in, value_in))
    mine = gate(count, key_in, value_in)
    filts = {k: send(own[k], k, count) for k in order}
    gates = {k: send(mine[k], k, count) for k in gated_order}
    filts[0], gates[0] = own[0], mine[0]
    late = gated_order[-2:]
    filt = filter_spectra(lag_of_block, *tabs[:2], filts)
    sums = early_products(tabs, filt, {k: gates[k] for k in gates if k not in late})
    sums, found = late_products(order[:1], tabs, filt, sums, {k: gates[k] for k in late})
    found.update(inverses(order[1:] + [0], tabs, sums))
    convs = {k: send(found[k], k, count) for k in order}
    convs[0] = found[0]
    pre, square = gated_output(query, skip[None, :], order[: count // 2] + [0], convs, mine)
    others = lax.axis_size("chan")
    squares = [square] + [
        lax.ppermute(square, "chan", [(d, d ^ step) for d in range(others)]) for step in reversed(range(1, others))
    ]
    return scaled(columns * others, pre, squares, out_gain[None, :])


def solution(mesh):
    in_specs = (
        P("tok", "chan"),
        P("tok", "chan"),
        P("tok", "chan"),
        P("tok", "chan"),
        P(),
        P("chan"),
        P("chan"),
    )
    return jax.shard_map(local, mesh=mesh, in_specs=in_specs, out_specs=P("tok", "chan"), check_vma=False)
```

time: 93.2 us -> 89.2 us (0.957)
  waiting for transfers between devices: 43.8 us -> 23.4 us
  starting transfers between devices: 29.8 us -> 43.4 us
  Pallas kernels: 12.6 us -> 14.8 us
    ppermute x18 -> x21, waiting for transfers between devices: 41.1 us -> 20.6 us  [send(): return lax.ppermute(block, 'tok', [(d, d ^ step) for d in range(count)])]
    ppermute x18 -> x21, starting transfers between devices: 27.9 us -> 41.5 us  [send(): return lax.ppermute(block, 'tok', [(d, d ^ step) for d in range(count)])]
    pallas_call x5 -> x7, Pallas kernels: 9.46 us -> 11.7 us  [the longest x1 3.97 us: late_products(): pl.pallas_call(functools.partial(late_kernel, count, steps, first), out_s...]
    unnamed x26 -> x22, local copies, waits for them, and re-layouts: 5.61 us -> 6.26 us
  transfers between devices with their start and end apart: 21 -> 24, of which waited for: 11 -> 9; matrix products, arithmetic and copies ran while one was open for 0% -> 0% of each run, Pallas kernels for 7% -> 10%
where the time goes in v10:
time: 89.2 us; the launch traced here: 88.9 us
  starting transfers between devices  43.4 us (49%)
  waiting for transfers between devices  23.4 us (26%)
  Pallas kernels  14.8 us (17%)
  local copies, waits for them, and re-layouts  7.17 us (8%)
    ppermute x21, starting transfers between devices, send(): return lax.ppermute(block, 'tok', [(d, d ^ step) for d in range(count)])  41.5 us
    ppermute x21, waiting for transfers between devices, send(): return lax.ppermute(block, 'tok', [(d, d ^ step) for d in range(count)])  20.6 us
    unnamed x22, local copies, waits for them, and re-layouts  6.26 us
    pallas_call x1, Pallas kernels, late_products(): pl.pallas_call(functools.partial(late_kernel, count, steps, first), out_s...  3.97 us
    pallas_call x1, Pallas kernels, early_products(): pl.pallas_call(functools.partial(early_kernel, count, steps), out_shape=j...  3.88 us
    ppermute x3, waiting for transfers between devices, local(): lax.ppermute(square, 'chan', [(d, d ^ step) for d in range(others)])  2.71 us
    pallas_call x1, Pallas kernels, filter_spectra(): pl.pallas_call(functools.partial(filter_kernel, steps), out_shape=jax.Sha...  2.09 us
    ppermute x3, starting transfers between devices, local(): lax.ppermute(square, 'chan', [(d, d ^ step) for d in range(others)])  1.94 us
  transfers between devices with their start and end apart: 24, of which 9 were waited for; matrix products, arithmetic and copies ran while one was open for 0% of the time, Pallas kernels for 10%

profile of v10, /device:TPU:0, one launch (start us, length us, event | category | flops | bytes accessed | tf_op | source)
XLA Modules:
  0.0 88.9 jit_solution(9464875422260270478)
XLA Ops:
  0.9 4.1 %collective-permute-start = (bf16[256,256]{1,0:T(8,128)(2,1)S(1)}, bf16[256,256]{1,0:T(8,128)(2,1)S(1)}, u32[]{:S(2)}, u32[]{:S(2)}) collective-permute-start(bf16[256,256]{1,0:T(8,128)(2,1)S(1)} %constant_dynamic-slice_fusion), channel_id=1, source_target_pairs={{0,16},{4,20},{8,24},{12,28},{16,0},{20,4},{24,8},{28,12},{1,17},{... | collective-permute-start | bytes 393224 | tf_op jit(solution)/shard_map/ppermute | solution.py:40
  6.5 1.6 %collective-permute-start.1 = (bf16[256,256]{1,0:T(8,128)(2,1)S(1)}, bf16[256,256]{1,0:T(8,128)(2,1)S(1)}, u32[]{:S(2)}, u32[]{:S(2)}) collective-permute-start(bf16[256,256]{1,0:T(8,128)(2,1)S(1)} %get-tuple-element.36), channel_id=1, source_target_pairs={{0,8},{4,12},{8,0},{12,4},{16,24},{20,28},{24,16},{28,20},{1,9},{5... | collective-permute-start | bytes 393224 | tf_op jit(solution)/shard_map/ppermute | solution.py:40
  8.1 1.8 %collective-permute-start.3 = (bf16[256,256]{1,0:T(8,128)(2,1)S(1)}, bf16[256,256]{1,0:T(8,128)(2,1)S(1)}, u32[]{:S(2)}, u32[]{:S(2)}) collective-permute-start(bf16[256,256]{1,0:T(8,128)(2,1)S(1)} %get-tuple-element.38), channel_id=1, source_target_pairs={{0,12},{4,8},{8,4},{12,0},{16,28},{20,24},{24,20},{28,16},{1,13},{... | collective-permute-start | bytes 393224 | tf_op jit(solution)/shard_map/ppermute | solution.py:40
  9.9 3.5 %collective-permute-start.4 = (bf16[256,256]{1,0:T(8,128)(2,1)S(1)}, bf16[256,256]{1,0:T(8,128)(2,1)S(1)}, u32[]{:S(2)}, u32[]{:S(2)}) collective-permute-start(bf16[256,256]{1,0:T(8,128)(2,1)S(1)} %get-tuple-element.39), channel_id=1, source_target_pairs={{0,20},{4,16},{8,28},{12,24},{16,4},{20,0},{24,12},{28,8},{1,21},{... | collective-permute-start | bytes 393224 | tf_op jit(solution)/shard_map/ppermute | solution.py:40
  13.4 4.0 %collective-permute-start.5 = (bf16[256,256]{1,0:T(8,128)(2,1)S(1)}, bf16[256,256]{1,0:T(8,128)(2,1)S(1)}, u32[]{:S(2)}, u32[]{:S(2)}) collective-permute-start(bf16[256,256]{1,0:T(8,128)(2,1)S(1)} %get-tuple-element.40), channel_id=1, source_target_pairs={{0,28},{4,24},{8,20},{12,16},{16,12},{20,8},{24,4},{28,0},{1,29},{... | collective-permute-start | bytes 393224 | tf_op jit(solution)/shard_map/ppermute | solution.py:40
  17.4 1.5 %collective-permute-start.6 = (bf16[256,256]{1,0:T(8,128)(2,1)S(1)}, bf16[256,256]{1,0:T(8,128)(2,1)S(1)}, u32[]{:S(2)}, u32[]{:S(2)}) collective-permute-start(bf16[256,256]{1,0:T(8,128)(2,1)S(1)} %get-tuple-element.41), channel_id=1, source_target_pairs={{0,4},{4,0},{8,12},{12,8},{16,20},{20,16},{24,28},{28,24},{1,5},{5... | collective-permute-start | bytes 393224 | tf_op jit(solution)/shard_map/ppermute | solution.py:40
  22.1 4.6 %collective-permute-start.7 = (bf16[256,256]{1,0:T(8,128)(2,1)S(1)}, bf16[256,256]{1,0:T(8,128)(2,1)S(1)}, u32[]{:S(2)}, u32[]{:S(2)}) collective-permute-start(bf16[256,256]{1,0:T(8,128)(2,1)S(1)} %get-tuple-element.46.refs_5_), channel_id=1, source_target_pairs={{0,16},{4,20},{8,24},{12,28},{16,0},{20,4},{24,8},{28,12},{1,17},{... | collective-permute-start | bytes 393224 | tf_op jit(solution)/shard_map/ppermute | solution.py:40
  26.7 3.5 %collective-permute-done.4.refs_4_ = bf16[256,256]{1,0:T(8,128)(2,1)S(1)} collective-permute-done((bf16[256,256]{1,0:T(8,128)(2,1)S(1)}, bf16[256,256]{1,0:T(8,128)(2,1)S(1)}, u32[]{:S(2)}, u32[]{:S(2)}) %collective-permute-start.4) | collective-permute-done | bytes 131104 | tf_op jit(solution)/shard_map/ppermute | solution.py:40
  31.4 1.9 %collective-permute-start.10 = (bf16[256,256]{1,0:T(8,128)(2,1)S(1)}, bf16[256,256]{1,0:T(8,128)(2,1)S(1)}, u32[]{:S(2)}, u32[]{:S(2)}) collective-permute-start(bf16[256,256]{1,0:T(8,128)(2,1)S(1)} %get-tuple-element.49.refs_8_), channel_id=1, source_target_pairs={{0,12},{4,8},{8,4},{12,0},{16,28},{20,24},{24,20},{28,16},{1,13},{... | collective-permute-start | bytes 393224 | tf_op jit(solution)/shard_map/ppermute | solution.py:40
  33.3 3.2 %collective-permute-start.11 = (bf16[256,256]{1,0:T(8,128)(2,1)S(1)}, bf16[256,256]{1,0:T(8,128)(2,1)S(1)}, u32[]{:S(2)}, u32[]{:S(2)}) collective-permute-start(bf16[256,256]{1,0:T(8,128)(2,1)S(1)} %get-tuple-element.50.refs_7_), channel_id=1, source_target_pairs={{0,4},{4,0},{8,12},{12,8},{16,20},{20,16},{24,28},{28,24},{1,5},{5... | collective-permute-start | bytes 393224 | tf_op jit(solution)/shard_map/ppermute | solution.py:40
  39.0 2.1 %shard_map.110.fs = f32[16,512,256]{2,1,0:T(8,128)S(1)} custom-call(s32[8]{0:T(128)S(1)} %copy-done.10, bf16[512,256]{1,0:T(8,128)(2,1)S(1)} %copy-done.2, bf16[512,256]{1,0:T(8,128)(2,1)S(1)} %copy-done.1, bf16[256,256]{1,0:T(8,128)(2,1)S(1)} %collective-permute-done.refs_0_, bf16[256,256]{1,0:T(8,128)(2,1)S(1)} %collective-permute-done.1.refs_1_, ...), custom_call_target="tpu_custom_call" | custom-call | flops 1073741824 | bytes 5242880 | tf_op jit(solution)/shard_map/pallas_call | solution.py:154
  41.2 1.8 %collective-permute-start.13 = (bf16[256,256]{1,0:T(8,128)(2,1)S(1)}, bf16[256,256]{1,0:T(8,128)(2,1)S(1)}, u32[]{:S(2)}, u32[]{:S(2)}) collective-permute-start(bf16[256,256]{1,0:T(8,128)(2,1)S(1)} %get-tuple-element.53.refs_6_), channel_id=1, source_target_pairs={{0,28},{4,24},{8,20},{12,16},{16,12},{20,8},{24,4},{28,0},{1,29},{... | collective-permute-start | bytes 393224 | tf_op jit(solution)/shard_map/ppermute | solution.py:40
  43.1 3.9 %shard_map.112.sums = f32[8,512,256]{2,1,0:T(8,128)S(1)} custom-call(bf16[512,256]{1,0:T(8,128)(2,1)S(1)} %copy-done.2, bf16[512,256]{1,0:T(8,128)(2,1)S(1)} %copy-done.1, f32[16,512,256]{2,1,0:T(8,128)S(1)} %shard_map.110.fs, bf16[256,256]{1,0:T(8,128)(2,1)S(1)} %collective-permute-done.7.refs_0_, bf16[256,256]{1,0:T(8,128)(2,1)S(1)} %collective-permute-done.8.refs_1_, ...), custom_call_target="tpu_custom_call" | custom-call | flops 2147483648 | bytes 5242880 | tf_op jit(solution)/shard_map/pallas_call | solution.py:221
  46.9 4.7 %collective-permute-done.12.refs_0_ = bf16[256,256]{1,0:T(8,128)(2,1)S(1)} collective-permute-done((bf16[256,256]{1,0:T(8,128)(2,1)S(1)}, bf16[256,256]{1,0:T(8,128)(2,1)S(1)}, u32[]{:S(2)}, u32[]{:S(2)}) %collective-permute-start.12) | collective-permute-done | bytes 131104 | tf_op jit(solution)/shard_map/ppermute | solution.py:40
  51.6 4.0 %shard_map.113 = (f32[8,512,256]{2,1,0:T(8,128)S(1)}, bf16[256,256]{1,0:T(8,128)(2,1)S(1)}) custom-call(bf16[512,256]{1,0:T(8,128)(2,1)S(1)} %copy-done.2, bf16[512,256]{1,0:T(8,128)(2,1)S(1)} %copy-done.1, bf16[256,512]{1,0:T(8,128)(2,1)S(1)} %copy-done.7, bf16[256,512]{1,0:T(8,128)(2,1)S(1)} %copy-done.6, ...), custom_call_target="tpu_custom_call", output_to_operand_aliasing={{0}: (5, {})} | custom-call | flops 1610612736 | bytes 5242880 | tf_op jit(solution)/shard_map/pallas_call | solution.py:272
  55.6 3.7 %collective-permute-start.14 = (bf16[256,256]{1,0:T(8,128)(2,1)S(1)}, bf16[256,256]{1,0:T(8,128)(2,1)S(1)}, u32[]{:S(2)}, u32[]{:S(2)}) collective-permute-start(bf16[256,256]{1,0:T(8,128)(2,1)S(1)} %get-tuple-element.54), channel_id=1, source_target_pairs={{0,16},{4,20},{8,24},{12,28},{16,0},{20,4},{24,8},{28,12},{1,17},{... | collective-permute-start | bytes 393224 | tf_op jit(solution)/shard_map/ppermute | solution.py:40
  59.3 1.6 %shard_map.114 = (bf16[256,256]{1,0:T(8,128)(2,1)S(1)}, bf16[256,256]{1,0:T(8,128)(2,1)S(1)}, bf16[256,256]{1,0:T(8,128)(2,1)S(1)}, bf16[256,256]{1,0:T(8,128)(2...) custom-call(bf16[256,512]{1,0:T(8,128)(2,1)S(1)} %copy-done.7, ...), custom_call_target="tpu_custom_call" | custom-call | flops 1409286144 | bytes 4587520 | tf_op jit(solution)/shard_map/pallas_call | solution.py:294
  64.0 2.4 %collective-permute-start.18 = (bf16[256,256]{1,0:T(8,128)(2,1)S(1)}, bf16[256,256]{1,0:T(8,128)(2,1)S(1)}, u32[]{:S(2)}, u32[]{:S(2)}) collective-permute-start(bf16[256,256]{1,0:T(8,128)(2,1)S(1)} %get-tuple-element.62), channel_id=1, source_target_pairs={{0,20},{4,16},{8,28},{12,24},{16,4},{20,0},{24,12},{28,8},{1,21},{... | collective-permute-start | bytes 393224 | tf_op jit(solution)/shard_map/ppermute | solution.py:40
  66.7 2.0 %collective-permute-start.19 = (bf16[256,256]{1,0:T(8,128)(2,1)S(1)}, bf16[256,256]{1,0:T(8,128)(2,1)S(1)}, u32[]{:S(2)}, u32[]{:S(2)}) collective-permute-start(bf16[256,256]{1,0:T(8,128)(2,1)S(1)} %get-tuple-element.63), channel_id=1, source_target_pairs={{0,28},{4,24},{8,20},{12,16},{16,12},{20,8},{24,4},{28,0},{1,29},{... | collective-permute-start | bytes 393224 | tf_op jit(solution)/shard_map/ppermute | solution.py:40
  68.7 2.9 %collective-permute-done.15.refs_1_ = bf16[256,256]{1,0:T(8,128)(2,1)S(1)} collective-permute-done((bf16[256,256]{1,0:T(8,128)(2,1)S(1)}, bf16[256,256]{1,0:T(8,128)(2,1)S(1)}, u32[]{:S(2)}, u32[]{:S(2)}) %collective-permute-start.15) | collective-permute-done | bytes 131104 | tf_op jit(solution)/shard_map/ppermute | solution.py:40
  72.8 3.4 %collective-permute-done.17.refs_3_ = bf16[256,256]{1,0:T(8,128)(2,1)S(1)} collective-permute-done((bf16[256,256]{1,0:T(8,128)(2,1)S(1)}, bf16[256,256]{1,0:T(8,128)(2,1)S(1)}, u32[]{:S(2)}, u32[]{:S(2)}) %collective-permute-start.17) | collective-permute-done | bytes 131104 | tf_op jit(solution)/shard_map/ppermute | solution.py:40
  76.6 4.4 %collective-permute-done.18.refs_2_ = bf16[256,256]{1,0:T(8,128)(2,1)S(1)} collective-permute-done((bf16[256,256]{1,0:T(8,128)(2,1)S(1)}, bf16[256,256]{1,0:T(8,128)(2,1)S(1)}, u32[]{:S(2)}, u32[]{:S(2)}) %collective-permute-start.18) | collective-permute-done | bytes 131104 | tf_op jit(solution)/shard_map/ppermute | solution.py:40
  82.8 1.6 %collective-permute-start.22 = (f32[1,256]{1,0:T(1,128)S(1)}, f32[1,256]{1,0:T(1,128)S(1)}, u32[]{:S(2)}, u32[]{:S(2)}) collective-permute-start(f32[1,256]{1,0:T(1,128)S(1)} %get-tuple-element.66.refs_0_), channel_id=1, source_target_pairs={{0,2},{1,3},{2,0},{3,1},{4,6},{5,7},{6,4},{7,5},{8,10},{9,11},{10,... | collective-permute-start | bytes 3080 | tf_op jit(solution)/shard_map/ppermute | solution.py:421
  84.7 1.8 %collective-permute-done.22.refs_2_ = f32[1,256]{1,0:T(1,128)S(1)} collective-permute-done((f32[1,256]{1,0:T(1,128)S(1)}, f32[1,256]{1,0:T(1,128)S(1)}, u32[]{:S(2)}, u32[]{:S(2)}) %collective-permute-start.22) | collective-permute-done | bytes 1056 | tf_op jit(solution)/shard_map/ppermute | solution.py:421
  (56 shorter events, 18.9 us)
Async XLA Ops:
  0.9 12.5 %collective-permute-start = (bf16[256,256]{1,0:T(8,128)(2,1)S(1)}, bf16[256,256]{1,0:T(8,128)(2,1)S(1)}, u32[]{:S(2)}, u32[]{:S(2)}) collective-permute-start(bf16[256,256]{1,0:T(8,128)(2,1)S(1)} %constant_dynamic-slice_fusion), channel_id=1, source_target_pairs={{0,16},{4,20},{8,24},{12,28},{16,0},{20,4},{24,8},{28,12},{1,17},{... | collective-permute-start | bytes 393224 | tf_op jit(solution)/shard_map/ppermute | solution.py:40
  6.5 10.9 %collective-permute-start.1 = (bf16[256,256]{1,0:T(8,128)(2,1)S(1)}, bf16[256,256]{1,0:T(8,128)(2,1)S(1)}, u32[]{:S(2)}, u32[]{:S(2)}) collective-permute-start(bf16[256,256]{1,0:T(8,128)(2,1)S(1)} %get-tuple-element.36), channel_id=1, source_target_pairs={{0,8},{4,12},{8,0},{12,4},{16,24},{20,28},{24,16},{28,20},{1,9},{5... | collective-permute-start | bytes 393224 | tf_op jit(solution)/shard_map/ppermute | solution.py:40
  8.1 14.0 %collective-permute-start.2 = (bf16[256,256]{1,0:T(8,128)(2,1)S(1)}, bf16[256,256]{1,0:T(8,128)(2,1)S(1)}, u32[]{:S(2)}, u32[]{:S(2)}) collective-permute-start(bf16[256,256]{1,0:T(8,128)(2,1)S(1)} %get-tuple-element.37), channel_id=1, source_target_pairs={{0,24},{4,28},{8,16},{12,20},{16,8},{20,12},{24,0},{28,4},{1,25},{... | collective-permute-start | bytes 393224 | tf_op jit(solution)/shard_map/ppermute | solution.py:40
  8.1 18.6 %collective-permute-start.3 = (bf16[256,256]{1,0:T(8,128)(2,1)S(1)}, bf16[256,256]{1,0:T(8,128)(2,1)S(1)}, u32[]{:S(2)}, u32[]{:S(2)}) collective-permute-start(bf16[256,256]{1,0:T(8,128)(2,1)S(1)} %get-tuple-element.38), channel_id=1, source_target_pairs={{0,12},{4,8},{8,4},{12,0},{16,28},{20,24},{24,20},{28,16},{1,13},{... | collective-permute-start | bytes 393224 | tf_op jit(solution)/shard_map/ppermute | solution.py:40
  9.9 20.3 %collective-permute-start.4 = (bf16[256,256]{1,0:T(8,128)(2,1)S(1)}, bf16[256,256]{1,0:T(8,128)(2,1)S(1)}, u32[]{:S(2)}, u32[]{:S(2)}) collective-permute-start(bf16[256,256]{1,0:T(8,128)(2,1)S(1)} %get-tuple-element.39), channel_id=1, source_target_pairs={{0,20},{4,16},{8,28},{12,24},{16,4},{20,0},{24,12},{28,8},{1,21},{... | collective-permute-start | bytes 393224 | tf_op jit(solution)/shard_map/ppermute | solution.py:40
  13.4 18.0 %collective-permute-start.5 = (bf16[256,256]{1,0:T(8,128)(2,1)S(1)}, bf16[256,256]{1,0:T(8,128)(2,1)S(1)}, u32[]{:S(2)}, u32[]{:S(2)}) collective-permute-start(bf16[256,256]{1,0:T(8,128)(2,1)S(1)} %get-tuple-element.40), channel_id=1, source_target_pairs={{0,28},{4,24},{8,20},{12,16},{16,12},{20,8},{24,4},{28,0},{1,29},{... | collective-permute-start | bytes 393224 | tf_op jit(solution)/shard_map/ppermute | solution.py:40
  17.4 15.9 %collective-permute-start.6 = (bf16[256,256]{1,0:T(8,128)(2,1)S(1)}, bf16[256,256]{1,0:T(8,128)(2,1)S(1)}, u32[]{:S(2)}, u32[]{:S(2)}) collective-permute-start(bf16[256,256]{1,0:T(8,128)(2,1)S(1)} %get-tuple-element.41), channel_id=1, source_target_pairs={{0,4},{4,0},{8,12},{12,8},{16,20},{20,16},{24,28},{28,24},{1,5},{5... | collective-permute-start | bytes 393224 | tf_op jit(solution)/shard_map/ppermute | solution.py:40
  22.1 19.0 %collective-permute-start.7 = (bf16[256,256]{1,0:T(8,128)(2,1)S(1)}, bf16[256,256]{1,0:T(8,128)(2,1)S(1)}, u32[]{:S(2)}, u32[]{:S(2)}) collective-permute-start(bf16[256,256]{1,0:T(8,128)(2,1)S(1)} %get-tuple-element.46.refs_5_), channel_id=1, source_target_pairs={{0,16},{4,20},{8,24},{12,28},{16,0},{20,4},{24,8},{28,12},{1,17},{... | collective-permute-start | bytes 393224 | tf_op jit(solution)/shard_map/ppermute | solution.py:40
  26.7 14.5 %collective-permute-start.8 = (bf16[256,256]{1,0:T(8,128)(2,1)S(1)}, bf16[256,256]{1,0:T(8,128)(2,1)S(1)}, u32[]{:S(2)}, u32[]{:S(2)}) collective-permute-start(bf16[256,256]{1,0:T(8,128)(2,1)S(1)} %get-tuple-element.47.refs_6_), channel_id=1, source_target_pairs={{0,8},{4,12},{8,0},{12,4},{16,24},{20,28},{24,16},{28,20},{1,9},{5... | collective-permute-start | bytes 393224 | tf_op jit(solution)/shard_map/ppermute | solution.py:40
  30.2 12.8 %collective-permute-start.9 = (bf16[256,256]{1,0:T(8,128)(2,1)S(1)}, bf16[256,256]{1,0:T(8,128)(2,1)S(1)}, u32[]{:S(2)}, u32[]{:S(2)}) collective-permute-start(bf16[256,256]{1,0:T(8,128)(2,1)S(1)} %get-tuple-element.48.refs_7_), channel_id=1, source_target_pairs={{0,24},{4,28},{8,16},{12,20},{16,8},{20,12},{24,0},{28,4},{1,25},{... | collective-permute-start | bytes 393224 | tf_op jit(solution)/shard_map/ppermute | solution.py:40
  31.4 11.7 %collective-permute-start.10 = (bf16[256,256]{1,0:T(8,128)(2,1)S(1)}, bf16[256,256]{1,0:T(8,128)(2,1)S(1)}, u32[]{:S(2)}, u32[]{:S(2)}) collective-permute-start(bf16[256,256]{1,0:T(8,128)(2,1)S(1)} %get-tuple-element.49.refs_8_), channel_id=1, source_target_pairs={{0,12},{4,8},{8,4},{12,0},{16,28},{20,24},{24,20},{28,16},{1,13},{... | collective-permute-start | bytes 393224 | tf_op jit(solution)/shard_map/ppermute | solution.py:40
  33.3 9.8 %collective-permute-start.11 = (bf16[256,256]{1,0:T(8,128)(2,1)S(1)}, bf16[256,256]{1,0:T(8,128)(2,1)S(1)}, u32[]{:S(2)}, u32[]{:S(2)}) collective-permute-start(bf16[256,256]{1,0:T(8,128)(2,1)S(1)} %get-tuple-element.50.refs_7_), channel_id=1, source_target_pairs={{0,4},{4,0},{8,12},{12,8},{16,20},{20,16},{24,28},{28,24},{1,5},{5... | collective-permute-start | bytes 393224 | tf_op jit(solution)/shard_map/ppermute | solution.py:40
  41.1 10.5 %collective-permute-start.12 = (bf16[256,256]{1,0:T(8,128)(2,1)S(1)}, bf16[256,256]{1,0:T(8,128)(2,1)S(1)}, u32[]{:S(2)}, u32[]{:S(2)}) collective-permute-start(bf16[256,256]{1,0:T(8,128)(2,1)S(1)} %get-tuple-element.52.refs_5_), channel_id=1, source_target_pairs={{0,20},{4,16},{8,28},{12,24},{16,4},{20,0},{24,12},{28,8},{1,21},{... | collective-permute-start | bytes 393224 | tf_op jit(solution)/shard_map/ppermute | solution.py:40
  41.2 10.4 %collective-permute-start.13 = (bf16[256,256]{1,0:T(8,128)(2,1)S(1)}, bf16[256,256]{1,0:T(8,128)(2,1)S(1)}, u32[]{:S(2)}, u32[]{:S(2)}) collective-permute-start(bf16[256,256]{1,0:T(8,128)(2,1)S(1)} %get-tuple-element.53.refs_6_), channel_id=1, source_target_pairs={{0,28},{4,24},{8,20},{12,16},{16,12},{20,8},{24,4},{28,0},{1,29},{... | collective-permute-start | bytes 393224 | tf_op jit(solution)/shard_map/ppermute | solution.py:40
  55.6 11.1 %collective-permute-start.14 = (bf16[256,256]{1,0:T(8,128)(2,1)S(1)}, bf16[256,256]{1,0:T(8,128)(2,1)S(1)}, u32[]{:S(2)}, u32[]{:S(2)}) collective-permute-start(bf16[256,256]{1,0:T(8,128)(2,1)S(1)} %get-tuple-element.54), channel_id=1, source_target_pairs={{0,16},{4,20},{8,24},{12,28},{16,0},{20,4},{24,8},{28,12},{1,17},{... | collective-permute-start | bytes 393224 | tf_op jit(solution)/shard_map/ppermute | solution.py:40
  60.9 10.7 %collective-permute-start.15 = (bf16[256,256]{1,0:T(8,128)(2,1)S(1)}, bf16[256,256]{1,0:T(8,128)(2,1)S(1)}, u32[]{:S(2)}, u32[]{:S(2)}) collective-permute-start(bf16[256,256]{1,0:T(8,128)(2,1)S(1)} %get-tuple-element.56), channel_id=1, source_target_pairs={{0,8},{4,12},{8,0},{12,4},{16,24},{20,28},{24,16},{28,20},{1,9},{5... | collective-permute-start | bytes 393224 | tf_op jit(solution)/shard_map/ppermute | solution.py:40
  61.0 11.8 %collective-permute-start.16 = (bf16[256,256]{1,0:T(8,128)(2,1)S(1)}, bf16[256,256]{1,0:T(8,128)(2,1)S(1)}, u32[]{:S(2)}, u32[]{:S(2)}) collective-permute-start(bf16[256,256]{1,0:T(8,128)(2,1)S(1)} %get-tuple-element.57), channel_id=1, source_target_pairs={{0,24},{4,28},{8,16},{12,20},{16,8},{20,12},{24,0},{28,4},{1,25},{... | collective-permute-start | bytes 393224 | tf_op jit(solution)/shard_map/ppermute | solution.py:40
  62.5 13.7 %collective-permute-start.17 = (bf16[256,256]{1,0:T(8,128)(2,1)S(1)}, bf16[256,256]{1,0:T(8,128)(2,1)S(1)}, u32[]{:S(2)}, u32[]{:S(2)}) collective-permute-start(bf16[256,256]{1,0:T(8,128)(2,1)S(1)} %get-tuple-element.58), channel_id=1, source_target_pairs={{0,12},{4,8},{8,4},{12,0},{16,28},{20,24},{24,20},{28,16},{1,13},{... | collective-permute-start | bytes 393224 | tf_op jit(solution)/shard_map/ppermute | solution.py:40
  64.0 17.0 %collective-permute-start.18 = (bf16[256,256]{1,0:T(8,128)(2,1)S(1)}, bf16[256,256]{1,0:T(8,128)(2,1)S(1)}, u32[]{:S(2)}, u32[]{:S(2)}) collective-permute-start(bf16[256,256]{1,0:T(8,128)(2,1)S(1)} %get-tuple-element.62), channel_id=1, source_target_pairs={{0,20},{4,16},{8,28},{12,24},{16,4},{20,0},{24,12},{28,8},{1,21},{... | collective-permute-start | bytes 393224 | tf_op jit(solution)/shard_map/ppermute | solution.py:40
  66.7 14.2 %collective-permute-start.19 = (bf16[256,256]{1,0:T(8,128)(2,1)S(1)}, bf16[256,256]{1,0:T(8,128)(2,1)S(1)}, u32[]{:S(2)}, u32[]{:S(2)}) collective-permute-start(bf16[256,256]{1,0:T(8,128)(2,1)S(1)} %get-tuple-element.63), channel_id=1, source_target_pairs={{0,28},{4,24},{8,20},{12,16},{16,12},{20,8},{24,4},{28,0},{1,29},{... | collective-permute-start | bytes 393224 | tf_op jit(solution)/shard_map/ppermute | solution.py:40
  71.6 10.8 %collective-permute-start.20 = (bf16[256,256]{1,0:T(8,128)(2,1)S(1)}, bf16[256,256]{1,0:T(8,128)(2,1)S(1)}, u32[]{:S(2)}, u32[]{:S(2)}) collective-permute-start(bf16[256,256]{1,0:T(8,128)(2,1)S(1)} %get-tuple-element.64), channel_id=1, source_target_pairs={{0,4},{4,0},{8,12},{12,8},{16,20},{20,16},{24,28},{28,24},{1,5},{5... | collective-permute-start | bytes 393224 | tf_op jit(solution)/shard_map/ppermute | solution.py:40
  82.8 1.9 %collective-permute-start.23 = (f32[1,256]{1,0:T(1,128)S(1)}, f32[1,256]{1,0:T(1,128)S(1)}, u32[]{:S(2)}, u32[]{:S(2)}) collective-permute-start(f32[1,256]{1,0:T(1,128)S(1)} %get-tuple-element.66.refs_0_), channel_id=1, source_target_pairs={{0,1},{1,0},{2,3},{3,2},{4,5},{5,4},{6,7},{7,6},{8,9},{9,8},{10,11... | collective-permute-start | bytes 3080 | tf_op jit(solution)/shard_map/ppermute | solution.py:421
  82.8 3.6 %collective-permute-start.22 = (f32[1,256]{1,0:T(1,128)S(1)}, f32[1,256]{1,0:T(1,128)S(1)}, u32[]{:S(2)}, u32[]{:S(2)}) collective-permute-start(f32[1,256]{1,0:T(1,128)S(1)} %get-tuple-element.66.refs_0_), channel_id=1, source_target_pairs={{0,2},{1,3},{2,0},{3,1},{4,6},{5,7},{6,4},{7,5},{8,10},{9,11},{10,... | collective-permute-start | bytes 3080 | tf_op jit(solution)/shard_map/ppermute | solution.py:421
  84.4 3.0 %collective-permute-start.21 = (f32[1,256]{1,0:T(1,128)S(1)}, f32[1,256]{1,0:T(1,128)S(1)}, u32[]{:S(2)}, u32[]{:S(2)}) collective-permute-start(f32[1,256]{1,0:T(1,128)S(1)} %get-tuple-element.66.refs_0_), channel_id=1, source_target_pairs={{0,3},{1,2},{2,1},{3,0},{4,7},{5,6},{6,5},{7,4},{8,11},{9,10},{10,... | collective-permute-start | bytes 3080 | tf_op jit(solution)/shard_map/ppermute | solution.py:421
  (11 other events, 91.0 us)

commit v11 on v10

--- a/solution.py
+++ b/solution.py
@@ -3,7 +3,6 @@
 
 import jax
 import jax.numpy as jnp
-import ml_dtypes
 import numpy as np
 from jax import lax
 from jax.experimental import pallas as pl
@@ -11,15 +10,10 @@
 from jax.sharding import PartitionSpec as P
 
 MIB = 1024 * 1024
+ALL = 56 * MIB
 BIG = 48 * MIB
 WHOLE = pl.BlockSpec(memory_space=pltpu.VMEM)
 IN_HBM = pl.BlockSpec(memory_space=pltpu.HBM)
-
-
-def split_bf16(table):
-    high = table.astype(ml_dtypes.bfloat16)
-    low = (table - high.astype(np.float64)).astype(ml_dtypes.bfloat16)
-    return high, low
 
 
 def tables(width):
@@ -29,7 +23,7 @@
     angle = math.pi / (2 * width) * steps
     forward = np.concatenate([np.cos(angle), -np.sin(angle)], axis=0)
     inverse = forward.T / width
-    return split_bf16(forward) + split_bf16(inverse)
+    return forward.astype(np.float32), inverse.astype(np.float32)
 
 
 def partner(step):
@@ -77,9 +71,9 @@
         functools.partial(split_kernel, steps, part),
         out_shape=[jax.ShapeDtypeStruct((width, part), jnp.bfloat16)] * len(steps),
         in_specs=[IN_HBM],
-        out_specs=[WHOLE] * len(steps),
+        out_specs=[IN_HBM] * len(steps),
         scratch_shapes=[pltpu.SemaphoreType.DMA((len(steps),))],
-        compiler_params=pltpu.CompilerParams(vmem_limit_bytes=16 * MIB),
+        compiler_params=pltpu.CompilerParams(vmem_limit_bytes=ALL),
         cost_estimate=pl.CostEstimate(flops=0, bytes_accessed=4 * width * columns, transcendentals=0),
     )(filter_store)
     return dict(zip(steps, found))
@@ -98,11 +92,16 @@
         )
         for copy in copies[-1]:
             copy.start()
+    stores = []
     for k in range(count):
         for copy in copies[k]:
             copy.wait()
         product = key_buf[k].astype(jnp.float32) * value_buf[k].astype(jnp.float32)
-        outs[k][...] = product.astype(jnp.bfloat16)
+        key_buf[k] = product.astype(jnp.bfloat16)
+        stores.append(pltpu.make_async_copy(key_buf.at[k], outs[k], sems.at[2, k]))
+        stores[-1].start()
+    for copy in stores:
+        copy.wait()
 
 
 def gate(count, key_in, value_in):
@@ -116,9 +115,9 @@
         functools.partial(gate_kernel, count, part),
         out_shape=[jax.ShapeDtypeStruct((width, part), jnp.bfloat16)] * count,
         in_specs=[IN_HBM] * 2,
-        out_specs=[WHOLE] * count,
-        scratch_shapes=[block, block, pltpu.SemaphoreType.DMA((2, count))],
-        compiler_params=pltpu.CompilerParams(vmem_limit_bytes=16 * MIB),
+        out_specs=[IN_HBM] * count,
+        scratch_shapes=[block, block, pltpu.SemaphoreType.DMA((3, count))],
+        compiler_params=pltpu.CompilerParams(vmem_limit_bytes=ALL),
         cost_estimate=pl.CostEstimate(flops=width * columns, bytes_accessed=6 * width * columns, transcendentals=0),
     )(key_in, value_in)
 
@@ -131,12 +130,19 @@
     return dot(high, block) + dot(low, block)
 
 
-def filter_kernel(steps, lag_ref, high_ref, low_ref, *refs):
-    blocks, out = refs[:-1], refs[-1]
+def halves(value):
+    high = value.astype(jnp.bfloat16)
+    return high, (value - high.astype(jnp.float32)).astype(jnp.bfloat16)
+
+
+def filter_kernel(steps, lag_ref, forward_ref, inverse_ref, *refs):
     count = len(steps)
+    blocks, (out, fh_ref, fl_ref, ih_ref, il_ref) = refs[:count], refs[count:]
+    fh_ref[...], fl_ref[...] = halves(forward_ref[...])
+    ih_ref[...], il_ref[...] = halves(inverse_ref[...])
     for at, (k, block) in enumerate(zip(steps, blocks)):
         out[at] = jnp.zeros(out.shape[1:], jnp.float32)
-        out[count + lag_ref[partner(k)]] = transform(high_ref[...], low_ref[...], block[...])
+        out[count + lag_ref[partner(k)]] = transform(fh_ref[...], fl_ref[...], block[...])
 
 
 def transform_cost(count, width, columns, passes):
@@ -147,18 +153,27 @@
     )
 
 
-def filter_spectra(lag_of_block, high, low, blocks):
+def filter_spectra(lag_of_block, blocks):
     steps = list(blocks)
     count = len(steps)
     width, columns = blocks[0].shape
-    return pl.pallas_call(
+    forward = jax.ShapeDtypeStruct((2 * width, width), jnp.bfloat16)
+    backward = jax.ShapeDtypeStruct((width, 2 * width), jnp.bfloat16)
+    found = pl.pallas_call(
         functools.partial(filter_kernel, steps),
-        out_shape=jax.ShapeDtypeStruct((2 * count, 2 * width, columns), jnp.float32),
+        out_shape=[
+            jax.ShapeDtypeStruct((2 * count, 2 * width, columns), jnp.float32),
+            forward,
+            forward,
+            backward,
+            backward,
+        ],
         in_specs=[pl.BlockSpec(memory_space=pltpu.SMEM)] + [WHOLE] * (2 + count),
-        out_specs=WHOLE,
+        out_specs=[WHOLE] * 5,
         compiler_params=pltpu.CompilerParams(vmem_limit_bytes=16 * MIB),
         cost_estimate=transform_cost(count, width, columns, 2),
-    )(lag_of_block, high, low, *[blocks[k] for k in steps])
+    )(lag_of_block, *[jnp.asarray(table) for table in tables(width)], *[blocks[k] for k in steps])
+    return found[0], found[1:]
 
 
 def tiles(width, columns, tile):
@@ -230,8 +245,7 @@
 
 
 def inverse(table_high, table_low, total):
-    high = total.astype(jnp.bfloat16)
-    low = (total - high.astype(jnp.float32)).astype(jnp.bfloat16)
+    high, low = halves(total)
     return (dot(table_high, high) + dot(table_high, low) + dot(table_low, high)).astype(jnp.bfloat16)
 
 
@@ -243,22 +257,27 @@
     starts = [count - partner(k) for k in steps]
 
     def tile(re_rows, im_rows, lanes, sign):
-        g = [(gs[at, re_rows, lanes], gs[at, im_rows, lanes]) for at in range(len(steps))]
-        last = None
+        def both(ref, i):
+            return ref[i, re_rows, lanes], ref[i, im_rows, lanes]
+
+        g = [both(gs, at) for at in range(len(steps))]
+        f = [[both(fs, start + j) for start in starts] for j in range(count)]
+        s = [both(ss, j) for j in range(count)]
+        d = []
         for j in range(count):
             d_re = d_im = None
-            for start, (g_re, g_im) in zip(starts, g):
-                f_re, f_im = fs[start + j, re_rows, lanes], fs[start + j, im_rows, lanes]
+            for (f_re, f_im), (g_re, g_im) in zip(f[j], g):
                 p_re, p_im = f_re * g_re - f_im * g_im, f_re * g_im + f_im * g_re
                 d_re, d_im = (p_re, p_im) if d_re is None else (d_re + p_re, d_im + p_im)
-            s_re, s_im = ss[j, re_rows, lanes] + d_re, ss[j, im_rows, lanes] + d_im
-            if last is not None and sign > 0:
-                s_re, s_im = s_re - last[1], s_im + last[0]
-            elif last is not None:
-                s_re, s_im = s_re + last[1], s_im - last[0]
+            d.append((d_re, d_im))
+        for j in range(count):
+            s_re, s_im = s[j][0] + d[j][0], s[j][1] + d[j][1]
+            if j and sign > 0:
+                s_re, s_im = s_re - d[j - 1][1], s_im + d[j - 1][0]
+            elif j:
+                s_re, s_im = s_re + d[j - 1][1], s_im - d[j - 1][0]
             ss[j, re_rows, lanes] = s_re
             ss[j, im_rows, lanes] = s_im
-            last = (d_re, d_im)
 
     tiles(width, columns, tile)
     for k, out in zip(first, outs):
@@ -397,19 +416,20 @@
 def local(query, key_in, value_in, filter_store, lag_of_block, skip, out_gain):
     width, columns = query.shape
     count = lax.axis_size("tok")
-    tabs = [jnp.asarray(t) for t in tables(width)]
     part = columns // count
     order = sending_order(count)
     gated_order = order[:-3] + order[-1:] + order[-3:-1]
-    own = split(count, order[1:] + [0], filter_store)
-    own[order[0]] = piece(filter_store, order[0], part)
+    own = split(count, order + [0], filter_store)
     own[0], key_in, value_in = lax.optimization_barrier((own[0], key_in, value_in))
     mine = gate(count, key_in, value_in)
     filts = {k: send(own[k], k, count) for k in order}
     gates = {k: send(mine[k], k, count) for k in gated_order}
     filts[0], gates[0] = own[0], mine[0]
+    held = gated_order[:2]
+    filts[0], *arrived = lax.optimization_barrier((filts[0], *[gates[k] for k in held]))
+    gates.update(zip(held, arrived))
     late = gated_order[-2:]
-    filt = filter_spectra(lag_of_block, *tabs[:2], filts)
+    filt, tabs = filter_spectra(lag_of_block, filts)
     sums = early_products(tabs, filt, {k: gates[k] for k in gates if k not in late})
     sums, found = late_products(order[:1], tabs, filt, sums, {k: gates[k] for k in late})
     found.update(inverses(order[1:] + [0], tabs, sums))

time: 89.2 us -> 121 us (1.36)
  Pallas kernels: 14.8 us -> 49.2 us
  local copies, waits for them, and re-layouts: 7.17 us -> 4.59 us
    pallas_call x1, Pallas kernels: 0.21 us -> 32.9 us  [split(): pl.pallas_call(functools.partial(split_kernel, steps, part), out_shape=[j...]
    pallas_call x1, Pallas kernels: 0.74 us -> 2.51 us  [gate(): pl.pallas_call(functools.partial(gate_kernel, count, part), out_shape=[ja...]
    unnamed x22 -> x30, local copies, waits for them, and re-layouts: 6.26 us -> 4.59 us
  transfers between devices with their start and end apart: 24 -> 24, of which waited for: 9 -> 8; matrix products, arithmetic and copies ran while one was open for 0% -> 0% of each run, Pallas kernels for 10% -> 9%
where the time goes in v11:
time: 121 us
  Pallas kernels  49.2 us (41%)
  starting transfers between devices  42.9 us (35%)
  waiting for transfers between devices  23.7 us (20%)
  local copies, waits for them, and re-layouts  4.59 us (4%)
    ppermute x21, starting transfers between devices, send(): return lax.ppermute(block, 'tok', [(d, d ^ step) for d in range(count)])  41 us
    pallas_call x1, Pallas kernels, split(): pl.pallas_call(functools.partial(split_kernel, steps, part), out_shape=[j...  32.9 us
    ppermute x21, waiting for transfers between devices, send(): return lax.ppermute(block, 'tok', [(d, d ^ step) for d in range(count)])  20.9 us
    unnamed x30, local copies, waits for them, and re-layouts  4.59 us
    pallas_call x1, Pallas kernels, early_products(): pl.pallas_call(functools.partial(early_kernel, count, steps), out_shape=j...  3.87 us
    pallas_call x1, Pallas kernels, late_products(): pl.pallas_call(functools.partial(late_kernel, count, steps, first), out_s...  3.68 us
    ppermute x3, waiting for transfers between devices, local(): lax.ppermute(square, 'chan', [(d, d ^ step) for d in range(others)])  2.84 us
    pallas_call x1, Pallas kernels, gate(): pl.pallas_call(functools.partial(gate_kernel, count, part), out_shape=[ja...  2.51 us
  transfers between devices with their start and end apart: 24, of which 8 were waited for; matrix products, arithmetic and copies ran while one was open for 0% of the time, Pallas kernels for 9%

profile of v11, /device:TPU:0, one launch (start us, length us, event | category | flops | bytes accessed | tf_op | source)
XLA Modules:
  0.0 120.6 jit_solution(17913650063942208556)
XLA Ops:
  0.0 32.9 %shard_map.91 = (bf16[256,256]{1,0:T(8,128)(2,1)}, bf16[256,256]{1,0:T(8,128)(2,1)}, bf16[256,256]{1,0:T(8,128)(2,1)}, bf16[256,256]{1,0:T(8,128)(2,1)}, bf16[25...) custom-call(bf16[256,2048]{1,0:T(8,128)(2,1)} %filt_ref.1), custom_call_target="tpu_custom_call" | custom-call | bytes 2097152 | tf_op jit(solution)/shard_map/pallas_call | solution.py:70
  32.9 4.1 %collective-permute-start = (bf16[256,256]{1,0:T(8,128)(2,1)}, bf16[256,256]{1,0:T(8,128)(2,1)S(1)}, u32[]{:S(2)}, u32[]{:S(2)}) collective-permute-start(bf16[256,256]{1,0:T(8,128)(2,1)} %get-tuple-element.45), channel_id=1, source_target_pairs={{0,16},{4,20},{8,24},{12,28},{16,0},{20,4},{24,8},{28,12},{1,17},{... | collective-permute-start | bytes 393224 | tf_op jit(solution)/shard_map/ppermute | solution.py:34
  37.0 1.6 %collective-permute-start.1 = (bf16[256,256]{1,0:T(8,128)(2,1)}, bf16[256,256]{1,0:T(8,128)(2,1)S(1)}, u32[]{:S(2)}, u32[]{:S(2)}) collective-permute-start(bf16[256,256]{1,0:T(8,128)(2,1)} %get-tuple-element.46), channel_id=1, source_target_pairs={{0,8},{4,12},{8,0},{12,4},{16,24},{20,28},{24,16},{28,20},{1,9},{5... | collective-permute-start | bytes 393224 | tf_op jit(solution)/shard_map/ppermute | solution.py:34
  38.6 1.8 %collective-permute-start.3 = (bf16[256,256]{1,0:T(8,128)(2,1)}, bf16[256,256]{1,0:T(8,128)(2,1)S(1)}, u32[]{:S(2)}, u32[]{:S(2)}) collective-permute-start(bf16[256,256]{1,0:T(8,128)(2,1)} %get-tuple-element.48), channel_id=1, source_target_pairs={{0,12},{4,8},{8,4},{12,0},{16,28},{20,24},{24,20},{28,16},{1,13},{... | collective-permute-start | bytes 393224 | tf_op jit(solution)/shard_map/ppermute | solution.py:34
  40.4 3.5 %collective-permute-start.4 = (bf16[256,256]{1,0:T(8,128)(2,1)}, bf16[256,256]{1,0:T(8,128)(2,1)S(1)}, u32[]{:S(2)}, u32[]{:S(2)}) collective-permute-start(bf16[256,256]{1,0:T(8,128)(2,1)} %get-tuple-element.49), channel_id=1, source_target_pairs={{0,20},{4,16},{8,28},{12,24},{16,4},{20,0},{24,12},{28,8},{1,21},{... | collective-permute-start | bytes 393224 | tf_op jit(solution)/shard_map/ppermute | solution.py:34
  43.9 2.5 %shard_map.92 = (bf16[256,256]{1,0:T(8,128)(2,1)}, bf16[256,256]{1,0:T(8,128)(2,1)}, bf16[256,256]{1,0:T(8,128)(2,1)}, bf16[256,256]{1,0:T(8,128)(2,1)}, bf16[25...) custom-call(bf16[256,2048]{1,0:T(8,128)(2,1)} %key_ref, ...), custom_call_target="tpu_custom_call" | custom-call | flops 524288 | bytes 3145728 | tf_op jit(solution)/shard_map/pallas_call | solution.py:114
  46.8 2.8 %collective-permute-start.8 = (bf16[256,256]{1,0:T(8,128)(2,1)}, bf16[256,256]{1,0:T(8,128)(2,1)S(1)}, u32[]{:S(2)}, u32[]{:S(2)}) collective-permute-start(bf16[256,256]{1,0:T(8,128)(2,1)} %get-tuple-element.57.refs_6_), channel_id=1, source_target_pairs={{0,8},{4,12},{8,0},{12,4},{16,24},{20,28},{24,16},{28,20},{1,9},{5... | collective-permute-start | bytes 393224 | tf_op jit(solution)/shard_map/ppermute | solution.py:34
  49.6 2.4 %collective-permute-start.5 = (bf16[256,256]{1,0:T(8,128)(2,1)}, bf16[256,256]{1,0:T(8,128)(2,1)S(1)}, u32[]{:S(2)}, u32[]{:S(2)}) collective-permute-start(bf16[256,256]{1,0:T(8,128)(2,1)} %get-tuple-element.50), channel_id=1, source_target_pairs={{0,28},{4,24},{8,20},{12,16},{16,12},{20,8},{24,4},{28,0},{1,29},{... | collective-permute-start | bytes 393224 | tf_op jit(solution)/shard_map/ppermute | solution.py:34
  52.5 8.3 %collective-permute-done.4.refs_4_ = bf16[256,256]{1,0:T(8,128)(2,1)S(1)} collective-permute-done((bf16[256,256]{1,0:T(8,128)(2,1)}, bf16[256,256]{1,0:T(8,128)(2,1)S(1)}, u32[]{:S(2)}, u32[]{:S(2)}) %collective-permute-start.4) | collective-permute-done | bytes 131104 | tf_op jit(solution)/shard_map/ppermute | solution.py:34
  60.8 2.6 %collective-permute-start.9 = (bf16[256,256]{1,0:T(8,128)(2,1)}, bf16[256,256]{1,0:T(8,128)(2,1)S(1)}, u32[]{:S(2)}, u32[]{:S(2)}) collective-permute-start(bf16[256,256]{1,0:T(8,128)(2,1)} %get-tuple-element.66.refs_7_), channel_id=1, source_target_pairs={{0,24},{4,28},{8,16},{12,20},{16,8},{20,12},{24,0},{28,4},{1,25},{... | collective-permute-start | bytes 393224 | tf_op jit(solution)/shard_map/ppermute | solution.py:34
  65.2 3.5 %collective-permute-start.11 = (bf16[256,256]{1,0:T(8,128)(2,1)}, bf16[256,256]{1,0:T(8,128)(2,1)S(1)}, u32[]{:S(2)}, u32[]{:S(2)}) collective-permute-start(bf16[256,256]{1,0:T(8,128)(2,1)} %get-tuple-element.68.refs_7_), channel_id=1, source_target_pairs={{0,4},{4,0},{8,12},{12,8},{16,20},{20,16},{24,28},{28,24},{1,5},{5... | collective-permute-start | bytes 393224 | tf_op jit(solution)/shard_map/ppermute | solution.py:34
  68.7 4.0 %collective-permute-start.12 = (bf16[256,256]{1,0:T(8,128)(2,1)}, bf16[256,256]{1,0:T(8,128)(2,1)S(1)}, u32[]{:S(2)}, u32[]{:S(2)}) collective-permute-start(bf16[256,256]{1,0:T(8,128)(2,1)} %get-tuple-element.70.refs_5_), channel_id=1, source_target_pairs={{0,20},{4,16},{8,28},{12,24},{16,4},{20,0},{24,12},{28,8},{1,21},{... | collective-permute-start | bytes 393224 | tf_op jit(solution)/shard_map/ppermute | solution.py:34
  72.7 2.1 %collective-permute-start.13 = (bf16[256,256]{1,0:T(8,128)(2,1)}, bf16[256,256]{1,0:T(8,128)(2,1)S(1)}, u32[]{:S(2)}, u32[]{:S(2)}) collective-permute-start(bf16[256,256]{1,0:T(8,128)(2,1)} %get-tuple-element.71.refs_6_), channel_id=1, source_target_pairs={{0,28},{4,24},{8,20},{12,16},{16,12},{20,8},{24,4},{28,0},{1,29},{... | collective-permute-start | bytes 393224 | tf_op jit(solution)/shard_map/ppermute | solution.py:34
  78.4 2.2 %shard_map.93 = (f32[16,512,256]{2,1,0:T(8,128)S(1)}, bf16[512,256]{1,0:T(8,128)(2,1)S(1)}, bf16[512,256]{1,0:T(8,128)(2,1)S(1)}, bf16[256,512]{1,0:T(8,128)(2,1)S(1)}, bf16[256,512]{1,0:T(8,128)(2,1)S(1)}) custom-call(s32[8]{0:T(128)S(1)} %copy-done.12, f32[512,256]{1,0:T(8,128)S(1)} %copy-done.14, f32[256,512]{1,0:T(8,128)S(1)} %copy-done.13, ...), custom_call_target="tpu_custom_call" | custom-call | flops 1073741824 | bytes 5242880 | tf_op jit(solution)/shard_map/pallas_call | solution.py:162
  81.6 3.9 %shard_map.94.sums = f32[8,512,256]{2,1,0:T(8,128)S(1)} custom-call(bf16[512,256]{1,0:T(8,128)(2,1)S(1)} %get-tuple-element.59.fh_ref, bf16[512,256]{1,0:T(8,128)(2,1)S(1)} %get-tuple-element.60.fl_ref, f32[16,512,256]{2,1,0:T(8,128)S(1)} %get-tuple-element.63.fs, bf16[256,256]{1,0:T(8,128)(2,1)S(1)} %collective-permute-done.7.refs_0_, ...), custom_call_target="tpu_custom_call" | custom-call | flops 2147483648 | bytes 5242880 | tf_op jit(solution)/shard_map/pallas_call | solution.py:236
  85.5 3.7 %shard_map.95 = (f32[8,512,256]{2,1,0:T(8,128)S(1)}, bf16[256,256]{1,0:T(8,128)(2,1)S(1)}) custom-call(bf16[512,256]{1,0:T(8,128)(2,1)S(1)} %get-tuple-element.59.fh_ref, bf16[512,256]{1,0:T(8,128)(2,1)S(1)} %get-tuple-element.60.fl_ref, bf16[256,512]{1,0:T(8,128)(2,1)S(1)} %get-tuple-element.61.ih_ref, ...), custom_call_target="tpu_custom_call", output_to_operand_aliasing={{0}: (5, {})} | custom-call | flops 1610612736 | bytes 5242880 | tf_op jit(solution)/shard_map/pallas_call | solution.py:291
  89.3 2.3 %collective-permute-start.14 = (bf16[256,256]{1,0:T(8,128)(2,1)S(1)}, bf16[256,256]{1,0:T(8,128)(2,1)S(1)}, u32[]{:S(2)}, u32[]{:S(2)}) collective-permute-start(bf16[256,256]{1,0:T(8,128)(2,1)S(1)} %get-tuple-element.72), channel_id=1, source_target_pairs={{0,16},{4,20},{8,24},{12,28},{16,0},{20,4},{24,8},{28,12},{1,17},{... | collective-permute-start | bytes 393224 | tf_op jit(solution)/shard_map/ppermute | solution.py:34
  91.5 1.6 %shard_map.96 = (bf16[256,256]{1,0:T(8,128)(2,1)S(1)}, bf16[256,256]{1,0:T(8,128)(2,1)S(1)}, bf16[256,256]{1,0:T(8,128)(2,1)S(1)}, bf16[256,256]{1,0:T(8,128)(2,...) custom-call(bf16[256,512]{1,0:T(8,128)(2,1)S(1)} %get-tuple-element.61.ih_ref, ...), custom_call_target="tpu_custom_call" | custom-call | flops 1409286144 | bytes 4587520 | tf_op jit(solution)/shard_map/pallas_call | solution.py:313
  93.2 3.1 %collective-permute-start.15 = (bf16[256,256]{1,0:T(8,128)(2,1)S(1)}, bf16[256,256]{1,0:T(8,128)(2,1)S(1)}, u32[]{:S(2)}, u32[]{:S(2)}) collective-permute-start(bf16[256,256]{1,0:T(8,128)(2,1)S(1)} %get-tuple-element.74), channel_id=1, source_target_pairs={{0,8},{4,12},{8,0},{12,4},{16,24},{20,28},{24,16},{28,20},{1,9},{5... | collective-permute-start | bytes 393224 | tf_op jit(solution)/shard_map/ppermute | solution.py:34
  96.6 4.9 %collective-permute-start.18 = (bf16[256,256]{1,0:T(8,128)(2,1)S(1)}, bf16[256,256]{1,0:T(8,128)(2,1)S(1)}, u32[]{:S(2)}, u32[]{:S(2)}) collective-permute-start(bf16[256,256]{1,0:T(8,128)(2,1)S(1)} %get-tuple-element.80), channel_id=1, source_target_pairs={{0,20},{4,16},{8,28},{12,24},{16,4},{20,0},{24,12},{28,8},{1,21},{... | collective-permute-start | bytes 393224 | tf_op jit(solution)/shard_map/ppermute | solution.py:34
  101.5 2.8 %collective-permute-done.15.refs_1_ = bf16[256,256]{1,0:T(8,128)(2,1)S(1)} collective-permute-done((bf16[256,256]{1,0:T(8,128)(2,1)S(1)}, bf16[256,256]{1,0:T(8,128)(2,1)S(1)}, u32[]{:S(2)}, u32[]{:S(2)}) %collective-permute-start.15) | collective-permute-done | bytes 131104 | tf_op jit(solution)/shard_map/ppermute | solution.py:34
  106.4 7.5 %collective-permute-done.18.refs_2_ = bf16[256,256]{1,0:T(8,128)(2,1)S(1)} collective-permute-done((bf16[256,256]{1,0:T(8,128)(2,1)S(1)}, bf16[256,256]{1,0:T(8,128)(2,1)S(1)}, u32[]{:S(2)}, u32[]{:S(2)}) %collective-permute-start.18) | collective-permute-done | bytes 131104 | tf_op jit(solution)/shard_map/ppermute | solution.py:34
  114.4 1.7 %collective-permute-start.22 = (f32[1,256]{1,0:T(1,128)S(1)}, f32[1,256]{1,0:T(1,128)S(1)}, u32[]{:S(2)}, u32[]{:S(2)}) collective-permute-start(f32[1,256]{1,0:T(1,128)S(1)} %get-tuple-element.84.refs_0_), channel_id=1, source_target_pairs={{0,2},{1,3},{2,0},{3,1},{4,6},{5,7},{6,4},{7,5},{8,10},{9,11},{10,... | collective-permute-start | bytes 3080 | tf_op jit(solution)/shard_map/ppermute | solution.py:441
  116.3 1.8 %collective-permute-done.22.refs_2_ = f32[1,256]{1,0:T(1,128)S(1)} collective-permute-done((f32[1,256]{1,0:T(1,128)S(1)}, f32[1,256]{1,0:T(1,128)S(1)}, u32[]{:S(2)}, u32[]{:S(2)}) %collective-permute-start.22) | collective-permute-done | bytes 1056 | tf_op jit(solution)/shard_map/ppermute | solution.py:441
  (63 shorter events, 12.9 us)
Async XLA Ops:
  32.9 13.5 %collective-permute-start = (bf16[256,256]{1,0:T(8,128)(2,1)}, bf16[256,256]{1,0:T(8,128)(2,1)S(1)}, u32[]{:S(2)}, u32[]{:S(2)}) collective-permute-start(bf16[256,256]{1,0:T(8,128)(2,1)} %get-tuple-element.45), channel_id=1, source_target_pairs={{0,16},{4,20},{8,24},{12,28},{16,0},{20,4},{24,8},{28,12},{1,17},{... | collective-permute-start | bytes 393224 | tf_op jit(solution)/shard_map/ppermute | solution.py:34
  37.0 9.7 %collective-permute-start.1 = (bf16[256,256]{1,0:T(8,128)(2,1)}, bf16[256,256]{1,0:T(8,128)(2,1)S(1)}, u32[]{:S(2)}, u32[]{:S(2)}) collective-permute-start(bf16[256,256]{1,0:T(8,128)(2,1)} %get-tuple-element.46), channel_id=1, source_target_pairs={{0,8},{4,12},{8,0},{12,4},{16,24},{20,28},{24,16},{28,20},{1,9},{5... | collective-permute-start | bytes 393224 | tf_op jit(solution)/shard_map/ppermute | solution.py:34
  38.6 11.0 %collective-permute-start.2 = (bf16[256,256]{1,0:T(8,128)(2,1)}, bf16[256,256]{1,0:T(8,128)(2,1)S(1)}, u32[]{:S(2)}, u32[]{:S(2)}) collective-permute-start(bf16[256,256]{1,0:T(8,128)(2,1)} %get-tuple-element.47), channel_id=1, source_target_pairs={{0,24},{4,28},{8,16},{12,20},{16,8},{20,12},{24,0},{28,4},{1,25},{... | collective-permute-start | bytes 393224 | tf_op jit(solution)/shard_map/ppermute | solution.py:34
  38.6 13.4 %collective-permute-start.3 = (bf16[256,256]{1,0:T(8,128)(2,1)}, bf16[256,256]{1,0:T(8,128)(2,1)S(1)}, u32[]{:S(2)}, u32[]{:S(2)}) collective-permute-start(bf16[256,256]{1,0:T(8,128)(2,1)} %get-tuple-element.48), channel_id=1, source_target_pairs={{0,12},{4,8},{8,4},{12,0},{16,28},{20,24},{24,20},{28,16},{1,13},{... | collective-permute-start | bytes 393224 | tf_op jit(solution)/shard_map/ppermute | solution.py:34
  40.4 20.4 %collective-permute-start.4 = (bf16[256,256]{1,0:T(8,128)(2,1)}, bf16[256,256]{1,0:T(8,128)(2,1)S(1)}, u32[]{:S(2)}, u32[]{:S(2)}) collective-permute-start(bf16[256,256]{1,0:T(8,128)(2,1)} %get-tuple-element.49), channel_id=1, source_target_pairs={{0,20},{4,16},{8,28},{12,24},{16,4},{20,0},{24,12},{28,8},{1,21},{... | collective-permute-start | bytes 393224 | tf_op jit(solution)/shard_map/ppermute | solution.py:34
  46.4 17.6 %collective-permute-start.7 = (bf16[256,256]{1,0:T(8,128)(2,1)}, bf16[256,256]{1,0:T(8,128)(2,1)S(1)}, u32[]{:S(2)}, u32[]{:S(2)}) collective-permute-start(bf16[256,256]{1,0:T(8,128)(2,1)} %get-tuple-element.56.refs_5_), channel_id=1, source_target_pairs={{0,16},{4,20},{8,24},{12,28},{16,0},{20,4},{24,8},{28,12},{1,17},{... | collective-permute-start | bytes 393224 | tf_op jit(solution)/shard_map/ppermute | solution.py:34
  46.8 18.5 %collective-permute-start.8 = (bf16[256,256]{1,0:T(8,128)(2,1)}, bf16[256,256]{1,0:T(8,128)(2,1)S(1)}, u32[]{:S(2)}, u32[]{:S(2)}) collective-permute-start(bf16[256,256]{1,0:T(8,128)(2,1)} %get-tuple-element.57.refs_6_), channel_id=1, source_target_pairs={{0,8},{4,12},{8,0},{12,4},{16,24},{20,28},{24,16},{28,20},{1,9},{5... | collective-permute-start | bytes 393224 | tf_op jit(solution)/shard_map/ppermute | solution.py:34
  49.6 19.1 %collective-permute-start.5 = (bf16[256,256]{1,0:T(8,128)(2,1)}, bf16[256,256]{1,0:T(8,128)(2,1)S(1)}, u32[]{:S(2)}, u32[]{:S(2)}) collective-permute-start(bf16[256,256]{1,0:T(8,128)(2,1)} %get-tuple-element.50), channel_id=1, source_target_pairs={{0,28},{4,24},{8,20},{12,16},{16,12},{20,8},{24,4},{28,0},{1,29},{... | collective-permute-start | bytes 393224 | tf_op jit(solution)/shard_map/ppermute | solution.py:34
  52.0 20.7 %collective-permute-start.6 = (bf16[256,256]{1,0:T(8,128)(2,1)}, bf16[256,256]{1,0:T(8,128)(2,1)S(1)}, u32[]{:S(2)}, u32[]{:S(2)}) collective-permute-start(bf16[256,256]{1,0:T(8,128)(2,1)} %get-tuple-element.51), channel_id=1, source_target_pairs={{0,4},{4,0},{8,12},{12,8},{16,20},{20,16},{24,28},{28,24},{1,5},{5... | collective-permute-start | bytes 393224 | tf_op jit(solution)/shard_map/ppermute | solution.py:34
  60.8 19.8 %collective-permute-start.9 = (bf16[256,256]{1,0:T(8,128)(2,1)}, bf16[256,256]{1,0:T(8,128)(2,1)S(1)}, u32[]{:S(2)}, u32[]{:S(2)}) collective-permute-start(bf16[256,256]{1,0:T(8,128)(2,1)} %get-tuple-element.66.refs_7_), channel_id=1, source_target_pairs={{0,24},{4,28},{8,16},{12,20},{16,8},{20,12},{24,0},{28,4},{1,25},{... | collective-permute-start | bytes 393224 | tf_op jit(solution)/shard_map/ppermute | solution.py:34
  64.1 16.6 %collective-permute-start.10 = (bf16[256,256]{1,0:T(8,128)(2,1)}, bf16[256,256]{1,0:T(8,128)(2,1)S(1)}, u32[]{:S(2)}, u32[]{:S(2)}) collective-permute-start(bf16[256,256]{1,0:T(8,128)(2,1)} %get-tuple-element.67.refs_8_), channel_id=1, source_target_pairs={{0,12},{4,8},{8,4},{12,0},{16,28},{20,24},{24,20},{28,16},{1,13},{... | collective-permute-start | bytes 393224 | tf_op jit(solution)/shard_map/ppermute | solution.py:34
  65.2 15.4 %collective-permute-start.11 = (bf16[256,256]{1,0:T(8,128)(2,1)}, bf16[256,256]{1,0:T(8,128)(2,1)S(1)}, u32[]{:S(2)}, u32[]{:S(2)}) collective-permute-start(bf16[256,256]{1,0:T(8,128)(2,1)} %get-tuple-element.68.refs_7_), channel_id=1, source_target_pairs={{0,4},{4,0},{8,12},{12,8},{16,20},{20,16},{24,28},{28,24},{1,5},{5... | collective-permute-start | bytes 393224 | tf_op jit(solution)/shard_map/ppermute | solution.py:34
  68.7 16.8 %collective-permute-start.12 = (bf16[256,256]{1,0:T(8,128)(2,1)}, bf16[256,256]{1,0:T(8,128)(2,1)S(1)}, u32[]{:S(2)}, u32[]{:S(2)}) collective-permute-start(bf16[256,256]{1,0:T(8,128)(2,1)} %get-tuple-element.70.refs_5_), channel_id=1, source_target_pairs={{0,20},{4,16},{8,28},{12,24},{16,4},{20,0},{24,12},{28,8},{1,21},{... | collective-permute-start | bytes 393224 | tf_op jit(solution)/shard_map/ppermute | solution.py:34
  72.7 12.7 %collective-permute-start.13 = (bf16[256,256]{1,0:T(8,128)(2,1)}, bf16[256,256]{1,0:T(8,128)(2,1)S(1)}, u32[]{:S(2)}, u32[]{:S(2)}) collective-permute-start(bf16[256,256]{1,0:T(8,128)(2,1)} %get-tuple-element.71.refs_6_), channel_id=1, source_target_pairs={{0,28},{4,24},{8,20},{12,16},{16,12},{20,8},{24,4},{28,0},{1,29},{... | collective-permute-start | bytes 393224 | tf_op jit(solution)/shard_map/ppermute | solution.py:34
  89.3 12.3 %collective-permute-start.14 = (bf16[256,256]{1,0:T(8,128)(2,1)S(1)}, bf16[256,256]{1,0:T(8,128)(2,1)S(1)}, u32[]{:S(2)}, u32[]{:S(2)}) collective-permute-start(bf16[256,256]{1,0:T(8,128)(2,1)S(1)} %get-tuple-element.72), channel_id=1, source_target_pairs={{0,16},{4,20},{8,24},{12,28},{16,0},{20,4},{24,8},{28,12},{1,17},{... | collective-permute-start | bytes 393224 | tf_op jit(solution)/shard_map/ppermute | solution.py:34
  93.2 11.1 %collective-permute-start.15 = (bf16[256,256]{1,0:T(8,128)(2,1)S(1)}, bf16[256,256]{1,0:T(8,128)(2,1)S(1)}, u32[]{:S(2)}, u32[]{:S(2)}) collective-permute-start(bf16[256,256]{1,0:T(8,128)(2,1)S(1)} %get-tuple-element.74), channel_id=1, source_target_pairs={{0,8},{4,12},{8,0},{12,4},{16,24},{20,28},{24,16},{28,20},{1,9},{5... | collective-permute-start | bytes 393224 | tf_op jit(solution)/shard_map/ppermute | solution.py:34
  96.2 8.3 %collective-permute-start.16 = (bf16[256,256]{1,0:T(8,128)(2,1)S(1)}, bf16[256,256]{1,0:T(8,128)(2,1)S(1)}, u32[]{:S(2)}, u32[]{:S(2)}) collective-permute-start(bf16[256,256]{1,0:T(8,128)(2,1)S(1)} %get-tuple-element.75), channel_id=1, source_target_pairs={{0,24},{4,28},{8,16},{12,20},{16,8},{20,12},{24,0},{28,4},{1,25},{... | collective-permute-start | bytes 393224 | tf_op jit(solution)/shard_map/ppermute | solution.py:34
  96.2 9.7 %collective-permute-start.17 = (bf16[256,256]{1,0:T(8,128)(2,1)S(1)}, bf16[256,256]{1,0:T(8,128)(2,1)S(1)}, u32[]{:S(2)}, u32[]{:S(2)}) collective-permute-start(bf16[256,256]{1,0:T(8,128)(2,1)S(1)} %get-tuple-element.76), channel_id=1, source_target_pairs={{0,12},{4,8},{8,4},{12,0},{16,28},{20,24},{24,20},{28,16},{1,13},{... | collective-permute-start | bytes 393224 | tf_op jit(solution)/shard_map/ppermute | solution.py:34
  96.6 17.3 %collective-permute-start.18 = (bf16[256,256]{1,0:T(8,128)(2,1)S(1)}, bf16[256,256]{1,0:T(8,128)(2,1)S(1)}, u32[]{:S(2)}, u32[]{:S(2)}) collective-permute-start(bf16[256,256]{1,0:T(8,128)(2,1)S(1)} %get-tuple-element.80), channel_id=1, source_target_pairs={{0,20},{4,16},{8,28},{12,24},{16,4},{20,0},{24,12},{28,8},{1,21},{... | collective-permute-start | bytes 393224 | tf_op jit(solution)/shard_map/ppermute | solution.py:34
  101.5 12.4 %collective-permute-start.19 = (bf16[256,256]{1,0:T(8,128)(2,1)S(1)}, bf16[256,256]{1,0:T(8,128)(2,1)S(1)}, u32[]{:S(2)}, u32[]{:S(2)}) collective-permute-start(bf16[256,256]{1,0:T(8,128)(2,1)S(1)} %get-tuple-element.81), channel_id=1, source_target_pairs={{0,28},{4,24},{8,20},{12,16},{16,12},{20,8},{24,4},{28,0},{1,29},{... | collective-permute-start | bytes 393224 | tf_op jit(solution)/shard_map/ppermute | solution.py:34
  104.3 9.6 %collective-permute-start.20 = (bf16[256,256]{1,0:T(8,128)(2,1)S(1)}, bf16[256,256]{1,0:T(8,128)(2,1)S(1)}, u32[]{:S(2)}, u32[]{:S(2)}) collective-permute-start(bf16[256,256]{1,0:T(8,128)(2,1)S(1)} %get-tuple-element.82), channel_id=1, source_target_pairs={{0,4},{4,0},{8,12},{12,8},{16,20},{20,16},{24,28},{28,24},{1,5},{5... | collective-permute-start | bytes 393224 | tf_op jit(solution)/shard_map/ppermute | solution.py:34
  114.3 1.9 %collective-permute-start.23 = (f32[1,256]{1,0:T(1,128)S(1)}, f32[1,256]{1,0:T(1,128)S(1)}, u32[]{:S(2)}, u32[]{:S(2)}) collective-permute-start(f32[1,256]{1,0:T(1,128)S(1)} %get-tuple-element.84.refs_0_), channel_id=1, source_target_pairs={{0,1},{1,0},{2,3},{3,2},{4,5},{5,4},{6,7},{7,6},{8,9},{9,8},{10,11... | collective-permute-start | bytes 3080 | tf_op jit(solution)/shard_map/ppermute | solution.py:441
  114.4 3.6 %collective-permute-start.22 = (f32[1,256]{1,0:T(1,128)S(1)}, f32[1,256]{1,0:T(1,128)S(1)}, u32[]{:S(2)}, u32[]{:S(2)}) collective-permute-start(f32[1,256]{1,0:T(1,128)S(1)} %get-tuple-element.84.refs_0_), channel_id=1, source_target_pairs={{0,2},{1,3},{2,0},{3,1},{4,6},{5,7},{6,4},{7,5},{8,10},{9,11},{10,... | collective-permute-start | bytes 3080 | tf_op jit(solution)/shard_map/ppermute | solution.py:441
  116.1 3.0 %collective-permute-start.21 = (f32[1,256]{1,0:T(1,128)S(1)}, f32[1,256]{1,0:T(1,128)S(1)}, u32[]{:S(2)}, u32[]{:S(2)}) collective-permute-start(f32[1,256]{1,0:T(1,128)S(1)} %get-tuple-element.84.refs_0_), channel_id=1, source_target_pairs={{0,3},{1,2},{2,1},{3,0},{4,7},{5,6},{6,5},{7,4},{8,11},{9,10},{10,... | collective-permute-start | bytes 3080 | tf_op jit(solution)/shard_map/ppermute | solution.py:441
  (15 other events, 205.0 us)

commit v12 on v5

--- a/solution.py
+++ b/solution.py
@@ -182,7 +182,7 @@
 
 
 def product_kernel(count, steps, first, fh_ref, fl_ref, ih_ref, il_ref, fs, gs, *refs):
-    blocks, (gs, sh, sl), outs, ss = refs[: len(steps)], refs[len(steps) : len(steps) + 3], refs[len(steps) + 3 : -1], refs[-1]
+    blocks, (gs, ss), outs = refs[: len(steps)], refs[len(steps) : len(steps) + 2], refs[len(steps) + 2 :]
     width, columns = outs[0].shape
     for k, block in zip(steps, blocks):
         gs[partner(k)] = transform(fh_ref[...], fl_ref[...], block[...])
@@ -227,65 +227,63 @@
     def _(row):
         products(row, -1)
 
-    for at, k in enumerate(first + [k for k in range(count) if k not in first]):
-        total = ss[partner(k)]
-        high = total.astype(jnp.bfloat16)
-        low = (total - high.astype(jnp.float32)).astype(jnp.bfloat16)
-        if k in first:
-            outs[at][...] = inverse(ih_ref[...], il_ref[...], high, low)
-        else:
-            sh[partner(k)] = high
-            sl[partner(k)] = low
-
-
-def inverse(table_high, table_low, high, low):
+    for k, out in zip(first, outs):
+        out[...] = inverse(ih_ref[...], il_ref[...], ss[partner(k)])
+
+
+def inverse(table_high, table_low, total):
+    high = total.astype(jnp.bfloat16)
+    low = (total - high.astype(jnp.float32)).astype(jnp.bfloat16)
     return (dot(table_high, high) + dot(table_high, low) + dot(table_low, high)).astype(jnp.bfloat16)
 
 
-def products(count, first, tabs, filt, gated, blocks):
+def products(first, tabs, filt, gated, blocks):
     steps = list(blocks)
-    width, columns = blocks[steps[0]].shape
-    half = jax.ShapeDtypeStruct((count, 2 * width, columns), jnp.bfloat16)
+    count, twice, columns = gated.shape
+    width = twice // 2
     found = pl.pallas_call(
         functools.partial(product_kernel, count, steps, first),
-        out_shape=[jax.ShapeDtypeStruct(gated.shape, jnp.float32), half, half]
+        out_shape=[jax.ShapeDtypeStruct(gated.shape, jnp.float32)] * 2
         + [jax.ShapeDtypeStruct((width, columns), jnp.bfloat16)] * len(first),
         in_specs=[WHOLE] * (6 + len(steps)),
-        out_specs=[WHOLE] * (3 + len(first)),
-        scratch_shapes=[pltpu.VMEM(gated.shape, jnp.float32)],
+        out_specs=[WHOLE] * (2 + len(first)),
         input_output_aliases={5: 0},
         compiler_params=pltpu.CompilerParams(vmem_limit_bytes=20 * MIB),
         cost_estimate=transform_cost(count, blocks[steps[0]], 7),
     )(*tabs, filt, gated, *[blocks[k] for k in steps])
-    return found[1], found[2], dict(zip(first, found[3:]))
-
-
-def inverse_kernel(steps, ih_ref, il_ref, sh, sl, *outs):
+    return found[1], dict(zip(first, found[2:]))
+
+
+def inverse_kernel(steps, ih_ref, il_ref, ss, *outs):
     for k, out in zip(steps, outs):
-        out[...] = inverse(ih_ref[...], il_ref[...], sh[partner(k)], sl[partner(k)])
-
-
-def inverses(steps, tabs, high, low):
-    count, twice, columns = high.shape
-    block = jax.ShapeDtypeStruct((twice // 2, columns), jnp.bfloat16)
+        out[...] = inverse(ih_ref[...], il_ref[...], ss[partner(k)])
+
+
+def inverses(steps, tabs, sums):
+    count, twice, columns = sums.shape
+    width = twice // 2
     found = pl.pallas_call(
         functools.partial(inverse_kernel, steps),
-        out_shape=[block] * len(steps),
-        in_specs=[WHOLE] * 4,
+        out_shape=[jax.ShapeDtypeStruct((width, columns), jnp.bfloat16)] * len(steps),
+        in_specs=[WHOLE] * 3,
         out_specs=[WHOLE] * len(steps),
         compiler_params=pltpu.CompilerParams(vmem_limit_bytes=16 * MIB),
-        cost_estimate=transform_cost(len(steps), block, 3),
-    )(*tabs[2:], high, low)
+        cost_estimate=transform_cost(len(steps), jax.ShapeDtypeStruct((width, columns), jnp.bfloat16), 3),
+    )(*tabs[2:], sums)
     return dict(zip(steps, found))
 
 
-def pre_kernel(steps, query_ref, skip_ref, *refs):
+def pre_kernel(steps, before, after, query_ref, skip_ref, *refs):
     count = len(steps)
+    refs = list(refs)
+    total = jnp.zeros((query_ref.shape[0], 128), jnp.float32)
+    if before:
+        refs.pop(0)
+        total = refs.pop(0)[...]
     convs, gates, (pre_ref, square_ref) = refs[:count], refs[count : 2 * count], refs[2 * count :]
     width, part = convs[0].shape
-    total = jnp.zeros((width, 128), jnp.float32)
     for at_k, k in enumerate(steps):
-        start = partner(k) * part if count > 1 else 0
+        start = partner(k) * part if part < query_ref.shape[1] else 0
         for at in range(0, part, 128):
             lanes, cols = pl.ds(at, 128), pl.ds(pl.multiple_of(start + at, 128), 128)
             gated = gates[at_k][:, lanes].astype(jnp.float32)
@@ -293,40 +291,52 @@
             pre = query_ref[:, cols].astype(jnp.float32) * (conv + skip_ref[:, cols] * gated)
             pre_ref[:, cols] = pre
             total = total + pre * pre
-    square_ref[...] = jnp.sum(total.T, axis=0, keepdims=True)
+    if after:
+        square_ref[...] = total
+    else:
+        square_ref[...] = jnp.sum(total.T, axis=0, keepdims=True)
 
 
 def together(blocks):
-    blocks = [blocks[k] for k in range(len(blocks))]
-    count = len(blocks)
+    count, width = len(blocks), blocks[0].shape[0]
     order = jnp.arange(count, dtype=jnp.int32) ^ lax.axis_index("tok")
-    stacked = jnp.take(jnp.stack(blocks), order, axis=0)
-    return {0: stacked.transpose(1, 0, 2).reshape(blocks[0].shape[0], -1)}
-
-
-def gated_output(query, skip, convs, gates):
+    stacked = jnp.take(jnp.stack([blocks[k] for k in range(count)]), order, axis=0)
+    return {0: stacked.transpose(1, 0, 2).reshape(width, -1)}
+
+
+def gated_output(query, skip, early, convs, gates):
     width, columns = query.shape
-    steps = list(convs)
+    groups = [early, [k for k in convs if k not in early]]
     if convs[0].shape[1] % 128:
-        convs, gates, steps = together(convs), together(gates), [0]
-    count = len(steps)
-    return pl.pallas_call(
-        functools.partial(pre_kernel, steps),
-        out_shape=(
-            jax.ShapeDtypeStruct((width, columns), jnp.float32),
-            jax.ShapeDtypeStruct((1, width), jnp.float32),
-        ),
-        in_specs=[WHOLE] * (2 + 2 * count),
-        out_specs=(WHOLE, WHOLE),
-        compiler_params=pltpu.CompilerParams(vmem_limit_bytes=16 * MIB),
-        cost_estimate=pl.CostEstimate(flops=6 * width * columns, bytes_accessed=10 * width * columns, transcendentals=0),
-    )(query, skip, *[convs[k] for k in steps], *[gates[k] for k in steps])
-
-
-def scale_kernel(channels, steps, pre_ref, square_ref, gain_ref, out_ref, buf, sems):
+        convs, gates, groups = together(convs), together(gates), [[0]]
+    found = []
+    for at, steps in enumerate(groups):
+        rest = at + 1 < len(groups)
+        found = pl.pallas_call(
+            functools.partial(pre_kernel, steps, at > 0, rest),
+            out_shape=(
+                jax.ShapeDtypeStruct((width, columns), jnp.float32),
+                jax.ShapeDtypeStruct((width, 128) if rest else (1, width), jnp.float32),
+            ),
+            in_specs=[WHOLE] * (2 + len(found) + 2 * len(steps)),
+            out_specs=(WHOLE, WHOLE),
+            input_output_aliases={2: 0} if found else {},
+            compiler_params=pltpu.CompilerParams(vmem_limit_bytes=16 * MIB),
+            cost_estimate=pl.CostEstimate(
+                flops=3 * width * columns, bytes_accessed=5 * width * columns, transcendentals=0
+            ),
+        )(query, skip, *found, *[convs[k] for k in steps], *[gates[k] for k in steps])
+    return found
+
+
+def scale_kernel(channels, steps, pre_ref, gain_ref, *refs):
+    squares, (out_ref, buf, sems) = refs[:-3], refs[-3:]
     width = pre_ref.shape[0]
     rows = width // steps
-    scale = lax.rsqrt(square_ref[...] * (1.0 / channels) + 1e-06)
+    total = squares[0][...]
+    for square in squares[1:]:
+        total = total + square[...]
+    scale = lax.rsqrt(total * (1.0 / channels) + 1e-06)
     scale = jnp.broadcast_to(scale, (128, width)).T
     copies = []
     for s in range(steps):
@@ -341,18 +351,18 @@
         copy.wait()
 
 
-def scaled(channels, pre, square, out_gain):
+def scaled(channels, pre, squares, out_gain):
     width, columns = pre.shape
     steps = 8
     return pl.pallas_call(
         functools.partial(scale_kernel, channels, steps),
         out_shape=jax.ShapeDtypeStruct((width, columns), jnp.float32),
-        in_specs=[WHOLE] * 3,
+        in_specs=[WHOLE] * (2 + len(squares)),
         out_specs=IN_HBM,
         scratch_shapes=[pltpu.VMEM((width, columns), jnp.float32), pltpu.SemaphoreType.DMA((steps,))],
         compiler_params=pltpu.CompilerParams(vmem_limit_bytes=16 * MIB),
         cost_estimate=pl.CostEstimate(flops=2 * width * columns, bytes_accessed=8 * width * columns, transcendentals=0),
-    )(pre, square, out_gain)
+    )(pre, out_gain, *squares)
 
 
 def local(query, key_in, value_in, filter_store, lag_of_block, skip, out_gain):
@@ -372,16 +382,18 @@
     filt = filter_spectra(lag_of_block, *tabs[:2], filts)
     early = order[: count // 2] + [0]
     gated = gated_spectra(count, *tabs[:2], {k: gates[k] for k in early})
-    first = order[:2]
-    high, low, found = products(count, first, tabs, filt, gated, {k: gates[k] for k in gates if k not in early})
-    rest = order[2:] + [0]
-    found.update(inverses(rest, tabs, high, low))
+    first = order[:1]
+    sums, found = products(first, tabs, filt, gated, {k: gates[k] for k in gates if k not in early})
+    found.update(inverses(order[1:] + [0], tabs, sums))
     for k in order:
         convs[k] = send(found[k], k, count)
     convs[0] = found[0]
-    pre, square = gated_output(query, skip[None, :], convs, mine)
-    square = lax.psum(square, "chan")
-    return scaled(columns * lax.axis_size("chan"), pre, square, out_gain[None, :])
+    pre, square = gated_output(query, skip[None, :], order[: count // 2] + [0], convs, mine)
+    others = lax.axis_size("chan")
+    squares = [square] + [
+        lax.ppermute(square, "chan", [(d, d ^ step) for d in range(others)]) for step in reversed(range(1, others))
+    ]
+    return scaled(columns * others, pre, squares, out_gain[None, :])
 
 
 def solution(mesh):

time: 89.5 us -> 87.4 us (0.977)
  blocking collectives: 5.71 us -> 0 us
  local copies, waits for them, and re-layouts: 3.71 us -> 5.62 us
  starting transfers between devices: 42.5 us -> 44 us
  waiting for transfers between devices: 24.5 us -> 25.5 us
    psum x1 -> x0, blocking collectives: 5.71 us -> none  [local(): square = lax.psum(square, 'chan')]
    ppermute x0 -> x3, waiting for transfers between devices: none -> 2.8 us  [local(): lax.ppermute(square, 'chan', [(d, d ^ step) for d in range(others)])]
    ppermute x0 -> x3, starting transfers between devices: none -> 1.93 us  [local(): lax.ppermute(square, 'chan', [(d, d ^ step) for d in range(others)])]
    unnamed x22 -> x26, local copies, waits for them, and re-layouts: 3.71 us -> 5.62 us
    ppermute x21, waiting for transfers between devices: 24.5 us -> 22.7 us  [send(): return lax.ppermute(block, 'tok', [(d, d ^ step) for d in range(count)])]
    pallas_call x2 -> x3, Pallas kernels: 2.28 us -> 2.4 us  [the longest x1 1.61 us: inverses(): pl.pallas_call(functools.partial(inverse_kernel, steps), out_shape=[jax.S...]
  transfers between devices with their start and end apart: 21 -> 24, of which waited for: 8 -> 11; matrix products, arithmetic and copies ran while one was open for 0% -> 0% of each run, Pallas kernels for 6% -> 6%
where the time goes in v12:
time: 87.4 us; the launch traced here: 87.2 us
  starting transfers between devices  44 us (50%)
  waiting for transfers between devices  25.5 us (29%)
  Pallas kernels  11.8 us (14%)
  local copies, waits for them, and re-layouts  5.62 us (6%)
    ppermute x21, starting transfers between devices, send(): return lax.ppermute(block, 'tok', [(d, d ^ step) for d in range(count)])  42.1 us
    ppermute x21, waiting for transfers between devices, send(): return lax.ppermute(block, 'tok', [(d, d ^ step) for d in range(count)])  22.7 us
    unnamed x26, local copies, waits for them, and re-layouts  5.62 us
    pallas_call x1, Pallas kernels, products(): pl.pallas_call(functools.partial(product_kernel, count, steps, first), ou...  4.1 us
    ppermute x3, waiting for transfers between devices, local(): lax.ppermute(square, 'chan', [(d, d ^ step) for d in range(others)])  2.8 us
    ppermute x3, starting transfers between devices, local(): lax.ppermute(square, 'chan', [(d, d ^ step) for d in range(others)])  1.93 us
    pallas_call x1, Pallas kernels, filter_spectra(): pl.pallas_call(functools.partial(filter_kernel, steps), out_shape=spectra...  1.93 us
  transfers between devices with their start and end apart: 24, of which 11 were waited for; matrix products, arithmetic and copies ran while one was open for 0% of the time, Pallas kernels for 6%

profile of v12, /device:TPU:0, one launch (start us, length us, event | category | flops | bytes accessed | tf_op | source)
XLA Modules:
  0.0 87.2 jit_solution(3864476176310273046)
XLA Ops:
  1.5 4.1 %collective-permute-start = (bf16[256,256]{1,0:T(8,128)(2,1)S(1)}, bf16[256,256]{1,0:T(8,128)(2,1)S(1)}, u32[]{:S(2)}, u32[]{:S(2)}) collective-permute-start(bf16[256,256]{1,0:T(8,128)(2,1)S(1)} %get-tuple-element.37), channel_id=1, source_target_pairs={{0,16},{4,20},{8,24},{12,28},{16,0},{20,4},{24,8},{28,12},{1,17},{... | collective-permute-start | bytes 393224 | tf_op jit(solution)/shard_map/ppermute | solution.py:40
  5.6 1.6 %collective-permute-start.1 = (bf16[256,256]{1,0:T(8,128)(2,1)S(1)}, bf16[256,256]{1,0:T(8,128)(2,1)S(1)}, u32[]{:S(2)}, u32[]{:S(2)}) collective-permute-start(bf16[256,256]{1,0:T(8,128)(2,1)S(1)} %get-tuple-element.38), channel_id=1, source_target_pairs={{0,8},{4,12},{8,0},{12,4},{16,24},{20,28},{24,16},{28,20},{1,9},{5... | collective-permute-start | bytes 393224 | tf_op jit(solution)/shard_map/ppermute | solution.py:40
  7.2 1.8 %collective-permute-start.3 = (bf16[256,256]{1,0:T(8,128)(2,1)S(1)}, bf16[256,256]{1,0:T(8,128)(2,1)S(1)}, u32[]{:S(2)}, u32[]{:S(2)}) collective-permute-start(bf16[256,256]{1,0:T(8,128)(2,1)S(1)} %get-tuple-element.40), channel_id=1, source_target_pairs={{0,12},{4,8},{8,4},{12,0},{16,28},{20,24},{24,20},{28,16},{1,13},{... | collective-permute-start | bytes 393224 | tf_op jit(solution)/shard_map/ppermute | solution.py:40
  9.0 3.5 %collective-permute-start.4 = (bf16[256,256]{1,0:T(8,128)(2,1)S(1)}, bf16[256,256]{1,0:T(8,128)(2,1)S(1)}, u32[]{:S(2)}, u32[]{:S(2)}) collective-permute-start(bf16[256,256]{1,0:T(8,128)(2,1)S(1)} %get-tuple-element.41), channel_id=1, source_target_pairs={{0,20},{4,16},{8,28},{12,24},{16,4},{20,0},{24,12},{28,8},{1,21},{... | collective-permute-start | bytes 393224 | tf_op jit(solution)/shard_map/ppermute | solution.py:40
  15.8 2.2 %collective-permute-start.8 = (bf16[256,256]{1,0:T(8,128)(2,1)S(1)}, bf16[256,256]{1,0:T(8,128)(2,1)S(1)}, u32[]{:S(2)}, u32[]{:S(2)}) collective-permute-start(bf16[256,256]{1,0:T(8,128)(2,1)S(1)} %get-tuple-element.49.refs_6_), channel_id=1, source_target_pairs={{0,8},{4,12},{8,0},{12,4},{16,24},{20,28},{24,16},{28,20},{1,9},{5... | collective-permute-start | bytes 393224 | tf_op jit(solution)/shard_map/ppermute | solution.py:40
  17.9 2.2 %collective-permute-start.9 = (bf16[256,256]{1,0:T(8,128)(2,1)S(1)}, bf16[256,256]{1,0:T(8,128)(2,1)S(1)}, u32[]{:S(2)}, u32[]{:S(2)}) collective-permute-start(bf16[256,256]{1,0:T(8,128)(2,1)S(1)} %get-tuple-element.50.refs_7_), channel_id=1, source_target_pairs={{0,24},{4,28},{8,16},{12,20},{16,8},{20,12},{24,0},{28,4},{1,25},{... | collective-permute-start | bytes 393224 | tf_op jit(solution)/shard_map/ppermute | solution.py:40
  20.5 5.8 %collective-permute-start.10 = (bf16[256,256]{1,0:T(8,128)(2,1)S(1)}, bf16[256,256]{1,0:T(8,128)(2,1)S(1)}, u32[]{:S(2)}, u32[]{:S(2)}) collective-permute-start(bf16[256,256]{1,0:T(8,128)(2,1)S(1)} %get-tuple-element.51.refs_8_), channel_id=1, source_target_pairs={{0,12},{4,8},{8,4},{12,0},{16,28},{20,24},{24,20},{28,16},{1,13},{... | collective-permute-start | bytes 393224 | tf_op jit(solution)/shard_map/ppermute | solution.py:40
  26.3 2.9 %collective-permute-done.4.refs_4_ = bf16[256,256]{1,0:T(8,128)(2,1)S(1)} collective-permute-done((bf16[256,256]{1,0:T(8,128)(2,1)S(1)}, bf16[256,256]{1,0:T(8,128)(2,1)S(1)}, u32[]{:S(2)}, u32[]{:S(2)}) %collective-permute-start.4) | collective-permute-done | bytes 131104 | tf_op jit(solution)/shard_map/ppermute | solution.py:40
  29.2 3.1 %collective-permute-start.5 = (bf16[256,256]{1,0:T(8,128)(2,1)S(1)}, bf16[256,256]{1,0:T(8,128)(2,1)S(1)}, u32[]{:S(2)}, u32[]{:S(2)}) collective-permute-start(bf16[256,256]{1,0:T(8,128)(2,1)S(1)} %get-tuple-element.42), channel_id=1, source_target_pairs={{0,28},{4,24},{8,20},{12,16},{16,12},{20,8},{24,4},{28,0},{1,29},{... | collective-permute-start | bytes 393224 | tf_op jit(solution)/shard_map/ppermute | solution.py:40
  32.4 3.0 %collective-permute-start.6 = (bf16[256,256]{1,0:T(8,128)(2,1)S(1)}, bf16[256,256]{1,0:T(8,128)(2,1)S(1)}, u32[]{:S(2)}, u32[]{:S(2)}) collective-permute-start(bf16[256,256]{1,0:T(8,128)(2,1)S(1)} %get-tuple-element.43), channel_id=1, source_target_pairs={{0,4},{4,0},{8,12},{12,8},{16,20},{20,16},{24,28},{28,24},{1,5},{5... | collective-permute-start | bytes 393224 | tf_op jit(solution)/shard_map/ppermute | solution.py:40
  35.4 1.8 %collective-permute-start.12 = (bf16[256,256]{1,0:T(8,128)(2,1)S(1)}, bf16[256,256]{1,0:T(8,128)(2,1)S(1)}, u32[]{:S(2)}, u32[]{:S(2)}) collective-permute-start(bf16[256,256]{1,0:T(8,128)(2,1)S(1)} %get-tuple-element.54.refs_6_), channel_id=1, source_target_pairs={{0,28},{4,24},{8,20},{12,16},{16,12},{20,8},{24,4},{28,0},{1,29},{... | collective-permute-start | bytes 393224 | tf_op jit(solution)/shard_map/ppermute | solution.py:40
  41.2 1.9 %shard_map.110.fs = f32[8,512,256]{2,1,0:T(8,128)S(1)} custom-call(s32[8]{0:T(128)S(1)} %copy-done.10, bf16[512,256]{1,0:T(8,128)(2,1)S(1)} %copy-done.7, bf16[512,256]{1,0:T(8,128)(2,1)S(1)} %copy-done.5, bf16[256,256]{1,0:T(8,128)(2,1)S(1)} %collective-permute-done.refs_0_, bf16[256,256]{1,0:T(8,128)(2,1)S(1)} %collective-permute-done.1.refs_1_, ...), custom_call_target="tpu_custom_call" | custom-call | flops 1073741824 | bytes 5242880 | tf_op jit(solution)/shard_map/pallas_call | solution.py:162
  43.1 7.4 %collective-permute-done.11.refs_0_ = bf16[256,256]{1,0:T(8,128)(2,1)S(1)} collective-permute-done((bf16[256,256]{1,0:T(8,128)(2,1)S(1)}, bf16[256,256]{1,0:T(8,128)(2,1)S(1)}, u32[]{:S(2)}, u32[]{:S(2)}) %collective-permute-start.11) | collective-permute-done | bytes 131104 | tf_op jit(solution)/shard_map/ppermute | solution.py:40
  50.6 4.1 %shard_map.113 = (f32[8,512,256]{2,1,0:T(8,128)S(1)}, f32[8,512,256]{2,1,0:T(8,128)S(1)}, bf16[256,256]{1,0:T(8,128)(2,1)S(1)}) custom-call(bf16[512,256]{1,0:T(8,128)(2,1)S(1)} %copy-done.7, bf16[512,256]{1,0:T(8,128)(2,1)S(1)} %copy-done.5, bf16[256,512]{1,0:T(8,128)(2,1)S(1)} %copy-done.12, ...), custom_call_target="tpu_custom_call", output_to_operand_aliasing={{0}: (5, {})} | custom-call | flops 3758096384 | bytes 5242880 | tf_op jit(solution)/shard_map/pallas_call | solution.py:244
  54.7 4.4 %collective-permute-start.14 = (bf16[256,256]{1,0:T(8,128)(2,1)S(1)}, bf16[256,256]{1,0:T(8,128)(2,1)S(1)}, u32[]{:S(2)}, u32[]{:S(2)}) collective-permute-start(bf16[256,256]{1,0:T(8,128)(2,1)S(1)} %get-tuple-element.56), channel_id=1, source_target_pairs={{0,16},{4,20},{8,24},{12,28},{16,0},{20,4},{24,8},{28,12},{1,17},{... | collective-permute-start | bytes 393224 | tf_op jit(solution)/shard_map/ppermute | solution.py:40
  59.1 1.6 %shard_map.114 = (bf16[256,256]{1,0:T(8,128)(2,1)S(1)}, bf16[256,256]{1,0:T(8,128)(2,1)S(1)}, bf16[256,256]{1,0:T(8,128)(2,1)S(1)}, bf16[256,256]{1,0:T(8,128)(2...) custom-call(bf16[256,512]{1,0:T(8,128)(2,1)S(1)} %copy-done.12, ...), custom_call_target="tpu_custom_call" | custom-call | flops 1409286144 | bytes 4587520 | tf_op jit(solution)/shard_map/pallas_call | solution.py:265
  60.8 2.3 %collective-permute-start.16 = (bf16[256,256]{1,0:T(8,128)(2,1)S(1)}, bf16[256,256]{1,0:T(8,128)(2,1)S(1)}, u32[]{:S(2)}, u32[]{:S(2)}) collective-permute-start(bf16[256,256]{1,0:T(8,128)(2,1)S(1)} %get-tuple-element.59), channel_id=1, source_target_pairs={{0,24},{4,28},{8,16},{12,20},{16,8},{20,12},{24,0},{28,4},{1,25},{... | collective-permute-start | bytes 393224 | tf_op jit(solution)/shard_map/ppermute | solution.py:40
  64.2 1.9 %collective-permute-start.18 = (bf16[256,256]{1,0:T(8,128)(2,1)S(1)}, bf16[256,256]{1,0:T(8,128)(2,1)S(1)}, u32[]{:S(2)}, u32[]{:S(2)}) collective-permute-start(bf16[256,256]{1,0:T(8,128)(2,1)S(1)} %get-tuple-element.64), channel_id=1, source_target_pairs={{0,20},{4,16},{8,28},{12,24},{16,4},{20,0},{24,12},{28,8},{1,21},{... | collective-permute-start | bytes 393224 | tf_op jit(solution)/shard_map/ppermute | solution.py:40
  66.6 1.8 %collective-permute-start.19 = (bf16[256,256]{1,0:T(8,128)(2,1)S(1)}, bf16[256,256]{1,0:T(8,128)(2,1)S(1)}, u32[]{:S(2)}, u32[]{:S(2)}) collective-permute-start(bf16[256,256]{1,0:T(8,128)(2,1)S(1)} %get-tuple-element.65), channel_id=1, source_target_pairs={{0,28},{4,24},{8,20},{12,16},{16,12},{20,8},{24,4},{28,0},{1,29},{... | collective-permute-start | bytes 393224 | tf_op jit(solution)/shard_map/ppermute | solution.py:40
  68.4 1.8 %collective-permute-done.15.refs_1_ = bf16[256,256]{1,0:T(8,128)(2,1)S(1)} collective-permute-done((bf16[256,256]{1,0:T(8,128)(2,1)S(1)}, bf16[256,256]{1,0:T(8,128)(2,1)S(1)}, u32[]{:S(2)}, u32[]{:S(2)}) %collective-permute-start.15) | collective-permute-done | bytes 131104 | tf_op jit(solution)/shard_map/ppermute | solution.py:40
  71.1 3.3 %collective-permute-done.17.refs_3_ = bf16[256,256]{1,0:T(8,128)(2,1)S(1)} collective-permute-done((bf16[256,256]{1,0:T(8,128)(2,1)S(1)}, bf16[256,256]{1,0:T(8,128)(2,1)S(1)}, u32[]{:S(2)}, u32[]{:S(2)}) %collective-permute-start.17) | collective-permute-done | bytes 131104 | tf_op jit(solution)/shard_map/ppermute | solution.py:40
  74.9 5.3 %collective-permute-done.18.refs_2_ = bf16[256,256]{1,0:T(8,128)(2,1)S(1)} collective-permute-done((bf16[256,256]{1,0:T(8,128)(2,1)S(1)}, bf16[256,256]{1,0:T(8,128)(2,1)S(1)}, u32[]{:S(2)}, u32[]{:S(2)}) %collective-permute-start.18) | collective-permute-done | bytes 131104 | tf_op jit(solution)/shard_map/ppermute | solution.py:40
  81.0 1.7 %collective-permute-start.22 = (f32[1,256]{1,0:T(1,128)S(1)}, f32[1,256]{1,0:T(1,128)S(1)}, u32[]{:S(2)}, u32[]{:S(2)}) collective-permute-start(f32[1,256]{1,0:T(1,128)S(1)} %get-tuple-element.68.refs_0_), channel_id=1, source_target_pairs={{0,2},{1,3},{2,0},{3,1},{4,6},{5,7},{6,4},{7,5},{8,10},{9,11},{10,... | collective-permute-start | bytes 3080 | tf_op jit(solution)/shard_map/ppermute | solution.py:394
  82.8 1.8 %collective-permute-done.22.refs_2_ = f32[1,256]{1,0:T(1,128)S(1)} collective-permute-done((f32[1,256]{1,0:T(1,128)S(1)}, f32[1,256]{1,0:T(1,128)S(1)}, u32[]{:S(2)}, u32[]{:S(2)}) %collective-permute-start.22) | collective-permute-done | bytes 1056 | tf_op jit(solution)/shard_map/ppermute | solution.py:394
  (59 shorter events, 15.7 us)
Async XLA Ops:
  1.5 14.2 %collective-permute-start = (bf16[256,256]{1,0:T(8,128)(2,1)S(1)}, bf16[256,256]{1,0:T(8,128)(2,1)S(1)}, u32[]{:S(2)}, u32[]{:S(2)}) collective-permute-start(bf16[256,256]{1,0:T(8,128)(2,1)S(1)} %get-tuple-element.37), channel_id=1, source_target_pairs={{0,16},{4,20},{8,24},{12,28},{16,0},{20,4},{24,8},{28,12},{1,17},{... | collective-permute-start | bytes 393224 | tf_op jit(solution)/shard_map/ppermute | solution.py:40
  5.6 10.2 %collective-permute-start.1 = (bf16[256,256]{1,0:T(8,128)(2,1)S(1)}, bf16[256,256]{1,0:T(8,128)(2,1)S(1)}, u32[]{:S(2)}, u32[]{:S(2)}) collective-permute-start(bf16[256,256]{1,0:T(8,128)(2,1)S(1)} %get-tuple-element.38), channel_id=1, source_target_pairs={{0,8},{4,12},{8,0},{12,4},{16,24},{20,28},{24,16},{28,20},{1,9},{5... | collective-permute-start | bytes 393224 | tf_op jit(solution)/shard_map/ppermute | solution.py:40
  7.2 10.8 %collective-permute-start.2 = (bf16[256,256]{1,0:T(8,128)(2,1)S(1)}, bf16[256,256]{1,0:T(8,128)(2,1)S(1)}, u32[]{:S(2)}, u32[]{:S(2)}) collective-permute-start(bf16[256,256]{1,0:T(8,128)(2,1)S(1)} %get-tuple-element.39), channel_id=1, source_target_pairs={{0,24},{4,28},{8,16},{12,20},{16,8},{20,12},{24,0},{28,4},{1,25},{... | collective-permute-start | bytes 393224 | tf_op jit(solution)/shard_map/ppermute | solution.py:40
  7.2 13.3 %collective-permute-start.3 = (bf16[256,256]{1,0:T(8,128)(2,1)S(1)}, bf16[256,256]{1,0:T(8,128)(2,1)S(1)}, u32[]{:S(2)}, u32[]{:S(2)}) collective-permute-start(bf16[256,256]{1,0:T(8,128)(2,1)S(1)} %get-tuple-element.40), channel_id=1, source_target_pairs={{0,12},{4,8},{8,4},{12,0},{16,28},{20,24},{24,20},{28,16},{1,13},{... | collective-permute-start | bytes 393224 | tf_op jit(solution)/shard_map/ppermute | solution.py:40
  9.0 20.3 %collective-permute-start.4 = (bf16[256,256]{1,0:T(8,128)(2,1)S(1)}, bf16[256,256]{1,0:T(8,128)(2,1)S(1)}, u32[]{:S(2)}, u32[]{:S(2)}) collective-permute-start(bf16[256,256]{1,0:T(8,128)(2,1)S(1)} %get-tuple-element.41), channel_id=1, source_target_pairs={{0,20},{4,16},{8,28},{12,24},{16,4},{20,0},{24,12},{28,8},{1,21},{... | collective-permute-start | bytes 393224 | tf_op jit(solution)/shard_map/ppermute | solution.py:40
  15.7 16.8 %collective-permute-start.7 = (bf16[256,256]{1,0:T(8,128)(2,1)S(1)}, bf16[256,256]{1,0:T(8,128)(2,1)S(1)}, u32[]{:S(2)}, u32[]{:S(2)}) collective-permute-start(bf16[256,256]{1,0:T(8,128)(2,1)S(1)} %get-tuple-element.48.refs_5_), channel_id=1, source_target_pairs={{0,16},{4,20},{8,24},{12,28},{16,0},{20,4},{24,8},{28,12},{1,17},{... | collective-permute-start | bytes 393224 | tf_op jit(solution)/shard_map/ppermute | solution.py:40
  15.8 19.6 %collective-permute-start.8 = (bf16[256,256]{1,0:T(8,128)(2,1)S(1)}, bf16[256,256]{1,0:T(8,128)(2,1)S(1)}, u32[]{:S(2)}, u32[]{:S(2)}) collective-permute-start(bf16[256,256]{1,0:T(8,128)(2,1)S(1)} %get-tuple-element.49.refs_6_), channel_id=1, source_target_pairs={{0,8},{4,12},{8,0},{12,4},{16,24},{20,28},{24,16},{28,20},{1,9},{5... | collective-permute-start | bytes 393224 | tf_op jit(solution)/shard_map/ppermute | solution.py:40
  17.9 17.5 %collective-permute-start.9 = (bf16[256,256]{1,0:T(8,128)(2,1)S(1)}, bf16[256,256]{1,0:T(8,128)(2,1)S(1)}, u32[]{:S(2)}, u32[]{:S(2)}) collective-permute-start(bf16[256,256]{1,0:T(8,128)(2,1)S(1)} %get-tuple-element.50.refs_7_), channel_id=1, source_target_pairs={{0,24},{4,28},{8,16},{12,20},{16,8},{20,12},{24,0},{28,4},{1,25},{... | collective-permute-start | bytes 393224 | tf_op jit(solution)/shard_map/ppermute | solution.py:40
  20.5 16.7 %collective-permute-start.10 = (bf16[256,256]{1,0:T(8,128)(2,1)S(1)}, bf16[256,256]{1,0:T(8,128)(2,1)S(1)}, u32[]{:S(2)}, u32[]{:S(2)}) collective-permute-start(bf16[256,256]{1,0:T(8,128)(2,1)S(1)} %get-tuple-element.51.refs_8_), channel_id=1, source_target_pairs={{0,12},{4,8},{8,4},{12,0},{16,28},{20,24},{24,20},{28,16},{1,13},{... | collective-permute-start | bytes 393224 | tf_op jit(solution)/shard_map/ppermute | solution.py:40
  29.2 11.9 %collective-permute-start.5 = (bf16[256,256]{1,0:T(8,128)(2,1)S(1)}, bf16[256,256]{1,0:T(8,128)(2,1)S(1)}, u32[]{:S(2)}, u32[]{:S(2)}) collective-permute-start(bf16[256,256]{1,0:T(8,128)(2,1)S(1)} %get-tuple-element.42), channel_id=1, source_target_pairs={{0,28},{4,24},{8,20},{12,16},{16,12},{20,8},{24,4},{28,0},{1,29},{... | collective-permute-start | bytes 393224 | tf_op jit(solution)/shard_map/ppermute | solution.py:40
  32.4 8.7 %collective-permute-start.6 = (bf16[256,256]{1,0:T(8,128)(2,1)S(1)}, bf16[256,256]{1,0:T(8,128)(2,1)S(1)}, u32[]{:S(2)}, u32[]{:S(2)}) collective-permute-start(bf16[256,256]{1,0:T(8,128)(2,1)S(1)} %get-tuple-element.43), channel_id=1, source_target_pairs={{0,4},{4,0},{8,12},{12,8},{16,20},{20,16},{24,28},{28,24},{1,5},{5... | collective-permute-start | bytes 393224 | tf_op jit(solution)/shard_map/ppermute | solution.py:40
  35.4 15.2 %collective-permute-start.11 = (bf16[256,256]{1,0:T(8,128)(2,1)S(1)}, bf16[256,256]{1,0:T(8,128)(2,1)S(1)}, u32[]{:S(2)}, u32[]{:S(2)}) collective-permute-start(bf16[256,256]{1,0:T(8,128)(2,1)S(1)} %get-tuple-element.53.refs_5_), channel_id=1, source_target_pairs={{0,20},{4,16},{8,28},{12,24},{16,4},{20,0},{24,12},{28,8},{1,21},{... | collective-permute-start | bytes 393224 | tf_op jit(solution)/shard_map/ppermute | solution.py:40
  35.4 15.2 %collective-permute-start.12 = (bf16[256,256]{1,0:T(8,128)(2,1)S(1)}, bf16[256,256]{1,0:T(8,128)(2,1)S(1)}, u32[]{:S(2)}, u32[]{:S(2)}) collective-permute-start(bf16[256,256]{1,0:T(8,128)(2,1)S(1)} %get-tuple-element.54.refs_6_), channel_id=1, source_target_pairs={{0,28},{4,24},{8,20},{12,16},{16,12},{20,8},{24,4},{28,0},{1,29},{... | collective-permute-start | bytes 393224 | tf_op jit(solution)/shard_map/ppermute | solution.py:40
  37.2 13.3 %collective-permute-start.13 = (bf16[256,256]{1,0:T(8,128)(2,1)S(1)}, bf16[256,256]{1,0:T(8,128)(2,1)S(1)}, u32[]{:S(2)}, u32[]{:S(2)}) collective-permute-start(bf16[256,256]{1,0:T(8,128)(2,1)S(1)} %get-tuple-element.55.refs_7_), channel_id=1, source_target_pairs={{0,4},{4,0},{8,12},{12,8},{16,20},{20,16},{24,28},{28,24},{1,5},{5... | collective-permute-start | bytes 393224 | tf_op jit(solution)/shard_map/ppermute | solution.py:40
  54.7 11.9 %collective-permute-start.14 = (bf16[256,256]{1,0:T(8,128)(2,1)S(1)}, bf16[256,256]{1,0:T(8,128)(2,1)S(1)}, u32[]{:S(2)}, u32[]{:S(2)}) collective-permute-start(bf16[256,256]{1,0:T(8,128)(2,1)S(1)} %get-tuple-element.56), channel_id=1, source_target_pairs={{0,16},{4,20},{8,24},{12,28},{16,0},{20,4},{24,8},{28,12},{1,17},{... | collective-permute-start | bytes 393224 | tf_op jit(solution)/shard_map/ppermute | solution.py:40
  60.7 9.6 %collective-permute-start.15 = (bf16[256,256]{1,0:T(8,128)(2,1)S(1)}, bf16[256,256]{1,0:T(8,128)(2,1)S(1)}, u32[]{:S(2)}, u32[]{:S(2)}) collective-permute-start(bf16[256,256]{1,0:T(8,128)(2,1)S(1)} %get-tuple-element.58), channel_id=1, source_target_pairs={{0,8},{4,12},{8,0},{12,4},{16,24},{20,28},{24,16},{28,20},{1,9},{5... | collective-permute-start | bytes 393224 | tf_op jit(solution)/shard_map/ppermute | solution.py:40
  60.8 10.3 %collective-permute-start.16 = (bf16[256,256]{1,0:T(8,128)(2,1)S(1)}, bf16[256,256]{1,0:T(8,128)(2,1)S(1)}, u32[]{:S(2)}, u32[]{:S(2)}) collective-permute-start(bf16[256,256]{1,0:T(8,128)(2,1)S(1)} %get-tuple-element.59), channel_id=1, source_target_pairs={{0,24},{4,28},{8,16},{12,20},{16,8},{20,12},{24,0},{28,4},{1,25},{... | collective-permute-start | bytes 393224 | tf_op jit(solution)/shard_map/ppermute | solution.py:40
  63.0 11.4 %collective-permute-start.17 = (bf16[256,256]{1,0:T(8,128)(2,1)S(1)}, bf16[256,256]{1,0:T(8,128)(2,1)S(1)}, u32[]{:S(2)}, u32[]{:S(2)}) collective-permute-start(bf16[256,256]{1,0:T(8,128)(2,1)S(1)} %get-tuple-element.60), channel_id=1, source_target_pairs={{0,12},{4,8},{8,4},{12,0},{16,28},{20,24},{24,20},{28,16},{1,13},{... | collective-permute-start | bytes 393224 | tf_op jit(solution)/shard_map/ppermute | solution.py:40
  64.2 15.9 %collective-permute-start.18 = (bf16[256,256]{1,0:T(8,128)(2,1)S(1)}, bf16[256,256]{1,0:T(8,128)(2,1)S(1)}, u32[]{:S(2)}, u32[]{:S(2)}) collective-permute-start(bf16[256,256]{1,0:T(8,128)(2,1)S(1)} %get-tuple-element.64), channel_id=1, source_target_pairs={{0,20},{4,16},{8,28},{12,24},{16,4},{20,0},{24,12},{28,8},{1,21},{... | collective-permute-start | bytes 393224 | tf_op jit(solution)/shard_map/ppermute | solution.py:40
  66.6 13.5 %collective-permute-start.19 = (bf16[256,256]{1,0:T(8,128)(2,1)S(1)}, bf16[256,256]{1,0:T(8,128)(2,1)S(1)}, u32[]{:S(2)}, u32[]{:S(2)}) collective-permute-start(bf16[256,256]{1,0:T(8,128)(2,1)S(1)} %get-tuple-element.65), channel_id=1, source_target_pairs={{0,28},{4,24},{8,20},{12,16},{16,12},{20,8},{24,4},{28,0},{1,29},{... | collective-permute-start | bytes 393224 | tf_op jit(solution)/shard_map/ppermute | solution.py:40
  70.3 10.3 %collective-permute-start.20 = (bf16[256,256]{1,0:T(8,128)(2,1)S(1)}, bf16[256,256]{1,0:T(8,128)(2,1)S(1)}, u32[]{:S(2)}, u32[]{:S(2)}) collective-permute-start(bf16[256,256]{1,0:T(8,128)(2,1)S(1)} %get-tuple-element.66), channel_id=1, source_target_pairs={{0,4},{4,0},{8,12},{12,8},{16,20},{20,16},{24,28},{28,24},{1,5},{5... | collective-permute-start | bytes 393224 | tf_op jit(solution)/shard_map/ppermute | solution.py:40
  80.9 1.9 %collective-permute-start.23 = (f32[1,256]{1,0:T(1,128)S(1)}, f32[1,256]{1,0:T(1,128)S(1)}, u32[]{:S(2)}, u32[]{:S(2)}) collective-permute-start(f32[1,256]{1,0:T(1,128)S(1)} %get-tuple-element.68.refs_0_), channel_id=1, source_target_pairs={{0,1},{1,0},{2,3},{3,2},{4,5},{5,4},{6,7},{7,6},{8,9},{9,8},{10,11... | collective-permute-start | bytes 3080 | tf_op jit(solution)/shard_map/ppermute | solution.py:394
  81.0 3.6 %collective-permute-start.22 = (f32[1,256]{1,0:T(1,128)S(1)}, f32[1,256]{1,0:T(1,128)S(1)}, u32[]{:S(2)}, u32[]{:S(2)}) collective-permute-start(f32[1,256]{1,0:T(1,128)S(1)} %get-tuple-element.68.refs_0_), channel_id=1, source_target_pairs={{0,2},{1,3},{2,0},{3,1},{4,6},{5,7},{6,4},{7,5},{8,10},{9,11},{10,... | collective-permute-start | bytes 3080 | tf_op jit(solution)/shard_map/ppermute | solution.py:394
  82.6 3.0 %collective-permute-start.21 = (f32[1,256]{1,0:T(1,128)S(1)}, f32[1,256]{1,0:T(1,128)S(1)}, u32[]{:S(2)}, u32[]{:S(2)}) collective-permute-start(f32[1,256]{1,0:T(1,128)S(1)} %get-tuple-element.68.refs_0_), channel_id=1, source_target_pairs={{0,3},{1,2},{2,1},{3,0},{4,7},{5,6},{6,5},{7,4},{8,11},{9,10},{10,... | collective-permute-start | bytes 3080 | tf_op jit(solution)/shard_map/ppermute | solution.py:394
  (13 other events, 208.8 us)

commit v13 on v10

--- a/solution.py
+++ b/solution.py
@@ -54,35 +54,14 @@
     return pl.ds(pl.multiple_of(partner(step) * part, 128), part)
 
 
-def piece(x, step, part):
-    return lax.dynamic_slice_in_dim(x, partner(step) * part, part, axis=1)
-
-
-def split_kernel(steps, part, filt_ref, *refs):
-    outs, sems = refs[:-1], refs[-1]
+def split_kernel(count, part, filt_ref, *refs):
+    outs, sems = refs[:count], refs[count]
     copies = []
-    for at, k in enumerate(steps):
-        copies.append(pltpu.make_async_copy(filt_ref.at[:, columns_of(k, part)], outs[at], sems.at[at]))
+    for k in range(count):
+        copies.append(pltpu.make_async_copy(filt_ref.at[:, columns_of(k, part)], outs[k], sems.at[k]))
         copies[-1].start()
     for copy in copies:
         copy.wait()
-
-
-def split(count, steps, filter_store):
-    width, columns = filter_store.shape
-    part = columns // count
-    if part % 128:
-        return {k: piece(filter_store, k, part) for k in steps}
-    found = pl.pallas_call(
-        functools.partial(split_kernel, steps, part),
-        out_shape=[jax.ShapeDtypeStruct((width, part), jnp.bfloat16)] * len(steps),
-        in_specs=[IN_HBM],
-        out_specs=[WHOLE] * len(steps),
-        scratch_shapes=[pltpu.SemaphoreType.DMA((len(steps),))],
-        compiler_params=pltpu.CompilerParams(vmem_limit_bytes=16 * MIB),
-        cost_estimate=pl.CostEstimate(flops=0, bytes_accessed=4 * width * columns, transcendentals=0),
-    )(filter_store)
-    return dict(zip(steps, found))
 
 
 def gate_kernel(count, part, key_ref, value_ref, *refs):
@@ -105,12 +84,33 @@
         outs[k][...] = product.astype(jnp.bfloat16)
 
 
+def pieces(x, count):
+    part = x.shape[1] // count
+    return [lax.dynamic_slice_in_dim(x, partner(k) * part, part, axis=1) for k in range(count)]
+
+
+def split(count, filter_store):
+    width, columns = filter_store.shape
+    part = columns // count
+    if part % 128:
+        return pieces(filter_store, count)
+    return pl.pallas_call(
+        functools.partial(split_kernel, count, part),
+        out_shape=[jax.ShapeDtypeStruct((width, part), jnp.bfloat16)] * count,
+        in_specs=[IN_HBM],
+        out_specs=[WHOLE] * count,
+        scratch_shapes=[pltpu.SemaphoreType.DMA((count,))],
+        compiler_params=pltpu.CompilerParams(vmem_limit_bytes=BIG),
+        cost_estimate=pl.CostEstimate(flops=0, bytes_accessed=4 * width * columns, transcendentals=0),
+    )(filter_store)
+
+
 def gate(count, key_in, value_in):
     width, columns = key_in.shape
     part = columns // count
     if part % 128:
         gated = (key_in.astype(jnp.float32) * value_in.astype(jnp.float32)).astype(jnp.bfloat16)
-        return [piece(gated, k, part) for k in range(count)]
+        return pieces(gated, count)
     block = pltpu.VMEM((count, width, part), jnp.bfloat16)
     return pl.pallas_call(
         functools.partial(gate_kernel, count, part),
@@ -118,7 +118,7 @@
         in_specs=[IN_HBM] * 2,
         out_specs=[WHOLE] * count,
         scratch_shapes=[block, block, pltpu.SemaphoreType.DMA((2, count))],
-        compiler_params=pltpu.CompilerParams(vmem_limit_bytes=16 * MIB),
+        compiler_params=pltpu.CompilerParams(vmem_limit_bytes=BIG),
         cost_estimate=pl.CostEstimate(flops=width * columns, bytes_accessed=6 * width * columns, transcendentals=0),
     )(key_in, value_in)
 
@@ -129,14 +129,6 @@
 
 def transform(high, low, block):
     return dot(high, block) + dot(low, block)
-
-
-def filter_kernel(steps, lag_ref, high_ref, low_ref, *refs):
-    blocks, out = refs[:-1], refs[-1]
-    count = len(steps)
-    for at, (k, block) in enumerate(zip(steps, blocks)):
-        out[at] = jnp.zeros(out.shape[1:], jnp.float32)
-        out[count + lag_ref[partner(k)]] = transform(high_ref[...], low_ref[...], block[...])
 
 
 def transform_cost(count, width, columns, passes):
@@ -147,20 +139,6 @@
     )
 
 
-def filter_spectra(lag_of_block, high, low, blocks):
-    steps = list(blocks)
-    count = len(steps)
-    width, columns = blocks[0].shape
-    return pl.pallas_call(
-        functools.partial(filter_kernel, steps),
-        out_shape=jax.ShapeDtypeStruct((2 * count, 2 * width, columns), jnp.float32),
-        in_specs=[pl.BlockSpec(memory_space=pltpu.SMEM)] + [WHOLE] * (2 + count),
-        out_specs=WHOLE,
-        compiler_params=pltpu.CompilerParams(vmem_limit_bytes=16 * MIB),
-        cost_estimate=transform_cost(count, width, columns, 2),
-    )(lag_of_block, high, low, *[blocks[k] for k in steps])
-
-
 def tiles(width, columns, tile):
     half = width // 16
     lane = min(128, columns)
@@ -180,14 +158,34 @@
         run(row, -1)
 
 
-def early_kernel(count, steps, fh_ref, fl_ref, fs, *refs):
-    blocks, (ss, gs) = refs[: len(steps)], refs[len(steps) :]
+def gated_kernel(steps, high_ref, low_ref, *refs):
+    blocks, out = refs[:-1], refs[-1]
+    for k in range(out.shape[0]):
+        if k not in steps:
+            out[partner(k)] = jnp.zeros(out.shape[1:], jnp.float32)
+    for k, block in zip(steps, blocks):
+        out[partner(k)] = transform(high_ref[...], low_ref[...], block[...])
+
+
+def gated_spectra(count, high, low, blocks):
+    steps = list(blocks)
     width, columns = blocks[0].shape
-    for k in range(count):
-        if k not in steps:
-            gs[partner(k)] = jnp.zeros(gs.shape[1:], jnp.float32)
-    for k, block in zip(steps, blocks):
-        gs[partner(k)] = transform(fh_ref[...], fl_ref[...], block[...])
+    return pl.pallas_call(
+        functools.partial(gated_kernel, steps),
+        out_shape=jax.ShapeDtypeStruct((count, 2 * width, columns), jnp.float32),
+        in_specs=[WHOLE] * (2 + len(steps)),
+        out_specs=WHOLE,
+        compiler_params=pltpu.CompilerParams(vmem_limit_bytes=16 * MIB),
+        cost_estimate=transform_cost(len(steps), width, columns, 2),
+    )(high, low, *[blocks[k] for k in steps])
+
+
+def early_kernel(count, steps, lag_ref, high_ref, low_ref, *refs):
+    blocks, (gs, fs, ss) = refs[:count], refs[count:]
+    width, columns = gs.shape[1] // 2, gs.shape[2]
+    for at, (k, block) in enumerate(zip(steps, blocks)):
+        fs[at] = jnp.zeros(fs.shape[1:], jnp.float32)
+        fs[count + lag_ref[partner(k)]] = transform(high_ref[...], low_ref[...], block[...])
 
     def tile(re_rows, im_rows, lanes, sign):
         f = [(fs[count + i, re_rows, lanes], fs[count + i, im_rows, lanes]) for i in range(count)]
@@ -213,20 +211,20 @@
     tiles(width, columns, tile)
 
 
-def early_products(tabs, filt, blocks):
+def early_products(lag_of_block, high, low, blocks, gated):
     steps = list(blocks)
-    count = filt.shape[0] // 2
-    width, columns = blocks[0].shape
-    shape = (count, 2 * width, columns)
+    count, twice, columns = gated.shape
     return pl.pallas_call(
         functools.partial(early_kernel, count, steps),
-        out_shape=jax.ShapeDtypeStruct(shape, jnp.float32),
-        in_specs=[WHOLE] * (3 + len(steps)),
-        out_specs=WHOLE,
-        scratch_shapes=[pltpu.VMEM(shape, jnp.float32)],
+        out_shape=[
+            jax.ShapeDtypeStruct((2 * count, twice, columns), jnp.float32),
+            jax.ShapeDtypeStruct(gated.shape, jnp.float32),
+        ],
+        in_specs=[pl.BlockSpec(memory_space=pltpu.SMEM)] + [WHOLE] * (3 + count),
+        out_specs=[WHOLE, WHOLE],
         compiler_params=pltpu.CompilerParams(vmem_limit_bytes=16 * MIB),
-        cost_estimate=transform_cost(count, width, columns, 4),
-    )(*tabs[:2], filt, *[blocks[k] for k in steps])
+        cost_estimate=transform_cost(count, twice // 2, columns, 2),
+    )(lag_of_block, high, low, *[blocks[k] for k in steps], gated)
 
 
 def inverse(table_high, table_low, total):
@@ -240,25 +238,30 @@
     width, columns = blocks[0].shape
     for at, block in enumerate(blocks):
         gs[at] = transform(fh_ref[...], fl_ref[...], block[...])
-    starts = [count - partner(k) for k in steps]
+    shifted = [fs.at[pl.ds(count - partner(k), count)] for k in steps]
 
     def tile(re_rows, im_rows, lanes, sign):
-        g = [(gs[at, re_rows, lanes], gs[at, im_rows, lanes]) for at in range(len(steps))]
-        last = None
+        def both(ref, i):
+            return ref[i, re_rows, lanes], ref[i, im_rows, lanes]
+
+        g = [both(gs, at) for at in range(len(steps))]
+        f = [[both(view, j) for view in shifted] for j in range(count)]
+        s = [both(ss, j) for j in range(count)]
+        d = []
         for j in range(count):
             d_re = d_im = None
-            for start, (g_re, g_im) in zip(starts, g):
-                f_re, f_im = fs[start + j, re_rows, lanes], fs[start + j, im_rows, lanes]
+            for (f_re, f_im), (g_re, g_im) in zip(f[j], g):
                 p_re, p_im = f_re * g_re - f_im * g_im, f_re * g_im + f_im * g_re
                 d_re, d_im = (p_re, p_im) if d_re is None else (d_re + p_re, d_im + p_im)
-            s_re, s_im = ss[j, re_rows, lanes] + d_re, ss[j, im_rows, lanes] + d_im
-            if last is not None and sign > 0:
-                s_re, s_im = s_re - last[1], s_im + last[0]
-            elif last is not None:
-                s_re, s_im = s_re + last[1], s_im - last[0]
+            d.append((d_re, d_im))
+        for j in range(count):
+            s_re, s_im = s[j][0] + d[j][0], s[j][1] + d[j][1]
+            if j and sign > 0:
+                s_re, s_im = s_re - d[j - 1][1], s_im + d[j - 1][0]
+            elif j:
+                s_re, s_im = s_re + d[j - 1][1], s_im - d[j - 1][0]
             ss[j, re_rows, lanes] = s_re
             ss[j, im_rows, lanes] = s_im
-            last = (d_re, d_im)
 
     tiles(width, columns, tile)
     for k, out in zip(first, outs):
@@ -398,22 +401,25 @@
     width, columns = query.shape
     count = lax.axis_size("tok")
     tabs = [jnp.asarray(t) for t in tables(width)]
-    part = columns // count
+    own = split(count, filter_store)
     order = sending_order(count)
-    gated_order = order[:-3] + order[-1:] + order[-3:-1]
-    own = split(count, order[1:] + [0], filter_store)
-    own[order[0]] = piece(filter_store, order[0], part)
-    own[0], key_in, value_in = lax.optimization_barrier((own[0], key_in, value_in))
+    gates, convs = {}, {}
+    filts = {k: send(own[k], k, count) for k in order}
+    filts[order[0]], key_in, value_in = lax.optimization_barrier((filts[order[0]], key_in, value_in))
     mine = gate(count, key_in, value_in)
-    filts = {k: send(own[k], k, count) for k in order}
-    gates = {k: send(mine[k], k, count) for k in gated_order}
+    for k in order:
+        gates[k] = send(mine[k], k, count)
     filts[0], gates[0] = own[0], mine[0]
-    late = gated_order[-2:]
-    filt = filter_spectra(lag_of_block, *tabs[:2], filts)
-    sums = early_products(tabs, filt, {k: gates[k] for k in gates if k not in late})
-    sums, found = late_products(order[:1], tabs, filt, sums, {k: gates[k] for k in late})
+    early = order[: count // 2] + [0]
+    gated = gated_spectra(count, *tabs[:2], {k: gates[k] for k in early})
+    filt, sums = early_products(lag_of_block, *tabs[:2], filts, gated)
+    sums, found = late_products(order[:1], tabs, filt, sums, {k: gates[k] for k in gates if k not in early})
     found.update(inverses(order[1:] + [0], tabs, sums))
-    convs = {k: send(found[k], k, count) for k in order}
+    for at, k in enumerate(order):
+        block = found[k]
+        if at == 6:
+            block, convs[order[0]] = lax.optimization_barrier((block, convs[order[0]]))
+        convs[k] = send(block, k, count)
     convs[0] = found[0]
     pre, square = gated_output(query, skip[None, :], order[: count // 2] + [0], convs, mine)
     others = lax.axis_size("chan")

time: 89.2 us -> 89 us (level)
  starting transfers between devices: 43.4 us -> 48.8 us
  waiting for transfers between devices: 23.4 us -> 19.6 us
  local copies, waits for them, and re-layouts: 7.17 us -> 5.62 us
    ppermute x21, starting transfers between devices: 41.5 us -> 46.9 us  [send(): return lax.ppermute(block, 'tok', [(d, d ^ step) for d in range(count)])]
    ppermute x21, waiting for transfers between devices: 20.6 us -> 16.8 us  [send(): return lax.ppermute(block, 'tok', [(d, d ^ step) for d in range(count)])]
    dynamic_slice x1 -> x0, local copies, waits for them, and re-layouts: 0.91 us -> none  [piece(): return lax.dynamic_slice_in_dim(x, partner(step) * part, part, axis=1)]
    unnamed x22 -> x24, local copies, waits for them, and re-layouts: 6.26 us -> 5.62 us
  transfers between devices with their start and end apart: 24 -> 24, of which waited for: 9 -> 8; matrix products, arithmetic and copies ran while one was open for 0% -> 0% of each run, Pallas kernels for 10% -> 10%
where the time goes in v13:
time: 89 us; the launch traced here: 88.7 us
  starting transfers between devices  48.8 us (55%)
  waiting for transfers between devices  19.6 us (22%)
  Pallas kernels  14.4 us (16%)
  local copies, waits for them, and re-layouts  5.62 us (6%)
    ppermute x21, starting transfers between devices, send(): return lax.ppermute(block, 'tok', [(d, d ^ step) for d in range(count)])  46.9 us
    ppermute x21, waiting for transfers between devices, send(): return lax.ppermute(block, 'tok', [(d, d ^ step) for d in range(count)])  16.8 us
    unnamed x24, local copies, waits for them, and re-layouts  5.62 us
    pallas_call x1, Pallas kernels, early_products(): pl.pallas_call(functools.partial(early_kernel, count, steps), out_shape=[...  4.87 us
    pallas_call x1, Pallas kernels, late_products(): pl.pallas_call(functools.partial(late_kernel, count, steps, first), out_s...  3.74 us
    ppermute x3, waiting for transfers between devices, local(): lax.ppermute(square, 'chan', [(d, d ^ step) for d in range(others)])  2.85 us
    ppermute x3, starting transfers between devices, local(): lax.ppermute(square, 'chan', [(d, d ^ step) for d in range(others)])  1.93 us
  transfers between devices with their start and end apart: 24, of which 8 were waited for; matrix products, arithmetic and copies ran while one was open for 0% of the time, Pallas kernels for 10%

profile of v13, /device:TPU:0, one launch (start us, length us, event | category | flops | bytes accessed | tf_op | source)
XLA Modules:
  0.0 88.7 jit_solution(16423098248045426913)
XLA Ops:
  1.5 4.1 %collective-permute-start = (bf16[256,256]{1,0:T(8,128)(2,1)S(1)}, bf16[256,256]{1,0:T(8,128)(2,1)S(1)}, u32[]{:S(2)}, u32[]{:S(2)}) collective-permute-start(bf16[256,256]{1,0:T(8,128)(2,1)S(1)} %get-tuple-element.41), channel_id=1, source_target_pairs={{0,16},{4,20},{8,24},{12,28},{16,0},{20,4},{24,8},{28,12},{1,17},{... | collective-permute-start | bytes 393224 | tf_op jit(solution)/shard_map/ppermute | solution.py:40
  5.6 1.6 %collective-permute-start.1 = (bf16[256,256]{1,0:T(8,128)(2,1)S(1)}, bf16[256,256]{1,0:T(8,128)(2,1)S(1)}, u32[]{:S(2)}, u32[]{:S(2)}) collective-permute-start(bf16[256,256]{1,0:T(8,128)(2,1)S(1)} %get-tuple-element.43), channel_id=1, source_target_pairs={{0,8},{4,12},{8,0},{12,4},{16,24},{20,28},{24,16},{28,20},{1,9},{5... | collective-permute-start | bytes 393224 | tf_op jit(solution)/shard_map/ppermute | solution.py:40
  7.2 1.8 %collective-permute-start.3 = (bf16[256,256]{1,0:T(8,128)(2,1)S(1)}, bf16[256,256]{1,0:T(8,128)(2,1)S(1)}, u32[]{:S(2)}, u32[]{:S(2)}) collective-permute-start(bf16[256,256]{1,0:T(8,128)(2,1)S(1)} %get-tuple-element.45), channel_id=1, source_target_pairs={{0,12},{4,8},{8,4},{12,0},{16,28},{20,24},{24,20},{28,16},{1,13},{... | collective-permute-start | bytes 393224 | tf_op jit(solution)/shard_map/ppermute | solution.py:40
  9.0 3.5 %collective-permute-start.4 = (bf16[256,256]{1,0:T(8,128)(2,1)S(1)}, bf16[256,256]{1,0:T(8,128)(2,1)S(1)}, u32[]{:S(2)}, u32[]{:S(2)}) collective-permute-start(bf16[256,256]{1,0:T(8,128)(2,1)S(1)} %get-tuple-element.46), channel_id=1, source_target_pairs={{0,20},{4,16},{8,28},{12,24},{16,4},{20,0},{24,12},{28,8},{1,21},{... | collective-permute-start | bytes 393224 | tf_op jit(solution)/shard_map/ppermute | solution.py:40
  17.9 4.2 %collective-permute-start.7 = (bf16[256,256]{1,0:T(8,128)(2,1)S(1)}, bf16[256,256]{1,0:T(8,128)(2,1)S(1)}, u32[]{:S(2)}, u32[]{:S(2)}) collective-permute-start(bf16[256,256]{1,0:T(8,128)(2,1)S(1)} %get-tuple-element.52.refs_5_), channel_id=1, source_target_pairs={{0,16},{4,20},{8,24},{12,28},{16,0},{20,4},{24,8},{28,12},{1,17},{... | collective-permute-start | bytes 393224 | tf_op jit(solution)/shard_map/ppermute | solution.py:40
  22.1 1.5 %collective-permute-start.9 = (bf16[256,256]{1,0:T(8,128)(2,1)S(1)}, bf16[256,256]{1,0:T(8,128)(2,1)S(1)}, u32[]{:S(2)}, u32[]{:S(2)}) collective-permute-start(bf16[256,256]{1,0:T(8,128)(2,1)S(1)} %get-tuple-element.54.refs_7_), channel_id=1, source_target_pairs={{0,24},{4,28},{8,16},{12,20},{16,8},{20,12},{24,0},{28,4},{1,25},{... | collective-permute-start | bytes 393224 | tf_op jit(solution)/shard_map/ppermute | solution.py:40
  23.6 2.0 %collective-permute-done.4.refs_4_ = bf16[256,256]{1,0:T(8,128)(2,1)S(1)} collective-permute-done((bf16[256,256]{1,0:T(8,128)(2,1)S(1)}, bf16[256,256]{1,0:T(8,128)(2,1)S(1)}, u32[]{:S(2)}, u32[]{:S(2)}) %collective-permute-start.4) | collective-permute-done | bytes 131104 | tf_op jit(solution)/shard_map/ppermute | solution.py:40
  25.6 3.9 %collective-permute-start.5 = (bf16[256,256]{1,0:T(8,128)(2,1)S(1)}, bf16[256,256]{1,0:T(8,128)(2,1)S(1)}, u32[]{:S(2)}, u32[]{:S(2)}) collective-permute-start(bf16[256,256]{1,0:T(8,128)(2,1)S(1)} %get-tuple-element.47), channel_id=1, source_target_pairs={{0,28},{4,24},{8,20},{12,16},{16,12},{20,8},{24,4},{28,0},{1,29},{... | collective-permute-start | bytes 393224 | tf_op jit(solution)/shard_map/ppermute | solution.py:40
  29.5 1.5 %collective-permute-start.6 = (bf16[256,256]{1,0:T(8,128)(2,1)S(1)}, bf16[256,256]{1,0:T(8,128)(2,1)S(1)}, u32[]{:S(2)}, u32[]{:S(2)}) collective-permute-start(bf16[256,256]{1,0:T(8,128)(2,1)S(1)} %get-tuple-element.48), channel_id=1, source_target_pairs={{0,4},{4,0},{8,12},{12,8},{16,20},{20,16},{24,28},{28,24},{1,5},{5... | collective-permute-start | bytes 393224 | tf_op jit(solution)/shard_map/ppermute | solution.py:40
  31.0 10.8 %collective-permute-start.12 = (bf16[256,256]{1,0:T(8,128)(2,1)S(1)}, bf16[256,256]{1,0:T(8,128)(2,1)S(1)}, u32[]{:S(2)}, u32[]{:S(2)}) collective-permute-start(bf16[256,256]{1,0:T(8,128)(2,1)S(1)} %get-tuple-element.60.refs_6_), channel_id=1, source_target_pairs={{0,28},{4,24},{8,20},{12,16},{16,12},{20,8},{24,4},{28,0},{1,29},{... | collective-permute-start | bytes 393224 | tf_op jit(solution)/shard_map/ppermute | solution.py:40
  41.8 1.9 %collective-permute-start.13 = (bf16[256,256]{1,0:T(8,128)(2,1)S(1)}, bf16[256,256]{1,0:T(8,128)(2,1)S(1)}, u32[]{:S(2)}, u32[]{:S(2)}) collective-permute-start(bf16[256,256]{1,0:T(8,128)(2,1)S(1)} %get-tuple-element.61.refs_7_), channel_id=1, source_target_pairs={{0,4},{4,0},{8,12},{12,8},{16,20},{20,16},{24,28},{28,24},{1,5},{5... | collective-permute-start | bytes 393224 | tf_op jit(solution)/shard_map/ppermute | solution.py:40
  46.7 4.9 %shard_map.112 = (f32[16,512,256]{2,1,0:T(8,128)S(1)}, f32[8,512,256]{2,1,0:T(8,128)S(1)}) custom-call(s32[8]{0:T(128)S(1)} %copy-done.11, bf16[512,256]{1,0:T(8,128)(2,1)S(1)} %copy-done.1, bf16[512,256]{1,0:T(8,128)(2,1)S(1)} %copy-done.3, bf16[256,256]{1,0:T(8,128)(2,1)S(1)} %collective-permute-done.refs_0_, ...), custom_call_target="tpu_custom_call" | custom-call | flops 1073741824 | bytes 5242880 | tf_op jit(solution)/shard_map/pallas_call | solution.py:217
  51.6 3.7 %shard_map.113 = (f32[8,512,256]{2,1,0:T(8,128)S(1)}, bf16[256,256]{1,0:T(8,128)(2,1)S(1)}) custom-call(bf16[512,256]{1,0:T(8,128)(2,1)S(1)} %copy-done.2, bf16[512,256]{1,0:T(8,128)(2,1)S(1)} %copy-done.3, bf16[256,512]{1,0:T(8,128)(2,1)S(1)} %copy-done.7, bf16[256,512]{1,0:T(8,128)(2,1)S(1)} %copy-done.8, ...), custom_call_target="tpu_custom_call", output_to_operand_aliasing={{0}: (5, {})} | custom-call | flops 1610612736 | bytes 5242880 | tf_op jit(solution)/shard_map/pallas_call | solution.py:275
  55.4 3.3 %collective-permute-start.14 = (bf16[256,256]{1,0:T(8,128)(2,1)S(1)}, bf16[256,256]{1,0:T(8,128)(2,1)S(1)}, u32[]{:S(2)}, u32[]{:S(2)}) collective-permute-start(bf16[256,256]{1,0:T(8,128)(2,1)S(1)} %get-tuple-element.64), channel_id=1, source_target_pairs={{0,16},{4,20},{8,24},{12,28},{16,0},{20,4},{24,8},{28,12},{1,17},{... | collective-permute-start | bytes 393224 | tf_op jit(solution)/shard_map/ppermute | solution.py:40
  58.7 1.6 %shard_map.114 = (bf16[256,256]{1,0:T(8,128)(2,1)S(1)}, bf16[256,256]{1,0:T(8,128)(2,1)S(1)}, bf16[256,256]{1,0:T(8,128)(2,1)S(1)}, bf16[256,256]{1,0:T(8,128)(2...) custom-call(bf16[256,512]{1,0:T(8,128)(2,1)S(1)} %copy-done.7, ...), custom_call_target="tpu_custom_call" | custom-call | flops 1409286144 | bytes 4587520 | tf_op jit(solution)/shard_map/pallas_call | solution.py:297
  60.4 1.5 %collective-permute-start.16 = (bf16[256,256]{1,0:T(8,128)(2,1)S(1)}, bf16[256,256]{1,0:T(8,128)(2,1)S(1)}, u32[]{:S(2)}, u32[]{:S(2)}) collective-permute-start(bf16[256,256]{1,0:T(8,128)(2,1)S(1)} %get-tuple-element.67), channel_id=1, source_target_pairs={{0,24},{4,28},{8,16},{12,20},{16,8},{20,12},{24,0},{28,4},{1,25},{... | collective-permute-start | bytes 393224 | tf_op jit(solution)/shard_map/ppermute | solution.py:40
  62.4 3.4 %collective-permute-start.18 = (bf16[256,256]{1,0:T(8,128)(2,1)S(1)}, bf16[256,256]{1,0:T(8,128)(2,1)S(1)}, u32[]{:S(2)}, u32[]{:S(2)}) collective-permute-start(bf16[256,256]{1,0:T(8,128)(2,1)S(1)} %get-tuple-element.72), channel_id=1, source_target_pairs={{0,20},{4,16},{8,28},{12,24},{16,4},{20,0},{24,12},{28,8},{1,21},{... | collective-permute-start | bytes 393224 | tf_op jit(solution)/shard_map/ppermute | solution.py:40
  65.8 1.4 %collective-permute-start.19 = (bf16[256,256]{1,0:T(8,128)(2,1)S(1)}, bf16[256,256]{1,0:T(8,128)(2,1)S(1)}, u32[]{:S(2)}, u32[]{:S(2)}) collective-permute-start(bf16[256,256]{1,0:T(8,128)(2,1)S(1)} %get-tuple-element.73), channel_id=1, source_target_pairs={{0,28},{4,24},{8,20},{12,16},{16,12},{20,8},{24,4},{28,0},{1,29},{... | collective-permute-start | bytes 393224 | tf_op jit(solution)/shard_map/ppermute | solution.py:40
  67.2 3.5 %collective-permute-done.15.refs_1_ = bf16[256,256]{1,0:T(8,128)(2,1)S(1)} collective-permute-done((bf16[256,256]{1,0:T(8,128)(2,1)S(1)}, bf16[256,256]{1,0:T(8,128)(2,1)S(1)}, u32[]{:S(2)}, u32[]{:S(2)}) %collective-permute-start.15) | collective-permute-done | bytes 131104 | tf_op jit(solution)/shard_map/ppermute | solution.py:40
  71.5 3.8 %collective-permute-done.17.refs_3_ = bf16[256,256]{1,0:T(8,128)(2,1)S(1)} collective-permute-done((bf16[256,256]{1,0:T(8,128)(2,1)S(1)}, bf16[256,256]{1,0:T(8,128)(2,1)S(1)}, u32[]{:S(2)}, u32[]{:S(2)}) %collective-permute-start.17) | collective-permute-done | bytes 131104 | tf_op jit(solution)/shard_map/ppermute | solution.py:40
  75.8 3.8 %collective-permute-done.18.refs_2_ = bf16[256,256]{1,0:T(8,128)(2,1)S(1)} collective-permute-done((bf16[256,256]{1,0:T(8,128)(2,1)S(1)}, bf16[256,256]{1,0:T(8,128)(2,1)S(1)}, u32[]{:S(2)}, u32[]{:S(2)}) %collective-permute-start.18) | collective-permute-done | bytes 131104 | tf_op jit(solution)/shard_map/ppermute | solution.py:40
  79.6 2.5 %collective-permute-done.20.refs_4_ = bf16[256,256]{1,0:T(8,128)(2,1)S(1)} collective-permute-done((bf16[256,256]{1,0:T(8,128)(2,1)S(1)}, bf16[256,256]{1,0:T(8,128)(2,1)S(1)}, u32[]{:S(2)}, u32[]{:S(2)}) %collective-permute-start.20) | collective-permute-done | bytes 131104 | tf_op jit(solution)/shard_map/ppermute | solution.py:40
  85.5 1.7 %collective-permute-done.22.refs_2_ = f32[1,256]{1,0:T(1,128)S(1)} collective-permute-done((f32[1,256]{1,0:T(1,128)S(1)}, f32[1,256]{1,0:T(1,128)S(1)}, u32[]{:S(2)}, u32[]{:S(2)}) %collective-permute-start.22) | collective-permute-done | bytes 1056 | tf_op jit(solution)/shard_map/ppermute | solution.py:427
  87.2 1.5 %shard_map.117 = f32[256,2048]{1,0:T(8,128)} custom-call(f32[256,2048]{1,0:T(8,128)S(1)} %get-tuple-element.75.pre_ref, f32[1,2048]{1,0:T(1,128)S(1)} %bitcast.4, f32[1,256]{1,0:T(1,128)S(1)} %get-tuple-element.76.refs_0_, f32[1,256]{1,0:T(1,128)S(1)} %collective-permute-done.21.refs_1_, f32[1,256]{1,0:T(1,128)S(1)} %collective-permute-done.22.refs_2_, ...), custom_call_target="tpu_custom_call" | custom-call | flops 1048576 | bytes 4194304 | tf_op jit(solution)/shard_map/pallas_call | solution.py:389
  (57 shorter events, 15.0 us)
Async XLA Ops:
  1.5 12.1 %collective-permute-start = (bf16[256,256]{1,0:T(8,128)(2,1)S(1)}, bf16[256,256]{1,0:T(8,128)(2,1)S(1)}, u32[]{:S(2)}, u32[]{:S(2)}) collective-permute-start(bf16[256,256]{1,0:T(8,128)(2,1)S(1)} %get-tuple-element.41), channel_id=1, source_target_pairs={{0,16},{4,20},{8,24},{12,28},{16,0},{20,4},{24,8},{28,12},{1,17},{... | collective-permute-start | bytes 393224 | tf_op jit(solution)/shard_map/ppermute | solution.py:40
  5.6 12.3 %collective-permute-start.1 = (bf16[256,256]{1,0:T(8,128)(2,1)S(1)}, bf16[256,256]{1,0:T(8,128)(2,1)S(1)}, u32[]{:S(2)}, u32[]{:S(2)}) collective-permute-start(bf16[256,256]{1,0:T(8,128)(2,1)S(1)} %get-tuple-element.43), channel_id=1, source_target_pairs={{0,8},{4,12},{8,0},{12,4},{16,24},{20,28},{24,16},{28,20},{1,9},{5... | collective-permute-start | bytes 393224 | tf_op jit(solution)/shard_map/ppermute | solution.py:40
  7.2 15.0 %collective-permute-start.2 = (bf16[256,256]{1,0:T(8,128)(2,1)S(1)}, bf16[256,256]{1,0:T(8,128)(2,1)S(1)}, u32[]{:S(2)}, u32[]{:S(2)}) collective-permute-start(bf16[256,256]{1,0:T(8,128)(2,1)S(1)} %get-tuple-element.44), channel_id=1, source_target_pairs={{0,24},{4,28},{8,16},{12,20},{16,8},{20,12},{24,0},{28,4},{1,25},{... | collective-permute-start | bytes 393224 | tf_op jit(solution)/shard_map/ppermute | solution.py:40
  7.2 15.0 %collective-permute-start.3 = (bf16[256,256]{1,0:T(8,128)(2,1)S(1)}, bf16[256,256]{1,0:T(8,128)(2,1)S(1)}, u32[]{:S(2)}, u32[]{:S(2)}) collective-permute-start(bf16[256,256]{1,0:T(8,128)(2,1)S(1)} %get-tuple-element.45), channel_id=1, source_target_pairs={{0,12},{4,8},{8,4},{12,0},{16,28},{20,24},{24,20},{28,16},{1,13},{... | collective-permute-start | bytes 393224 | tf_op jit(solution)/shard_map/ppermute | solution.py:40
  9.0 16.6 %collective-permute-start.4 = (bf16[256,256]{1,0:T(8,128)(2,1)S(1)}, bf16[256,256]{1,0:T(8,128)(2,1)S(1)}, u32[]{:S(2)}, u32[]{:S(2)}) collective-permute-start(bf16[256,256]{1,0:T(8,128)(2,1)S(1)} %get-tuple-element.46), channel_id=1, source_target_pairs={{0,20},{4,16},{8,28},{12,24},{16,4},{20,0},{24,12},{28,8},{1,21},{... | collective-permute-start | bytes 393224 | tf_op jit(solution)/shard_map/ppermute | solution.py:40
  16.7 12.8 %collective-permute-start.10 = (bf16[256,256]{1,0:T(8,128)(2,1)S(1)}, bf16[256,256]{1,0:T(8,128)(2,1)S(1)}, u32[]{:S(2)}, u32[]{:S(2)}) collective-permute-start(bf16[256,256]{1,0:T(8,128)(2,1)S(1)} %get-tuple-element.55.refs_8_), channel_id=1, source_target_pairs={{0,12},{4,8},{8,4},{12,0},{16,28},{20,24},{24,20},{28,16},{1,13},{... | collective-permute-start | bytes 393224 | tf_op jit(solution)/shard_map/ppermute | solution.py:40
  17.9 13.1 %collective-permute-start.7 = (bf16[256,256]{1,0:T(8,128)(2,1)S(1)}, bf16[256,256]{1,0:T(8,128)(2,1)S(1)}, u32[]{:S(2)}, u32[]{:S(2)}) collective-permute-start(bf16[256,256]{1,0:T(8,128)(2,1)S(1)} %get-tuple-element.52.refs_5_), channel_id=1, source_target_pairs={{0,16},{4,20},{8,24},{12,28},{16,0},{20,4},{24,8},{28,12},{1,17},{... | collective-permute-start | bytes 393224 | tf_op jit(solution)/shard_map/ppermute | solution.py:40
  22.1 8.9 %collective-permute-start.8 = (bf16[256,256]{1,0:T(8,128)(2,1)S(1)}, bf16[256,256]{1,0:T(8,128)(2,1)S(1)}, u32[]{:S(2)}, u32[]{:S(2)}) collective-permute-start(bf16[256,256]{1,0:T(8,128)(2,1)S(1)} %get-tuple-element.53.refs_6_), channel_id=1, source_target_pairs={{0,8},{4,12},{8,0},{12,4},{16,24},{20,28},{24,16},{28,20},{1,9},{5... | collective-permute-start | bytes 393224 | tf_op jit(solution)/shard_map/ppermute | solution.py:40
  22.1 19.7 %collective-permute-start.9 = (bf16[256,256]{1,0:T(8,128)(2,1)S(1)}, bf16[256,256]{1,0:T(8,128)(2,1)S(1)}, u32[]{:S(2)}, u32[]{:S(2)}) collective-permute-start(bf16[256,256]{1,0:T(8,128)(2,1)S(1)} %get-tuple-element.54.refs_7_), channel_id=1, source_target_pairs={{0,24},{4,28},{8,16},{12,20},{16,8},{20,12},{24,0},{28,4},{1,25},{... | collective-permute-start | bytes 393224 | tf_op jit(solution)/shard_map/ppermute | solution.py:40
  25.6 21.0 %collective-permute-start.5 = (bf16[256,256]{1,0:T(8,128)(2,1)S(1)}, bf16[256,256]{1,0:T(8,128)(2,1)S(1)}, u32[]{:S(2)}, u32[]{:S(2)}) collective-permute-start(bf16[256,256]{1,0:T(8,128)(2,1)S(1)} %get-tuple-element.47), channel_id=1, source_target_pairs={{0,28},{4,24},{8,20},{12,16},{16,12},{20,8},{24,4},{28,0},{1,29},{... | collective-permute-start | bytes 393224 | tf_op jit(solution)/shard_map/ppermute | solution.py:40
  29.5 17.2 %collective-permute-start.6 = (bf16[256,256]{1,0:T(8,128)(2,1)S(1)}, bf16[256,256]{1,0:T(8,128)(2,1)S(1)}, u32[]{:S(2)}, u32[]{:S(2)}) collective-permute-start(bf16[256,256]{1,0:T(8,128)(2,1)S(1)} %get-tuple-element.48), channel_id=1, source_target_pairs={{0,4},{4,0},{8,12},{12,8},{16,20},{20,16},{24,28},{28,24},{1,5},{5... | collective-permute-start | bytes 393224 | tf_op jit(solution)/shard_map/ppermute | solution.py:40
  31.0 20.6 %collective-permute-start.11 = (bf16[256,256]{1,0:T(8,128)(2,1)S(1)}, bf16[256,256]{1,0:T(8,128)(2,1)S(1)}, u32[]{:S(2)}, u32[]{:S(2)}) collective-permute-start(bf16[256,256]{1,0:T(8,128)(2,1)S(1)} %get-tuple-element.59.refs_5_), channel_id=1, source_target_pairs={{0,20},{4,16},{8,28},{12,24},{16,4},{20,0},{24,12},{28,8},{1,21},{... | collective-permute-start | bytes 393224 | tf_op jit(solution)/shard_map/ppermute | solution.py:40
  31.0 20.6 %collective-permute-start.12 = (bf16[256,256]{1,0:T(8,128)(2,1)S(1)}, bf16[256,256]{1,0:T(8,128)(2,1)S(1)}, u32[]{:S(2)}, u32[]{:S(2)}) collective-permute-start(bf16[256,256]{1,0:T(8,128)(2,1)S(1)} %get-tuple-element.60.refs_6_), channel_id=1, source_target_pairs={{0,28},{4,24},{8,20},{12,16},{16,12},{20,8},{24,4},{28,0},{1,29},{... | collective-permute-start | bytes 393224 | tf_op jit(solution)/shard_map/ppermute | solution.py:40
  41.8 9.7 %collective-permute-start.13 = (bf16[256,256]{1,0:T(8,128)(2,1)S(1)}, bf16[256,256]{1,0:T(8,128)(2,1)S(1)}, u32[]{:S(2)}, u32[]{:S(2)}) collective-permute-start(bf16[256,256]{1,0:T(8,128)(2,1)S(1)} %get-tuple-element.61.refs_7_), channel_id=1, source_target_pairs={{0,4},{4,0},{8,12},{12,8},{16,20},{20,16},{24,28},{28,24},{1,5},{5... | collective-permute-start | bytes 393224 | tf_op jit(solution)/shard_map/ppermute | solution.py:40
  55.4 10.4 %collective-permute-start.14 = (bf16[256,256]{1,0:T(8,128)(2,1)S(1)}, bf16[256,256]{1,0:T(8,128)(2,1)S(1)}, u32[]{:S(2)}, u32[]{:S(2)}) collective-permute-start(bf16[256,256]{1,0:T(8,128)(2,1)S(1)} %get-tuple-element.64), channel_id=1, source_target_pairs={{0,16},{4,20},{8,24},{12,28},{16,0},{20,4},{24,8},{28,12},{1,17},{... | collective-permute-start | bytes 393224 | tf_op jit(solution)/shard_map/ppermute | solution.py:40
  60.3 10.4 %collective-permute-start.15 = (bf16[256,256]{1,0:T(8,128)(2,1)S(1)}, bf16[256,256]{1,0:T(8,128)(2,1)S(1)}, u32[]{:S(2)}, u32[]{:S(2)}) collective-permute-start(bf16[256,256]{1,0:T(8,128)(2,1)S(1)} %get-tuple-element.66), channel_id=1, source_target_pairs={{0,8},{4,12},{8,0},{12,4},{16,24},{20,28},{24,16},{28,20},{1,9},{5... | collective-permute-start | bytes 393224 | tf_op jit(solution)/shard_map/ppermute | solution.py:40
  60.4 11.1 %collective-permute-start.16 = (bf16[256,256]{1,0:T(8,128)(2,1)S(1)}, bf16[256,256]{1,0:T(8,128)(2,1)S(1)}, u32[]{:S(2)}, u32[]{:S(2)}) collective-permute-start(bf16[256,256]{1,0:T(8,128)(2,1)S(1)} %get-tuple-element.67), channel_id=1, source_target_pairs={{0,24},{4,28},{8,16},{12,20},{16,8},{20,12},{24,0},{28,4},{1,25},{... | collective-permute-start | bytes 393224 | tf_op jit(solution)/shard_map/ppermute | solution.py:40
  61.9 13.4 %collective-permute-start.17 = (bf16[256,256]{1,0:T(8,128)(2,1)S(1)}, bf16[256,256]{1,0:T(8,128)(2,1)S(1)}, u32[]{:S(2)}, u32[]{:S(2)}) collective-permute-start(bf16[256,256]{1,0:T(8,128)(2,1)S(1)} %get-tuple-element.68), channel_id=1, source_target_pairs={{0,12},{4,8},{8,4},{12,0},{16,28},{20,24},{24,20},{28,16},{1,13},{... | collective-permute-start | bytes 393224 | tf_op jit(solution)/shard_map/ppermute | solution.py:40
  62.4 17.1 %collective-permute-start.18 = (bf16[256,256]{1,0:T(8,128)(2,1)S(1)}, bf16[256,256]{1,0:T(8,128)(2,1)S(1)}, u32[]{:S(2)}, u32[]{:S(2)}) collective-permute-start(bf16[256,256]{1,0:T(8,128)(2,1)S(1)} %get-tuple-element.72), channel_id=1, source_target_pairs={{0,20},{4,16},{8,28},{12,24},{16,4},{20,0},{24,12},{28,8},{1,21},{... | collective-permute-start | bytes 393224 | tf_op jit(solution)/shard_map/ppermute | solution.py:40
  65.8 13.8 %collective-permute-start.19 = (bf16[256,256]{1,0:T(8,128)(2,1)S(1)}, bf16[256,256]{1,0:T(8,128)(2,1)S(1)}, u32[]{:S(2)}, u32[]{:S(2)}) collective-permute-start(bf16[256,256]{1,0:T(8,128)(2,1)S(1)} %get-tuple-element.73), channel_id=1, source_target_pairs={{0,28},{4,24},{8,20},{12,16},{16,12},{20,8},{24,4},{28,0},{1,29},{... | collective-permute-start | bytes 393224 | tf_op jit(solution)/shard_map/ppermute | solution.py:40
  70.7 11.3 %collective-permute-start.20 = (bf16[256,256]{1,0:T(8,128)(2,1)S(1)}, bf16[256,256]{1,0:T(8,128)(2,1)S(1)}, u32[]{:S(2)}, u32[]{:S(2)}) collective-permute-start(bf16[256,256]{1,0:T(8,128)(2,1)S(1)} %get-tuple-element.74), channel_id=1, source_target_pairs={{0,4},{4,0},{8,12},{12,8},{16,20},{20,16},{24,28},{28,24},{1,5},{5... | collective-permute-start | bytes 393224 | tf_op jit(solution)/shard_map/ppermute | solution.py:40
  82.4 3.1 %collective-permute-start.21 = (f32[1,256]{1,0:T(1,128)S(1)}, f32[1,256]{1,0:T(1,128)S(1)}, u32[]{:S(2)}, u32[]{:S(2)}) collective-permute-start(f32[1,256]{1,0:T(1,128)S(1)} %get-tuple-element.76.refs_0_), channel_id=1, source_target_pairs={{0,3},{1,2},{2,1},{3,0},{4,7},{5,6},{6,5},{7,4},{8,11},{9,10},{10,... | collective-permute-start | bytes 3080 | tf_op jit(solution)/shard_map/ppermute | solution.py:427
  83.6 3.6 %collective-permute-start.22 = (f32[1,256]{1,0:T(1,128)S(1)}, f32[1,256]{1,0:T(1,128)S(1)}, u32[]{:S(2)}, u32[]{:S(2)}) collective-permute-start(f32[1,256]{1,0:T(1,128)S(1)} %get-tuple-element.76.refs_0_), channel_id=1, source_target_pairs={{0,2},{1,3},{2,0},{3,1},{4,6},{5,7},{6,4},{7,5},{8,10},{9,11},{10,... | collective-permute-start | bytes 3080 | tf_op jit(solution)/shard_map/ppermute | solution.py:427
  84.1 3.1 %collective-permute-start.23 = (f32[1,256]{1,0:T(1,128)S(1)}, f32[1,256]{1,0:T(1,128)S(1)}, u32[]{:S(2)}, u32[]{:S(2)}) collective-permute-start(f32[1,256]{1,0:T(1,128)S(1)} %get-tuple-element.76.refs_0_), channel_id=1, source_target_pairs={{0,1},{1,0},{2,3},{3,2},{4,5},{5,4},{6,7},{7,6},{8,9},{9,8},{10,11... | collective-permute-start | bytes 3080 | tf_op jit(solution)/shard_map/ppermute | solution.py:427
  (12 other events, 132.7 us)

commit v14 on v12

--- a/solution.py
+++ b/solution.py
@@ -376,11 +376,12 @@
     filts, gates, convs = {}, {}, {}
     for k in order:
         filts[k] = send(own[k], k, count)
-    for k in order:
+    gated_order = order[:2] + [order[3], order[2]] + order[4:]
+    for k in gated_order:
         gates[k] = send(mine[k], k, count)
     filts[0], gates[0] = held, mine[0]
     filt = filter_spectra(lag_of_block, *tabs[:2], filts)
-    early = order[: count // 2] + [0]
+    early = gated_order[: count // 2] + [0]
     gated = gated_spectra(count, *tabs[:2], {k: gates[k] for k in early})
     first = order[:1]
     sums, found = products(first, tabs, filt, gated, {k: gates[k] for k in gates if k not in early})

time: 87.4 us -> 89.2 us (1.021)
  starting transfers between devices: 44 us -> 53.1 us
  waiting for transfers between devices: 25.5 us -> 18.2 us
    ppermute x21, starting transfers between devices: 42.1 us -> 51 us  [send(): return lax.ppermute(block, 'tok', [(d, d ^ step) for d in range(count)])]
    ppermute x21, waiting for transfers between devices: 22.7 us -> 15.3 us  [send(): return lax.ppermute(block, 'tok', [(d, d ^ step) for d in range(count)])]
  transfers between devices with their start and end apart: 24 -> 24, of which waited for: 11 -> 10; matrix products, arithmetic and copies ran while one was open for 0% -> 0% of each run, Pallas kernels for 6% -> 6%
where the time goes in v14:
time: 89.2 us; the launch traced here: 88.9 us
  starting transfers between devices  53.1 us (60%)
  waiting for transfers between devices  18.2 us (20%)
  Pallas kernels  11.8 us (13%)
  local copies, waits for them, and re-layouts  5.62 us (6%)
    ppermute x21, starting transfers between devices, send(): return lax.ppermute(block, 'tok', [(d, d ^ step) for d in range(count)])  51 us
    ppermute x21, waiting for transfers between devices, send(): return lax.ppermute(block, 'tok', [(d, d ^ step) for d in range(count)])  15.3 us
    unnamed x26, local copies, waits for them, and re-layouts  5.62 us
    pallas_call x1, Pallas kernels, products(): pl.pallas_call(functools.partial(product_kernel, count, steps, first), ou...  4.1 us
    ppermute x3, waiting for transfers between devices, local(): lax.ppermute(square, 'chan', [(d, d ^ step) for d in range(others)])  2.92 us
    ppermute x3, starting transfers between devices, local(): lax.ppermute(square, 'chan', [(d, d ^ step) for d in range(others)])  2.08 us
    pallas_call x1, Pallas kernels, filter_spectra(): pl.pallas_call(functools.partial(filter_kernel, steps), out_shape=spectra...  1.93 us
  transfers between devices with their start and end apart: 24, of which 10 were waited for; matrix products, arithmetic and copies ran while one was open for 0% of the time, Pallas kernels for 6%

profile of v14, /device:TPU:0, one launch (start us, length us, event | category | flops | bytes accessed | tf_op | source)
XLA Modules:
  0.0 88.9 jit_solution(2353770996072485831)
XLA Ops:
  1.5 4.1 %collective-permute-start = (bf16[256,256]{1,0:T(8,128)(2,1)S(1)}, bf16[256,256]{1,0:T(8,128)(2,1)S(1)}, u32[]{:S(2)}, u32[]{:S(2)}) collective-permute-start(bf16[256,256]{1,0:T(8,128)(2,1)S(1)} %get-tuple-element.37), channel_id=1, source_target_pairs={{0,16},{4,20},{8,24},{12,28},{16,0},{20,4},{24,8},{28,12},{1,17},{... | collective-permute-start | bytes 393224 | tf_op jit(solution)/shard_map/ppermute | solution.py:40
  5.6 1.6 %collective-permute-start.1 = (bf16[256,256]{1,0:T(8,128)(2,1)S(1)}, bf16[256,256]{1,0:T(8,128)(2,1)S(1)}, u32[]{:S(2)}, u32[]{:S(2)}) collective-permute-start(bf16[256,256]{1,0:T(8,128)(2,1)S(1)} %get-tuple-element.38), channel_id=1, source_target_pairs={{0,8},{4,12},{8,0},{12,4},{16,24},{20,28},{24,16},{28,20},{1,9},{5... | collective-permute-start | bytes 393224 | tf_op jit(solution)/shard_map/ppermute | solution.py:40
  7.2 1.8 %collective-permute-start.3 = (bf16[256,256]{1,0:T(8,128)(2,1)S(1)}, bf16[256,256]{1,0:T(8,128)(2,1)S(1)}, u32[]{:S(2)}, u32[]{:S(2)}) collective-permute-start(bf16[256,256]{1,0:T(8,128)(2,1)S(1)} %get-tuple-element.40), channel_id=1, source_target_pairs={{0,12},{4,8},{8,4},{12,0},{16,28},{20,24},{24,20},{28,16},{1,13},{... | collective-permute-start | bytes 393224 | tf_op jit(solution)/shard_map/ppermute | solution.py:40
  9.0 3.5 %collective-permute-start.4 = (bf16[256,256]{1,0:T(8,128)(2,1)S(1)}, bf16[256,256]{1,0:T(8,128)(2,1)S(1)}, u32[]{:S(2)}, u32[]{:S(2)}) collective-permute-start(bf16[256,256]{1,0:T(8,128)(2,1)S(1)} %get-tuple-element.41), channel_id=1, source_target_pairs={{0,20},{4,16},{8,28},{12,24},{16,4},{20,0},{24,12},{28,8},{1,21},{... | collective-permute-start | bytes 393224 | tf_op jit(solution)/shard_map/ppermute | solution.py:40
  15.8 2.2 %collective-permute-start.8 = (bf16[256,256]{1,0:T(8,128)(2,1)S(1)}, bf16[256,256]{1,0:T(8,128)(2,1)S(1)}, u32[]{:S(2)}, u32[]{:S(2)}) collective-permute-start(bf16[256,256]{1,0:T(8,128)(2,1)S(1)} %get-tuple-element.49.refs_6_), channel_id=1, source_target_pairs={{0,8},{4,12},{8,0},{12,4},{16,24},{20,28},{24,16},{28,20},{1,9},{5... | collective-permute-start | bytes 393224 | tf_op jit(solution)/shard_map/ppermute | solution.py:40
  17.9 3.4 %collective-permute-start.9 = (bf16[256,256]{1,0:T(8,128)(2,1)S(1)}, bf16[256,256]{1,0:T(8,128)(2,1)S(1)}, u32[]{:S(2)}, u32[]{:S(2)}) collective-permute-start(bf16[256,256]{1,0:T(8,128)(2,1)S(1)} %get-tuple-element.50.refs_8_), channel_id=1, source_target_pairs={{0,12},{4,8},{8,4},{12,0},{16,28},{20,24},{24,20},{28,16},{1,13},{... | collective-permute-start | bytes 393224 | tf_op jit(solution)/shard_map/ppermute | solution.py:40
  21.3 5.9 %collective-permute-start.10 = (bf16[256,256]{1,0:T(8,128)(2,1)S(1)}, bf16[256,256]{1,0:T(8,128)(2,1)S(1)}, u32[]{:S(2)}, u32[]{:S(2)}) collective-permute-start(bf16[256,256]{1,0:T(8,128)(2,1)S(1)} %get-tuple-element.51.refs_7_), channel_id=1, source_target_pairs={{0,24},{4,28},{8,16},{12,20},{16,8},{20,12},{24,0},{28,4},{1,25},{... | collective-permute-start | bytes 393224 | tf_op jit(solution)/shard_map/ppermute | solution.py:40
  28.1 2.5 %collective-permute-start.5 = (bf16[256,256]{1,0:T(8,128)(2,1)S(1)}, bf16[256,256]{1,0:T(8,128)(2,1)S(1)}, u32[]{:S(2)}, u32[]{:S(2)}) collective-permute-start(bf16[256,256]{1,0:T(8,128)(2,1)S(1)} %get-tuple-element.42), channel_id=1, source_target_pairs={{0,28},{4,24},{8,20},{12,16},{16,12},{20,8},{24,4},{28,0},{1,29},{... | collective-permute-start | bytes 393224 | tf_op jit(solution)/shard_map/ppermute | solution.py:40
  31.0 1.5 %collective-permute-start.6 = (bf16[256,256]{1,0:T(8,128)(2,1)S(1)}, bf16[256,256]{1,0:T(8,128)(2,1)S(1)}, u32[]{:S(2)}, u32[]{:S(2)}) collective-permute-start(bf16[256,256]{1,0:T(8,128)(2,1)S(1)} %get-tuple-element.43), channel_id=1, source_target_pairs={{0,4},{4,0},{8,12},{12,8},{16,20},{20,16},{24,28},{28,24},{1,5},{5... | collective-permute-start | bytes 393224 | tf_op jit(solution)/shard_map/ppermute | solution.py:40
  32.6 11.3 %collective-permute-start.12 = (bf16[256,256]{1,0:T(8,128)(2,1)S(1)}, bf16[256,256]{1,0:T(8,128)(2,1)S(1)}, u32[]{:S(2)}, u32[]{:S(2)}) collective-permute-start(bf16[256,256]{1,0:T(8,128)(2,1)S(1)} %get-tuple-element.54.refs_6_), channel_id=1, source_target_pairs={{0,28},{4,24},{8,20},{12,16},{16,12},{20,8},{24,4},{28,0},{1,29},{... | collective-permute-start | bytes 393224 | tf_op jit(solution)/shard_map/ppermute | solution.py:40
  43.8 1.5 %collective-permute-start.13 = (bf16[256,256]{1,0:T(8,128)(2,1)S(1)}, bf16[256,256]{1,0:T(8,128)(2,1)S(1)}, u32[]{:S(2)}, u32[]{:S(2)}) collective-permute-start(bf16[256,256]{1,0:T(8,128)(2,1)S(1)} %get-tuple-element.55.refs_7_), channel_id=1, source_target_pairs={{0,4},{4,0},{8,12},{12,8},{16,20},{20,16},{24,28},{28,24},{1,5},{5... | collective-permute-start | bytes 393224 | tf_op jit(solution)/shard_map/ppermute | solution.py:40
  48.2 1.9 %shard_map.110.fs = f32[8,512,256]{2,1,0:T(8,128)S(1)} custom-call(s32[8]{0:T(128)S(1)} %copy-done.10, bf16[512,256]{1,0:T(8,128)(2,1)S(1)} %copy-done.7, bf16[512,256]{1,0:T(8,128)(2,1)S(1)} %copy-done.5, bf16[256,256]{1,0:T(8,128)(2,1)S(1)} %collective-permute-done.refs_0_, bf16[256,256]{1,0:T(8,128)(2,1)S(1)} %collective-permute-done.1.refs_1_, ...), custom_call_target="tpu_custom_call" | custom-call | flops 1073741824 | bytes 5242880 | tf_op jit(solution)/shard_map/pallas_call | solution.py:162
  50.8 4.1 %shard_map.113 = (f32[8,512,256]{2,1,0:T(8,128)S(1)}, f32[8,512,256]{2,1,0:T(8,128)S(1)}, bf16[256,256]{1,0:T(8,128)(2,1)S(1)}) custom-call(bf16[512,256]{1,0:T(8,128)(2,1)S(1)} %copy-done.7, bf16[512,256]{1,0:T(8,128)(2,1)S(1)} %copy-done.5, bf16[256,512]{1,0:T(8,128)(2,1)S(1)} %copy-done.12, ...), custom_call_target="tpu_custom_call", output_to_operand_aliasing={{0}: (5, {})} | custom-call | flops 3758096384 | bytes 5242880 | tf_op jit(solution)/shard_map/pallas_call | solution.py:244
  55.0 4.1 %collective-permute-start.14 = (bf16[256,256]{1,0:T(8,128)(2,1)S(1)}, bf16[256,256]{1,0:T(8,128)(2,1)S(1)}, u32[]{:S(2)}, u32[]{:S(2)}) collective-permute-start(bf16[256,256]{1,0:T(8,128)(2,1)S(1)} %get-tuple-element.56), channel_id=1, source_target_pairs={{0,16},{4,20},{8,24},{12,28},{16,0},{20,4},{24,8},{28,12},{1,17},{... | collective-permute-start | bytes 393224 | tf_op jit(solution)/shard_map/ppermute | solution.py:40
  59.1 1.6 %shard_map.114 = (bf16[256,256]{1,0:T(8,128)(2,1)S(1)}, bf16[256,256]{1,0:T(8,128)(2,1)S(1)}, bf16[256,256]{1,0:T(8,128)(2,1)S(1)}, bf16[256,256]{1,0:T(8,128)(2...) custom-call(bf16[256,512]{1,0:T(8,128)(2,1)S(1)} %copy-done.12, ...), custom_call_target="tpu_custom_call" | custom-call | flops 1409286144 | bytes 4587520 | tf_op jit(solution)/shard_map/pallas_call | solution.py:265
  60.8 1.5 %collective-permute-start.16 = (bf16[256,256]{1,0:T(8,128)(2,1)S(1)}, bf16[256,256]{1,0:T(8,128)(2,1)S(1)}, u32[]{:S(2)}, u32[]{:S(2)}) collective-permute-start(bf16[256,256]{1,0:T(8,128)(2,1)S(1)} %get-tuple-element.59), channel_id=1, source_target_pairs={{0,24},{4,28},{8,16},{12,20},{16,8},{20,12},{24,0},{28,4},{1,25},{... | collective-permute-start | bytes 393224 | tf_op jit(solution)/shard_map/ppermute | solution.py:40
  62.8 3.4 %collective-permute-start.18 = (bf16[256,256]{1,0:T(8,128)(2,1)S(1)}, bf16[256,256]{1,0:T(8,128)(2,1)S(1)}, u32[]{:S(2)}, u32[]{:S(2)}) collective-permute-start(bf16[256,256]{1,0:T(8,128)(2,1)S(1)} %get-tuple-element.64), channel_id=1, source_target_pairs={{0,20},{4,16},{8,28},{12,24},{16,4},{20,0},{24,12},{28,8},{1,21},{... | collective-permute-start | bytes 393224 | tf_op jit(solution)/shard_map/ppermute | solution.py:40
  67.5 3.1 %collective-permute-done.15.refs_1_ = bf16[256,256]{1,0:T(8,128)(2,1)S(1)} collective-permute-done((bf16[256,256]{1,0:T(8,128)(2,1)S(1)}, bf16[256,256]{1,0:T(8,128)(2,1)S(1)}, u32[]{:S(2)}, u32[]{:S(2)}) %collective-permute-start.15) | collective-permute-done | bytes 131104 | tf_op jit(solution)/shard_map/ppermute | solution.py:40
  71.4 3.7 %collective-permute-done.17.refs_3_ = bf16[256,256]{1,0:T(8,128)(2,1)S(1)} collective-permute-done((bf16[256,256]{1,0:T(8,128)(2,1)S(1)}, bf16[256,256]{1,0:T(8,128)(2,1)S(1)}, u32[]{:S(2)}, u32[]{:S(2)}) %collective-permute-start.17) | collective-permute-done | bytes 131104 | tf_op jit(solution)/shard_map/ppermute | solution.py:40
  75.6 4.0 %collective-permute-done.18.refs_2_ = bf16[256,256]{1,0:T(8,128)(2,1)S(1)} collective-permute-done((bf16[256,256]{1,0:T(8,128)(2,1)S(1)}, bf16[256,256]{1,0:T(8,128)(2,1)S(1)}, u32[]{:S(2)}, u32[]{:S(2)}) %collective-permute-start.18) | collective-permute-done | bytes 131104 | tf_op jit(solution)/shard_map/ppermute | solution.py:40
  79.5 2.5 %collective-permute-done.20.refs_4_ = bf16[256,256]{1,0:T(8,128)(2,1)S(1)} collective-permute-done((bf16[256,256]{1,0:T(8,128)(2,1)S(1)}, bf16[256,256]{1,0:T(8,128)(2,1)S(1)}, u32[]{:S(2)}, u32[]{:S(2)}) %collective-permute-start.20) | collective-permute-done | bytes 131104 | tf_op jit(solution)/shard_map/ppermute | solution.py:40
  82.5 1.9 %collective-permute-start.22 = (f32[1,256]{1,0:T(1,128)S(1)}, f32[1,256]{1,0:T(1,128)S(1)}, u32[]{:S(2)}, u32[]{:S(2)}) collective-permute-start(f32[1,256]{1,0:T(1,128)S(1)} %get-tuple-element.68.refs_0_), channel_id=1, source_target_pairs={{0,2},{1,3},{2,0},{3,1},{4,6},{5,7},{6,4},{7,5},{8,10},{9,11},{10,... | collective-permute-start | bytes 3080 | tf_op jit(solution)/shard_map/ppermute | solution.py:395
  84.5 1.6 %collective-permute-done.22.refs_2_ = f32[1,256]{1,0:T(1,128)S(1)} collective-permute-done((f32[1,256]{1,0:T(1,128)S(1)}, f32[1,256]{1,0:T(1,128)S(1)}, u32[]{:S(2)}, u32[]{:S(2)}) %collective-permute-start.22) | collective-permute-done | bytes 1056 | tf_op jit(solution)/shard_map/ppermute | solution.py:395
  87.4 1.5 %shard_map.117 = f32[256,2048]{1,0:T(8,128)} custom-call(f32[256,2048]{1,0:T(8,128)S(1)} %get-tuple-element.67.pre_ref, f32[1,2048]{1,0:T(1,128)S(1)} %bitcast.4, f32[1,256]{1,0:T(1,128)S(1)} %get-tuple-element.68.refs_0_, f32[1,256]{1,0:T(1,128)S(1)} %collective-permute-done.21.refs_1_, f32[1,256]{1,0:T(1,128)S(1)} %collective-permute-done.22.refs_2_, ...), custom_call_target="tpu_custom_call" | custom-call | flops 1048576 | bytes 4194304 | tf_op jit(solution)/shard_map/pallas_call | solution.py:357
  (59 shorter events, 14.6 us)
Async XLA Ops:
  1.5 14.2 %collective-permute-start = (bf16[256,256]{1,0:T(8,128)(2,1)S(1)}, bf16[256,256]{1,0:T(8,128)(2,1)S(1)}, u32[]{:S(2)}, u32[]{:S(2)}) collective-permute-start(bf16[256,256]{1,0:T(8,128)(2,1)S(1)} %get-tuple-element.37), channel_id=1, source_target_pairs={{0,16},{4,20},{8,24},{12,28},{16,0},{20,4},{24,8},{28,12},{1,17},{... | collective-permute-start | bytes 393224 | tf_op jit(solution)/shard_map/ppermute | solution.py:40
  5.6 10.2 %collective-permute-start.1 = (bf16[256,256]{1,0:T(8,128)(2,1)S(1)}, bf16[256,256]{1,0:T(8,128)(2,1)S(1)}, u32[]{:S(2)}, u32[]{:S(2)}) collective-permute-start(bf16[256,256]{1,0:T(8,128)(2,1)S(1)} %get-tuple-element.38), channel_id=1, source_target_pairs={{0,8},{4,12},{8,0},{12,4},{16,24},{20,28},{24,16},{28,20},{1,9},{5... | collective-permute-start | bytes 393224 | tf_op jit(solution)/shard_map/ppermute | solution.py:40
  7.2 10.8 %collective-permute-start.2 = (bf16[256,256]{1,0:T(8,128)(2,1)S(1)}, bf16[256,256]{1,0:T(8,128)(2,1)S(1)}, u32[]{:S(2)}, u32[]{:S(2)}) collective-permute-start(bf16[256,256]{1,0:T(8,128)(2,1)S(1)} %get-tuple-element.39), channel_id=1, source_target_pairs={{0,24},{4,28},{8,16},{12,20},{16,8},{20,12},{24,0},{28,4},{1,25},{... | collective-permute-start | bytes 393224 | tf_op jit(solution)/shard_map/ppermute | solution.py:40
  7.2 14.1 %collective-permute-start.3 = (bf16[256,256]{1,0:T(8,128)(2,1)S(1)}, bf16[256,256]{1,0:T(8,128)(2,1)S(1)}, u32[]{:S(2)}, u32[]{:S(2)}) collective-permute-start(bf16[256,256]{1,0:T(8,128)(2,1)S(1)} %get-tuple-element.40), channel_id=1, source_target_pairs={{0,12},{4,8},{8,4},{12,0},{16,28},{20,24},{24,20},{28,16},{1,13},{... | collective-permute-start | bytes 393224 | tf_op jit(solution)/shard_map/ppermute | solution.py:40
  9.0 19.1 %collective-permute-start.4 = (bf16[256,256]{1,0:T(8,128)(2,1)S(1)}, bf16[256,256]{1,0:T(8,128)(2,1)S(1)}, u32[]{:S(2)}, u32[]{:S(2)}) collective-permute-start(bf16[256,256]{1,0:T(8,128)(2,1)S(1)} %get-tuple-element.41), channel_id=1, source_target_pairs={{0,20},{4,16},{8,28},{12,24},{16,4},{20,0},{24,12},{28,8},{1,21},{... | collective-permute-start | bytes 393224 | tf_op jit(solution)/shard_map/ppermute | solution.py:40
  15.7 15.4 %collective-permute-start.7 = (bf16[256,256]{1,0:T(8,128)(2,1)S(1)}, bf16[256,256]{1,0:T(8,128)(2,1)S(1)}, u32[]{:S(2)}, u32[]{:S(2)}) collective-permute-start(bf16[256,256]{1,0:T(8,128)(2,1)S(1)} %get-tuple-element.48.refs_5_), channel_id=1, source_target_pairs={{0,16},{4,20},{8,24},{12,28},{16,0},{20,4},{24,8},{28,12},{1,17},{... | collective-permute-start | bytes 393224 | tf_op jit(solution)/shard_map/ppermute | solution.py:40
  15.8 16.8 %collective-permute-start.8 = (bf16[256,256]{1,0:T(8,128)(2,1)S(1)}, bf16[256,256]{1,0:T(8,128)(2,1)S(1)}, u32[]{:S(2)}, u32[]{:S(2)}) collective-permute-start(bf16[256,256]{1,0:T(8,128)(2,1)S(1)} %get-tuple-element.49.refs_6_), channel_id=1, source_target_pairs={{0,8},{4,12},{8,0},{12,4},{16,24},{20,28},{24,16},{28,20},{1,9},{5... | collective-permute-start | bytes 393224 | tf_op jit(solution)/shard_map/ppermute | solution.py:40
  17.9 14.7 %collective-permute-start.9 = (bf16[256,256]{1,0:T(8,128)(2,1)S(1)}, bf16[256,256]{1,0:T(8,128)(2,1)S(1)}, u32[]{:S(2)}, u32[]{:S(2)}) collective-permute-start(bf16[256,256]{1,0:T(8,128)(2,1)S(1)} %get-tuple-element.50.refs_8_), channel_id=1, source_target_pairs={{0,12},{4,8},{8,4},{12,0},{16,28},{20,24},{24,20},{28,16},{1,13},{... | collective-permute-start | bytes 393224 | tf_op jit(solution)/shard_map/ppermute | solution.py:40
  21.3 22.5 %collective-permute-start.10 = (bf16[256,256]{1,0:T(8,128)(2,1)S(1)}, bf16[256,256]{1,0:T(8,128)(2,1)S(1)}, u32[]{:S(2)}, u32[]{:S(2)}) collective-permute-start(bf16[256,256]{1,0:T(8,128)(2,1)S(1)} %get-tuple-element.51.refs_7_), channel_id=1, source_target_pairs={{0,24},{4,28},{8,16},{12,20},{16,8},{20,12},{24,0},{28,4},{1,25},{... | collective-permute-start | bytes 393224 | tf_op jit(solution)/shard_map/ppermute | solution.py:40
  28.1 20.0 %collective-permute-start.5 = (bf16[256,256]{1,0:T(8,128)(2,1)S(1)}, bf16[256,256]{1,0:T(8,128)(2,1)S(1)}, u32[]{:S(2)}, u32[]{:S(2)}) collective-permute-start(bf16[256,256]{1,0:T(8,128)(2,1)S(1)} %get-tuple-element.42), channel_id=1, source_target_pairs={{0,28},{4,24},{8,20},{12,16},{16,12},{20,8},{24,4},{28,0},{1,29},{... | collective-permute-start | bytes 393224 | tf_op jit(solution)/shard_map/ppermute | solution.py:40
  31.0 17.2 %collective-permute-start.6 = (bf16[256,256]{1,0:T(8,128)(2,1)S(1)}, bf16[256,256]{1,0:T(8,128)(2,1)S(1)}, u32[]{:S(2)}, u32[]{:S(2)}) collective-permute-start(bf16[256,256]{1,0:T(8,128)(2,1)S(1)} %get-tuple-element.43), channel_id=1, source_target_pairs={{0,4},{4,0},{8,12},{12,8},{16,20},{20,16},{24,28},{28,24},{1,5},{5... | collective-permute-start | bytes 393224 | tf_op jit(solution)/shard_map/ppermute | solution.py:40
  32.6 18.0 %collective-permute-start.11 = (bf16[256,256]{1,0:T(8,128)(2,1)S(1)}, bf16[256,256]{1,0:T(8,128)(2,1)S(1)}, u32[]{:S(2)}, u32[]{:S(2)}) collective-permute-start(bf16[256,256]{1,0:T(8,128)(2,1)S(1)} %get-tuple-element.53.refs_5_), channel_id=1, source_target_pairs={{0,20},{4,16},{8,28},{12,24},{16,4},{20,0},{24,12},{28,8},{1,21},{... | collective-permute-start | bytes 393224 | tf_op jit(solution)/shard_map/ppermute | solution.py:40
  32.6 18.0 %collective-permute-start.12 = (bf16[256,256]{1,0:T(8,128)(2,1)S(1)}, bf16[256,256]{1,0:T(8,128)(2,1)S(1)}, u32[]{:S(2)}, u32[]{:S(2)}) collective-permute-start(bf16[256,256]{1,0:T(8,128)(2,1)S(1)} %get-tuple-element.54.refs_6_), channel_id=1, source_target_pairs={{0,28},{4,24},{8,20},{12,16},{16,12},{20,8},{24,4},{28,0},{1,29},{... | collective-permute-start | bytes 393224 | tf_op jit(solution)/shard_map/ppermute | solution.py:40
  43.8 7.0 %collective-permute-start.13 = (bf16[256,256]{1,0:T(8,128)(2,1)S(1)}, bf16[256,256]{1,0:T(8,128)(2,1)S(1)}, u32[]{:S(2)}, u32[]{:S(2)}) collective-permute-start(bf16[256,256]{1,0:T(8,128)(2,1)S(1)} %get-tuple-element.55.refs_7_), channel_id=1, source_target_pairs={{0,4},{4,0},{8,12},{12,8},{16,20},{20,16},{24,28},{28,24},{1,5},{5... | collective-permute-start | bytes 393224 | tf_op jit(solution)/shard_map/ppermute | solution.py:40
  55.0 11.2 %collective-permute-start.14 = (bf16[256,256]{1,0:T(8,128)(2,1)S(1)}, bf16[256,256]{1,0:T(8,128)(2,1)S(1)}, u32[]{:S(2)}, u32[]{:S(2)}) collective-permute-start(bf16[256,256]{1,0:T(8,128)(2,1)S(1)} %get-tuple-element.56), channel_id=1, source_target_pairs={{0,16},{4,20},{8,24},{12,28},{16,0},{20,4},{24,8},{28,12},{1,17},{... | collective-permute-start | bytes 393224 | tf_op jit(solution)/shard_map/ppermute | solution.py:40
  60.7 10.0 %collective-permute-start.15 = (bf16[256,256]{1,0:T(8,128)(2,1)S(1)}, bf16[256,256]{1,0:T(8,128)(2,1)S(1)}, u32[]{:S(2)}, u32[]{:S(2)}) collective-permute-start(bf16[256,256]{1,0:T(8,128)(2,1)S(1)} %get-tuple-element.58), channel_id=1, source_target_pairs={{0,8},{4,12},{8,0},{12,4},{16,24},{20,28},{24,16},{28,20},{1,9},{5... | collective-permute-start | bytes 393224 | tf_op jit(solution)/shard_map/ppermute | solution.py:40
  60.8 10.7 %collective-permute-start.16 = (bf16[256,256]{1,0:T(8,128)(2,1)S(1)}, bf16[256,256]{1,0:T(8,128)(2,1)S(1)}, u32[]{:S(2)}, u32[]{:S(2)}) collective-permute-start(bf16[256,256]{1,0:T(8,128)(2,1)S(1)} %get-tuple-element.59), channel_id=1, source_target_pairs={{0,24},{4,28},{8,16},{12,20},{16,8},{20,12},{24,0},{28,4},{1,25},{... | collective-permute-start | bytes 393224 | tf_op jit(solution)/shard_map/ppermute | solution.py:40
  62.3 12.9 %collective-permute-start.17 = (bf16[256,256]{1,0:T(8,128)(2,1)S(1)}, bf16[256,256]{1,0:T(8,128)(2,1)S(1)}, u32[]{:S(2)}, u32[]{:S(2)}) collective-permute-start(bf16[256,256]{1,0:T(8,128)(2,1)S(1)} %get-tuple-element.60), channel_id=1, source_target_pairs={{0,12},{4,8},{8,4},{12,0},{16,28},{20,24},{24,20},{28,16},{1,13},{... | collective-permute-start | bytes 393224 | tf_op jit(solution)/shard_map/ppermute | solution.py:40
  62.8 16.8 %collective-permute-start.18 = (bf16[256,256]{1,0:T(8,128)(2,1)S(1)}, bf16[256,256]{1,0:T(8,128)(2,1)S(1)}, u32[]{:S(2)}, u32[]{:S(2)}) collective-permute-start(bf16[256,256]{1,0:T(8,128)(2,1)S(1)} %get-tuple-element.64), channel_id=1, source_target_pairs={{0,20},{4,16},{8,28},{12,24},{16,4},{20,0},{24,12},{28,8},{1,21},{... | collective-permute-start | bytes 393224 | tf_op jit(solution)/shard_map/ppermute | solution.py:40
  66.1 13.4 %collective-permute-start.19 = (bf16[256,256]{1,0:T(8,128)(2,1)S(1)}, bf16[256,256]{1,0:T(8,128)(2,1)S(1)}, u32[]{:S(2)}, u32[]{:S(2)}) collective-permute-start(bf16[256,256]{1,0:T(8,128)(2,1)S(1)} %get-tuple-element.65), channel_id=1, source_target_pairs={{0,28},{4,24},{8,20},{12,16},{16,12},{20,8},{24,4},{28,0},{1,29},{... | collective-permute-start | bytes 393224 | tf_op jit(solution)/shard_map/ppermute | solution.py:40
  70.7 11.4 %collective-permute-start.20 = (bf16[256,256]{1,0:T(8,128)(2,1)S(1)}, bf16[256,256]{1,0:T(8,128)(2,1)S(1)}, u32[]{:S(2)}, u32[]{:S(2)}) collective-permute-start(bf16[256,256]{1,0:T(8,128)(2,1)S(1)} %get-tuple-element.66), channel_id=1, source_target_pairs={{0,4},{4,0},{8,12},{12,8},{16,20},{20,16},{24,28},{28,24},{1,5},{5... | collective-permute-start | bytes 393224 | tf_op jit(solution)/shard_map/ppermute | solution.py:40
  82.4 2.1 %collective-permute-start.23 = (f32[1,256]{1,0:T(1,128)S(1)}, f32[1,256]{1,0:T(1,128)S(1)}, u32[]{:S(2)}, u32[]{:S(2)}) collective-permute-start(f32[1,256]{1,0:T(1,128)S(1)} %get-tuple-element.68.refs_0_), channel_id=1, source_target_pairs={{0,1},{1,0},{2,3},{3,2},{4,5},{5,4},{6,7},{7,6},{8,9},{9,8},{10,11... | collective-permute-start | bytes 3080 | tf_op jit(solution)/shard_map/ppermute | solution.py:395
  82.5 3.6 %collective-permute-start.22 = (f32[1,256]{1,0:T(1,128)S(1)}, f32[1,256]{1,0:T(1,128)S(1)}, u32[]{:S(2)}, u32[]{:S(2)}) collective-permute-start(f32[1,256]{1,0:T(1,128)S(1)} %get-tuple-element.68.refs_0_), channel_id=1, source_target_pairs={{0,2},{1,3},{2,0},{3,1},{4,6},{5,7},{6,4},{7,5},{8,10},{9,11},{10,... | collective-permute-start | bytes 3080 | tf_op jit(solution)/shard_map/ppermute | solution.py:395
  84.4 3.0 %collective-permute-start.21 = (f32[1,256]{1,0:T(1,128)S(1)}, f32[1,256]{1,0:T(1,128)S(1)}, u32[]{:S(2)}, u32[]{:S(2)}) collective-permute-start(f32[1,256]{1,0:T(1,128)S(1)} %get-tuple-element.68.refs_0_), channel_id=1, source_target_pairs={{0,3},{1,2},{2,1},{3,0},{4,7},{5,6},{6,5},{7,4},{8,11},{9,10},{10,... | collective-permute-start | bytes 3080 | tf_op jit(solution)/shard_map/ppermute | solution.py:395
  (13 other events, 218.9 us)

commit v15 on v13

--- a/solution.py
+++ b/solution.py
@@ -180,8 +180,9 @@
     )(high, low, *[blocks[k] for k in steps])
 
 
-def early_kernel(count, steps, lag_ref, high_ref, low_ref, *refs):
-    blocks, (gs, fs, ss) = refs[:count], refs[count:]
+def early_kernel(count, steps, last, lag_ref, high_ref, low_ref, *refs):
+    blocks, (block, _, gs, fs, ss) = refs[:count], refs[count:]
+    gs[partner(last)] = transform(high_ref[...], low_ref[...], block[...])
     width, columns = gs.shape[1] // 2, gs.shape[2]
     for at, (k, block) in enumerate(zip(steps, blocks)):
         fs[at] = jnp.zeros(fs.shape[1:], jnp.float32)
@@ -211,20 +212,22 @@
     tiles(width, columns, tile)
 
 
-def early_products(lag_of_block, high, low, blocks, gated):
+def early_products(lag_of_block, high, low, blocks, last, block, gated):
     steps = list(blocks)
     count, twice, columns = gated.shape
     return pl.pallas_call(
-        functools.partial(early_kernel, count, steps),
+        functools.partial(early_kernel, count, steps, last),
         out_shape=[
+            jax.ShapeDtypeStruct(gated.shape, jnp.float32),
             jax.ShapeDtypeStruct((2 * count, twice, columns), jnp.float32),
             jax.ShapeDtypeStruct(gated.shape, jnp.float32),
         ],
-        in_specs=[pl.BlockSpec(memory_space=pltpu.SMEM)] + [WHOLE] * (3 + count),
-        out_specs=[WHOLE, WHOLE],
+        in_specs=[pl.BlockSpec(memory_space=pltpu.SMEM)] + [WHOLE] * (4 + count),
+        out_specs=[WHOLE, WHOLE, WHOLE],
+        input_output_aliases={4 + count: 0},
         compiler_params=pltpu.CompilerParams(vmem_limit_bytes=16 * MIB),
         cost_estimate=transform_cost(count, twice // 2, columns, 2),
-    )(lag_of_block, high, low, *[blocks[k] for k in steps], gated)
+    )(lag_of_block, high, low, *[blocks[k] for k in steps], block, gated)[1:]
 
 
 def inverse(table_high, table_low, total):
@@ -412,8 +415,9 @@
     filts[0], gates[0] = own[0], mine[0]
     early = order[: count // 2] + [0]
     gated = gated_spectra(count, *tabs[:2], {k: gates[k] for k in early})
-    filt, sums = early_products(lag_of_block, *tabs[:2], filts, gated)
-    sums, found = late_products(order[:1], tabs, filt, sums, {k: gates[k] for k in gates if k not in early})
+    last = order[-1]
+    filt, sums = early_products(lag_of_block, *tabs[:2], filts, last, gates[last], gated)
+    sums, found = late_products(order[:1], tabs, filt, sums, {k: gates[k] for k in gates if k not in early + [last]})
     found.update(inverses(order[1:] + [0], tabs, sums))
     for at, k in enumerate(order):
         block = found[k]
@@ -423,10 +427,11 @@
     convs[0] = found[0]
     pre, square = gated_output(query, skip[None, :], order[: count // 2] + [0], convs, mine)
     others = lax.axis_size("chan")
-    squares = [square] + [
-        lax.ppermute(square, "chan", [(d, d ^ step) for d in range(others)]) for step in reversed(range(1, others))
-    ]
-    return scaled(columns * others, pre, squares, out_gain[None, :])
+    step = 1
+    while step < others:
+        square = square + lax.ppermute(square, "chan", [(d, d ^ step) for d in range(others)])
+        step *= 2
+    return scaled(columns * others, pre, [square], out_gain[None, :])
 
 
 def solution(mesh):

time: 89 us -> 87 us (0.978)
  starting transfers between devices: 48.8 us -> 40.2 us
  waiting for transfers between devices: 19.6 us -> 26.9 us
    ppermute x21, starting transfers between devices: 46.9 us -> 39.1 us  [send(): return lax.ppermute(block, 'tok', [(d, d ^ step) for d in range(count)])]
    ppermute x21, waiting for transfers between devices: 16.8 us -> 23.1 us  [send(): return lax.ppermute(block, 'tok', [(d, d ^ step) for d in range(count)])]
    ppermute x3 -> x2, starting transfers between devices: 1.93 us -> 1.05 us  [local(): lax.ppermute(square, 'chan', [(d, d ^ step) for d in range(others)])]
    ppermute x3 -> x2, waiting for transfers between devices: 2.85 us -> 3.72 us  [local(): lax.ppermute(square, 'chan', [(d, d ^ step) for d in range(others)])]
  transfers between devices with their start and end apart: 24 -> 23, of which waited for: 8 -> 10; matrix products, arithmetic and copies ran while one was open for 0% -> 0% of each run, Pallas kernels for 10% -> 10%
where the time goes in v15:
time: 87 us; the launch traced here: 86.7 us
  starting transfers between devices  40.2 us (46%)
  waiting for transfers between devices  26.9 us (31%)
  Pallas kernels  13.9 us (16%)
  local copies, waits for them, and re-layouts  5.62 us (6%)
    ppermute x21, starting transfers between devices, send(): return lax.ppermute(block, 'tok', [(d, d ^ step) for d in range(count)])  39.1 us
    ppermute x21, waiting for transfers between devices, send(): return lax.ppermute(block, 'tok', [(d, d ^ step) for d in range(count)])  23.1 us
    unnamed x24, local copies, waits for them, and re-layouts  5.62 us
    pallas_call x1, Pallas kernels, early_products(): pl.pallas_call(functools.partial(early_kernel, count, steps, last), out_s...  5.01 us
    ppermute x2, waiting for transfers between devices, local(): lax.ppermute(square, 'chan', [(d, d ^ step) for d in range(others)])  3.72 us
    pallas_call x1, Pallas kernels, late_products(): pl.pallas_call(functools.partial(late_kernel, count, steps, first), out_s...  3.03 us
  transfers between devices with their start and end apart: 23, of which 10 were waited for; matrix products, arithmetic and copies ran while one was open for 0% of the time, Pallas kernels for 10%

profile of v15, /device:TPU:0, one launch (start us, length us, event | category | flops | bytes accessed | tf_op | source)
XLA Modules:
  0.0 86.7 jit_solution(1993253821625064658)
XLA Ops:
  1.5 4.1 %collective-permute-start = (bf16[256,256]{1,0:T(8,128)(2,1)S(1)}, bf16[256,256]{1,0:T(8,128)(2,1)S(1)}, u32[]{:S(2)}, u32[]{:S(2)}) collective-permute-start(bf16[256,256]{1,0:T(8,128)(2,1)S(1)} %get-tuple-element.41), channel_id=1, source_target_pairs={{0,16},{4,20},{8,24},{12,28},{16,0},{20,4},{24,8},{28,12},{1,17},{... | collective-permute-start | bytes 393224 | tf_op jit(solution)/shard_map/ppermute | solution.py:40
  5.6 1.6 %collective-permute-start.1 = (bf16[256,256]{1,0:T(8,128)(2,1)S(1)}, bf16[256,256]{1,0:T(8,128)(2,1)S(1)}, u32[]{:S(2)}, u32[]{:S(2)}) collective-permute-start(bf16[256,256]{1,0:T(8,128)(2,1)S(1)} %get-tuple-element.43), channel_id=1, source_target_pairs={{0,8},{4,12},{8,0},{12,4},{16,24},{20,28},{24,16},{28,20},{1,9},{5... | collective-permute-start | bytes 393224 | tf_op jit(solution)/shard_map/ppermute | solution.py:40
  7.2 1.8 %collective-permute-start.3 = (bf16[256,256]{1,0:T(8,128)(2,1)S(1)}, bf16[256,256]{1,0:T(8,128)(2,1)S(1)}, u32[]{:S(2)}, u32[]{:S(2)}) collective-permute-start(bf16[256,256]{1,0:T(8,128)(2,1)S(1)} %get-tuple-element.45), channel_id=1, source_target_pairs={{0,12},{4,8},{8,4},{12,0},{16,28},{20,24},{24,20},{28,16},{1,13},{... | collective-permute-start | bytes 393224 | tf_op jit(solution)/shard_map/ppermute | solution.py:40
  9.0 3.5 %collective-permute-start.4 = (bf16[256,256]{1,0:T(8,128)(2,1)S(1)}, bf16[256,256]{1,0:T(8,128)(2,1)S(1)}, u32[]{:S(2)}, u32[]{:S(2)}) collective-permute-start(bf16[256,256]{1,0:T(8,128)(2,1)S(1)} %get-tuple-element.46), channel_id=1, source_target_pairs={{0,20},{4,16},{8,28},{12,24},{16,4},{20,0},{24,12},{28,8},{1,21},{... | collective-permute-start | bytes 393224 | tf_op jit(solution)/shard_map/ppermute | solution.py:40
  13.5 1.2 %copy-done.5 = bf16[256,2048]{1,0:T(8,128)(2,1)S(1)} copy-done((bf16[256,2048]{1,0:T(8,128)(2,1)S(1)}, bf16[256,2048]{1,0:T(8,128)(2,1)}, u32[]{:S(2)}) %copy-start.5) | copy-done | bytes 1048600
  16.7 3.9 %collective-permute-start.10 = (bf16[256,256]{1,0:T(8,128)(2,1)S(1)}, bf16[256,256]{1,0:T(8,128)(2,1)S(1)}, u32[]{:S(2)}, u32[]{:S(2)}) collective-permute-start(bf16[256,256]{1,0:T(8,128)(2,1)S(1)} %get-tuple-element.55.refs_7_), channel_id=1, source_target_pairs={{0,24},{4,28},{8,16},{12,20},{16,8},{20,12},{24,0},{28,4},{1,25},{... | collective-permute-start | bytes 393224 | tf_op jit(solution)/shard_map/ppermute | solution.py:40
  20.6 2.5 %collective-permute-start.8 = (bf16[256,256]{1,0:T(8,128)(2,1)S(1)}, bf16[256,256]{1,0:T(8,128)(2,1)S(1)}, u32[]{:S(2)}, u32[]{:S(2)}) collective-permute-start(bf16[256,256]{1,0:T(8,128)(2,1)S(1)} %get-tuple-element.53.refs_5_), channel_id=1, source_target_pairs={{0,16},{4,20},{8,24},{12,28},{16,0},{20,4},{24,8},{28,12},{1,17},{... | collective-permute-start | bytes 393224 | tf_op jit(solution)/shard_map/ppermute | solution.py:40
  23.6 5.9 %collective-permute-done.4.refs_4_ = bf16[256,256]{1,0:T(8,128)(2,1)S(1)} collective-permute-done((bf16[256,256]{1,0:T(8,128)(2,1)S(1)}, bf16[256,256]{1,0:T(8,128)(2,1)S(1)}, u32[]{:S(2)}, u32[]{:S(2)}) %collective-permute-start.4) | collective-permute-done | bytes 131104 | tf_op jit(solution)/shard_map/ppermute | solution.py:40
  29.6 2.4 %collective-permute-start.5 = (bf16[256,256]{1,0:T(8,128)(2,1)S(1)}, bf16[256,256]{1,0:T(8,128)(2,1)S(1)}, u32[]{:S(2)}, u32[]{:S(2)}) collective-permute-start(bf16[256,256]{1,0:T(8,128)(2,1)S(1)} %get-tuple-element.47), channel_id=1, source_target_pairs={{0,28},{4,24},{8,20},{12,16},{16,12},{20,8},{24,4},{28,0},{1,29},{... | collective-permute-start | bytes 393224 | tf_op jit(solution)/shard_map/ppermute | solution.py:40
  32.0 1.5 %collective-permute-start.6 = (bf16[256,256]{1,0:T(8,128)(2,1)S(1)}, bf16[256,256]{1,0:T(8,128)(2,1)S(1)}, u32[]{:S(2)}, u32[]{:S(2)}) collective-permute-start(bf16[256,256]{1,0:T(8,128)(2,1)S(1)} %get-tuple-element.48), channel_id=1, source_target_pairs={{0,4},{4,0},{8,12},{12,8},{16,20},{20,16},{24,28},{28,24},{1,5},{5... | collective-permute-start | bytes 393224 | tf_op jit(solution)/shard_map/ppermute | solution.py:40
  34.0 4.0 %collective-permute-done.8.refs_0_ = bf16[256,256]{1,0:T(8,128)(2,1)S(1)} collective-permute-done((bf16[256,256]{1,0:T(8,128)(2,1)S(1)}, bf16[256,256]{1,0:T(8,128)(2,1)S(1)}, u32[]{:S(2)}, u32[]{:S(2)}) %collective-permute-start.8) | collective-permute-done | bytes 131104 | tf_op jit(solution)/shard_map/ppermute | solution.py:40
  38.9 4.4 %collective-permute-start.13 = (bf16[256,256]{1,0:T(8,128)(2,1)S(1)}, bf16[256,256]{1,0:T(8,128)(2,1)S(1)}, u32[]{:S(2)}, u32[]{:S(2)}) collective-permute-start(bf16[256,256]{1,0:T(8,128)(2,1)S(1)} %get-tuple-element.61.refs_6_), channel_id=1, source_target_pairs={{0,28},{4,24},{8,20},{12,16},{16,12},{20,8},{24,4},{28,0},{1,29},{... | collective-permute-start | bytes 393224 | tf_op jit(solution)/shard_map/ppermute | solution.py:40
  46.1 5.0 %shard_map.112 = (f32[8,512,256]{2,1,0:T(8,128)S(1)}, f32[16,512,256]{2,1,0:T(8,128)S(1)}, f32[8,512,256]{2,1,0:T(8,128)S(1)}) custom-call(s32[8]{0:T(128)S(1)} %copy-done.11, bf16[512,256]{1,0:T(8,128)(2,1)S(1)} %copy-done.1, bf16[512,256]{1,0:T(8,128)(2,1)S(1)} %copy-done.3, ...), custom_call_target="tpu_custom_call", output_to_operand_aliasing={{0}: (12, {})} | custom-call | flops 1073741824 | bytes 5242880 | tf_op jit(solution)/shard_map/pallas_call | solution.py:218
  51.2 3.0 %shard_map.113 = (f32[8,512,256]{2,1,0:T(8,128)S(1)}, bf16[256,256]{1,0:T(8,128)(2,1)S(1)}) custom-call(bf16[512,256]{1,0:T(8,128)(2,1)S(1)} %copy-done.2, bf16[512,256]{1,0:T(8,128)(2,1)S(1)} %copy-done.3, bf16[256,512]{1,0:T(8,128)(2,1)S(1)} %copy-done.7, bf16[256,512]{1,0:T(8,128)(2,1)S(1)} %copy-done.8, ...), custom_call_target="tpu_custom_call", output_to_operand_aliasing={{0}: (5, {})} | custom-call | flops 1610612736 | bytes 5242880 | tf_op jit(solution)/shard_map/pallas_call | solution.py:278
  54.3 3.8 %collective-permute-start.14 = (bf16[256,256]{1,0:T(8,128)(2,1)S(1)}, bf16[256,256]{1,0:T(8,128)(2,1)S(1)}, u32[]{:S(2)}, u32[]{:S(2)}) collective-permute-start(bf16[256,256]{1,0:T(8,128)(2,1)S(1)} %get-tuple-element.64), channel_id=1, source_target_pairs={{0,16},{4,20},{8,24},{12,28},{16,0},{20,4},{24,8},{28,12},{1,17},{... | collective-permute-start | bytes 393224 | tf_op jit(solution)/shard_map/ppermute | solution.py:40
  58.0 1.6 %shard_map.114 = (bf16[256,256]{1,0:T(8,128)(2,1)S(1)}, bf16[256,256]{1,0:T(8,128)(2,1)S(1)}, bf16[256,256]{1,0:T(8,128)(2,1)S(1)}, bf16[256,256]{1,0:T(8,128)(2...) custom-call(bf16[256,512]{1,0:T(8,128)(2,1)S(1)} %copy-done.7, ...), custom_call_target="tpu_custom_call" | custom-call | flops 1409286144 | bytes 4587520 | tf_op jit(solution)/shard_map/pallas_call | solution.py:300
  59.8 1.5 %collective-permute-start.16 = (bf16[256,256]{1,0:T(8,128)(2,1)S(1)}, bf16[256,256]{1,0:T(8,128)(2,1)S(1)}, u32[]{:S(2)}, u32[]{:S(2)}) collective-permute-start(bf16[256,256]{1,0:T(8,128)(2,1)S(1)} %get-tuple-element.67), channel_id=1, source_target_pairs={{0,24},{4,28},{8,16},{12,20},{16,8},{20,12},{24,0},{28,4},{1,25},{... | collective-permute-start | bytes 393224 | tf_op jit(solution)/shard_map/ppermute | solution.py:40
  61.9 3.2 %collective-permute-start.18 = (bf16[256,256]{1,0:T(8,128)(2,1)S(1)}, bf16[256,256]{1,0:T(8,128)(2,1)S(1)}, u32[]{:S(2)}, u32[]{:S(2)}) collective-permute-start(bf16[256,256]{1,0:T(8,128)(2,1)S(1)} %get-tuple-element.72), channel_id=1, source_target_pairs={{0,20},{4,16},{8,28},{12,24},{16,4},{20,0},{24,12},{28,8},{1,21},{... | collective-permute-start | bytes 393224 | tf_op jit(solution)/shard_map/ppermute | solution.py:40
  65.5 1.9 %collective-permute-start.19 = (bf16[256,256]{1,0:T(8,128)(2,1)S(1)}, bf16[256,256]{1,0:T(8,128)(2,1)S(1)}, u32[]{:S(2)}, u32[]{:S(2)}) collective-permute-start(bf16[256,256]{1,0:T(8,128)(2,1)S(1)} %get-tuple-element.73), channel_id=1, source_target_pairs={{0,28},{4,24},{8,20},{12,16},{16,12},{20,8},{24,4},{28,0},{1,29},{... | collective-permute-start | bytes 393224 | tf_op jit(solution)/shard_map/ppermute | solution.py:40
  67.4 3.2 %collective-permute-done.15.refs_1_ = bf16[256,256]{1,0:T(8,128)(2,1)S(1)} collective-permute-done((bf16[256,256]{1,0:T(8,128)(2,1)S(1)}, bf16[256,256]{1,0:T(8,128)(2,1)S(1)}, u32[]{:S(2)}, u32[]{:S(2)}) %collective-permute-start.15) | collective-permute-done | bytes 131104 | tf_op jit(solution)/shard_map/ppermute | solution.py:40
  71.2 1.6 %collective-permute-done.17.refs_3_ = bf16[256,256]{1,0:T(8,128)(2,1)S(1)} collective-permute-done((bf16[256,256]{1,0:T(8,128)(2,1)S(1)}, bf16[256,256]{1,0:T(8,128)(2,1)S(1)}, u32[]{:S(2)}, u32[]{:S(2)}) %collective-permute-start.17) | collective-permute-done | bytes 131104 | tf_op jit(solution)/shard_map/ppermute | solution.py:40
  73.3 5.6 %collective-permute-done.18.refs_2_ = bf16[256,256]{1,0:T(8,128)(2,1)S(1)} collective-permute-done((bf16[256,256]{1,0:T(8,128)(2,1)S(1)}, bf16[256,256]{1,0:T(8,128)(2,1)S(1)}, u32[]{:S(2)}, u32[]{:S(2)}) %collective-permute-start.18) | collective-permute-done | bytes 131104 | tf_op jit(solution)/shard_map/ppermute | solution.py:40
  82.6 2.6 %collective-permute-done.22 = f32[1,256]{1,0:T(1,128)S(1)} collective-permute-done((f32[1,256]{1,0:T(1,128)S(1)}, f32[1,256]{1,0:T(1,128)S(1)}, u32[]{:S(2)}, u32[]{:S(2)}) %collective-permute-start.22) | collective-permute-done | bytes 1056 | tf_op jit(solution)/shard_map/ppermute | solution.py:432
  85.2 1.5 %shard_map.117 = f32[256,2048]{1,0:T(8,128)} custom-call(f32[256,2048]{1,0:T(8,128)S(1)} %get-tuple-element.75.pre_ref, f32[1,2048]{1,0:T(1,128)S(1)} %bitcast.4, f32[1,256]{1,0:T(1,128)S(1)} %add.7.refs_0_), custom_call_target="tpu_custom_call" | custom-call | flops 1048576 | bytes 4194304 | tf_op jit(solution)/shard_map/pallas_call | solution.py:392
  (57 shorter events, 15.3 us)
Async XLA Ops:
  1.2 44.9 %copy-start.11 = (s32[8]{0:T(128)S(1)}, s32[8]{0:T(128)}, u32[]{:S(2)}) copy-start(s32[8]{0:T(128)} %lag_ref.1) | copy-start | bytes 100
  1.5 12.1 %collective-permute-start = (bf16[256,256]{1,0:T(8,128)(2,1)S(1)}, bf16[256,256]{1,0:T(8,128)(2,1)S(1)}, u32[]{:S(2)}, u32[]{:S(2)}) collective-permute-start(bf16[256,256]{1,0:T(8,128)(2,1)S(1)} %get-tuple-element.41), channel_id=1, source_target_pairs={{0,16},{4,20},{8,24},{12,28},{16,0},{20,4},{24,8},{28,12},{1,17},{... | collective-permute-start | bytes 393224 | tf_op jit(solution)/shard_map/ppermute | solution.py:40
  5.6 15.0 %collective-permute-start.1 = (bf16[256,256]{1,0:T(8,128)(2,1)S(1)}, bf16[256,256]{1,0:T(8,128)(2,1)S(1)}, u32[]{:S(2)}, u32[]{:S(2)}) collective-permute-start(bf16[256,256]{1,0:T(8,128)(2,1)S(1)} %get-tuple-element.43), channel_id=1, source_target_pairs={{0,8},{4,12},{8,0},{12,4},{16,24},{20,28},{24,16},{28,20},{1,9},{5... | collective-permute-start | bytes 393224 | tf_op jit(solution)/shard_map/ppermute | solution.py:40
  7.2 13.5 %collective-permute-start.2 = (bf16[256,256]{1,0:T(8,128)(2,1)S(1)}, bf16[256,256]{1,0:T(8,128)(2,1)S(1)}, u32[]{:S(2)}, u32[]{:S(2)}) collective-permute-start(bf16[256,256]{1,0:T(8,128)(2,1)S(1)} %get-tuple-element.44), channel_id=1, source_target_pairs={{0,24},{4,28},{8,16},{12,20},{16,8},{20,12},{24,0},{28,4},{1,25},{... | collective-permute-start | bytes 393224 | tf_op jit(solution)/shard_map/ppermute | solution.py:40
  7.2 15.9 %collective-permute-start.3 = (bf16[256,256]{1,0:T(8,128)(2,1)S(1)}, bf16[256,256]{1,0:T(8,128)(2,1)S(1)}, u32[]{:S(2)}, u32[]{:S(2)}) collective-permute-start(bf16[256,256]{1,0:T(8,128)(2,1)S(1)} %get-tuple-element.45), channel_id=1, source_target_pairs={{0,12},{4,8},{8,4},{12,0},{16,28},{20,24},{24,20},{28,16},{1,13},{... | collective-permute-start | bytes 393224 | tf_op jit(solution)/shard_map/ppermute | solution.py:40
  9.0 20.6 %collective-permute-start.4 = (bf16[256,256]{1,0:T(8,128)(2,1)S(1)}, bf16[256,256]{1,0:T(8,128)(2,1)S(1)}, u32[]{:S(2)}, u32[]{:S(2)}) collective-permute-start(bf16[256,256]{1,0:T(8,128)(2,1)S(1)} %get-tuple-element.46), channel_id=1, source_target_pairs={{0,20},{4,16},{8,28},{12,24},{16,4},{20,0},{24,12},{28,8},{1,21},{... | collective-permute-start | bytes 393224 | tf_op jit(solution)/shard_map/ppermute | solution.py:40
  16.7 15.2 %collective-permute-start.10 = (bf16[256,256]{1,0:T(8,128)(2,1)S(1)}, bf16[256,256]{1,0:T(8,128)(2,1)S(1)}, u32[]{:S(2)}, u32[]{:S(2)}) collective-permute-start(bf16[256,256]{1,0:T(8,128)(2,1)S(1)} %get-tuple-element.55.refs_7_), channel_id=1, source_target_pairs={{0,24},{4,28},{8,16},{12,20},{16,8},{20,12},{24,0},{28,4},{1,25},{... | collective-permute-start | bytes 393224 | tf_op jit(solution)/shard_map/ppermute | solution.py:40
  20.6 12.8 %collective-permute-start.11 = (bf16[256,256]{1,0:T(8,128)(2,1)S(1)}, bf16[256,256]{1,0:T(8,128)(2,1)S(1)}, u32[]{:S(2)}, u32[]{:S(2)}) collective-permute-start(bf16[256,256]{1,0:T(8,128)(2,1)S(1)} %get-tuple-element.56.refs_8_), channel_id=1, source_target_pairs={{0,12},{4,8},{8,4},{12,0},{16,28},{20,24},{24,20},{28,16},{1,13},{... | collective-permute-start | bytes 393224 | tf_op jit(solution)/shard_map/ppermute | solution.py:40
  20.6 17.4 %collective-permute-start.8 = (bf16[256,256]{1,0:T(8,128)(2,1)S(1)}, bf16[256,256]{1,0:T(8,128)(2,1)S(1)}, u32[]{:S(2)}, u32[]{:S(2)}) collective-permute-start(bf16[256,256]{1,0:T(8,128)(2,1)S(1)} %get-tuple-element.53.refs_5_), channel_id=1, source_target_pairs={{0,16},{4,20},{8,24},{12,28},{16,0},{20,4},{24,8},{28,12},{1,17},{... | collective-permute-start | bytes 393224 | tf_op jit(solution)/shard_map/ppermute | solution.py:40
  23.1 15.8 %collective-permute-start.9 = (bf16[256,256]{1,0:T(8,128)(2,1)S(1)}, bf16[256,256]{1,0:T(8,128)(2,1)S(1)}, u32[]{:S(2)}, u32[]{:S(2)}) collective-permute-start(bf16[256,256]{1,0:T(8,128)(2,1)S(1)} %get-tuple-element.54.refs_6_), channel_id=1, source_target_pairs={{0,8},{4,12},{8,0},{12,4},{16,24},{20,28},{24,16},{28,20},{1,9},{5... | collective-permute-start | bytes 393224 | tf_op jit(solution)/shard_map/ppermute | solution.py:40
  29.6 16.6 %collective-permute-start.5 = (bf16[256,256]{1,0:T(8,128)(2,1)S(1)}, bf16[256,256]{1,0:T(8,128)(2,1)S(1)}, u32[]{:S(2)}, u32[]{:S(2)}) collective-permute-start(bf16[256,256]{1,0:T(8,128)(2,1)S(1)} %get-tuple-element.47), channel_id=1, source_target_pairs={{0,28},{4,24},{8,20},{12,16},{16,12},{20,8},{24,4},{28,0},{1,29},{... | collective-permute-start | bytes 393224 | tf_op jit(solution)/shard_map/ppermute | solution.py:40
  32.0 14.2 %collective-permute-start.6 = (bf16[256,256]{1,0:T(8,128)(2,1)S(1)}, bf16[256,256]{1,0:T(8,128)(2,1)S(1)}, u32[]{:S(2)}, u32[]{:S(2)}) collective-permute-start(bf16[256,256]{1,0:T(8,128)(2,1)S(1)} %get-tuple-element.48), channel_id=1, source_target_pairs={{0,4},{4,0},{8,12},{12,8},{16,20},{20,16},{24,28},{28,24},{1,5},{5... | collective-permute-start | bytes 393224 | tf_op jit(solution)/shard_map/ppermute | solution.py:40
  33.5 12.7 %collective-permute-start.7 = (bf16[256,256]{1,0:T(8,128)(2,1)S(1)}, bf16[256,256]{1,0:T(8,128)(2,1)S(1)}, u32[]{:S(2)}, u32[]{:S(2)}) collective-permute-start(bf16[256,256]{1,0:T(8,128)(2,1)S(1)} %get-tuple-element.52.refs_7_), channel_id=1, source_target_pairs={{0,4},{4,0},{8,12},{12,8},{16,20},{20,16},{24,28},{28,24},{1,5},{5... | collective-permute-start | bytes 393224 | tf_op jit(solution)/shard_map/ppermute | solution.py:40
  38.0 13.1 %collective-permute-start.12 = (bf16[256,256]{1,0:T(8,128)(2,1)S(1)}, bf16[256,256]{1,0:T(8,128)(2,1)S(1)}, u32[]{:S(2)}, u32[]{:S(2)}) collective-permute-start(bf16[256,256]{1,0:T(8,128)(2,1)S(1)} %get-tuple-element.60.refs_5_), channel_id=1, source_target_pairs={{0,20},{4,16},{8,28},{12,24},{16,4},{20,0},{24,12},{28,8},{1,21},{... | collective-permute-start | bytes 393224 | tf_op jit(solution)/shard_map/ppermute | solution.py:40
  38.9 12.3 %collective-permute-start.13 = (bf16[256,256]{1,0:T(8,128)(2,1)S(1)}, bf16[256,256]{1,0:T(8,128)(2,1)S(1)}, u32[]{:S(2)}, u32[]{:S(2)}) collective-permute-start(bf16[256,256]{1,0:T(8,128)(2,1)S(1)} %get-tuple-element.61.refs_6_), channel_id=1, source_target_pairs={{0,28},{4,24},{8,20},{12,16},{16,12},{20,8},{24,4},{28,0},{1,29},{... | collective-permute-start | bytes 393224 | tf_op jit(solution)/shard_map/ppermute | solution.py:40
  54.3 11.3 %collective-permute-start.14 = (bf16[256,256]{1,0:T(8,128)(2,1)S(1)}, bf16[256,256]{1,0:T(8,128)(2,1)S(1)}, u32[]{:S(2)}, u32[]{:S(2)}) collective-permute-start(bf16[256,256]{1,0:T(8,128)(2,1)S(1)} %get-tuple-element.64), channel_id=1, source_target_pairs={{0,16},{4,20},{8,24},{12,28},{16,0},{20,4},{24,8},{28,12},{1,17},{... | collective-permute-start | bytes 393224 | tf_op jit(solution)/shard_map/ppermute | solution.py:40
  59.7 10.9 %collective-permute-start.15 = (bf16[256,256]{1,0:T(8,128)(2,1)S(1)}, bf16[256,256]{1,0:T(8,128)(2,1)S(1)}, u32[]{:S(2)}, u32[]{:S(2)}) collective-permute-start(bf16[256,256]{1,0:T(8,128)(2,1)S(1)} %get-tuple-element.66), channel_id=1, source_target_pairs={{0,8},{4,12},{8,0},{12,4},{16,24},{20,28},{24,16},{28,20},{1,9},{5... | collective-permute-start | bytes 393224 | tf_op jit(solution)/shard_map/ppermute | solution.py:40
  59.8 11.5 %collective-permute-start.16 = (bf16[256,256]{1,0:T(8,128)(2,1)S(1)}, bf16[256,256]{1,0:T(8,128)(2,1)S(1)}, u32[]{:S(2)}, u32[]{:S(2)}) collective-permute-start(bf16[256,256]{1,0:T(8,128)(2,1)S(1)} %get-tuple-element.67), channel_id=1, source_target_pairs={{0,24},{4,28},{8,16},{12,20},{16,8},{20,12},{24,0},{28,4},{1,25},{... | collective-permute-start | bytes 393224 | tf_op jit(solution)/shard_map/ppermute | solution.py:40
  61.2 11.7 %collective-permute-start.17 = (bf16[256,256]{1,0:T(8,128)(2,1)S(1)}, bf16[256,256]{1,0:T(8,128)(2,1)S(1)}, u32[]{:S(2)}, u32[]{:S(2)}) collective-permute-start(bf16[256,256]{1,0:T(8,128)(2,1)S(1)} %get-tuple-element.68), channel_id=1, source_target_pairs={{0,12},{4,8},{8,4},{12,0},{16,28},{20,24},{24,20},{28,16},{1,13},{... | collective-permute-start | bytes 393224 | tf_op jit(solution)/shard_map/ppermute | solution.py:40
  61.9 17.0 %collective-permute-start.18 = (bf16[256,256]{1,0:T(8,128)(2,1)S(1)}, bf16[256,256]{1,0:T(8,128)(2,1)S(1)}, u32[]{:S(2)}, u32[]{:S(2)}) collective-permute-start(bf16[256,256]{1,0:T(8,128)(2,1)S(1)} %get-tuple-element.72), channel_id=1, source_target_pairs={{0,20},{4,16},{8,28},{12,24},{16,4},{20,0},{24,12},{28,8},{1,21},{... | collective-permute-start | bytes 393224 | tf_op jit(solution)/shard_map/ppermute | solution.py:40
  65.5 13.4 %collective-permute-start.19 = (bf16[256,256]{1,0:T(8,128)(2,1)S(1)}, bf16[256,256]{1,0:T(8,128)(2,1)S(1)}, u32[]{:S(2)}, u32[]{:S(2)}) collective-permute-start(bf16[256,256]{1,0:T(8,128)(2,1)S(1)} %get-tuple-element.73), channel_id=1, source_target_pairs={{0,28},{4,24},{8,20},{12,16},{16,12},{20,8},{24,4},{28,0},{1,29},{... | collective-permute-start | bytes 393224 | tf_op jit(solution)/shard_map/ppermute | solution.py:40
  70.6 9.5 %collective-permute-start.20 = (bf16[256,256]{1,0:T(8,128)(2,1)S(1)}, bf16[256,256]{1,0:T(8,128)(2,1)S(1)}, u32[]{:S(2)}, u32[]{:S(2)}) collective-permute-start(bf16[256,256]{1,0:T(8,128)(2,1)S(1)} %get-tuple-element.74), channel_id=1, source_target_pairs={{0,4},{4,0},{8,12},{12,8},{16,20},{20,16},{24,28},{28,24},{1,5},{5... | collective-permute-start | bytes 393224 | tf_op jit(solution)/shard_map/ppermute | solution.py:40
  80.4 1.2 %collective-permute-start.21 = (f32[1,256]{1,0:T(1,128)S(1)}, f32[1,256]{1,0:T(1,128)S(1)}, u32[]{:S(2)}, u32[]{:S(2)}) collective-permute-start(f32[1,256]{1,0:T(1,128)S(1)} %get-tuple-element.76), channel_id=1, source_target_pairs={{0,1},{1,0},{2,3},{3,2},{4,5},{5,4},{6,7},{7,6},{8,9},{9,8},{10,11... | collective-permute-start | bytes 3080 | tf_op jit(solution)/shard_map/ppermute | solution.py:432
  81.7 3.6 %collective-permute-start.22 = (f32[1,256]{1,0:T(1,128)S(1)}, f32[1,256]{1,0:T(1,128)S(1)}, u32[]{:S(2)}, u32[]{:S(2)}) collective-permute-start(f32[1,256]{1,0:T(1,128)S(1)} %add.6), channel_id=1, source_target_pairs={{0,2},{1,3},{2,0},{3,1},{4,6},{5,7},{6,4},{7,5},{8,10},{9,11},{10,... | collective-permute-start | bytes 3080 | tf_op jit(solution)/shard_map/ppermute | solution.py:432
  (11 other events, 83.8 us)

commit v16 on v15

--- a/solution.py
+++ b/solution.py
@@ -236,29 +236,52 @@
     return (dot(table_high, high) + dot(table_high, low) + dot(table_low, high)).astype(jnp.bfloat16)
 
 
-def late_kernel(count, steps, first, fh_ref, fl_ref, ih_ref, il_ref, fs, sums, *refs):
-    blocks, ss, outs, gs = refs[: len(steps)], refs[len(steps)], refs[len(steps) + 1 : -1], refs[-1]
+def first_kernel(count, steps, first, fh_ref, fl_ref, ih_ref, il_ref, fs, ss, *refs):
+    blocks, (gs, out, total) = refs[: len(steps)], refs[len(steps) :]
     width, columns = blocks[0].shape
     for at, block in enumerate(blocks):
         gs[at] = transform(fh_ref[...], fl_ref[...], block[...])
-    shifted = [fs.at[pl.ds(count - partner(k), count)] for k in steps]
+    here = partner(first)
+    views = [(fs.at[count - partner(k) + here], fs.at[count - partner(k) + here - 1]) for k in steps]
+    sums = ss.at[here]
+
+    def tile(re_rows, im_rows, lanes, sign):
+        s_re, s_im = sums[re_rows, lanes], sums[im_rows, lanes]
+        for at, (now, before) in enumerate(views):
+            g_re, g_im = gs[at, re_rows, lanes], gs[at, im_rows, lanes]
+            f_re, f_im = now[re_rows, lanes], now[im_rows, lanes]
+            b_re, b_im = before[re_rows, lanes], before[im_rows, lanes]
+            f_re, f_im = (f_re - b_im, f_im + b_re) if sign > 0 else (f_re + b_im, f_im - b_re)
+            s_re = s_re + f_re * g_re - f_im * g_im
+            s_im = s_im + f_re * g_im + f_im * g_re
+        total[re_rows, lanes] = s_re
+        total[im_rows, lanes] = s_im
+
+    tiles(width, columns, tile)
+    out[...] = inverse(ih_ref[...], il_ref[...], total[...])
+
+
+def rest_kernel(count, late, steps, ih_ref, il_ref, fs, sums, gs, *refs):
+    outs, ss = refs[:-1], refs[-1]
+    width, columns = outs[0].shape
+    shifted = [fs.at[pl.ds(count - partner(k), count)] for k in late]
 
     def tile(re_rows, im_rows, lanes, sign):
         def both(ref, i):
             return ref[i, re_rows, lanes], ref[i, im_rows, lanes]
 
-        g = [both(gs, at) for at in range(len(steps))]
-        f = [[both(view, j) for view in shifted] for j in range(count)]
-        s = [both(ss, j) for j in range(count)]
+        g = [both(gs, at) for at in range(len(late))]
         d = []
         for j in range(count):
             d_re = d_im = None
-            for (f_re, f_im), (g_re, g_im) in zip(f[j], g):
+            for view, (g_re, g_im) in zip(shifted, g):
+                f_re, f_im = both(view, j)
                 p_re, p_im = f_re * g_re - f_im * g_im, f_re * g_im + f_im * g_re
                 d_re, d_im = (p_re, p_im) if d_re is None else (d_re + p_re, d_im + p_im)
             d.append((d_re, d_im))
         for j in range(count):
-            s_re, s_im = s[j][0] + d[j][0], s[j][1] + d[j][1]
+            s_re, s_im = both(sums, j)
+            s_re, s_im = s_re + d[j][0], s_im + d[j][1]
             if j and sign > 0:
                 s_re, s_im = s_re - d[j - 1][1], s_im + d[j - 1][0]
             elif j:
@@ -267,44 +290,40 @@
             ss[j, im_rows, lanes] = s_im
 
     tiles(width, columns, tile)
-    for k, out in zip(first, outs):
+    for k, out in zip(steps, outs):
         out[...] = inverse(ih_ref[...], il_ref[...], ss[partner(k)])
 
 
-def late_products(first, tabs, filt, sums, blocks):
+def first_product(first, tabs, filt, sums, blocks):
     steps = list(blocks)
     count, twice, columns = sums.shape
     width = twice // 2
-    found = pl.pallas_call(
-        functools.partial(late_kernel, count, steps, first),
-        out_shape=[jax.ShapeDtypeStruct(sums.shape, jnp.float32)]
-        + [jax.ShapeDtypeStruct((width, columns), jnp.bfloat16)] * len(first),
+    return pl.pallas_call(
+        functools.partial(first_kernel, count, steps, first),
+        out_shape=[
+            jax.ShapeDtypeStruct((len(steps), twice, columns), jnp.float32),
+            jax.ShapeDtypeStruct((width, columns), jnp.bfloat16),
+        ],
         in_specs=[WHOLE] * (6 + len(steps)),
-        out_specs=[WHOLE] * (1 + len(first)),
-        scratch_shapes=[pltpu.VMEM((len(steps), twice, columns), jnp.float32)],
-        input_output_aliases={5: 0},
+        out_specs=[WHOLE, WHOLE],
+        scratch_shapes=[pltpu.VMEM((twice, columns), jnp.float32)],
         compiler_params=pltpu.CompilerParams(vmem_limit_bytes=16 * MIB),
-        cost_estimate=transform_cost(count, width, columns, 3),
+        cost_estimate=transform_cost(count, width, columns, 1),
     )(*tabs, filt, sums, *[blocks[k] for k in steps])
-    return found[0], dict(zip(first, found[1:]))
-
-
-def inverse_kernel(steps, ih_ref, il_ref, ss, *outs):
-    for k, out in zip(steps, outs):
-        out[...] = inverse(ih_ref[...], il_ref[...], ss[partner(k)])
-
-
-def inverses(steps, tabs, sums):
+
+
+def rest_products(steps, tabs, filt, sums, late, spectra):
     count, twice, columns = sums.shape
     width = twice // 2
     found = pl.pallas_call(
-        functools.partial(inverse_kernel, steps),
+        functools.partial(rest_kernel, count, late, steps),
         out_shape=[jax.ShapeDtypeStruct((width, columns), jnp.bfloat16)] * len(steps),
-        in_specs=[WHOLE] * 3,
+        in_specs=[WHOLE] * 5,
         out_specs=[WHOLE] * len(steps),
+        scratch_shapes=[pltpu.VMEM(sums.shape, jnp.float32)],
         compiler_params=pltpu.CompilerParams(vmem_limit_bytes=16 * MIB),
-        cost_estimate=transform_cost(len(steps), width, columns, 3),
-    )(*tabs[2:], sums)
+        cost_estimate=transform_cost(count, width, columns, 3),
+    )(*tabs[2:], filt, sums, spectra)
     return dict(zip(steps, found))
 
 
@@ -417,8 +436,10 @@
     gated = gated_spectra(count, *tabs[:2], {k: gates[k] for k in early})
     last = order[-1]
     filt, sums = early_products(lag_of_block, *tabs[:2], filts, last, gates[last], gated)
-    sums, found = late_products(order[:1], tabs, filt, sums, {k: gates[k] for k in gates if k not in early + [last]})
-    found.update(inverses(order[1:] + [0], tabs, sums))
+    late = {k: gates[k] for k in gates if k not in early + [last]}
+    spectra, ahead = first_product(order[0], tabs, filt, sums, late)
+    found = rest_products(order[1:] + [0], tabs, filt, sums, list(late), spectra)
+    found[order[0]] = ahead
     for at, k in enumerate(order):
         block = found[k]
         if at == 6:

time: 87 us -> 86.2 us (level)
  waiting for transfers between devices: 26.9 us -> 25.5 us
  transfers between devices with their start and end apart: 23 -> 23, of which waited for: 10 -> 9; matrix products, arithmetic and copies ran while one was open for 0% -> 0% of each run, Pallas kernels for 10% -> 12%
where the time goes in v16:
time: 86.2 us; the launch traced here: 85.9 us
  starting transfers between devices  40.4 us (47%)
  waiting for transfers between devices  25.5 us (30%)
  Pallas kernels  14.3 us (17%)
  local copies, waits for them, and re-layouts  5.61 us (7%)
    ppermute x21, starting transfers between devices, send(): return lax.ppermute(block, 'tok', [(d, d ^ step) for d in range(count)])  38.8 us
    ppermute x21, waiting for transfers between devices, send(): return lax.ppermute(block, 'tok', [(d, d ^ step) for d in range(count)])  22.3 us
    unnamed x24, local copies, waits for them, and re-layouts  5.61 us
    pallas_call x1, Pallas kernels, early_products(): pl.pallas_call(functools.partial(early_kernel, count, steps, last), out_s...  5.01 us
    pallas_call x1, Pallas kernels, rest_products(): pl.pallas_call(functools.partial(rest_kernel, count, late, steps), out_sh...  3.36 us
    ppermute x2, waiting for transfers between devices, local(): lax.ppermute(square, 'chan', [(d, d ^ step) for d in range(others)])  3.17 us
  transfers between devices with their start and end apart: 23, of which 9 were waited for; matrix products, arithmetic and copies ran while one was open for 0% of the time, Pallas kernels for 12%

profile of v16, /device:TPU:0, one launch (start us, length us, event | category | flops | bytes accessed | tf_op | source)
XLA Modules:
  0.0 85.9 jit_solution(15508500880987548554)
XLA Ops:
  1.5 4.1 %collective-permute-start = (bf16[256,256]{1,0:T(8,128)(2,1)S(1)}, bf16[256,256]{1,0:T(8,128)(2,1)S(1)}, u32[]{:S(2)}, u32[]{:S(2)}) collective-permute-start(bf16[256,256]{1,0:T(8,128)(2,1)S(1)} %get-tuple-element.41), channel_id=1, source_target_pairs={{0,16},{4,20},{8,24},{12,28},{16,0},{20,4},{24,8},{28,12},{1,17},{... | collective-permute-start | bytes 393224 | tf_op jit(solution)/shard_map/ppermute | solution.py:40
  5.6 1.6 %collective-permute-start.1 = (bf16[256,256]{1,0:T(8,128)(2,1)S(1)}, bf16[256,256]{1,0:T(8,128)(2,1)S(1)}, u32[]{:S(2)}, u32[]{:S(2)}) collective-permute-start(bf16[256,256]{1,0:T(8,128)(2,1)S(1)} %get-tuple-element.43), channel_id=1, source_target_pairs={{0,8},{4,12},{8,0},{12,4},{16,24},{20,28},{24,16},{28,20},{1,9},{5... | collective-permute-start | bytes 393224 | tf_op jit(solution)/shard_map/ppermute | solution.py:40
  7.2 1.8 %collective-permute-start.3 = (bf16[256,256]{1,0:T(8,128)(2,1)S(1)}, bf16[256,256]{1,0:T(8,128)(2,1)S(1)}, u32[]{:S(2)}, u32[]{:S(2)}) collective-permute-start(bf16[256,256]{1,0:T(8,128)(2,1)S(1)} %get-tuple-element.45), channel_id=1, source_target_pairs={{0,12},{4,8},{8,4},{12,0},{16,28},{20,24},{24,20},{28,16},{1,13},{... | collective-permute-start | bytes 393224 | tf_op jit(solution)/shard_map/ppermute | solution.py:40
  9.0 3.5 %collective-permute-start.4 = (bf16[256,256]{1,0:T(8,128)(2,1)S(1)}, bf16[256,256]{1,0:T(8,128)(2,1)S(1)}, u32[]{:S(2)}, u32[]{:S(2)}) collective-permute-start(bf16[256,256]{1,0:T(8,128)(2,1)S(1)} %get-tuple-element.46), channel_id=1, source_target_pairs={{0,20},{4,16},{8,28},{12,24},{16,4},{20,0},{24,12},{28,8},{1,21},{... | collective-permute-start | bytes 393224 | tf_op jit(solution)/shard_map/ppermute | solution.py:40
  16.7 3.9 %collective-permute-start.10 = (bf16[256,256]{1,0:T(8,128)(2,1)S(1)}, bf16[256,256]{1,0:T(8,128)(2,1)S(1)}, u32[]{:S(2)}, u32[]{:S(2)}) collective-permute-start(bf16[256,256]{1,0:T(8,128)(2,1)S(1)} %get-tuple-element.55.refs_7_), channel_id=1, source_target_pairs={{0,24},{4,28},{8,16},{12,20},{16,8},{20,12},{24,0},{28,4},{1,25},{... | collective-permute-start | bytes 393224 | tf_op jit(solution)/shard_map/ppermute | solution.py:40
  20.6 2.5 %collective-permute-start.8 = (bf16[256,256]{1,0:T(8,128)(2,1)S(1)}, bf16[256,256]{1,0:T(8,128)(2,1)S(1)}, u32[]{:S(2)}, u32[]{:S(2)}) collective-permute-start(bf16[256,256]{1,0:T(8,128)(2,1)S(1)} %get-tuple-element.53.refs_5_), channel_id=1, source_target_pairs={{0,16},{4,20},{8,24},{12,28},{16,0},{20,4},{24,8},{28,12},{1,17},{... | collective-permute-start | bytes 393224 | tf_op jit(solution)/shard_map/ppermute | solution.py:40
  23.6 5.9 %collective-permute-done.4.refs_4_ = bf16[256,256]{1,0:T(8,128)(2,1)S(1)} collective-permute-done((bf16[256,256]{1,0:T(8,128)(2,1)S(1)}, bf16[256,256]{1,0:T(8,128)(2,1)S(1)}, u32[]{:S(2)}, u32[]{:S(2)}) %collective-permute-start.4) | collective-permute-done | bytes 131104 | tf_op jit(solution)/shard_map/ppermute | solution.py:40
  29.6 2.4 %collective-permute-start.5 = (bf16[256,256]{1,0:T(8,128)(2,1)S(1)}, bf16[256,256]{1,0:T(8,128)(2,1)S(1)}, u32[]{:S(2)}, u32[]{:S(2)}) collective-permute-start(bf16[256,256]{1,0:T(8,128)(2,1)S(1)} %get-tuple-element.47), channel_id=1, source_target_pairs={{0,28},{4,24},{8,20},{12,16},{16,12},{20,8},{24,4},{28,0},{1,29},{... | collective-permute-start | bytes 393224 | tf_op jit(solution)/shard_map/ppermute | solution.py:40
  32.0 1.5 %collective-permute-start.6 = (bf16[256,256]{1,0:T(8,128)(2,1)S(1)}, bf16[256,256]{1,0:T(8,128)(2,1)S(1)}, u32[]{:S(2)}, u32[]{:S(2)}) collective-permute-start(bf16[256,256]{1,0:T(8,128)(2,1)S(1)} %get-tuple-element.48), channel_id=1, source_target_pairs={{0,4},{4,0},{8,12},{12,8},{16,20},{20,16},{24,28},{28,24},{1,5},{5... | collective-permute-start | bytes 393224 | tf_op jit(solution)/shard_map/ppermute | solution.py:40
  34.0 4.0 %collective-permute-done.8.refs_0_ = bf16[256,256]{1,0:T(8,128)(2,1)S(1)} collective-permute-done((bf16[256,256]{1,0:T(8,128)(2,1)S(1)}, bf16[256,256]{1,0:T(8,128)(2,1)S(1)}, u32[]{:S(2)}, u32[]{:S(2)}) %collective-permute-start.8) | collective-permute-done | bytes 131104 | tf_op jit(solution)/shard_map/ppermute | solution.py:40
  38.9 4.4 %collective-permute-start.13 = (bf16[256,256]{1,0:T(8,128)(2,1)S(1)}, bf16[256,256]{1,0:T(8,128)(2,1)S(1)}, u32[]{:S(2)}, u32[]{:S(2)}) collective-permute-start(bf16[256,256]{1,0:T(8,128)(2,1)S(1)} %get-tuple-element.61.refs_6_), channel_id=1, source_target_pairs={{0,28},{4,24},{8,20},{12,16},{16,12},{20,8},{24,4},{28,0},{1,29},{... | collective-permute-start | bytes 393224 | tf_op jit(solution)/shard_map/ppermute | solution.py:40
  46.1 5.0 %shard_map.112 = (f32[8,512,256]{2,1,0:T(8,128)S(1)}, f32[16,512,256]{2,1,0:T(8,128)S(1)}, f32[8,512,256]{2,1,0:T(8,128)S(1)}) custom-call(s32[8]{0:T(128)S(1)} %copy-done.11, bf16[512,256]{1,0:T(8,128)(2,1)S(1)} %copy-done.1, bf16[512,256]{1,0:T(8,128)(2,1)S(1)} %copy-done.3, ...), custom_call_target="tpu_custom_call", output_to_operand_aliasing={{0}: (12, {})} | custom-call | flops 1073741824 | bytes 5242880 | tf_op jit(solution)/shard_map/pallas_call | solution.py:218
  51.2 1.7 %shard_map.113 = (f32[2,512,256]{2,1,0:T(8,128)S(1)}, bf16[256,256]{1,0:T(8,128)(2,1)S(1)}) custom-call(bf16[512,256]{1,0:T(8,128)(2,1)S(1)} %copy-done.2, bf16[512,256]{1,0:T(8,128)(2,1)S(1)} %copy-done.3, bf16[256,512]{1,0:T(8,128)(2,1)S(1)} %copy-done.4, bf16[256,512]{1,0:T(8,128)(2,1)S(1)} %copy-done.5, f32[16,512,256]{2,1,0:T(8,128)S(1)} %get-tuple-element.58.fs, ...), custom_call_target="tpu_custom_call" | custom-call | flops 536870912 | bytes 5242880 | tf_op jit(solution)/shard_map/pallas_call | solution.py:301
  52.9 3.8 %collective-permute-start.14 = (bf16[256,256]{1,0:T(8,128)(2,1)S(1)}, bf16[256,256]{1,0:T(8,128)(2,1)S(1)}, u32[]{:S(2)}, u32[]{:S(2)}) collective-permute-start(bf16[256,256]{1,0:T(8,128)(2,1)S(1)} %get-tuple-element.64), channel_id=1, source_target_pairs={{0,16},{4,20},{8,24},{12,28},{16,0},{20,4},{24,8},{28,12},{1,17},{... | collective-permute-start | bytes 393224 | tf_op jit(solution)/shard_map/ppermute | solution.py:40
  56.7 3.4 %shard_map.114 = (bf16[256,256]{1,0:T(8,128)(2,1)S(1)}, bf16[256,256]{1,0:T(8,128)(2,1)S(1)}, bf16[256,256]{1,0:T(8,128)(2,1)S(1)}, bf16[256,256]{1,0:T(8,128)(2...) custom-call(bf16[256,512]{1,0:T(8,128)(2,1)S(1)} %copy-done.4, ...), custom_call_target="tpu_custom_call" | custom-call | flops 1610612736 | bytes 5242880 | tf_op jit(solution)/shard_map/pallas_call | solution.py:318
  60.2 1.5 %collective-permute-start.16 = (bf16[256,256]{1,0:T(8,128)(2,1)S(1)}, bf16[256,256]{1,0:T(8,128)(2,1)S(1)}, u32[]{:S(2)}, u32[]{:S(2)}) collective-permute-start(bf16[256,256]{1,0:T(8,128)(2,1)S(1)} %get-tuple-element.67), channel_id=1, source_target_pairs={{0,24},{4,28},{8,16},{12,20},{16,8},{20,12},{24,0},{28,4},{1,25},{... | collective-permute-start | bytes 393224 | tf_op jit(solution)/shard_map/ppermute | solution.py:40
  62.3 3.2 %collective-permute-start.18 = (bf16[256,256]{1,0:T(8,128)(2,1)S(1)}, bf16[256,256]{1,0:T(8,128)(2,1)S(1)}, u32[]{:S(2)}, u32[]{:S(2)}) collective-permute-start(bf16[256,256]{1,0:T(8,128)(2,1)S(1)} %get-tuple-element.72), channel_id=1, source_target_pairs={{0,20},{4,16},{8,28},{12,24},{16,4},{20,0},{24,12},{28,8},{1,21},{... | collective-permute-start | bytes 393224 | tf_op jit(solution)/shard_map/ppermute | solution.py:40
  65.5 1.6 %collective-permute-start.19 = (bf16[256,256]{1,0:T(8,128)(2,1)S(1)}, bf16[256,256]{1,0:T(8,128)(2,1)S(1)}, u32[]{:S(2)}, u32[]{:S(2)}) collective-permute-start(bf16[256,256]{1,0:T(8,128)(2,1)S(1)} %get-tuple-element.73), channel_id=1, source_target_pairs={{0,28},{4,24},{8,20},{12,16},{16,12},{20,8},{24,4},{28,0},{1,29},{... | collective-permute-start | bytes 393224 | tf_op jit(solution)/shard_map/ppermute | solution.py:40
  67.1 3.3 %collective-permute-done.15.refs_1_ = bf16[256,256]{1,0:T(8,128)(2,1)S(1)} collective-permute-done((bf16[256,256]{1,0:T(8,128)(2,1)S(1)}, bf16[256,256]{1,0:T(8,128)(2,1)S(1)}, u32[]{:S(2)}, u32[]{:S(2)}) %collective-permute-start.15) | collective-permute-done | bytes 131104 | tf_op jit(solution)/shard_map/ppermute | solution.py:40
  70.9 2.1 %collective-permute-done.17.refs_3_ = bf16[256,256]{1,0:T(8,128)(2,1)S(1)} collective-permute-done((bf16[256,256]{1,0:T(8,128)(2,1)S(1)}, bf16[256,256]{1,0:T(8,128)(2,1)S(1)}, u32[]{:S(2)}, u32[]{:S(2)}) %collective-permute-start.17) | collective-permute-done | bytes 131104 | tf_op jit(solution)/shard_map/ppermute | solution.py:40
  73.5 4.9 %collective-permute-done.18.refs_2_ = bf16[256,256]{1,0:T(8,128)(2,1)S(1)} collective-permute-done((bf16[256,256]{1,0:T(8,128)(2,1)S(1)}, bf16[256,256]{1,0:T(8,128)(2,1)S(1)}, u32[]{:S(2)}, u32[]{:S(2)}) %collective-permute-start.18) | collective-permute-done | bytes 131104 | tf_op jit(solution)/shard_map/ppermute | solution.py:40
  80.9 1.5 %collective-permute-start.22 = (f32[1,256]{1,0:T(1,128)S(1)}, f32[1,256]{1,0:T(1,128)S(1)}, u32[]{:S(2)}, u32[]{:S(2)}) collective-permute-start(f32[1,256]{1,0:T(1,128)S(1)} %add.6), channel_id=1, source_target_pairs={{0,2},{1,3},{2,0},{3,1},{4,6},{5,7},{6,4},{7,5},{8,10},{9,11},{10,... | collective-permute-start | bytes 3080 | tf_op jit(solution)/shard_map/ppermute | solution.py:453
  82.4 2.0 %collective-permute-done.22 = f32[1,256]{1,0:T(1,128)S(1)} collective-permute-done((f32[1,256]{1,0:T(1,128)S(1)}, f32[1,256]{1,0:T(1,128)S(1)}, u32[]{:S(2)}, u32[]{:S(2)}) %collective-permute-start.22) | collective-permute-done | bytes 1056 | tf_op jit(solution)/shard_map/ppermute | solution.py:453
  84.4 1.5 %shard_map.117 = f32[256,2048]{1,0:T(8,128)} custom-call(f32[256,2048]{1,0:T(8,128)S(1)} %get-tuple-element.75.pre_ref, f32[1,2048]{1,0:T(1,128)S(1)} %bitcast.4, f32[1,256]{1,0:T(1,128)S(1)} %add.7.refs_0_), custom_call_target="tpu_custom_call" | custom-call | flops 1048576 | bytes 4194304 | tf_op jit(solution)/shard_map/pallas_call | solution.py:411
  (57 shorter events, 14.7 us)
Async XLA Ops:
  1.2 44.9 %copy-start.11 = (s32[8]{0:T(128)S(1)}, s32[8]{0:T(128)}, u32[]{:S(2)}) copy-start(s32[8]{0:T(128)} %lag_ref.1) | copy-start | bytes 100
  1.5 12.1 %collective-permute-start = (bf16[256,256]{1,0:T(8,128)(2,1)S(1)}, bf16[256,256]{1,0:T(8,128)(2,1)S(1)}, u32[]{:S(2)}, u32[]{:S(2)}) collective-permute-start(bf16[256,256]{1,0:T(8,128)(2,1)S(1)} %get-tuple-element.41), channel_id=1, source_target_pairs={{0,16},{4,20},{8,24},{12,28},{16,0},{20,4},{24,8},{28,12},{1,17},{... | collective-permute-start | bytes 393224 | tf_op jit(solution)/shard_map/ppermute | solution.py:40
  5.6 15.0 %collective-permute-start.1 = (bf16[256,256]{1,0:T(8,128)(2,1)S(1)}, bf16[256,256]{1,0:T(8,128)(2,1)S(1)}, u32[]{:S(2)}, u32[]{:S(2)}) collective-permute-start(bf16[256,256]{1,0:T(8,128)(2,1)S(1)} %get-tuple-element.43), channel_id=1, source_target_pairs={{0,8},{4,12},{8,0},{12,4},{16,24},{20,28},{24,16},{28,20},{1,9},{5... | collective-permute-start | bytes 393224 | tf_op jit(solution)/shard_map/ppermute | solution.py:40
  7.2 13.5 %collective-permute-start.2 = (bf16[256,256]{1,0:T(8,128)(2,1)S(1)}, bf16[256,256]{1,0:T(8,128)(2,1)S(1)}, u32[]{:S(2)}, u32[]{:S(2)}) collective-permute-start(bf16[256,256]{1,0:T(8,128)(2,1)S(1)} %get-tuple-element.44), channel_id=1, source_target_pairs={{0,24},{4,28},{8,16},{12,20},{16,8},{20,12},{24,0},{28,4},{1,25},{... | collective-permute-start | bytes 393224 | tf_op jit(solution)/shard_map/ppermute | solution.py:40
  7.2 15.9 %collective-permute-start.3 = (bf16[256,256]{1,0:T(8,128)(2,1)S(1)}, bf16[256,256]{1,0:T(8,128)(2,1)S(1)}, u32[]{:S(2)}, u32[]{:S(2)}) collective-permute-start(bf16[256,256]{1,0:T(8,128)(2,1)S(1)} %get-tuple-element.45), channel_id=1, source_target_pairs={{0,12},{4,8},{8,4},{12,0},{16,28},{20,24},{24,20},{28,16},{1,13},{... | collective-permute-start | bytes 393224 | tf_op jit(solution)/shard_map/ppermute | solution.py:40
  9.0 20.6 %collective-permute-start.4 = (bf16[256,256]{1,0:T(8,128)(2,1)S(1)}, bf16[256,256]{1,0:T(8,128)(2,1)S(1)}, u32[]{:S(2)}, u32[]{:S(2)}) collective-permute-start(bf16[256,256]{1,0:T(8,128)(2,1)S(1)} %get-tuple-element.46), channel_id=1, source_target_pairs={{0,20},{4,16},{8,28},{12,24},{16,4},{20,0},{24,12},{28,8},{1,21},{... | collective-permute-start | bytes 393224 | tf_op jit(solution)/shard_map/ppermute | solution.py:40
  16.7 15.2 %collective-permute-start.10 = (bf16[256,256]{1,0:T(8,128)(2,1)S(1)}, bf16[256,256]{1,0:T(8,128)(2,1)S(1)}, u32[]{:S(2)}, u32[]{:S(2)}) collective-permute-start(bf16[256,256]{1,0:T(8,128)(2,1)S(1)} %get-tuple-element.55.refs_7_), channel_id=1, source_target_pairs={{0,24},{4,28},{8,16},{12,20},{16,8},{20,12},{24,0},{28,4},{1,25},{... | collective-permute-start | bytes 393224 | tf_op jit(solution)/shard_map/ppermute | solution.py:40
  20.6 12.8 %collective-permute-start.11 = (bf16[256,256]{1,0:T(8,128)(2,1)S(1)}, bf16[256,256]{1,0:T(8,128)(2,1)S(1)}, u32[]{:S(2)}, u32[]{:S(2)}) collective-permute-start(bf16[256,256]{1,0:T(8,128)(2,1)S(1)} %get-tuple-element.56.refs_8_), channel_id=1, source_target_pairs={{0,12},{4,8},{8,4},{12,0},{16,28},{20,24},{24,20},{28,16},{1,13},{... | collective-permute-start | bytes 393224 | tf_op jit(solution)/shard_map/ppermute | solution.py:40
  20.6 17.4 %collective-permute-start.8 = (bf16[256,256]{1,0:T(8,128)(2,1)S(1)}, bf16[256,256]{1,0:T(8,128)(2,1)S(1)}, u32[]{:S(2)}, u32[]{:S(2)}) collective-permute-start(bf16[256,256]{1,0:T(8,128)(2,1)S(1)} %get-tuple-element.53.refs_5_), channel_id=1, source_target_pairs={{0,16},{4,20},{8,24},{12,28},{16,0},{20,4},{24,8},{28,12},{1,17},{... | collective-permute-start | bytes 393224 | tf_op jit(solution)/shard_map/ppermute | solution.py:40
  23.1 15.8 %collective-permute-start.9 = (bf16[256,256]{1,0:T(8,128)(2,1)S(1)}, bf16[256,256]{1,0:T(8,128)(2,1)S(1)}, u32[]{:S(2)}, u32[]{:S(2)}) collective-permute-start(bf16[256,256]{1,0:T(8,128)(2,1)S(1)} %get-tuple-element.54.refs_6_), channel_id=1, source_target_pairs={{0,8},{4,12},{8,0},{12,4},{16,24},{20,28},{24,16},{28,20},{1,9},{5... | collective-permute-start | bytes 393224 | tf_op jit(solution)/shard_map/ppermute | solution.py:40
  29.6 16.5 %collective-permute-start.5 = (bf16[256,256]{1,0:T(8,128)(2,1)S(1)}, bf16[256,256]{1,0:T(8,128)(2,1)S(1)}, u32[]{:S(2)}, u32[]{:S(2)}) collective-permute-start(bf16[256,256]{1,0:T(8,128)(2,1)S(1)} %get-tuple-element.47), channel_id=1, source_target_pairs={{0,28},{4,24},{8,20},{12,16},{16,12},{20,8},{24,4},{28,0},{1,29},{... | collective-permute-start | bytes 393224 | tf_op jit(solution)/shard_map/ppermute | solution.py:40
  32.0 14.2 %collective-permute-start.6 = (bf16[256,256]{1,0:T(8,128)(2,1)S(1)}, bf16[256,256]{1,0:T(8,128)(2,1)S(1)}, u32[]{:S(2)}, u32[]{:S(2)}) collective-permute-start(bf16[256,256]{1,0:T(8,128)(2,1)S(1)} %get-tuple-element.48), channel_id=1, source_target_pairs={{0,4},{4,0},{8,12},{12,8},{16,20},{20,16},{24,28},{28,24},{1,5},{5... | collective-permute-start | bytes 393224 | tf_op jit(solution)/shard_map/ppermute | solution.py:40
  33.5 12.7 %collective-permute-start.7 = (bf16[256,256]{1,0:T(8,128)(2,1)S(1)}, bf16[256,256]{1,0:T(8,128)(2,1)S(1)}, u32[]{:S(2)}, u32[]{:S(2)}) collective-permute-start(bf16[256,256]{1,0:T(8,128)(2,1)S(1)} %get-tuple-element.52.refs_7_), channel_id=1, source_target_pairs={{0,4},{4,0},{8,12},{12,8},{16,20},{20,16},{24,28},{28,24},{1,5},{5... | collective-permute-start | bytes 393224 | tf_op jit(solution)/shard_map/ppermute | solution.py:40
  38.0 13.1 %collective-permute-start.12 = (bf16[256,256]{1,0:T(8,128)(2,1)S(1)}, bf16[256,256]{1,0:T(8,128)(2,1)S(1)}, u32[]{:S(2)}, u32[]{:S(2)}) collective-permute-start(bf16[256,256]{1,0:T(8,128)(2,1)S(1)} %get-tuple-element.60.refs_5_), channel_id=1, source_target_pairs={{0,20},{4,16},{8,28},{12,24},{16,4},{20,0},{24,12},{28,8},{1,21},{... | collective-permute-start | bytes 393224 | tf_op jit(solution)/shard_map/ppermute | solution.py:40
  38.9 12.3 %collective-permute-start.13 = (bf16[256,256]{1,0:T(8,128)(2,1)S(1)}, bf16[256,256]{1,0:T(8,128)(2,1)S(1)}, u32[]{:S(2)}, u32[]{:S(2)}) collective-permute-start(bf16[256,256]{1,0:T(8,128)(2,1)S(1)} %get-tuple-element.61.refs_6_), channel_id=1, source_target_pairs={{0,28},{4,24},{8,20},{12,16},{16,12},{20,8},{24,4},{28,0},{1,29},{... | collective-permute-start | bytes 393224 | tf_op jit(solution)/shard_map/ppermute | solution.py:40
  52.9 12.6 %collective-permute-start.14 = (bf16[256,256]{1,0:T(8,128)(2,1)S(1)}, bf16[256,256]{1,0:T(8,128)(2,1)S(1)}, u32[]{:S(2)}, u32[]{:S(2)}) collective-permute-start(bf16[256,256]{1,0:T(8,128)(2,1)S(1)} %get-tuple-element.64), channel_id=1, source_target_pairs={{0,16},{4,20},{8,24},{12,28},{16,0},{20,4},{24,8},{28,12},{1,17},{... | collective-permute-start | bytes 393224 | tf_op jit(solution)/shard_map/ppermute | solution.py:40
  60.1 10.3 %collective-permute-start.15 = (bf16[256,256]{1,0:T(8,128)(2,1)S(1)}, bf16[256,256]{1,0:T(8,128)(2,1)S(1)}, u32[]{:S(2)}, u32[]{:S(2)}) collective-permute-start(bf16[256,256]{1,0:T(8,128)(2,1)S(1)} %get-tuple-element.66), channel_id=1, source_target_pairs={{0,8},{4,12},{8,0},{12,4},{16,24},{20,28},{24,16},{28,20},{1,9},{5... | collective-permute-start | bytes 393224 | tf_op jit(solution)/shard_map/ppermute | solution.py:40
  60.2 10.8 %collective-permute-start.16 = (bf16[256,256]{1,0:T(8,128)(2,1)S(1)}, bf16[256,256]{1,0:T(8,128)(2,1)S(1)}, u32[]{:S(2)}, u32[]{:S(2)}) collective-permute-start(bf16[256,256]{1,0:T(8,128)(2,1)S(1)} %get-tuple-element.67), channel_id=1, source_target_pairs={{0,24},{4,28},{8,16},{12,20},{16,8},{20,12},{24,0},{28,4},{1,25},{... | collective-permute-start | bytes 393224 | tf_op jit(solution)/shard_map/ppermute | solution.py:40
  61.7 11.4 %collective-permute-start.17 = (bf16[256,256]{1,0:T(8,128)(2,1)S(1)}, bf16[256,256]{1,0:T(8,128)(2,1)S(1)}, u32[]{:S(2)}, u32[]{:S(2)}) collective-permute-start(bf16[256,256]{1,0:T(8,128)(2,1)S(1)} %get-tuple-element.68), channel_id=1, source_target_pairs={{0,12},{4,8},{8,4},{12,0},{16,28},{20,24},{24,20},{28,16},{1,13},{... | collective-permute-start | bytes 393224 | tf_op jit(solution)/shard_map/ppermute | solution.py:40
  62.3 16.1 %collective-permute-start.18 = (bf16[256,256]{1,0:T(8,128)(2,1)S(1)}, bf16[256,256]{1,0:T(8,128)(2,1)S(1)}, u32[]{:S(2)}, u32[]{:S(2)}) collective-permute-start(bf16[256,256]{1,0:T(8,128)(2,1)S(1)} %get-tuple-element.72), channel_id=1, source_target_pairs={{0,20},{4,16},{8,28},{12,24},{16,4},{20,0},{24,12},{28,8},{1,21},{... | collective-permute-start | bytes 393224 | tf_op jit(solution)/shard_map/ppermute | solution.py:40
  65.5 12.9 %collective-permute-start.19 = (bf16[256,256]{1,0:T(8,128)(2,1)S(1)}, bf16[256,256]{1,0:T(8,128)(2,1)S(1)}, u32[]{:S(2)}, u32[]{:S(2)}) collective-permute-start(bf16[256,256]{1,0:T(8,128)(2,1)S(1)} %get-tuple-element.73), channel_id=1, source_target_pairs={{0,28},{4,24},{8,20},{12,16},{16,12},{20,8},{24,4},{28,0},{1,29},{... | collective-permute-start | bytes 393224 | tf_op jit(solution)/shard_map/ppermute | solution.py:40
  70.4 8.8 %collective-permute-start.20 = (bf16[256,256]{1,0:T(8,128)(2,1)S(1)}, bf16[256,256]{1,0:T(8,128)(2,1)S(1)}, u32[]{:S(2)}, u32[]{:S(2)}) collective-permute-start(bf16[256,256]{1,0:T(8,128)(2,1)S(1)} %get-tuple-element.74), channel_id=1, source_target_pairs={{0,4},{4,0},{8,12},{12,8},{16,20},{20,16},{24,28},{28,24},{1,5},{5... | collective-permute-start | bytes 393224 | tf_op jit(solution)/shard_map/ppermute | solution.py:40
  79.7 1.2 %collective-permute-start.21 = (f32[1,256]{1,0:T(1,128)S(1)}, f32[1,256]{1,0:T(1,128)S(1)}, u32[]{:S(2)}, u32[]{:S(2)}) collective-permute-start(f32[1,256]{1,0:T(1,128)S(1)} %get-tuple-element.76), channel_id=1, source_target_pairs={{0,1},{1,0},{2,3},{3,2},{4,5},{5,4},{6,7},{7,6},{8,9},{9,8},{10,11... | collective-permute-start | bytes 3080 | tf_op jit(solution)/shard_map/ppermute | solution.py:453
  80.9 3.6 %collective-permute-start.22 = (f32[1,256]{1,0:T(1,128)S(1)}, f32[1,256]{1,0:T(1,128)S(1)}, u32[]{:S(2)}, u32[]{:S(2)}) collective-permute-start(f32[1,256]{1,0:T(1,128)S(1)} %add.6), channel_id=1, source_target_pairs={{0,2},{1,3},{2,0},{3,1},{4,6},{5,7},{6,4},{7,5},{8,10},{9,11},{10,... | collective-permute-start | bytes 3080 | tf_op jit(solution)/shard_map/ppermute | solution.py:453
  (11 other events, 77.9 us)

commit v17 on v16

--- a/solution.py
+++ b/solution.py
@@ -438,15 +438,16 @@
     filt, sums = early_products(lag_of_block, *tabs[:2], filts, last, gates[last], gated)
     late = {k: gates[k] for k in gates if k not in early + [last]}
     spectra, ahead = first_product(order[0], tabs, filt, sums, late)
-    found = rest_products(order[1:] + [0], tabs, filt, sums, list(late), spectra)
+    found = rest_products([order[2], order[1]] + order[3:] + [0], tabs, filt, sums, list(late), spectra)
     found[order[0]] = ahead
-    for at, k in enumerate(order):
+    returns = [order[0], order[2], order[1]] + order[3:]
+    for at, k in enumerate(returns):
         block = found[k]
         if at == 6:
             block, convs[order[0]] = lax.optimization_barrier((block, convs[order[0]]))
         convs[k] = send(block, k, count)
     convs[0] = found[0]
-    pre, square = gated_output(query, skip[None, :], order[: count // 2] + [0], convs, mine)
+    pre, square = gated_output(query, skip[None, :], returns[: count // 2] + [0], convs, mine)
     others = lax.axis_size("chan")
     step = 1
     while step < others:

time: 86.2 us -> 86.1 us (level)
  transfers between devices with their start and end apart: 23 -> 23, of which waited for: 9 -> 10; matrix products, arithmetic and copies ran while one was open for 0% -> 0% of each run, Pallas kernels for 12% -> 12%
where the time goes in v17:
time: 86.1 us; the launch traced here: 85.9 us
  starting transfers between devices  40.8 us (47%)
  waiting for transfers between devices  24.9 us (29%)
  Pallas kernels  14.3 us (17%)
  local copies, waits for them, and re-layouts  5.61 us (7%)
    ppermute x21, starting transfers between devices, send(): return lax.ppermute(block, 'tok', [(d, d ^ step) for d in range(count)])  39.5 us
    ppermute x21, waiting for transfers between devices, send(): return lax.ppermute(block, 'tok', [(d, d ^ step) for d in range(count)])  21.5 us
    unnamed x24, local copies, waits for them, and re-layouts  5.61 us
    pallas_call x1, Pallas kernels, early_products(): pl.pallas_call(functools.partial(early_kernel, count, steps, last), out_s...  5.01 us
    ppermute x2, waiting for transfers between devices, local(): lax.ppermute(square, 'chan', [(d, d ^ step) for d in range(others)])  3.48 us
    pallas_call x1, Pallas kernels, rest_products(): pl.pallas_call(functools.partial(rest_kernel, count, late, steps), out_sh...  3.36 us
  transfers between devices with their start and end apart: 23, of which 10 were waited for; matrix products, arithmetic and copies ran while one was open for 0% of the time, Pallas kernels for 12%

profile of v17, /device:TPU:0, one launch (start us, length us, event | category | flops | bytes accessed | tf_op | source)
XLA Modules:
  0.0 85.9 jit_solution(7961415214408244421)
XLA Ops:
  1.5 4.1 %collective-permute-start = (bf16[256,256]{1,0:T(8,128)(2,1)S(1)}, bf16[256,256]{1,0:T(8,128)(2,1)S(1)}, u32[]{:S(2)}, u32[]{:S(2)}) collective-permute-start(bf16[256,256]{1,0:T(8,128)(2,1)S(1)} %get-tuple-element.41), channel_id=1, source_target_pairs={{0,16},{4,20},{8,24},{12,28},{16,0},{20,4},{24,8},{28,12},{1,17},{... | collective-permute-start | bytes 393224 | tf_op jit(solution)/shard_map/ppermute | solution.py:40
  5.6 1.6 %collective-permute-start.1 = (bf16[256,256]{1,0:T(8,128)(2,1)S(1)}, bf16[256,256]{1,0:T(8,128)(2,1)S(1)}, u32[]{:S(2)}, u32[]{:S(2)}) collective-permute-start(bf16[256,256]{1,0:T(8,128)(2,1)S(1)} %get-tuple-element.43), channel_id=1, source_target_pairs={{0,8},{4,12},{8,0},{12,4},{16,24},{20,28},{24,16},{28,20},{1,9},{5... | collective-permute-start | bytes 393224 | tf_op jit(solution)/shard_map/ppermute | solution.py:40
  7.2 1.8 %collective-permute-start.3 = (bf16[256,256]{1,0:T(8,128)(2,1)S(1)}, bf16[256,256]{1,0:T(8,128)(2,1)S(1)}, u32[]{:S(2)}, u32[]{:S(2)}) collective-permute-start(bf16[256,256]{1,0:T(8,128)(2,1)S(1)} %get-tuple-element.45), channel_id=1, source_target_pairs={{0,12},{4,8},{8,4},{12,0},{16,28},{20,24},{24,20},{28,16},{1,13},{... | collective-permute-start | bytes 393224 | tf_op jit(solution)/shard_map/ppermute | solution.py:40
  9.0 3.5 %collective-permute-start.4 = (bf16[256,256]{1,0:T(8,128)(2,1)S(1)}, bf16[256,256]{1,0:T(8,128)(2,1)S(1)}, u32[]{:S(2)}, u32[]{:S(2)}) collective-permute-start(bf16[256,256]{1,0:T(8,128)(2,1)S(1)} %get-tuple-element.46), channel_id=1, source_target_pairs={{0,20},{4,16},{8,28},{12,24},{16,4},{20,0},{24,12},{28,8},{1,21},{... | collective-permute-start | bytes 393224 | tf_op jit(solution)/shard_map/ppermute | solution.py:40
  16.7 3.9 %collective-permute-start.10 = (bf16[256,256]{1,0:T(8,128)(2,1)S(1)}, bf16[256,256]{1,0:T(8,128)(2,1)S(1)}, u32[]{:S(2)}, u32[]{:S(2)}) collective-permute-start(bf16[256,256]{1,0:T(8,128)(2,1)S(1)} %get-tuple-element.55.refs_6_), channel_id=1, source_target_pairs={{0,24},{4,28},{8,16},{12,20},{16,8},{20,12},{24,0},{28,4},{1,25},{... | collective-permute-start | bytes 393224 | tf_op jit(solution)/shard_map/ppermute | solution.py:40
  20.6 2.5 %collective-permute-start.8 = (bf16[256,256]{1,0:T(8,128)(2,1)S(1)}, bf16[256,256]{1,0:T(8,128)(2,1)S(1)}, u32[]{:S(2)}, u32[]{:S(2)}) collective-permute-start(bf16[256,256]{1,0:T(8,128)(2,1)S(1)} %get-tuple-element.53.refs_5_), channel_id=1, source_target_pairs={{0,16},{4,20},{8,24},{12,28},{16,0},{20,4},{24,8},{28,12},{1,17},{... | collective-permute-start | bytes 393224 | tf_op jit(solution)/shard_map/ppermute | solution.py:40
  23.6 5.9 %collective-permute-done.4.refs_4_ = bf16[256,256]{1,0:T(8,128)(2,1)S(1)} collective-permute-done((bf16[256,256]{1,0:T(8,128)(2,1)S(1)}, bf16[256,256]{1,0:T(8,128)(2,1)S(1)}, u32[]{:S(2)}, u32[]{:S(2)}) %collective-permute-start.4) | collective-permute-done | bytes 131104 | tf_op jit(solution)/shard_map/ppermute | solution.py:40
  29.6 2.4 %collective-permute-start.5 = (bf16[256,256]{1,0:T(8,128)(2,1)S(1)}, bf16[256,256]{1,0:T(8,128)(2,1)S(1)}, u32[]{:S(2)}, u32[]{:S(2)}) collective-permute-start(bf16[256,256]{1,0:T(8,128)(2,1)S(1)} %get-tuple-element.47), channel_id=1, source_target_pairs={{0,28},{4,24},{8,20},{12,16},{16,12},{20,8},{24,4},{28,0},{1,29},{... | collective-permute-start | bytes 393224 | tf_op jit(solution)/shard_map/ppermute | solution.py:40
  32.0 1.5 %collective-permute-start.6 = (bf16[256,256]{1,0:T(8,128)(2,1)S(1)}, bf16[256,256]{1,0:T(8,128)(2,1)S(1)}, u32[]{:S(2)}, u32[]{:S(2)}) collective-permute-start(bf16[256,256]{1,0:T(8,128)(2,1)S(1)} %get-tuple-element.48), channel_id=1, source_target_pairs={{0,4},{4,0},{8,12},{12,8},{16,20},{20,16},{24,28},{28,24},{1,5},{5... | collective-permute-start | bytes 393224 | tf_op jit(solution)/shard_map/ppermute | solution.py:40
  34.0 4.0 %collective-permute-done.8.refs_0_ = bf16[256,256]{1,0:T(8,128)(2,1)S(1)} collective-permute-done((bf16[256,256]{1,0:T(8,128)(2,1)S(1)}, bf16[256,256]{1,0:T(8,128)(2,1)S(1)}, u32[]{:S(2)}, u32[]{:S(2)}) %collective-permute-start.8) | collective-permute-done | bytes 131104 | tf_op jit(solution)/shard_map/ppermute | solution.py:40
  38.9 4.4 %collective-permute-start.13 = (bf16[256,256]{1,0:T(8,128)(2,1)S(1)}, bf16[256,256]{1,0:T(8,128)(2,1)S(1)}, u32[]{:S(2)}, u32[]{:S(2)}) collective-permute-start(bf16[256,256]{1,0:T(8,128)(2,1)S(1)} %get-tuple-element.61.refs_6_), channel_id=1, source_target_pairs={{0,28},{4,24},{8,20},{12,16},{16,12},{20,8},{24,4},{28,0},{1,29},{... | collective-permute-start | bytes 393224 | tf_op jit(solution)/shard_map/ppermute | solution.py:40
  46.1 5.0 %shard_map.112 = (f32[8,512,256]{2,1,0:T(8,128)S(1)}, f32[16,512,256]{2,1,0:T(8,128)S(1)}, f32[8,512,256]{2,1,0:T(8,128)S(1)}) custom-call(s32[8]{0:T(128)S(1)} %copy-done.11, bf16[512,256]{1,0:T(8,128)(2,1)S(1)} %copy-done.1, bf16[512,256]{1,0:T(8,128)(2,1)S(1)} %copy-done.3, ...), custom_call_target="tpu_custom_call", output_to_operand_aliasing={{0}: (12, {})} | custom-call | flops 1073741824 | bytes 5242880 | tf_op jit(solution)/shard_map/pallas_call | solution.py:218
  51.2 1.7 %shard_map.113 = (f32[2,512,256]{2,1,0:T(8,128)S(1)}, bf16[256,256]{1,0:T(8,128)(2,1)S(1)}) custom-call(bf16[512,256]{1,0:T(8,128)(2,1)S(1)} %copy-done.2, bf16[512,256]{1,0:T(8,128)(2,1)S(1)} %copy-done.3, bf16[256,512]{1,0:T(8,128)(2,1)S(1)} %copy-done.4, bf16[256,512]{1,0:T(8,128)(2,1)S(1)} %copy-done.5, f32[16,512,256]{2,1,0:T(8,128)S(1)} %get-tuple-element.58.fs, ...), custom_call_target="tpu_custom_call" | custom-call | flops 536870912 | bytes 5242880 | tf_op jit(solution)/shard_map/pallas_call | solution.py:301
  52.9 3.8 %collective-permute-start.14 = (bf16[256,256]{1,0:T(8,128)(2,1)S(1)}, bf16[256,256]{1,0:T(8,128)(2,1)S(1)}, u32[]{:S(2)}, u32[]{:S(2)}) collective-permute-start(bf16[256,256]{1,0:T(8,128)(2,1)S(1)} %get-tuple-element.64), channel_id=1, source_target_pairs={{0,16},{4,20},{8,24},{12,28},{16,0},{20,4},{24,8},{28,12},{1,17},{... | collective-permute-start | bytes 393224 | tf_op jit(solution)/shard_map/ppermute | solution.py:40
  56.7 3.4 %shard_map.114 = (bf16[256,256]{1,0:T(8,128)(2,1)S(1)}, bf16[256,256]{1,0:T(8,128)(2,1)S(1)}, bf16[256,256]{1,0:T(8,128)(2,1)S(1)}, bf16[256,256]{1,0:T(8,128)(2...) custom-call(bf16[256,512]{1,0:T(8,128)(2,1)S(1)} %copy-done.4, ...), custom_call_target="tpu_custom_call" | custom-call | flops 1610612736 | bytes 5242880 | tf_op jit(solution)/shard_map/pallas_call | solution.py:318
  60.1 1.3 %collective-permute-start.15 = (bf16[256,256]{1,0:T(8,128)(2,1)S(1)}, bf16[256,256]{1,0:T(8,128)(2,1)S(1)}, u32[]{:S(2)}, u32[]{:S(2)}) collective-permute-start(bf16[256,256]{1,0:T(8,128)(2,1)S(1)} %get-tuple-element.66), channel_id=1, source_target_pairs={{0,24},{4,28},{8,16},{12,20},{16,8},{20,12},{24,0},{28,4},{1,25},{... | collective-permute-start | bytes 393224 | tf_op jit(solution)/shard_map/ppermute | solution.py:40
  62.7 2.8 %collective-permute-start.18 = (bf16[256,256]{1,0:T(8,128)(2,1)S(1)}, bf16[256,256]{1,0:T(8,128)(2,1)S(1)}, u32[]{:S(2)}, u32[]{:S(2)}) collective-permute-start(bf16[256,256]{1,0:T(8,128)(2,1)S(1)} %get-tuple-element.72), channel_id=1, source_target_pairs={{0,20},{4,16},{8,28},{12,24},{16,4},{20,0},{24,12},{28,8},{1,21},{... | collective-permute-start | bytes 393224 | tf_op jit(solution)/shard_map/ppermute | solution.py:40
  65.4 2.2 %collective-permute-start.19 = (bf16[256,256]{1,0:T(8,128)(2,1)S(1)}, bf16[256,256]{1,0:T(8,128)(2,1)S(1)}, u32[]{:S(2)}, u32[]{:S(2)}) collective-permute-start(bf16[256,256]{1,0:T(8,128)(2,1)S(1)} %get-tuple-element.73), channel_id=1, source_target_pairs={{0,28},{4,24},{8,20},{12,16},{16,12},{20,8},{24,4},{28,0},{1,29},{... | collective-permute-start | bytes 393224 | tf_op jit(solution)/shard_map/ppermute | solution.py:40
  69.1 3.8 %collective-permute-done.16.refs_2_ = bf16[256,256]{1,0:T(8,128)(2,1)S(1)} collective-permute-done((bf16[256,256]{1,0:T(8,128)(2,1)S(1)}, bf16[256,256]{1,0:T(8,128)(2,1)S(1)}, u32[]{:S(2)}, u32[]{:S(2)}) %collective-permute-start.16) | collective-permute-done | bytes 131104 | tf_op jit(solution)/shard_map/ppermute | solution.py:40
  72.9 2.9 %collective-permute-done.17.refs_3_ = bf16[256,256]{1,0:T(8,128)(2,1)S(1)} collective-permute-done((bf16[256,256]{1,0:T(8,128)(2,1)S(1)}, bf16[256,256]{1,0:T(8,128)(2,1)S(1)}, u32[]{:S(2)}, u32[]{:S(2)}) %collective-permute-start.17) | collective-permute-done | bytes 131104 | tf_op jit(solution)/shard_map/ppermute | solution.py:40
  76.3 1.6 %collective-permute-done.19.refs_3_ = bf16[256,256]{1,0:T(8,128)(2,1)S(1)} collective-permute-done((bf16[256,256]{1,0:T(8,128)(2,1)S(1)}, bf16[256,256]{1,0:T(8,128)(2,1)S(1)}, u32[]{:S(2)}, u32[]{:S(2)}) %collective-permute-start.19) | collective-permute-done | bytes 131104 | tf_op jit(solution)/shard_map/ppermute | solution.py:40
  77.8 1.4 %collective-permute-done.20.refs_4_ = bf16[256,256]{1,0:T(8,128)(2,1)S(1)} collective-permute-done((bf16[256,256]{1,0:T(8,128)(2,1)S(1)}, bf16[256,256]{1,0:T(8,128)(2,1)S(1)}, u32[]{:S(2)}, u32[]{:S(2)}) %collective-permute-start.20) | collective-permute-done | bytes 131104 | tf_op jit(solution)/shard_map/ppermute | solution.py:40
  82.0 2.4 %collective-permute-done.22 = f32[1,256]{1,0:T(1,128)S(1)} collective-permute-done((f32[1,256]{1,0:T(1,128)S(1)}, f32[1,256]{1,0:T(1,128)S(1)}, u32[]{:S(2)}, u32[]{:S(2)}) %collective-permute-start.22) | collective-permute-done | bytes 1056 | tf_op jit(solution)/shard_map/ppermute | solution.py:454
  84.4 1.5 %shard_map.117 = f32[256,2048]{1,0:T(8,128)} custom-call(f32[256,2048]{1,0:T(8,128)S(1)} %get-tuple-element.75.pre_ref, f32[1,2048]{1,0:T(1,128)S(1)} %bitcast.4, f32[1,256]{1,0:T(1,128)S(1)} %add.7.refs_0_), custom_call_target="tpu_custom_call" | custom-call | flops 1048576 | bytes 4194304 | tf_op jit(solution)/shard_map/pallas_call | solution.py:411
  (57 shorter events, 16.5 us)
Async XLA Ops:
  1.2 44.9 %copy-start.11 = (s32[8]{0:T(128)S(1)}, s32[8]{0:T(128)}, u32[]{:S(2)}) copy-start(s32[8]{0:T(128)} %lag_ref.1) | copy-start | bytes 100
  1.5 12.1 %collective-permute-start = (bf16[256,256]{1,0:T(8,128)(2,1)S(1)}, bf16[256,256]{1,0:T(8,128)(2,1)S(1)}, u32[]{:S(2)}, u32[]{:S(2)}) collective-permute-start(bf16[256,256]{1,0:T(8,128)(2,1)S(1)} %get-tuple-element.41), channel_id=1, source_target_pairs={{0,16},{4,20},{8,24},{12,28},{16,0},{20,4},{24,8},{28,12},{1,17},{... | collective-permute-start | bytes 393224 | tf_op jit(solution)/shard_map/ppermute | solution.py:40
  5.6 15.0 %collective-permute-start.1 = (bf16[256,256]{1,0:T(8,128)(2,1)S(1)}, bf16[256,256]{1,0:T(8,128)(2,1)S(1)}, u32[]{:S(2)}, u32[]{:S(2)}) collective-permute-start(bf16[256,256]{1,0:T(8,128)(2,1)S(1)} %get-tuple-element.43), channel_id=1, source_target_pairs={{0,8},{4,12},{8,0},{12,4},{16,24},{20,28},{24,16},{28,20},{1,9},{5... | collective-permute-start | bytes 393224 | tf_op jit(solution)/shard_map/ppermute | solution.py:40
  7.2 13.5 %collective-permute-start.2 = (bf16[256,256]{1,0:T(8,128)(2,1)S(1)}, bf16[256,256]{1,0:T(8,128)(2,1)S(1)}, u32[]{:S(2)}, u32[]{:S(2)}) collective-permute-start(bf16[256,256]{1,0:T(8,128)(2,1)S(1)} %get-tuple-element.44), channel_id=1, source_target_pairs={{0,24},{4,28},{8,16},{12,20},{16,8},{20,12},{24,0},{28,4},{1,25},{... | collective-permute-start | bytes 393224 | tf_op jit(solution)/shard_map/ppermute | solution.py:40
  7.2 15.9 %collective-permute-start.3 = (bf16[256,256]{1,0:T(8,128)(2,1)S(1)}, bf16[256,256]{1,0:T(8,128)(2,1)S(1)}, u32[]{:S(2)}, u32[]{:S(2)}) collective-permute-start(bf16[256,256]{1,0:T(8,128)(2,1)S(1)} %get-tuple-element.45), channel_id=1, source_target_pairs={{0,12},{4,8},{8,4},{12,0},{16,28},{20,24},{24,20},{28,16},{1,13},{... | collective-permute-start | bytes 393224 | tf_op jit(solution)/shard_map/ppermute | solution.py:40
  9.0 20.6 %collective-permute-start.4 = (bf16[256,256]{1,0:T(8,128)(2,1)S(1)}, bf16[256,256]{1,0:T(8,128)(2,1)S(1)}, u32[]{:S(2)}, u32[]{:S(2)}) collective-permute-start(bf16[256,256]{1,0:T(8,128)(2,1)S(1)} %get-tuple-element.46), channel_id=1, source_target_pairs={{0,20},{4,16},{8,28},{12,24},{16,4},{20,0},{24,12},{28,8},{1,21},{... | collective-permute-start | bytes 393224 | tf_op jit(solution)/shard_map/ppermute | solution.py:40
  16.7 15.2 %collective-permute-start.10 = (bf16[256,256]{1,0:T(8,128)(2,1)S(1)}, bf16[256,256]{1,0:T(8,128)(2,1)S(1)}, u32[]{:S(2)}, u32[]{:S(2)}) collective-permute-start(bf16[256,256]{1,0:T(8,128)(2,1)S(1)} %get-tuple-element.55.refs_6_), channel_id=1, source_target_pairs={{0,24},{4,28},{8,16},{12,20},{16,8},{20,12},{24,0},{28,4},{1,25},{... | collective-permute-start | bytes 393224 | tf_op jit(solution)/shard_map/ppermute | solution.py:40
  20.6 12.8 %collective-permute-start.11 = (bf16[256,256]{1,0:T(8,128)(2,1)S(1)}, bf16[256,256]{1,0:T(8,128)(2,1)S(1)}, u32[]{:S(2)}, u32[]{:S(2)}) collective-permute-start(bf16[256,256]{1,0:T(8,128)(2,1)S(1)} %get-tuple-element.56.refs_8_), channel_id=1, source_target_pairs={{0,12},{4,8},{8,4},{12,0},{16,28},{20,24},{24,20},{28,16},{1,13},{... | collective-permute-start | bytes 393224 | tf_op jit(solution)/shard_map/ppermute | solution.py:40
  20.6 17.4 %collective-permute-start.8 = (bf16[256,256]{1,0:T(8,128)(2,1)S(1)}, bf16[256,256]{1,0:T(8,128)(2,1)S(1)}, u32[]{:S(2)}, u32[]{:S(2)}) collective-permute-start(bf16[256,256]{1,0:T(8,128)(2,1)S(1)} %get-tuple-element.53.refs_5_), channel_id=1, source_target_pairs={{0,16},{4,20},{8,24},{12,28},{16,0},{20,4},{24,8},{28,12},{1,17},{... | collective-permute-start | bytes 393224 | tf_op jit(solution)/shard_map/ppermute | solution.py:40
  23.1 15.8 %collective-permute-start.9 = (bf16[256,256]{1,0:T(8,128)(2,1)S(1)}, bf16[256,256]{1,0:T(8,128)(2,1)S(1)}, u32[]{:S(2)}, u32[]{:S(2)}) collective-permute-start(bf16[256,256]{1,0:T(8,128)(2,1)S(1)} %get-tuple-element.54.refs_7_), channel_id=1, source_target_pairs={{0,8},{4,12},{8,0},{12,4},{16,24},{20,28},{24,16},{28,20},{1,9},{5... | collective-permute-start | bytes 393224 | tf_op jit(solution)/shard_map/ppermute | solution.py:40
  29.6 16.5 %collective-permute-start.5 = (bf16[256,256]{1,0:T(8,128)(2,1)S(1)}, bf16[256,256]{1,0:T(8,128)(2,1)S(1)}, u32[]{:S(2)}, u32[]{:S(2)}) collective-permute-start(bf16[256,256]{1,0:T(8,128)(2,1)S(1)} %get-tuple-element.47), channel_id=1, source_target_pairs={{0,28},{4,24},{8,20},{12,16},{16,12},{20,8},{24,4},{28,0},{1,29},{... | collective-permute-start | bytes 393224 | tf_op jit(solution)/shard_map/ppermute | solution.py:40
  32.0 14.2 %collective-permute-start.6 = (bf16[256,256]{1,0:T(8,128)(2,1)S(1)}, bf16[256,256]{1,0:T(8,128)(2,1)S(1)}, u32[]{:S(2)}, u32[]{:S(2)}) collective-permute-start(bf16[256,256]{1,0:T(8,128)(2,1)S(1)} %get-tuple-element.48), channel_id=1, source_target_pairs={{0,4},{4,0},{8,12},{12,8},{16,20},{20,16},{24,28},{28,24},{1,5},{5... | collective-permute-start | bytes 393224 | tf_op jit(solution)/shard_map/ppermute | solution.py:40
  33.5 12.7 %collective-permute-start.7 = (bf16[256,256]{1,0:T(8,128)(2,1)S(1)}, bf16[256,256]{1,0:T(8,128)(2,1)S(1)}, u32[]{:S(2)}, u32[]{:S(2)}) collective-permute-start(bf16[256,256]{1,0:T(8,128)(2,1)S(1)} %get-tuple-element.52.refs_7_), channel_id=1, source_target_pairs={{0,4},{4,0},{8,12},{12,8},{16,20},{20,16},{24,28},{28,24},{1,5},{5... | collective-permute-start | bytes 393224 | tf_op jit(solution)/shard_map/ppermute | solution.py:40
  38.0 13.1 %collective-permute-start.12 = (bf16[256,256]{1,0:T(8,128)(2,1)S(1)}, bf16[256,256]{1,0:T(8,128)(2,1)S(1)}, u32[]{:S(2)}, u32[]{:S(2)}) collective-permute-start(bf16[256,256]{1,0:T(8,128)(2,1)S(1)} %get-tuple-element.60.refs_5_), channel_id=1, source_target_pairs={{0,20},{4,16},{8,28},{12,24},{16,4},{20,0},{24,12},{28,8},{1,21},{... | collective-permute-start | bytes 393224 | tf_op jit(solution)/shard_map/ppermute | solution.py:40
  38.9 12.3 %collective-permute-start.13 = (bf16[256,256]{1,0:T(8,128)(2,1)S(1)}, bf16[256,256]{1,0:T(8,128)(2,1)S(1)}, u32[]{:S(2)}, u32[]{:S(2)}) collective-permute-start(bf16[256,256]{1,0:T(8,128)(2,1)S(1)} %get-tuple-element.61.refs_6_), channel_id=1, source_target_pairs={{0,28},{4,24},{8,20},{12,16},{16,12},{20,8},{24,4},{28,0},{1,29},{... | collective-permute-start | bytes 393224 | tf_op jit(solution)/shard_map/ppermute | solution.py:40
  52.9 12.5 %collective-permute-start.14 = (bf16[256,256]{1,0:T(8,128)(2,1)S(1)}, bf16[256,256]{1,0:T(8,128)(2,1)S(1)}, u32[]{:S(2)}, u32[]{:S(2)}) collective-permute-start(bf16[256,256]{1,0:T(8,128)(2,1)S(1)} %get-tuple-element.64), channel_id=1, source_target_pairs={{0,16},{4,20},{8,24},{12,28},{16,0},{20,4},{24,8},{28,12},{1,17},{... | collective-permute-start | bytes 393224 | tf_op jit(solution)/shard_map/ppermute | solution.py:40
  60.1 8.3 %collective-permute-start.15 = (bf16[256,256]{1,0:T(8,128)(2,1)S(1)}, bf16[256,256]{1,0:T(8,128)(2,1)S(1)}, u32[]{:S(2)}, u32[]{:S(2)}) collective-permute-start(bf16[256,256]{1,0:T(8,128)(2,1)S(1)} %get-tuple-element.66), channel_id=1, source_target_pairs={{0,24},{4,28},{8,16},{12,20},{16,8},{20,12},{24,0},{28,4},{1,25},{... | collective-permute-start | bytes 393224 | tf_op jit(solution)/shard_map/ppermute | solution.py:40
  61.4 11.5 %collective-permute-start.16 = (bf16[256,256]{1,0:T(8,128)(2,1)S(1)}, bf16[256,256]{1,0:T(8,128)(2,1)S(1)}, u32[]{:S(2)}, u32[]{:S(2)}) collective-permute-start(bf16[256,256]{1,0:T(8,128)(2,1)S(1)} %get-tuple-element.67), channel_id=1, source_target_pairs={{0,8},{4,12},{8,0},{12,4},{16,24},{20,28},{24,16},{28,20},{1,9},{5... | collective-permute-start | bytes 393224 | tf_op jit(solution)/shard_map/ppermute | solution.py:40
  61.4 14.4 %collective-permute-start.17 = (bf16[256,256]{1,0:T(8,128)(2,1)S(1)}, bf16[256,256]{1,0:T(8,128)(2,1)S(1)}, u32[]{:S(2)}, u32[]{:S(2)}) collective-permute-start(bf16[256,256]{1,0:T(8,128)(2,1)S(1)} %get-tuple-element.68), channel_id=1, source_target_pairs={{0,12},{4,8},{8,4},{12,0},{16,28},{20,24},{24,20},{28,16},{1,13},{... | collective-permute-start | bytes 393224 | tf_op jit(solution)/shard_map/ppermute | solution.py:40
  62.7 13.6 %collective-permute-start.18 = (bf16[256,256]{1,0:T(8,128)(2,1)S(1)}, bf16[256,256]{1,0:T(8,128)(2,1)S(1)}, u32[]{:S(2)}, u32[]{:S(2)}) collective-permute-start(bf16[256,256]{1,0:T(8,128)(2,1)S(1)} %get-tuple-element.72), channel_id=1, source_target_pairs={{0,20},{4,16},{8,28},{12,24},{16,4},{20,0},{24,12},{28,8},{1,21},{... | collective-permute-start | bytes 393224 | tf_op jit(solution)/shard_map/ppermute | solution.py:40
  65.4 12.4 %collective-permute-start.19 = (bf16[256,256]{1,0:T(8,128)(2,1)S(1)}, bf16[256,256]{1,0:T(8,128)(2,1)S(1)}, u32[]{:S(2)}, u32[]{:S(2)}) collective-permute-start(bf16[256,256]{1,0:T(8,128)(2,1)S(1)} %get-tuple-element.73), channel_id=1, source_target_pairs={{0,28},{4,24},{8,20},{12,16},{16,12},{20,8},{24,4},{28,0},{1,29},{... | collective-permute-start | bytes 393224 | tf_op jit(solution)/shard_map/ppermute | solution.py:40
  68.4 10.8 %collective-permute-start.20 = (bf16[256,256]{1,0:T(8,128)(2,1)S(1)}, bf16[256,256]{1,0:T(8,128)(2,1)S(1)}, u32[]{:S(2)}, u32[]{:S(2)}) collective-permute-start(bf16[256,256]{1,0:T(8,128)(2,1)S(1)} %get-tuple-element.74), channel_id=1, source_target_pairs={{0,4},{4,0},{8,12},{12,8},{16,20},{20,16},{24,28},{28,24},{1,5},{5... | collective-permute-start | bytes 393224 | tf_op jit(solution)/shard_map/ppermute | solution.py:40
  79.6 1.2 %collective-permute-start.21 = (f32[1,256]{1,0:T(1,128)S(1)}, f32[1,256]{1,0:T(1,128)S(1)}, u32[]{:S(2)}, u32[]{:S(2)}) collective-permute-start(f32[1,256]{1,0:T(1,128)S(1)} %get-tuple-element.76), channel_id=1, source_target_pairs={{0,1},{1,0},{2,3},{3,2},{4,5},{5,4},{6,7},{7,6},{8,9},{9,8},{10,11... | collective-permute-start | bytes 3080 | tf_op jit(solution)/shard_map/ppermute | solution.py:454
  80.8 3.6 %collective-permute-start.22 = (f32[1,256]{1,0:T(1,128)S(1)}, f32[1,256]{1,0:T(1,128)S(1)}, u32[]{:S(2)}, u32[]{:S(2)}) collective-permute-start(f32[1,256]{1,0:T(1,128)S(1)} %add.6), channel_id=1, source_target_pairs={{0,2},{1,3},{2,0},{3,1},{4,6},{5,7},{6,4},{7,5},{8,10},{9,11},{10,... | collective-permute-start | bytes 3080 | tf_op jit(solution)/shard_map/ppermute | solution.py:454
  (11 other events, 83.4 us)

commit v18 on v17

--- a/solution.py
+++ b/solution.py
@@ -438,9 +438,9 @@
     filt, sums = early_products(lag_of_block, *tabs[:2], filts, last, gates[last], gated)
     late = {k: gates[k] for k in gates if k not in early + [last]}
     spectra, ahead = first_product(order[0], tabs, filt, sums, late)
-    found = rest_products([order[2], order[1]] + order[3:] + [0], tabs, filt, sums, list(late), spectra)
+    found = rest_products([order[2], order[1], order[4], order[3]] + order[5:] + [0], tabs, filt, sums, list(late), spectra)
     found[order[0]] = ahead
-    returns = [order[0], order[2], order[1]] + order[3:]
+    returns = [order[0], order[2], order[1], order[4], order[3]] + order[5:]
     for at, k in enumerate(returns):
         block = found[k]
         if at == 6:

time: 86.1 us -> 86.3 us (level)
  no operation moved by 1% of the time
where the time goes in v18:
time: 86.3 us; the launch traced here: 86 us
  starting transfers between devices  40.9 us (47%)
  waiting for transfers between devices  25 us (29%)
  Pallas kernels  14.3 us (17%)
  local copies, waits for them, and re-layouts  5.61 us (7%)
    ppermute x21, starting transfers between devices, send(): return lax.ppermute(block, 'tok', [(d, d ^ step) for d in range(count)])  39.6 us
    ppermute x21, waiting for transfers between devices, send(): return lax.ppermute(block, 'tok', [(d, d ^ step) for d in range(count)])  21.5 us
    unnamed x24, local copies, waits for them, and re-layouts  5.61 us
    pallas_call x1, Pallas kernels, early_products(): pl.pallas_call(functools.partial(early_kernel, count, steps, last), out_s...  5.01 us
    ppermute x2, waiting for transfers between devices, local(): lax.ppermute(square, 'chan', [(d, d ^ step) for d in range(others)])  3.46 us
    pallas_call x1, Pallas kernels, rest_products(): pl.pallas_call(functools.partial(rest_kernel, count, late, steps), out_sh...  3.36 us
  transfers between devices with their start and end apart: 23, of which 10 were waited for; matrix products, arithmetic and copies ran while one was open for 0% of the time, Pallas kernels for 12%

profile of v18, /device:TPU:0, one launch (start us, length us, event | category | flops | bytes accessed | tf_op | source)
XLA Modules:
  0.0 86.0 jit_solution(3934708723847282567)
XLA Ops:
  1.5 4.1 %collective-permute-start = (bf16[256,256]{1,0:T(8,128)(2,1)S(1)}, bf16[256,256]{1,0:T(8,128)(2,1)S(1)}, u32[]{:S(2)}, u32[]{:S(2)}) collective-permute-start(bf16[256,256]{1,0:T(8,128)(2,1)S(1)} %get-tuple-element.41), channel_id=1, source_target_pairs={{0,16},{4,20},{8,24},{12,28},{16,0},{20,4},{24,8},{28,12},{1,17},{... | collective-permute-start | bytes 393224 | tf_op jit(solution)/shard_map/ppermute | solution.py:40
  5.6 1.6 %collective-permute-start.1 = (bf16[256,256]{1,0:T(8,128)(2,1)S(1)}, bf16[256,256]{1,0:T(8,128)(2,1)S(1)}, u32[]{:S(2)}, u32[]{:S(2)}) collective-permute-start(bf16[256,256]{1,0:T(8,128)(2,1)S(1)} %get-tuple-element.43), channel_id=1, source_target_pairs={{0,8},{4,12},{8,0},{12,4},{16,24},{20,28},{24,16},{28,20},{1,9},{5... | collective-permute-start | bytes 393224 | tf_op jit(solution)/shard_map/ppermute | solution.py:40
  7.2 1.8 %collective-permute-start.3 = (bf16[256,256]{1,0:T(8,128)(2,1)S(1)}, bf16[256,256]{1,0:T(8,128)(2,1)S(1)}, u32[]{:S(2)}, u32[]{:S(2)}) collective-permute-start(bf16[256,256]{1,0:T(8,128)(2,1)S(1)} %get-tuple-element.45), channel_id=1, source_target_pairs={{0,12},{4,8},{8,4},{12,0},{16,28},{20,24},{24,20},{28,16},{1,13},{... | collective-permute-start | bytes 393224 | tf_op jit(solution)/shard_map/ppermute | solution.py:40
  9.0 3.5 %collective-permute-start.4 = (bf16[256,256]{1,0:T(8,128)(2,1)S(1)}, bf16[256,256]{1,0:T(8,128)(2,1)S(1)}, u32[]{:S(2)}, u32[]{:S(2)}) collective-permute-start(bf16[256,256]{1,0:T(8,128)(2,1)S(1)} %get-tuple-element.46), channel_id=1, source_target_pairs={{0,20},{4,16},{8,28},{12,24},{16,4},{20,0},{24,12},{28,8},{1,21},{... | collective-permute-start | bytes 393224 | tf_op jit(solution)/shard_map/ppermute | solution.py:40
  16.7 3.9 %collective-permute-start.10 = (bf16[256,256]{1,0:T(8,128)(2,1)S(1)}, bf16[256,256]{1,0:T(8,128)(2,1)S(1)}, u32[]{:S(2)}, u32[]{:S(2)}) collective-permute-start(bf16[256,256]{1,0:T(8,128)(2,1)S(1)} %get-tuple-element.55.refs_6_), channel_id=1, source_target_pairs={{0,24},{4,28},{8,16},{12,20},{16,8},{20,12},{24,0},{28,4},{1,25},{... | collective-permute-start | bytes 393224 | tf_op jit(solution)/shard_map/ppermute | solution.py:40
  20.6 2.5 %collective-permute-start.8 = (bf16[256,256]{1,0:T(8,128)(2,1)S(1)}, bf16[256,256]{1,0:T(8,128)(2,1)S(1)}, u32[]{:S(2)}, u32[]{:S(2)}) collective-permute-start(bf16[256,256]{1,0:T(8,128)(2,1)S(1)} %get-tuple-element.53.refs_5_), channel_id=1, source_target_pairs={{0,16},{4,20},{8,24},{12,28},{16,0},{20,4},{24,8},{28,12},{1,17},{... | collective-permute-start | bytes 393224 | tf_op jit(solution)/shard_map/ppermute | solution.py:40
  23.6 5.9 %collective-permute-done.4.refs_4_ = bf16[256,256]{1,0:T(8,128)(2,1)S(1)} collective-permute-done((bf16[256,256]{1,0:T(8,128)(2,1)S(1)}, bf16[256,256]{1,0:T(8,128)(2,1)S(1)}, u32[]{:S(2)}, u32[]{:S(2)}) %collective-permute-start.4) | collective-permute-done | bytes 131104 | tf_op jit(solution)/shard_map/ppermute | solution.py:40
  29.6 2.4 %collective-permute-start.5 = (bf16[256,256]{1,0:T(8,128)(2,1)S(1)}, bf16[256,256]{1,0:T(8,128)(2,1)S(1)}, u32[]{:S(2)}, u32[]{:S(2)}) collective-permute-start(bf16[256,256]{1,0:T(8,128)(2,1)S(1)} %get-tuple-element.47), channel_id=1, source_target_pairs={{0,28},{4,24},{8,20},{12,16},{16,12},{20,8},{24,4},{28,0},{1,29},{... | collective-permute-start | bytes 393224 | tf_op jit(solution)/shard_map/ppermute | solution.py:40
  32.0 1.5 %collective-permute-start.6 = (bf16[256,256]{1,0:T(8,128)(2,1)S(1)}, bf16[256,256]{1,0:T(8,128)(2,1)S(1)}, u32[]{:S(2)}, u32[]{:S(2)}) collective-permute-start(bf16[256,256]{1,0:T(8,128)(2,1)S(1)} %get-tuple-element.48), channel_id=1, source_target_pairs={{0,4},{4,0},{8,12},{12,8},{16,20},{20,16},{24,28},{28,24},{1,5},{5... | collective-permute-start | bytes 393224 | tf_op jit(solution)/shard_map/ppermute | solution.py:40
  34.0 4.0 %collective-permute-done.8.refs_0_ = bf16[256,256]{1,0:T(8,128)(2,1)S(1)} collective-permute-done((bf16[256,256]{1,0:T(8,128)(2,1)S(1)}, bf16[256,256]{1,0:T(8,128)(2,1)S(1)}, u32[]{:S(2)}, u32[]{:S(2)}) %collective-permute-start.8) | collective-permute-done | bytes 131104 | tf_op jit(solution)/shard_map/ppermute | solution.py:40
  38.9 4.4 %collective-permute-start.13 = (bf16[256,256]{1,0:T(8,128)(2,1)S(1)}, bf16[256,256]{1,0:T(8,128)(2,1)S(1)}, u32[]{:S(2)}, u32[]{:S(2)}) collective-permute-start(bf16[256,256]{1,0:T(8,128)(2,1)S(1)} %get-tuple-element.61.refs_6_), channel_id=1, source_target_pairs={{0,28},{4,24},{8,20},{12,16},{16,12},{20,8},{24,4},{28,0},{1,29},{... | collective-permute-start | bytes 393224 | tf_op jit(solution)/shard_map/ppermute | solution.py:40
  46.1 5.0 %shard_map.112 = (f32[8,512,256]{2,1,0:T(8,128)S(1)}, f32[16,512,256]{2,1,0:T(8,128)S(1)}, f32[8,512,256]{2,1,0:T(8,128)S(1)}) custom-call(s32[8]{0:T(128)S(1)} %copy-done.11, bf16[512,256]{1,0:T(8,128)(2,1)S(1)} %copy-done.1, bf16[512,256]{1,0:T(8,128)(2,1)S(1)} %copy-done.3, ...), custom_call_target="tpu_custom_call", output_to_operand_aliasing={{0}: (12, {})} | custom-call | flops 1073741824 | bytes 5242880 | tf_op jit(solution)/shard_map/pallas_call | solution.py:218
  51.2 1.7 %shard_map.113 = (f32[2,512,256]{2,1,0:T(8,128)S(1)}, bf16[256,256]{1,0:T(8,128)(2,1)S(1)}) custom-call(bf16[512,256]{1,0:T(8,128)(2,1)S(1)} %copy-done.2, bf16[512,256]{1,0:T(8,128)(2,1)S(1)} %copy-done.3, bf16[256,512]{1,0:T(8,128)(2,1)S(1)} %copy-done.4, bf16[256,512]{1,0:T(8,128)(2,1)S(1)} %copy-done.5, f32[16,512,256]{2,1,0:T(8,128)S(1)} %get-tuple-element.58.fs, ...), custom_call_target="tpu_custom_call" | custom-call | flops 536870912 | bytes 5242880 | tf_op jit(solution)/shard_map/pallas_call | solution.py:301
  52.9 3.8 %collective-permute-start.14 = (bf16[256,256]{1,0:T(8,128)(2,1)S(1)}, bf16[256,256]{1,0:T(8,128)(2,1)S(1)}, u32[]{:S(2)}, u32[]{:S(2)}) collective-permute-start(bf16[256,256]{1,0:T(8,128)(2,1)S(1)} %get-tuple-element.64), channel_id=1, source_target_pairs={{0,16},{4,20},{8,24},{12,28},{16,0},{20,4},{24,8},{28,12},{1,17},{... | collective-permute-start | bytes 393224 | tf_op jit(solution)/shard_map/ppermute | solution.py:40
  56.7 3.4 %shard_map.114 = (bf16[256,256]{1,0:T(8,128)(2,1)S(1)}, bf16[256,256]{1,0:T(8,128)(2,1)S(1)}, bf16[256,256]{1,0:T(8,128)(2,1)S(1)}, bf16[256,256]{1,0:T(8,128)(2...) custom-call(bf16[256,512]{1,0:T(8,128)(2,1)S(1)} %copy-done.4, ...), custom_call_target="tpu_custom_call" | custom-call | flops 1610612736 | bytes 5242880 | tf_op jit(solution)/shard_map/pallas_call | solution.py:318
  60.1 1.3 %collective-permute-start.15 = (bf16[256,256]{1,0:T(8,128)(2,1)S(1)}, bf16[256,256]{1,0:T(8,128)(2,1)S(1)}, u32[]{:S(2)}, u32[]{:S(2)}) collective-permute-start(bf16[256,256]{1,0:T(8,128)(2,1)S(1)} %get-tuple-element.66), channel_id=1, source_target_pairs={{0,24},{4,28},{8,16},{12,20},{16,8},{20,12},{24,0},{28,4},{1,25},{... | collective-permute-start | bytes 393224 | tf_op jit(solution)/shard_map/ppermute | solution.py:40
  61.4 3.3 %collective-permute-start.17 = (bf16[256,256]{1,0:T(8,128)(2,1)S(1)}, bf16[256,256]{1,0:T(8,128)(2,1)S(1)}, u32[]{:S(2)}, u32[]{:S(2)}) collective-permute-start(bf16[256,256]{1,0:T(8,128)(2,1)S(1)} %get-tuple-element.68), channel_id=1, source_target_pairs={{0,20},{4,16},{8,28},{12,24},{16,4},{20,0},{24,12},{28,8},{1,21},{... | collective-permute-start | bytes 393224 | tf_op jit(solution)/shard_map/ppermute | solution.py:40
  65.4 2.2 %collective-permute-start.19 = (bf16[256,256]{1,0:T(8,128)(2,1)S(1)}, bf16[256,256]{1,0:T(8,128)(2,1)S(1)}, u32[]{:S(2)}, u32[]{:S(2)}) collective-permute-start(bf16[256,256]{1,0:T(8,128)(2,1)S(1)} %get-tuple-element.73), channel_id=1, source_target_pairs={{0,28},{4,24},{8,20},{12,16},{16,12},{20,8},{24,4},{28,0},{1,29},{... | collective-permute-start | bytes 393224 | tf_op jit(solution)/shard_map/ppermute | solution.py:40
  69.2 2.0 %collective-permute-done.16.refs_2_ = bf16[256,256]{1,0:T(8,128)(2,1)S(1)} collective-permute-done((bf16[256,256]{1,0:T(8,128)(2,1)S(1)}, bf16[256,256]{1,0:T(8,128)(2,1)S(1)}, u32[]{:S(2)}, u32[]{:S(2)}) %collective-permute-start.16) | collective-permute-done | bytes 131104 | tf_op jit(solution)/shard_map/ppermute | solution.py:40
  71.3 4.9 %collective-permute-done.17.refs_3_ = bf16[256,256]{1,0:T(8,128)(2,1)S(1)} collective-permute-done((bf16[256,256]{1,0:T(8,128)(2,1)S(1)}, bf16[256,256]{1,0:T(8,128)(2,1)S(1)}, u32[]{:S(2)}, u32[]{:S(2)}) %collective-permute-start.17) | collective-permute-done | bytes 131104 | tf_op jit(solution)/shard_map/ppermute | solution.py:40
  76.6 1.2 %collective-permute-done.19.refs_3_ = bf16[256,256]{1,0:T(8,128)(2,1)S(1)} collective-permute-done((bf16[256,256]{1,0:T(8,128)(2,1)S(1)}, bf16[256,256]{1,0:T(8,128)(2,1)S(1)}, u32[]{:S(2)}, u32[]{:S(2)}) %collective-permute-start.19) | collective-permute-done | bytes 131104 | tf_op jit(solution)/shard_map/ppermute | solution.py:40
  77.9 1.5 %collective-permute-done.20.refs_4_ = bf16[256,256]{1,0:T(8,128)(2,1)S(1)} collective-permute-done((bf16[256,256]{1,0:T(8,128)(2,1)S(1)}, bf16[256,256]{1,0:T(8,128)(2,1)S(1)}, u32[]{:S(2)}, u32[]{:S(2)}) %collective-permute-start.20) | collective-permute-done | bytes 131104 | tf_op jit(solution)/shard_map/ppermute | solution.py:40
  82.2 2.3 %collective-permute-done.22 = f32[1,256]{1,0:T(1,128)S(1)} collective-permute-done((f32[1,256]{1,0:T(1,128)S(1)}, f32[1,256]{1,0:T(1,128)S(1)}, u32[]{:S(2)}, u32[]{:S(2)}) %collective-permute-start.22) | collective-permute-done | bytes 1056 | tf_op jit(solution)/shard_map/ppermute | solution.py:454
  84.5 1.5 %shard_map.117 = f32[256,2048]{1,0:T(8,128)} custom-call(f32[256,2048]{1,0:T(8,128)S(1)} %get-tuple-element.75.pre_ref, f32[1,2048]{1,0:T(1,128)S(1)} %bitcast.4, f32[1,256]{1,0:T(1,128)S(1)} %add.7.refs_0_), custom_call_target="tpu_custom_call" | custom-call | flops 1048576 | bytes 4194304 | tf_op jit(solution)/shard_map/pallas_call | solution.py:411
  (57 shorter events, 16.1 us)
Async XLA Ops:
  1.2 44.9 %copy-start.11 = (s32[8]{0:T(128)S(1)}, s32[8]{0:T(128)}, u32[]{:S(2)}) copy-start(s32[8]{0:T(128)} %lag_ref.1) | copy-start | bytes 100
  1.5 12.1 %collective-permute-start = (bf16[256,256]{1,0:T(8,128)(2,1)S(1)}, bf16[256,256]{1,0:T(8,128)(2,1)S(1)}, u32[]{:S(2)}, u32[]{:S(2)}) collective-permute-start(bf16[256,256]{1,0:T(8,128)(2,1)S(1)} %get-tuple-element.41), channel_id=1, source_target_pairs={{0,16},{4,20},{8,24},{12,28},{16,0},{20,4},{24,8},{28,12},{1,17},{... | collective-permute-start | bytes 393224 | tf_op jit(solution)/shard_map/ppermute | solution.py:40
  5.6 15.0 %collective-permute-start.1 = (bf16[256,256]{1,0:T(8,128)(2,1)S(1)}, bf16[256,256]{1,0:T(8,128)(2,1)S(1)}, u32[]{:S(2)}, u32[]{:S(2)}) collective-permute-start(bf16[256,256]{1,0:T(8,128)(2,1)S(1)} %get-tuple-element.43), channel_id=1, source_target_pairs={{0,8},{4,12},{8,0},{12,4},{16,24},{20,28},{24,16},{28,20},{1,9},{5... | collective-permute-start | bytes 393224 | tf_op jit(solution)/shard_map/ppermute | solution.py:40
  7.2 13.5 %collective-permute-start.2 = (bf16[256,256]{1,0:T(8,128)(2,1)S(1)}, bf16[256,256]{1,0:T(8,128)(2,1)S(1)}, u32[]{:S(2)}, u32[]{:S(2)}) collective-permute-start(bf16[256,256]{1,0:T(8,128)(2,1)S(1)} %get-tuple-element.44), channel_id=1, source_target_pairs={{0,24},{4,28},{8,16},{12,20},{16,8},{20,12},{24,0},{28,4},{1,25},{... | collective-permute-start | bytes 393224 | tf_op jit(solution)/shard_map/ppermute | solution.py:40
  7.2 15.9 %collective-permute-start.3 = (bf16[256,256]{1,0:T(8,128)(2,1)S(1)}, bf16[256,256]{1,0:T(8,128)(2,1)S(1)}, u32[]{:S(2)}, u32[]{:S(2)}) collective-permute-start(bf16[256,256]{1,0:T(8,128)(2,1)S(1)} %get-tuple-element.45), channel_id=1, source_target_pairs={{0,12},{4,8},{8,4},{12,0},{16,28},{20,24},{24,20},{28,16},{1,13},{... | collective-permute-start | bytes 393224 | tf_op jit(solution)/shard_map/ppermute | solution.py:40
  9.0 20.6 %collective-permute-start.4 = (bf16[256,256]{1,0:T(8,128)(2,1)S(1)}, bf16[256,256]{1,0:T(8,128)(2,1)S(1)}, u32[]{:S(2)}, u32[]{:S(2)}) collective-permute-start(bf16[256,256]{1,0:T(8,128)(2,1)S(1)} %get-tuple-element.46), channel_id=1, source_target_pairs={{0,20},{4,16},{8,28},{12,24},{16,4},{20,0},{24,12},{28,8},{1,21},{... | collective-permute-start | bytes 393224 | tf_op jit(solution)/shard_map/ppermute | solution.py:40
  16.7 15.2 %collective-permute-start.10 = (bf16[256,256]{1,0:T(8,128)(2,1)S(1)}, bf16[256,256]{1,0:T(8,128)(2,1)S(1)}, u32[]{:S(2)}, u32[]{:S(2)}) collective-permute-start(bf16[256,256]{1,0:T(8,128)(2,1)S(1)} %get-tuple-element.55.refs_6_), channel_id=1, source_target_pairs={{0,24},{4,28},{8,16},{12,20},{16,8},{20,12},{24,0},{28,4},{1,25},{... | collective-permute-start | bytes 393224 | tf_op jit(solution)/shard_map/ppermute | solution.py:40
  20.6 12.8 %collective-permute-start.11 = (bf16[256,256]{1,0:T(8,128)(2,1)S(1)}, bf16[256,256]{1,0:T(8,128)(2,1)S(1)}, u32[]{:S(2)}, u32[]{:S(2)}) collective-permute-start(bf16[256,256]{1,0:T(8,128)(2,1)S(1)} %get-tuple-element.56.refs_5_), channel_id=1, source_target_pairs={{0,12},{4,8},{8,4},{12,0},{16,28},{20,24},{24,20},{28,16},{1,13},{... | collective-permute-start | bytes 393224 | tf_op jit(solution)/shard_map/ppermute | solution.py:40
  20.6 17.4 %collective-permute-start.8 = (bf16[256,256]{1,0:T(8,128)(2,1)S(1)}, bf16[256,256]{1,0:T(8,128)(2,1)S(1)}, u32[]{:S(2)}, u32[]{:S(2)}) collective-permute-start(bf16[256,256]{1,0:T(8,128)(2,1)S(1)} %get-tuple-element.53.refs_5_), channel_id=1, source_target_pairs={{0,16},{4,20},{8,24},{12,28},{16,0},{20,4},{24,8},{28,12},{1,17},{... | collective-permute-start | bytes 393224 | tf_op jit(solution)/shard_map/ppermute | solution.py:40
  23.1 15.8 %collective-permute-start.9 = (bf16[256,256]{1,0:T(8,128)(2,1)S(1)}, bf16[256,256]{1,0:T(8,128)(2,1)S(1)}, u32[]{:S(2)}, u32[]{:S(2)}) collective-permute-start(bf16[256,256]{1,0:T(8,128)(2,1)S(1)} %get-tuple-element.54.refs_7_), channel_id=1, source_target_pairs={{0,8},{4,12},{8,0},{12,4},{16,24},{20,28},{24,16},{28,20},{1,9},{5... | collective-permute-start | bytes 393224 | tf_op jit(solution)/shard_map/ppermute | solution.py:40
  29.6 16.5 %collective-permute-start.5 = (bf16[256,256]{1,0:T(8,128)(2,1)S(1)}, bf16[256,256]{1,0:T(8,128)(2,1)S(1)}, u32[]{:S(2)}, u32[]{:S(2)}) collective-permute-start(bf16[256,256]{1,0:T(8,128)(2,1)S(1)} %get-tuple-element.47), channel_id=1, source_target_pairs={{0,28},{4,24},{8,20},{12,16},{16,12},{20,8},{24,4},{28,0},{1,29},{... | collective-permute-start | bytes 393224 | tf_op jit(solution)/shard_map/ppermute | solution.py:40
  32.0 14.2 %collective-permute-start.6 = (bf16[256,256]{1,0:T(8,128)(2,1)S(1)}, bf16[256,256]{1,0:T(8,128)(2,1)S(1)}, u32[]{:S(2)}, u32[]{:S(2)}) collective-permute-start(bf16[256,256]{1,0:T(8,128)(2,1)S(1)} %get-tuple-element.48), channel_id=1, source_target_pairs={{0,4},{4,0},{8,12},{12,8},{16,20},{20,16},{24,28},{28,24},{1,5},{5... | collective-permute-start | bytes 393224 | tf_op jit(solution)/shard_map/ppermute | solution.py:40
  33.5 12.7 %collective-permute-start.7 = (bf16[256,256]{1,0:T(8,128)(2,1)S(1)}, bf16[256,256]{1,0:T(8,128)(2,1)S(1)}, u32[]{:S(2)}, u32[]{:S(2)}) collective-permute-start(bf16[256,256]{1,0:T(8,128)(2,1)S(1)} %get-tuple-element.52.refs_7_), channel_id=1, source_target_pairs={{0,4},{4,0},{8,12},{12,8},{16,20},{20,16},{24,28},{28,24},{1,5},{5... | collective-permute-start | bytes 393224 | tf_op jit(solution)/shard_map/ppermute | solution.py:40
  38.0 13.1 %collective-permute-start.12 = (bf16[256,256]{1,0:T(8,128)(2,1)S(1)}, bf16[256,256]{1,0:T(8,128)(2,1)S(1)}, u32[]{:S(2)}, u32[]{:S(2)}) collective-permute-start(bf16[256,256]{1,0:T(8,128)(2,1)S(1)} %get-tuple-element.60.refs_8_), channel_id=1, source_target_pairs={{0,20},{4,16},{8,28},{12,24},{16,4},{20,0},{24,12},{28,8},{1,21},{... | collective-permute-start | bytes 393224 | tf_op jit(solution)/shard_map/ppermute | solution.py:40
  38.9 12.3 %collective-permute-start.13 = (bf16[256,256]{1,0:T(8,128)(2,1)S(1)}, bf16[256,256]{1,0:T(8,128)(2,1)S(1)}, u32[]{:S(2)}, u32[]{:S(2)}) collective-permute-start(bf16[256,256]{1,0:T(8,128)(2,1)S(1)} %get-tuple-element.61.refs_6_), channel_id=1, source_target_pairs={{0,28},{4,24},{8,20},{12,16},{16,12},{20,8},{24,4},{28,0},{1,29},{... | collective-permute-start | bytes 393224 | tf_op jit(solution)/shard_map/ppermute | solution.py:40
  52.9 12.5 %collective-permute-start.14 = (bf16[256,256]{1,0:T(8,128)(2,1)S(1)}, bf16[256,256]{1,0:T(8,128)(2,1)S(1)}, u32[]{:S(2)}, u32[]{:S(2)}) collective-permute-start(bf16[256,256]{1,0:T(8,128)(2,1)S(1)} %get-tuple-element.64), channel_id=1, source_target_pairs={{0,16},{4,20},{8,24},{12,28},{16,0},{20,4},{24,8},{28,12},{1,17},{... | collective-permute-start | bytes 393224 | tf_op jit(solution)/shard_map/ppermute | solution.py:40
  60.1 8.3 %collective-permute-start.15 = (bf16[256,256]{1,0:T(8,128)(2,1)S(1)}, bf16[256,256]{1,0:T(8,128)(2,1)S(1)}, u32[]{:S(2)}, u32[]{:S(2)}) collective-permute-start(bf16[256,256]{1,0:T(8,128)(2,1)S(1)} %get-tuple-element.66), channel_id=1, source_target_pairs={{0,24},{4,28},{8,16},{12,20},{16,8},{20,12},{24,0},{28,4},{1,25},{... | collective-permute-start | bytes 393224 | tf_op jit(solution)/shard_map/ppermute | solution.py:40
  61.4 9.8 %collective-permute-start.16 = (bf16[256,256]{1,0:T(8,128)(2,1)S(1)}, bf16[256,256]{1,0:T(8,128)(2,1)S(1)}, u32[]{:S(2)}, u32[]{:S(2)}) collective-permute-start(bf16[256,256]{1,0:T(8,128)(2,1)S(1)} %get-tuple-element.67), channel_id=1, source_target_pairs={{0,8},{4,12},{8,0},{12,4},{16,24},{20,28},{24,16},{28,20},{1,9},{5... | collective-permute-start | bytes 393224 | tf_op jit(solution)/shard_map/ppermute | solution.py:40
  61.4 14.7 %collective-permute-start.17 = (bf16[256,256]{1,0:T(8,128)(2,1)S(1)}, bf16[256,256]{1,0:T(8,128)(2,1)S(1)}, u32[]{:S(2)}, u32[]{:S(2)}) collective-permute-start(bf16[256,256]{1,0:T(8,128)(2,1)S(1)} %get-tuple-element.68), channel_id=1, source_target_pairs={{0,20},{4,16},{8,28},{12,24},{16,4},{20,0},{24,12},{28,8},{1,21},{... | collective-permute-start | bytes 393224 | tf_op jit(solution)/shard_map/ppermute | solution.py:40
  64.7 11.9 %collective-permute-start.18 = (bf16[256,256]{1,0:T(8,128)(2,1)S(1)}, bf16[256,256]{1,0:T(8,128)(2,1)S(1)}, u32[]{:S(2)}, u32[]{:S(2)}) collective-permute-start(bf16[256,256]{1,0:T(8,128)(2,1)S(1)} %get-tuple-element.72), channel_id=1, source_target_pairs={{0,12},{4,8},{8,4},{12,0},{16,28},{20,24},{24,20},{28,16},{1,13},{... | collective-permute-start | bytes 393224 | tf_op jit(solution)/shard_map/ppermute | solution.py:40
  65.4 12.4 %collective-permute-start.19 = (bf16[256,256]{1,0:T(8,128)(2,1)S(1)}, bf16[256,256]{1,0:T(8,128)(2,1)S(1)}, u32[]{:S(2)}, u32[]{:S(2)}) collective-permute-start(bf16[256,256]{1,0:T(8,128)(2,1)S(1)} %get-tuple-element.73), channel_id=1, source_target_pairs={{0,28},{4,24},{8,20},{12,16},{16,12},{20,8},{24,4},{28,0},{1,29},{... | collective-permute-start | bytes 393224 | tf_op jit(solution)/shard_map/ppermute | solution.py:40
  68.4 11.0 %collective-permute-start.20 = (bf16[256,256]{1,0:T(8,128)(2,1)S(1)}, bf16[256,256]{1,0:T(8,128)(2,1)S(1)}, u32[]{:S(2)}, u32[]{:S(2)}) collective-permute-start(bf16[256,256]{1,0:T(8,128)(2,1)S(1)} %get-tuple-element.74), channel_id=1, source_target_pairs={{0,4},{4,0},{8,12},{12,8},{16,20},{20,16},{24,28},{28,24},{1,5},{5... | collective-permute-start | bytes 393224 | tf_op jit(solution)/shard_map/ppermute | solution.py:40
  79.7 1.2 %collective-permute-start.21 = (f32[1,256]{1,0:T(1,128)S(1)}, f32[1,256]{1,0:T(1,128)S(1)}, u32[]{:S(2)}, u32[]{:S(2)}) collective-permute-start(f32[1,256]{1,0:T(1,128)S(1)} %get-tuple-element.76), channel_id=1, source_target_pairs={{0,1},{1,0},{2,3},{3,2},{4,5},{5,4},{6,7},{7,6},{8,9},{9,8},{10,11... | collective-permute-start | bytes 3080 | tf_op jit(solution)/shard_map/ppermute | solution.py:454
  80.9 3.6 %collective-permute-start.22 = (f32[1,256]{1,0:T(1,128)S(1)}, f32[1,256]{1,0:T(1,128)S(1)}, u32[]{:S(2)}, u32[]{:S(2)}) collective-permute-start(f32[1,256]{1,0:T(1,128)S(1)} %add.6), channel_id=1, source_target_pairs={{0,2},{1,3},{2,0},{3,1},{4,6},{5,7},{6,4},{7,5},{8,10},{9,11},{10,... | collective-permute-start | bytes 3080 | tf_op jit(solution)/shard_map/ppermute | solution.py:454
  (11 other events, 84.2 us)
